TPU v7x, 32 devices: a whole 2x2x4 slice. The times are simulated.
32 devices in a mesh: dp: 2 (over y), expert: 16 (over z, x, core).
Axes of the slice: x: 2, y: 2, z: 4, core: 2. Of those that a mesh axis runs over, the one named last changes fastest.
Arguments:
- tokens: bfloat16 [32768, 768], P(('dp', 'expert')), may hold values from -6 to 6
- seq_ids: int32 [32768], P(('dp', 'expert')), may hold values from 0 to 3, as said below
- routes: int32 [32768, 1], P(('dp', 'expert')), may hold values from 0 to 15; in each aligned block of 1024 rows (0 to 1023, 1024 to 2047, ...) at most 128 rows name the same one
- cotangent: bfloat16 [32768, 768], P(('dp', 'expert')), may hold values from -6 to 6
- w_query: bfloat16 [768, 768], P(('dp', 'expert')), may hold values from -0.02734375 to 0.02734375
- w_key: bfloat16 [768, 768], P(('dp', 'expert')), may hold values from -0.21875 to 0.21875
- w_value: bfloat16 [768, 768], P(('dp', 'expert')), may hold values from -0.21875 to 0.21875
- w_out: bfloat16 [768, 768], P(('dp', 'expert')), may hold values from -3.5 to 3.5
- rel_table: bfloat16 [32, 12], P('dp'), may hold values from -6 to 6
- gain_attn: bfloat16 [768], P(('dp', 'expert')), may hold values from 0.099609375 to 1.8984375
- gain_ffn: bfloat16 [768], P(('dp', 'expert')), may hold values from 0.099609375 to 1.8984375
- router: bfloat16 [768, 16], P(('dp', 'expert')), may hold values from -0.109375 to 0.109375
- expert_in: bfloat16 [16, 768, 3072], P('expert', 'dp'), may hold values from -0.21875 to 0.21875
- expert_out: bfloat16 [16, 3072, 768], P('expert', 'dp'), may hold values from -10 to 10
Outputs:
- mixed: float32 [32768, 768], P(('dp', 'expert'))
- grad_tokens: float32 [32768, 768], P(('dp', 'expert'))
- grad_w_query: float32 [768, 768], P(('dp', 'expert'))
- grad_w_key: float32 [768, 768], P(('dp', 'expert'))
- grad_w_value: float32 [768, 768], P(('dp', 'expert'))
- grad_w_out: float32 [768, 768], P(('dp', 'expert'))
- grad_rel_table: float32 [32, 12], P('dp')
- grad_gain_attn: float32 [768], P(('dp', 'expert'))
- grad_gain_ffn: float32 [768], P(('dp', 'expert'))
- grad_router: float32 [768, 16], P(('dp', 'expert'))
- grad_expert_in: float32 [16, 768, 3072], P('expert', 'dp')
- grad_expert_out: float32 [16, 3072, 768], P('expert', 'dp')
Inputs may be any that keep to these rules, and one draw needn't show every extreme that they name: `seq_ids`: within each device's 1024 tokens the ids never fall; tokens with equal ids on one device form one sequence; some device holds a single sequence of all its 1024 tokens. `routes`: no expert is named by more than 128 of one device's tokens.
All inputs are finite; a program needn't handle non-finite values.
Results may differ from a plain program's by a relative error of at most 0.015.
Values may be sent and summed in bfloat16 or wider, within the bound.
No kernel may reach another device: no remote copies, remote signals or barrier semaphores. Data moves between devices by JAX's collectives and lax.ppermute only.
A program may use at most 320 MiB of HBM per device.

v0:
```python
import functools

import jax
import jax.numpy as jnp
from jax import lax
from jax.experimental import pallas as pl
from jax.experimental.pallas import tpu as pltpu
from jax.sharding import PartitionSpec as P

D = 768
HEADS = 12
HEAD_DIM = 64
BUCKETS = 32
TOK = 1024
TILE = 128
TILES = TOK // TILE
QBLK = 256
FF_TILE = 512
HALVES = 2
SPLIT = 3 * D // 2
LANES = 128

EPSILON = 1e-06
DISTANCE_EDGES = (12, 16, 23, 32, 46, 64, 91)
FAR_BEFORE = 15
FAR_AFTER = 31
UNPAIRED = -1e30
BF = jnp.bfloat16
F32 = jnp.float32
VMEM_LIMIT = 56 * 1024 * 1024


def dot(left, right, left_dim=1, right_dim=0):
    return lax.dot_general(
        left, right, (((left_dim,), (right_dim,)), ((), ())), preferred_element_type=F32
    )


def params(semantics=None):
    return pltpu.CompilerParams(vmem_limit_bytes=VMEM_LIMIT, dimension_semantics=semantics)


def cost(flops, bytes_accessed, transcendentals=0):
    return pl.CostEstimate(
        flops=int(flops), bytes_accessed=int(bytes_accessed), transcendentals=int(transcendentals)
    )


def whole(shape):
    return pl.BlockSpec(shape, lambda *_: (0,) * len(shape))


def inverse_rms(values):
    return lax.rsqrt(jnp.mean(values * values, axis=-1, keepdims=True) + EPSILON)


def bucket_of(offset):
    distance = jnp.abs(offset)
    distant = 8 + sum(((distance >= boundary).astype(jnp.int32) for boundary in DISTANCE_EDGES))
    return jnp.where(distance < 8, distance, distant) + jnp.where(offset > 0, 16, 0)


def place_in_buffers(route, rank, experts, capacity):
    share = capacity // HALVES
    part = (rank >= share).astype(jnp.int32)
    return part * (experts * share) + route * share + (rank - part * share)


def slots_kernel(experts, capacity, route_col, route_row, cot, slot_col, slot_row, sending):
    padded = -(-experts // LANES) * LANES
    picked = (
        lax.broadcasted_iota(jnp.int32, (TOK, padded), 1) == route_col[...]
    ).astype(BF)
    picked_t = (
        lax.broadcasted_iota(jnp.int32, (padded, TOK), 0) == route_row[...]
    ).astype(BF)
    upto = (
        lax.broadcasted_iota(jnp.int32, (TOK, TOK), 0)
        <= lax.broadcasted_iota(jnp.int32, (TOK, TOK), 1)
    ).astype(BF)
    from_t = (
        lax.broadcasted_iota(jnp.int32, (TOK, TOK), 0)
        >= lax.broadcasted_iota(jnp.int32, (TOK, TOK), 1)
    ).astype(BF)
    counts = dot(from_t, picked) * picked.astype(F32)
    rank = jnp.sum(counts, axis=1, keepdims=True).astype(jnp.int32) - 1
    slot_col[...] = place_in_buffers(route_col[...], rank, experts, capacity)
    counts_t = dot(picked_t, upto) * picked_t.astype(F32)
    rank_row = jnp.sum(counts_t, axis=0, keepdims=True).astype(jnp.int32) - 1
    slot_row[...] = place_in_buffers(route_row[...], rank_row, experts, capacity)
    dispatch(route_row[...] * capacity + rank_row, cot[...], [sending])


def dispatch(row, rows, parts):
    step = 512
    offset = 0
    for sending in parts:
        for first in range(0, sending.shape[0], step):
            chosen = (
                lax.broadcasted_iota(jnp.int32, (step, TOK), 0) + (first + offset) == row
            ).astype(BF)
            sending[first : first + step, :] = dot(chosen, rows).astype(BF)
        offset += sending.shape[0]


def make_slots(routes, cotangent, experts, capacity):
    total = experts * capacity
    return pl.pallas_call(
        functools.partial(slots_kernel, experts, capacity),
        out_shape=(
            jax.ShapeDtypeStruct((TOK, 1), jnp.int32),
            jax.ShapeDtypeStruct((1, TOK), jnp.int32),
            jax.ShapeDtypeStruct((total, D), BF),
        ),
        compiler_params=params(),
        cost_estimate=cost(2 * total * TOK * D, 6 * total * D),
        name="slots",
    )(routes, routes.reshape(1, TOK), cotangent)


def project_kernel(tokens, gain, left, right, normed, qkv):
    x = tokens[...].astype(F32)
    low = (x * inverse_rms(x) * gain[...]).astype(BF)
    normed[...] = low
    qkv[:, :SPLIT] = dot(low, left[...]).astype(BF)
    qkv[:, SPLIT:] = dot(low, right[:, :SPLIT]).astype(BF)


def project(tokens, gain, left, right):
    block = 256
    rows = pl.BlockSpec((block, D), lambda r: (r, 0))
    return pl.pallas_call(
        project_kernel,
        grid=(TOK // block,),
        in_specs=[rows, whole((1, D)), whole(left.shape), whole(right.shape)],
        out_specs=[rows, pl.BlockSpec((block, 3 * D), lambda r: (r, 0))],
        out_shape=[
            jax.ShapeDtypeStruct((TOK, D), BF),
            jax.ShapeDtypeStruct((TOK, 3 * D), BF),
        ],
        compiler_params=params(("arbitrary",)),
        cost_estimate=cost(6 * TOK * D * D, 12 * TOK * D),
        name="project",
    )(tokens, gain, left, right)


def lane_features(seq_col, rel_table):
    lane = jnp.arange(LANES, dtype=jnp.int32)[None, :]
    feature = lane % HEAD_DIM
    tile = jnp.arange(TOK, dtype=jnp.int32)[:, None] // TILE
    on_tile = feature - 4
    query_features = jnp.where(
        feature < 4,
        jnp.where(feature == seq_col, 0.0, UNPAIRED),
        jnp.where(on_tile == tile, 1.0, 0.0),
    ).astype(BF)
    wide = jnp.arange(D, dtype=jnp.int32)[None, :]
    feature = wide % HEAD_DIM
    on_tile = feature - 4
    swapped = jnp.arange(HEADS, dtype=jnp.int32) ^ 1
    before = jnp.repeat(rel_table[FAR_BEFORE][swapped], HEAD_DIM)[None, :]
    after = jnp.repeat(rel_table[FAR_AFTER][swapped], HEAD_DIM)[None, :]
    apart = tile - on_tile
    far = jnp.where(apart >= 2, after, jnp.where(apart <= -2, before, 0.0))
    key_features = jnp.where(
        feature < 4,
        jnp.where(feature == seq_col, 1.0, 0.0),
        jnp.where(on_tile < TILES, far, 0.0),
    ).astype(BF)
    return query_features, key_features


def band_offsets():
    place = jnp.arange(4 * LANES, dtype=jnp.int32)
    return 255 - (place + 383) % 512


def band_onehot():
    return (
        bucket_of(band_offsets())[:, None] == jnp.arange(BUCKETS, dtype=jnp.int32)[None, :]
    ).astype(F32)


def near_rows(tile):
    first = max(tile - 1, 0)
    last = min(tile + 2, TILES)
    return first, last


def spread_band(values):
    wide = jnp.broadcast_to(values, (3 * TILE, 4 * LANES))
    return pltpu.roll(wide, 0, 1, stride=1, stride_axis=0)[:, :TILE]


def attend_kernel(q_ref, k_ref, v_ref, qx_ref, kx_ref, band_ref, out_ref, lse_ref, st, pb, ot):
    low = lax.broadcasted_iota(jnp.int32, (TOK, LANES), 1) < HEAD_DIM
    v_t = v_ref[...].astype(F32).T.astype(BF)
    for side in range(2):
        own = low if side == 0 else ~low
        queries = jnp.where(own, q_ref[...], qx_ref[...])
        keys = jnp.where(own, k_ref[...], kx_ref[...])
        band = spread_band(band_ref[side])
        for block in range(TOK // QBLK):
            rows = slice(block * QBLK, (block + 1) * QBLK)
            slot = block % 2
            st[slot] = dot(keys, queries[rows], 1, 1)
            for part in range(QBLK // TILE):
                tile = block * (QBLK // TILE) + part
                first, last = near_rows(tile)
                at = (slot, slice(first * TILE, last * TILE), slice(part * TILE, (part + 1) * TILE))
                st[at] += band[(first - tile + 1) * TILE : (last - tile + 1) * TILE]
            top = jnp.max(st[slot, 0:TILE], axis=0, keepdims=True)
            for chunk in range(1, TILES):
                top = jnp.maximum(
                    top,
                    jnp.max(
                        st[slot, chunk * TILE : (chunk + 1) * TILE], axis=0, keepdims=True
                    ),
                )
            total = jnp.zeros((1, QBLK), F32)
            for chunk in range(TILES):
                at = slice(chunk * TILE, (chunk + 1) * TILE)
                raised = jnp.exp(st[slot, at] - top)
                total = total + jnp.sum(raised, axis=0, keepdims=True)
                pb[slot, at] = raised.astype(BF)
            half = slice(side * HEAD_DIM, (side + 1) * HEAD_DIM)
            ot[half, rows] = dot(v_t[half], pb[slot]) * (1.0 / total)
            lse_ref[side, :, rows] = top + jnp.log(total)
    out_ref[...] = ot[...].T.astype(BF)


def attend(qkv, query_features, key_features, band):
    pairs = HEADS // 2
    return pl.pallas_call(
        attend_kernel,
        grid=(pairs,),
        in_specs=[
            pl.BlockSpec((TOK, LANES), lambda p: (0, p)),
            pl.BlockSpec((TOK, LANES), lambda p: (0, p + pairs)),
            pl.BlockSpec((TOK, LANES), lambda p: (0, p + 2 * pairs)),
            whole((TOK, LANES)),
            pl.BlockSpec((TOK, LANES), lambda p: (0, p)),
            pl.BlockSpec((2, 1, 4 * LANES), lambda p: (p, 0, 0)),
        ],
        out_specs=[
            pl.BlockSpec((TOK, LANES), lambda p: (0, p)),
            pl.BlockSpec((2, 1, TOK), lambda p: (p, 0, 0)),
        ],
        out_shape=[
            jax.ShapeDtypeStruct((TOK, D), BF),
            jax.ShapeDtypeStruct((HEADS, 1, TOK), F32),
        ],
        scratch_shapes=[
            pltpu.VMEM((2, TOK, QBLK), F32),
            pltpu.VMEM((2, TOK, QBLK), BF),
            pltpu.VMEM((LANES, TOK), F32),
        ],
        compiler_params=params(("arbitrary",)),
        cost_estimate=cost(2 * 3 * HEADS * TOK * TOK * 256, 10 * TOK * D, HEADS * TOK * TOK),
        name="attend",
    )(qkv, qkv, qkv, query_features, key_features, band)


def attend_back_kernel(
    q_ref, k_ref, v_ref, do_ref, qx_ref, kx_ref, lse_ref, band_ref,
    dq_ref, dk_ref, dv_ref, tiles_ref, diag_ref,
    st, dp, pb, sb, dqt, dkt, dvt, near,
):
    low = lax.broadcasted_iota(jnp.int32, (TOK, LANES), 1) < HEAD_DIM
    k_t = k_ref[...].astype(F32).T.astype(BF)
    for side in range(2):
        own = low if side == 0 else ~low
        queries = jnp.where(own, q_ref[...], qx_ref[...])
        keys = jnp.where(own, k_ref[...], kx_ref[...])
        values = jnp.where(own, v_ref[...], jnp.zeros((), BF))
        band = spread_band(band_ref[side])
        near[...] = jnp.zeros_like(near)
        half = slice(side * HEAD_DIM, (side + 1) * HEAD_DIM)
        for block in range(TOK // QBLK):
            rows = slice(block * QBLK, (block + 1) * QBLK)
            slot = block % 2
            st[slot] = dot(keys, queries[rows], 1, 1)
            dp[slot] = dot(values, do_ref[rows, :], 1, 1)
            for part in range(QBLK // TILE):
                tile = block * (QBLK // TILE) + part
                first, last = near_rows(tile)
                at = (slot, slice(first * TILE, last * TILE), slice(part * TILE, (part + 1) * TILE))
                st[at] += band[(first - tile + 1) * TILE : (last - tile + 1) * TILE]
            lse = lse_ref[side, :, rows]
            spread = jnp.zeros((1, QBLK), F32)
            for chunk in range(TILES):
                at = slice(chunk * TILE, (chunk + 1) * TILE)
                weights = jnp.exp(st[slot, at] - lse)
                st[slot, at] = weights
                pb[slot, at] = weights.astype(BF)
                spread = spread + jnp.sum(weights * dp[slot, at], axis=0, keepdims=True)
            for chunk in range(TILES):
                at = slice(chunk * TILE, (chunk + 1) * TILE)
                sb[slot, at] = (st[slot, at] * (dp[slot, at] - spread)).astype(BF)
            for part in range(QBLK // TILE):
                tile = block * (QBLK // TILE) + part
                first, last = near_rows(tile)
                at = (slot, slice(first * TILE, last * TILE), slice(part * TILE, (part + 1) * TILE))
                near[(first - tile + 1) * TILE : (last - tile + 1) * TILE, :TILE] += sb[at].astype(F32)
            dv = dot(pb[slot], do_ref[rows, :])
            dk = dot(sb[slot], queries[rows])
            if block == 0:
                dvt[side] = dv
                dkt[side] = dk
            else:
                dvt[side] += dv
                dkt[side] += dk
            dqt[half, rows] = dot(k_t[half], sb[slot])
        for tile in range(TILES):
            tiles_ref[side, tile : tile + 1, :] = jnp.sum(
                dkt[side, tile * TILE : (tile + 1) * TILE], axis=0, keepdims=True
            )
        folded = near[0:8, :]
        for first in range(8, 3 * TILE, 8):
            folded = folded + pltpu.roll(near[first : first + 8, :], 4 * LANES - first, 1)
        diagonal = folded[0:1]
        for row in range(1, 8):
            diagonal = diagonal + pltpu.roll(folded[row : row + 1], 4 * LANES - row, 1)
        diag_ref[side] = diagonal
    dq_ref[...] = dqt[...].T.astype(BF)
    dk_ref[...] = jnp.where(low, dkt[0], dkt[1]).astype(BF)
    dv_ref[...] = jnp.where(low, dvt[0], dvt[1]).astype(BF)


def attend_back(qkv, grad_context, query_features, key_features, lse, band):
    pairs = HEADS // 2
    column = pl.BlockSpec((TOK, LANES), lambda p: (0, p))
    return pl.pallas_call(
        attend_back_kernel,
        grid=(pairs,),
        in_specs=[
            column,
            pl.BlockSpec((TOK, LANES), lambda p: (0, p + pairs)),
            pl.BlockSpec((TOK, LANES), lambda p: (0, p + 2 * pairs)),
            column,
            whole((TOK, LANES)),
            column,
            pl.BlockSpec((2, 1, TOK), lambda p: (p, 0, 0)),
            pl.BlockSpec((2, 1, 4 * LANES), lambda p: (p, 0, 0)),
        ],
        out_specs=[
            column,
            column,
            column,
            pl.BlockSpec((2, TILES, LANES), lambda p: (p, 0, 0)),
            pl.BlockSpec((2, 1, 4 * LANES), lambda p: (p, 0, 0)),
        ],
        out_shape=[
            jax.ShapeDtypeStruct((TOK, D), BF),
            jax.ShapeDtypeStruct((TOK, D), BF),
            jax.ShapeDtypeStruct((TOK, D), BF),
            jax.ShapeDtypeStruct((HEADS, TILES, LANES), F32),
            jax.ShapeDtypeStruct((HEADS, 1, 4 * LANES), F32),
        ],
        scratch_shapes=[
            pltpu.VMEM((2, TOK, QBLK), F32),
            pltpu.VMEM((2, TOK, QBLK), F32),
            pltpu.VMEM((2, TOK, QBLK), BF),
            pltpu.VMEM((2, TOK, QBLK), BF),
            pltpu.VMEM((LANES, TOK), F32),
            pltpu.VMEM((2, TOK, LANES), F32),
            pltpu.VMEM((2, TOK, LANES), F32),
            pltpu.VMEM((3 * TILE, 4 * LANES), F32),
        ],
        compiler_params=params(("arbitrary",)),
        cost_estimate=cost(2 * 5 * HEADS * TOK * TOK * 256, 16 * TOK * D, HEADS * TOK * TOK),
        name="attend_back",
    )(qkv, qkv, qkv, grad_context, query_features, key_features, lse, band)


def table_gradient(tiles, diagonals):
    near = jnp.einsum(
        "hl,lb->bh", diagonals[:, 0, :], band_onehot(), precision=lax.Precision.HIGHEST
    )
    sums = jnp.concatenate(
        [tiles[h : h + 1, :, (HEAD_DIM if h % 2 == 0 else 0) + 4 :][:, :, :TILES] for h in range(HEADS)],
        axis=0,
    )
    apart = (
        jnp.arange(TILES, dtype=jnp.int32)[:, None] - jnp.arange(TILES, dtype=jnp.int32)[None, :]
    )[None]
    before = jnp.sum(jnp.where(apart <= -2, sums, 0.0), axis=(1, 2))
    after = jnp.sum(jnp.where(apart >= 2, sums, 0.0), axis=(1, 2))
    place = jnp.arange(BUCKETS, dtype=jnp.int32)[:, None]
    return (
        near
        + jnp.where(place == FAR_BEFORE, before[None, :], 0.0)
        + jnp.where(place == FAR_AFTER, after[None, :], 0.0)
    )


def middle_kernel(context, tokens, w_out, gain, router, route_col, slot_row, experts,
                  middle, sending_low, sending_high, gate, normed):
    for first in range(0, TOK, 256):
        at = slice(first, first + 256)
        mid = tokens[at, :].astype(F32) + dot(context[at, :], w_out[...])
        middle[at, :] = mid
        low = (mid * inverse_rms(mid) * gain[...]).astype(BF)
        normed[at, :] = low
        probs = router_softmax(low, router[...], experts)
        lane = lax.broadcasted_iota(jnp.int32, probs.shape, 1)
        gate[at, :] = jnp.sum(
            jnp.where(lane == route_col[at, :], probs, 0.0), axis=1, keepdims=True
        )
    dispatch(slot_row[...], normed[...], [sending_low, sending_high])


def router_softmax(rows, router, experts):
    logits = dot(rows, router)
    lane = lax.broadcasted_iota(jnp.int32, logits.shape, 1)
    logits = jnp.where(lane < experts, logits, UNPAIRED)
    raised = jnp.exp(logits - jnp.max(logits, axis=1, keepdims=True))
    return raised / jnp.sum(raised, axis=1, keepdims=True)


def make_middle(context, tokens, w_out, gain, router, routes, slot_row, experts, capacity):
    total = experts * capacity

    def kernel(*refs):
        middle_kernel(*refs[:7], experts, *refs[7:])

    return pl.pallas_call(
        kernel,
        out_shape=(
            jax.ShapeDtypeStruct((TOK, D), F32),
            jax.ShapeDtypeStruct((total // 2, D), BF),
            jax.ShapeDtypeStruct((total // 2, D), BF),
            jax.ShapeDtypeStruct((TOK, 1), F32),
        ),
        scratch_shapes=[pltpu.VMEM((TOK, D), BF)],
        compiler_params=params(),
        cost_estimate=cost(2 * total * TOK * D + 2 * TOK * D * D, 12 * TOK * D + 2 * total * D),
        name="middle",
    )(context, tokens, w_out, gain, router, routes, slot_row)


def gelu_parts(v):
    size = jnp.abs(v)
    t = 1.0 / (1.0 + (0.3275911 * 0.7071067811865476) * size)
    bell = jnp.exp(-0.5 * (v * v))
    series = t * (
        0.5 * 0.254829592
        + t * (0.5 * -0.284496736 + t * (0.5 * 1.421413741 + t * (0.5 * -1.453152027 + t * (0.5 * 1.061405429))))
    )
    tail = series * bell
    phi = jnp.where(v < 0, tail, 1.0 - tail)
    return v * phi, phi + v * (bell * 0.3989422804014327)


def expert_kernel(experts, x, c3, w_first, w_second, router, router_t, mine,
                  act_ref, dh_ref, result, grad_x, gate_ref, grad_router, acc_r, acc_x):
    step = pl.program_id(0)
    rows = x.shape[0]
    chunk = 256
    per = chunk // c3.shape[1]
    for first in range(0, rows, chunk):
        at = slice(first, first + chunk)
        hidden = dot(x[at, :], w_first[...])
        cot = c3[first // chunk * per : (first // chunk + 1) * per].reshape(chunk, D)
        grad_act = dot(cot, w_second[...], 1, 1)
        act, slope = gelu_parts(hidden)
        act = act.astype(BF)
        grad_hidden = (grad_act * slope).astype(BF)
        act_ref[at, :] = act
        dh_ref[at, :] = grad_hidden
        part_r = dot(act, w_second[...])
        part_x = dot(grad_hidden, w_first[...], 1, 1)

        @pl.when(step == 0)
        def _():
            acc_r[at, :] = part_r
            acc_x[at, :] = part_x

        @pl.when(step > 0)
        def _():
            acc_r[at, :] += part_r
            acc_x[at, :] += part_x

    @pl.when(step == pl.num_programs(0) - 1)
    def _():
        total_router = jnp.zeros(grad_router.shape, F32)
        for first in range(0, rows, chunk):
            at = slice(first, first + chunk)
            rounded = acc_r[at, :].astype(BF)
            result[at, :] = rounded
            probs = router_softmax(x[at, :], router[...], experts)
            lane = lax.broadcasted_iota(jnp.int32, probs.shape, 1)
            here = lane == mine[0, 0]
            gate = jnp.sum(jnp.where(here, probs, 0.0), axis=1, keepdims=True)
            grad_gate = jnp.sum(
                c3[first // chunk * per : (first // chunk + 1) * per].reshape(chunk, D).astype(F32) * rounded.astype(F32), axis=1, keepdims=True
            )
            grad_logits = (
                probs * (jnp.where(here, grad_gate, 0.0) - gate * grad_gate)
            ).astype(BF)
            gate_ref[at, :] = gate
            grad_x[at, :] = (acc_x[at, :] * gate + dot(grad_logits, router_t[...])).astype(BF)
            total_router = total_router + dot(x[at, :], grad_logits, 0, 0)
        grad_router[...] = total_router


def run_expert(part, x, c, w_first, w_second, router, router_t, mine, experts):
    rows = x.shape[0]
    hidden_size = w_first.shape[1]
    lanes = router.shape[1]
    return pl.pallas_call(
        functools.partial(expert_kernel, experts),
        grid=(hidden_size // FF_TILE,),
        in_specs=[
            whole((rows, D)),
            pl.BlockSpec((c.shape[0], c.shape[1] // HALVES, D), lambda f: (0, part, 0)),
            pl.BlockSpec((D, FF_TILE), lambda f: (0, f)),
            pl.BlockSpec((FF_TILE, D), lambda f: (f, 0)),
            whole((D, lanes)),
            whole((lanes, D)),
            pl.BlockSpec(memory_space=pltpu.SMEM),
        ],
        out_specs=[
            pl.BlockSpec((rows, FF_TILE), lambda f: (0, f)),
            pl.BlockSpec((rows, FF_TILE), lambda f: (0, f)),
            whole((rows, D)),
            whole((rows, D)),
            whole((rows, 1)),
            whole((D, lanes)),
        ],
        out_shape=[
            jax.ShapeDtypeStruct((rows, hidden_size), BF),
            jax.ShapeDtypeStruct((rows, hidden_size), BF),
            jax.ShapeDtypeStruct((rows, D), BF),
            jax.ShapeDtypeStruct((rows, D), BF),
            jax.ShapeDtypeStruct((rows, 1), F32),
            jax.ShapeDtypeStruct((D, lanes), F32),
        ],
        scratch_shapes=[pltpu.VMEM((rows, D), F32), pltpu.VMEM((rows, D), F32)],
        compiler_params=params(("arbitrary",)),
        cost_estimate=cost(
            8 * rows * D * hidden_size, 4 * rows * hidden_size + 4 * D * hidden_size
        ),
        name="expert",
    )(x, c, w_first, w_second, router, router_t, mine)


def expert_weights_kernel(parts, *refs):
    xs, gates = refs[:parts], refs[parts : 2 * parts]
    acts, dhs = refs[2 * parts : 3 * parts], refs[3 * parts : 4 * parts]
    cots, grad_first, grad_second, x_t, c_t = refs[4 * parts :]
    rows = xs[0].shape[0]
    share = cots.shape[1] // parts
    chunk = 256
    per = chunk // share

    @pl.when(pl.program_id(0) == 0)
    def _():
        for part in range(parts):
            for first in range(0, rows, chunk):
                at = slice(first, first + chunk)
                to = slice(part * rows + first, part * rows + first + chunk)
                gate = gates[part][at, :]
                x_t[:, to] = (xs[part][at, :].astype(F32) * gate).T.astype(BF)
                cot = cots[
                    first // chunk * per : (first // chunk + 1) * per,
                    part * share : (part + 1) * share,
                ].reshape(chunk, D)
                c_t[:, to] = (cot.astype(F32) * gate).T.astype(BF)

    first_sum, second_sum = None, None
    for part in range(parts):
        at = slice(part * rows, (part + 1) * rows)
        one = dot(x_t[:, at], dhs[part][...])
        two = dot(c_t[:, at], acts[part][...])
        first_sum = one if first_sum is None else first_sum + one
        second_sum = two if second_sum is None else second_sum + two
    grad_first[...] = first_sum.astype(BF)
    grad_second[...] = second_sum.T.astype(BF)


def expert_weights(xs, cots, gates, acts, dhs):
    parts = len(xs)
    rows = xs[0].shape[0]
    hidden_size = acts[0].shape[1]
    tile = pl.BlockSpec((rows, FF_TILE), lambda f: (0, f))
    return pl.pallas_call(
        functools.partial(expert_weights_kernel, parts),
        grid=(hidden_size // FF_TILE,),
        in_specs=[whole((rows, D))] * parts
        + [whole((rows, 1))] * parts
        + [tile] * (2 * parts)
        + [whole(cots.shape)],
        out_specs=[
            pl.BlockSpec((D, FF_TILE), lambda f: (0, f)),
            pl.BlockSpec((FF_TILE, D), lambda f: (f, 0)),
        ],
        out_shape=[
            jax.ShapeDtypeStruct((D, hidden_size), BF),
            jax.ShapeDtypeStruct((hidden_size, D), BF),
        ],
        scratch_shapes=[
            pltpu.VMEM((D, parts * rows), BF),
            pltpu.VMEM((D, parts * rows), BF),
        ],
        compiler_params=params(("arbitrary",)),
        cost_estimate=cost(
            4 * parts * rows * D * hidden_size, 4 * (parts * rows + D) * hidden_size
        ),
        name="expert_weights",
    )(*xs, *gates, *acts, *dhs, cots)


def rms_back(values, factor, grad):
    inverse = inverse_rms(values)
    scaled = grad * factor
    mean = jnp.mean(scaled * values, axis=-1, keepdims=True)
    return (
        inverse * scaled - values * (inverse * inverse * inverse * mean),
        jnp.sum(grad * values * inverse, axis=0, keepdims=True),
    )


def undispatch(slot_col, parts):
    out = None
    offset = 0
    for part in parts:
        total = part.shape[0]
        place = lax.broadcasted_iota(jnp.int32, (slot_col.shape[0], total), 1) + offset
        found = dot((place == slot_col).astype(BF), part[...])
        out = found if out is None else out + found
        offset += total
    return out


def middle_back_kernel(parts, *refs):
    backs = refs[:parts]
    slot_col, middle, cot, gain, w_out, grad_middle, grad_attn, grad_context, grad_gain = refs[parts:]
    grad_normed = undispatch(slot_col[...], backs)
    part, gain_part = rms_back(middle[...], gain[...], grad_normed)
    grad = cot[...].astype(F32) + part
    grad_middle[...] = grad
    low = grad.astype(BF)
    grad_attn[...] = low
    grad_context[...] = dot(low, w_out[...], 1, 1).astype(BF)

    @pl.when(pl.program_id(0) == 0)
    def _():
        grad_gain[...] = gain_part

    @pl.when(pl.program_id(0) > 0)
    def _():
        grad_gain[...] += gain_part


def middle_back(backs, slot_col, middle, cot, gain, w_out):
    parts = len(backs)
    block = 256
    rows = pl.BlockSpec((block, D), lambda r: (r, 0))
    return pl.pallas_call(
        functools.partial(middle_back_kernel, parts),
        grid=(TOK // block,),
        in_specs=[whole(back.shape) for back in backs]
        + [
            pl.BlockSpec((block, 1), lambda r: (r, 0)),
            rows,
            rows,
            whole((1, D)),
            whole((D, D)),
        ],
        out_specs=[rows, rows, rows, whole((1, D))],
        out_shape=[
            jax.ShapeDtypeStruct((TOK, D), F32),
            jax.ShapeDtypeStruct((TOK, D), BF),
            jax.ShapeDtypeStruct((TOK, D), BF),
            jax.ShapeDtypeStruct((1, D), F32),
        ],
        compiler_params=params(("arbitrary",)),
        cost_estimate=cost(2 * 2 * TOK * TOK * D + 2 * TOK * D * D, 16 * TOK * D),
        name="middle_back",
    )(*backs, slot_col, middle, cot, gain, w_out)


def mix_kernel(parts, *refs):
    backs = refs[:parts]
    slot_col, middle, gate, mixed = refs[parts:]
    mixed[...] = middle[...] + gate[...] * undispatch(slot_col[...], backs)


def mix(backs, slot_col, middle, gate):
    parts = len(backs)
    block = 256
    rows = pl.BlockSpec((block, D), lambda r: (r, 0))
    column = pl.BlockSpec((block, 1), lambda r: (r, 0))
    return pl.pallas_call(
        functools.partial(mix_kernel, parts),
        grid=(TOK // block,),
        in_specs=[whole(back.shape) for back in backs] + [column, rows, column],
        out_specs=rows,
        out_shape=jax.ShapeDtypeStruct((TOK, D), F32),
        compiler_params=params(("arbitrary",)),
        cost_estimate=cost(2 * 2 * TOK * TOK * D, 12 * TOK * D),
        name="mix",
    )(*backs, slot_col, middle, gate)


def tokens_back_kernel(gq, gk, gv, left, right, tokens, gain, grad_middle, grad_tokens, grad_gain):
    cut = SPLIT - D
    grad_normed = (
        dot(gq[...], left[:, :D], 1, 1)
        + dot(gk[:, :cut], left[:, D:], 1, 1)
        + dot(gk[:, cut:], right[:, : D - cut], 1, 1)
        + dot(gv[...], right[:, D - cut : SPLIT], 1, 1)
    )
    part, gain_part = rms_back(tokens[...].astype(F32), gain[...], grad_normed)
    grad_tokens[...] = grad_middle[...] + part

    @pl.when(pl.program_id(0) == 0)
    def _():
        grad_gain[...] = gain_part

    @pl.when(pl.program_id(0) > 0)
    def _():
        grad_gain[...] += gain_part


def tokens_back(gq, gk, gv, left, right, tokens, gain, grad_middle):
    block = 256
    rows = pl.BlockSpec((block, D), lambda r: (r, 0))
    return pl.pallas_call(
        tokens_back_kernel,
        grid=(TOK // block,),
        in_specs=[rows, rows, rows, whole(left.shape), whole(right.shape), rows, whole((1, D)), rows],
        out_specs=[rows, whole((1, D))],
        out_shape=[
            jax.ShapeDtypeStruct((TOK, D), F32),
            jax.ShapeDtypeStruct((1, D), F32),
        ],
        compiler_params=params(("arbitrary",)),
        cost_estimate=cost(6 * TOK * D * D, 16 * TOK * D),
        name="tokens_back",
    )(gq, gk, gv, left, right, tokens, gain, grad_middle)


def weights_back_kernel(normed, gq, gk, gv, left, right):
    cut = SPLIT - D
    turned = normed[...].astype(F32).T.astype(BF)
    left[:, :D] = dot(turned, gq[...])
    left[:, D:] = dot(turned, gk[:, :cut])
    right[:, : D - cut] = dot(turned, gk[:, cut:])
    right[:, D - cut :] = dot(turned, gv[...])


def weights_back(normed, gq, gk, gv):
    return pl.pallas_call(
        weights_back_kernel,
        out_shape=(
            jax.ShapeDtypeStruct((D, SPLIT), F32),
            jax.ShapeDtypeStruct((D, SPLIT), F32),
        ),
        compiler_params=params(),
        cost_estimate=cost(6 * TOK * D * D, 8 * TOK * D + 12 * D * D),
        name="weights_back",
    )(normed, gq, gk, gv)


def swap(block, axis, bit):
    size = lax.axis_size(axis)
    return lax.ppermute(block, axis, [(place, place ^ bit) for place in range(size)])


def on_upper(axis, bit):
    return (lax.axis_index(axis) // bit) % 2 == 1


def axis_bits(*axes):
    found = []
    for axis in axes:
        bit = lax.axis_size(axis) // 2
        while bit >= 1:
            found.append((axis, bit))
            bit //= 2
    return found


def orders():
    bits = axis_bits("dp", "expert")
    dp = [at for at, (axis, _) in enumerate(bits) if axis == "dp"]
    core = len(bits) - 1
    along = [at for at, (axis, bit) in enumerate(bits) if axis == "expert" and bit == 2]
    rest = [at for at in range(core) if at not in dp and at not in along]
    return (rest + along + dp + [core], rest + dp + along + [core])


def gather_rows(shard, order):
    bits = axis_bits("dp", "expert")
    block = shard.reshape((1,) * len(bits) + shard.shape)
    for place in order:
        axis, bit = bits[place]
        other = swap(block, axis, bit)
        upper = on_upper(axis, bit)
        block = jnp.concatenate(
            [jnp.where(upper, other, block), jnp.where(upper, block, other)], axis=place
        )
    return block.reshape((-1,) + shard.shape[1:])


def scatter_sum(total, order):
    bits = axis_bits("dp", "expert")
    rows = total.shape[0] >> len(bits)
    block = total.reshape((2,) * len(bits) + (rows,) + total.shape[1:])
    for place in reversed(order):
        axis, bit = bits[place]
        lower = lax.slice_in_dim(block, 0, 1, axis=place)
        higher = lax.slice_in_dim(block, 1, 2, axis=place)
        upper = on_upper(axis, bit)
        sent = jnp.where(upper, lower, higher).astype(BF)
        block = jnp.where(upper, higher, lower) + swap(sent, axis, bit).astype(F32)
    return block.reshape(block.shape[len(bits) :])


def sum_all(total):
    for axis, bit in axis_bits("dp", "expert"):
        total = total + swap(total, axis, bit)
    return total


def gather_dp(block, axis):
    if lax.axis_size("dp") != 2:
        return lax.all_gather(block, "dp", axis=axis, tiled=True)
    other = swap(block, "dp", 1)
    upper = on_upper("dp", 1)
    return jnp.concatenate(
        [jnp.where(upper, other, block), jnp.where(upper, block, other)], axis=axis
    )


def scatter_dp(total):
    if lax.axis_size("dp") != 2:
        return lax.psum_scatter(
            total[None], "dp", scatter_dimension=1, tiled=True
        ).astype(F32)
    half = total.shape[0] // 2
    upper = on_upper("dp", 1)
    sent = jnp.where(upper, total[:half], total[half:])
    kept = jnp.where(upper, total[half:], total[:half])
    return (kept.astype(F32) + swap(sent, "dp", 1).astype(F32))[None]


def after(value, *others):
    return lax.optimization_barrier((value, *others))[0]


def body(
    tokens, seq_ids, routes, cotangent, w_query, w_key, w_value, w_out,
    rel_table, gain_attn, gain_ffn, router, expert_in, expert_out,
):
    experts = lax.axis_size("expert")
    capacity = 2 * TOK // experts
    shard = w_query.shape[0]
    lanes = -(-(experts + 2) // LANES) * LANES
    everyone = ("dp", "expert")

    small = jnp.concatenate(
        [
            router,
            gain_attn[:, None],
            gain_ffn[:, None],
            jnp.zeros((shard, lanes - experts - 2), BF),
        ],
        axis=1,
    )
    cut = SPLIT - D
    first, second = orders()
    left = gather_rows(jnp.concatenate([w_query, w_key[:, :cut]], axis=1), first)
    right = gather_rows(jnp.concatenate([w_key[:, cut:], w_value, small], axis=1), second)
    full_out = lax.all_gather(w_out, everyone, axis=0, tiled=True)
    table = gather_dp(rel_table, 0).astype(F32)
    w_first = gather_dp(after(expert_in, left, right), 1)[0]
    w_second = lax.all_gather(after(expert_out, full_out), "dp", axis=1, tiled=True)[0]

    slot_col, slot_row, sending_cot = make_slots(routes, cotangent, experts, capacity)

    def exchange(rows):
        return lax.all_to_all(
            rows.reshape(experts, -1, D), "expert", split_axis=0, concat_axis=0, tiled=True
        )

    cots = exchange(after(sending_cot, left, right))

    extra = right[:, SPLIT:]
    full_router = jnp.where(jnp.arange(lanes)[None, :] < experts, extra, jnp.zeros((), BF))
    router_t = full_router.T
    attn_gain = extra[:, experts].astype(F32).reshape(1, D)
    ffn_gain = extra[:, experts + 1].astype(F32).reshape(1, D)

    normed, qkv = project(tokens, attn_gain, left, right)
    query_features, key_features = lane_features(seq_ids.reshape(TOK, 1), table)
    band = jnp.sum(band_onehot()[None, :, :] * table.T[:, None, :], axis=2)[:, None, :]
    context, lse = attend(qkv, query_features, key_features, band)

    middle, *sending, gate = make_middle(
        context, tokens, full_out, ffn_gain, full_router, routes, slot_row, experts, capacity
    )
    rows_in = [exchange(part).reshape(-1, D) for part in sending]
    mine = lax.axis_index("expert").astype(jnp.int32).reshape(1, 1)
    acts, dhs, results, grads, gates, router_parts = zip(
        *(
            run_expert(
                part, rows, cots, w_first, w_second, full_router, router_t, mine, experts
            )
            for part, rows in enumerate(rows_in)
        )
    )
    grads_home = [exchange(part).reshape(-1, D) for part in grads]
    grad_first, grad_second = expert_weights(rows_in, cots, gates, acts, dhs)
    results_home = [
        exchange(after(part, *grads_home)).reshape(-1, D) for part in results
    ]
    grads_home[0] = after(grads_home[0], grad_first, grad_second)
    grad_expert_in = scatter_dp(grad_first)
    grad_expert_out = scatter_dp(grad_second)

    grad_middle, grad_attn, grad_context, grad_gain_f = middle_back(
        grads_home, slot_col, middle, cotangent, ffn_gain, full_out
    )
    grad_w_out = lax.psum_scatter(
        dot(context, grad_attn, 0, 0), everyone, scatter_dimension=0, tiled=True
    )
    gq, gk, gv, tiles, diagonals = attend_back(
        qkv, grad_context, query_features, key_features, lse, band
    )
    grad_left, grad_right = weights_back(normed, gq, gk, gv)
    grad_tokens, grad_gain_a = tokens_back(
        after(gq, grad_left, grad_right), gk, gv, left, right, tokens, attn_gain, grad_middle
    )
    grad_left = scatter_sum(grad_left, first)
    grad_right = scatter_sum(grad_right, second)
    mixed = mix(results_home, slot_col, middle, gate)
    grad_router = sum(router_parts)[:, :experts]
    grad_table = table_gradient(tiles, diagonals)

    sizes = (D * experts, D, D, BUCKETS * HEADS)
    sums = sum_all(
        jnp.concatenate(
            [
                part.reshape(-1, LANES)
                for part in (grad_router, grad_gain_a, grad_gain_f, grad_table)
            ],
            axis=0,
        )
    ).reshape(-1)
    ends = [sum(sizes[: at + 1]) for at in range(len(sizes))]
    grad_router, grad_gain_a, grad_gain_f, grad_table = (
        sums[end - size : end] for end, size in zip(ends, sizes)
    )
    number = lax.axis_index("dp") * experts + lax.axis_index("expert")
    table_height = BUCKETS // lax.axis_size("dp")

    def own(rows, height, place):
        return lax.dynamic_slice_in_dim(rows, place * height, height, 0)

    return (
        mixed,
        grad_tokens,
        grad_left[:, :D],
        jnp.concatenate([grad_left[:, D:], grad_right[:, : D - cut]], axis=1),
        grad_right[:, D - cut :],
        grad_w_out,
        own(grad_table.reshape(BUCKETS, HEADS), table_height, lax.axis_index("dp")),
        own(grad_gain_a, shard, number),
        own(grad_gain_f, shard, number),
        own(grad_router.reshape(D, experts), shard, number),
        grad_expert_in,
        grad_expert_out,
    )


def solution(mesh):
    rows = P(("dp", "expert"), None)
    flat = P(("dp", "expert"))
    expert = P("expert", "dp", None)
    return jax.shard_map(
        body,
        mesh=mesh,
        in_specs=(
            rows, flat, rows, rows, rows, rows, rows, rows,
            P("dp", None), flat, flat, rows, expert, expert,
        ),
        out_specs=(
            rows, rows, rows, rows, rows, rows,
            P("dp", None), flat, flat, rows, expert, expert,
        ),
        check_vma=False,
    )
```

profile of v0, /device:TPU:0, one launch (start us, length us, event | category | flops | bytes accessed | tf_op | source)
XLA Modules:
  0.0 651.3 jit_solution(15893318372830278769)
XLA Ops:
  19.8 7.8 %slots.1 = (s32[1024,1]{1,0:T(8,128)}, s32[1,1024]{1,0:T(1,128)}, bf16[2048,768]{1,0:T(8,128)(2,1)}) custom-call(s32[1024,1]{1,0:T(8,128)} %copy.49.route_col.refs_5_, s32[1,1024]{1,0:T(1,128)} %bitcast.89, bf16[1024,768]{1,0:T(8,128)(2,1)} %refs_4_.1), custom_call_target="tpu_custom_call" | custom-call | flops 3221225472 | bytes 9437184 | tf_op jit(solution)/shard_map/slots/pallas_call | solution.py:108
  64.8 8.4 %project.1 = (bf16[1024,768]{1,0:T(8,128)(2,1)}, bf16[1024,2304]{1,0:T(8,128)(2,1)}) custom-call(bf16[1024,768]{1,0:T(8,128)(2,1)} %tokens.3, f32[1,768]{1,0:T(1,128)} %reshape.381.gain, bf16[768,1152]{1,0:T(8,128)(2,1)} %bitcast.73, bf16[768,1280]{1,0:T(8,128)(2,1)} %bitcast.70), custom_call_target="tpu_custom_call" | custom-call | flops 3623878656 | bytes 9437184 | tf_op jit(solution)/shard_map/project/pallas_call | solution.py:132
  73.2 37.0 %attend.1 = (bf16[1024,768]{1,0:T(8,128)(2,1)}, f32[12,1,1024]{2,1,0:T(1,128)}) custom-call(bf16[1024,2304]{1,0:T(8,128)(2,1)} %get-tuple-element.57.q_ref.k_ref.v_ref, bf16[1024,2304]{1,0:T(8,128)(2,1)} %get-tuple-element.57.q_ref.k_ref.v_ref, bf16[1024,2304]{1,0:T(8,128)(2,1)} %get-tuple-element.57.q_ref.k_ref.v_ref, ...), custom_call_target="tpu_custom_call" | custom-call | flops 19327352832 | bytes 7864320 | tf_op jit(solution)/shard_map/attend/pallas_call | solution.py:234
  110.2 9.4 %middle.1 = (f32[1024,768]{1,0:T(8,128)}, bf16[1024,768]{1,0:T(8,128)(2,1)}, bf16[1024,768]{1,0:T(8,128)(2,1)}, f32[1024,1]{1,0:T(8,128)}) custom-call(bf16[1024,768]{1,0:T(8,128)(2,1)} %get-tuple-element.58.refs_0_, bf16[1024,768]{1,0:T(8,128)(2,1)} %tokens.3, bf16[768,768]{1,0:T(8,128)(2,1)} %all-gather.3.cloned.1.call-done.refs_2_.refs_6_, ...), custom_call_target="tpu_custom_call" | custom-call | flops 4429185024 | bytes 12582912 | tf_op jit(solution)/shard_map/middle/pallas_call | solution.py:427
  124.7 32.0 %all-to-all-done = bf16[16,64,768]{2,1,0:T(8,128)(2,1)S(1)} async-done(((bf16[16,64,768]{2,1,0:T(8,128)(2,1)}), bf16[16,64,768]{2,1,0:T(8,128)(2,1)S(1)}, u32[]{:S(2)}, u32[]{:S(2)}) %all-to-all-start) | async-done | bytes 1572896 | tf_op jit(solution)/shard_map/all_to_all | solution.py:885
  157.8 9.1 %all-to-all-start.1 = ((bf16[16,128,768]{2,1,0:T(8,128)(2,1)}), bf16[16,128,768]{2,1,0:T(8,128)(2,1)S(1)}, u32[]{:S(2)}, u32[]{:S(2)}) async-start(bf16[16,128,768]{2,1,0:T(8,128)(2,1)} %bitcast.13), calls=%async_computation.1 | async-start | bytes 6291456 | tf_op jit(solution)/shard_map/all_to_all | solution.py:885
  170.0 56.3 %all-to-all-done.1.c3.refs_8_ = bf16[16,128,768]{2,1,0:T(8,128)(2,1)S(1)} async-done(((bf16[16,128,768]{2,1,0:T(8,128)(2,1)}), bf16[16,128,768]{2,1,0:T(8,128)(2,1)S(1)}, u32[]{:S(2)}, u32[]{:S(2)}) %all-to-all-start.1) | async-done | bytes 3145760 | tf_op jit(solution)/shard_map/all_to_all | solution.py:885
  226.3 15.9 %all-to-all-start.3 = ((bf16[16,64,768]{2,1,0:T(8,128)(2,1)}), bf16[16,64,768]{2,1,0:T(8,128)(2,1)}, u32[]{:S(2)}, u32[]{:S(2)}) async-start(bf16[16,64,768]{2,1,0:T(8,128)(2,1)} %bitcast.80), calls=%async_computation.3 | async-start | bytes 3145728 | tf_op jit(solution)/shard_map/all_to_all | solution.py:885
  242.2 19.7 %collective-permute-done.11 = bf16[1,384,3072]{2,1,0:T(8,128)(2,1)} collective-permute-done((bf16[1,384,3072]{2,1,0:T(8,128)(2,1)}, bf16[1,384,3072]{2,1,0:T(8,128)(2,1)}, u32[]{:S(2)}, u32[]{:S(2)}) %collective-permute-start.11) | collective-permute-done | bytes 2359328 | tf_op jit(solution)/shard_map/ppermute | solution.py:769
  272.3 42.6 %expert.2 = (bf16[1024,3072]{1,0:T(8,128)(2,1)}, bf16[1024,3072]{1,0:T(8,128)(2,1)}, bf16[1024,768]{1,0:T(8,128)(2,1)}, bf16[1024,768]{1,0:T(8,128)(2,1)}, f32[1024,1]{1,0:T(8,128)}, /*index=5*/f32[768,128]{1,0:T(8,128)}) custom-call(bf16[1024,768]{1,0:T(8,128)(2,1)} %bitcast.76, bf16[16,128,768]{2,1,0:T(8,128)(2,1)} %copy-done.3, ...), custom_call_target="tpu_custom_call" | custom-call | flops 19327352832 | bytes 22020096 | tf_op jit(solution)/shard_map/expert/pallas_call | solution.py:511
  320.9 42.4 %expert.3 = (bf16[1024,3072]{1,0:T(8,128)(2,1)}, bf16[1024,3072]{1,0:T(8,128)(2,1)}, bf16[1024,768]{1,0:T(8,128)(2,1)}, bf16[1024,768]{1,0:T(8,128)(2,1)}, f32[1024,1]{1,0:T(8,128)}, /*index=5*/f32[768,128]{1,0:T(8,128)}) custom-call(bf16[1024,768]{1,0:T(8,128)(2,1)} %bitcast.21.x.refs_1_, bf16[16,128,768]{2,1,0:T(8,128)(2,1)} %copy-done.3, ...), custom_call_target="tpu_custom_call" | custom-call | flops 19327352832 | bytes 22020096 | tf_op jit(solution)/shard_map/expert/pallas_call | solution.py:511
  363.3 6.2 all-to-all-start.4
  369.6 29.3 %expert_weights.1 = (bf16[768,3072]{1,0:T(8,128)(2,1)}, bf16[3072,768]{1,0:T(8,128)(2,1)}) custom-call(bf16[1024,768]{1,0:T(8,128)(2,1)} %bitcast.77, bf16[1024,768]{1,0:T(8,128)(2,1)} %bitcast.21.x.refs_1_, f32[1024,1]{1,0:T(8,128)} %get-tuple-element.75.refs_2_, f32[1024,1]{1,0:T(8,128)} %get-tuple-element.76.refs_3_, ...), custom_call_target="tpu_custom_call" | custom-call | flops 19327352832 | bytes 34603008 | tf_op jit(solution)/shard_map/expert_weights/pallas_call | solution.py:587
  405.6 12.9 %middle_back.1 = (f32[1024,768]{1,0:T(8,128)}, bf16[1024,768]{1,0:T(8,128)(2,1)}, bf16[1024,768]{1,0:T(8,128)(2,1)}, f32[1,768]{1,0:T(1,128)}) custom-call(bf16[1024,768]{1,0:T(8,128)(2,1)} %bitcast.78, bf16[1024,768]{1,0:T(8,128)(2,1)} %bitcast.23.refs_1_, s32[1024,1]{1,0:T(8,128)} %get-tuple-element.72.refs_2_, f32[1024,768]{1,0:T(8,128)} %get-tuple-element.73.refs_3_, ...), custom_call_target="tpu_custom_call" | custom-call | flops 4429185024 | bytes 12582912 | tf_op jit(solution)/shard_map/middle_back/pallas_call | solution.py:660
  418.5 49.8 %attend_back.1 = (bf16[1024,768]{1,0:T(8,128)(2,1)}, bf16[1024,768]{1,0:T(8,128)(2,1)}, bf16[1024,768]{1,0:T(8,128)(2,1)}, f32[12,8,128]{2,1,0:T(8,128)}, f32[12,1,512]{2,1,0:T(1,128)}) custom-call(bf16[1024,2304]{1,0:T(8,128)(2,1)} %get-tuple-element.57.q_ref.k_ref.v_ref, bf16[1024,2304]{1,0:T(8,128)(2,1)} %get-tuple-element.57.q_ref.k_ref.v_ref, ...), custom_call_target="tpu_custom_call" | custom-call | flops 32212254720 | bytes 12582912 | tf_op jit(solution)/shard_map/attend_back/pallas_call | solution.py:333
  478.6 8.9 %weights_back.1 = (f32[768,1152]{1,0:T(8,128)}, f32[768,1152]{1,0:T(8,128)}) custom-call(bf16[1024,768]{1,0:T(8,128)(2,1)} %get-tuple-element.87.normed, bf16[1024,768]{1,0:T(8,128)(2,1)} %get-tuple-element.92.gq, bf16[1024,768]{1,0:T(8,128)(2,1)} %get-tuple-element.88.gk, bf16[1024,768]{1,0:T(8,128)(2,1)} %get-tuple-element.89.gv), custom_call_target="tpu_custom_call" | custom-call | flops 3623878656 | bytes 13369344 | tf_op jit(solution)/shard_map/weights_back/pallas_call | solution.py:755
  487.5 10.4 %tokens_back.1 = (f32[1024,768]{1,0:T(8,128)}, f32[1,768]{1,0:T(1,128)}) custom-call(bf16[1024,768]{1,0:T(8,128)(2,1)} %get-tuple-element.92.gq, bf16[1024,768]{1,0:T(8,128)(2,1)} %get-tuple-element.88.gk, bf16[1024,768]{1,0:T(8,128)(2,1)} %get-tuple-element.89.gv, bf16[768,1152]{1,0:T(8,128)(2,1)} %bitcast.74, bf16[768,1280]{1,0:T(8,128)(2,1)} %bitcast.72, ...), custom_call_target="tpu_custom_call" | custom-call | flops 3623878656 | bytes 12582912 | tf_op jit(solution)/shard_map/tokens_back/pallas_call | solution.py:730
  499.6 6.8 %collective-permute-done.27 = bf16[384,3072]{1,0:T(8,128)(2,1)} collective-permute-done((bf16[384,3072]{1,0:T(8,128)(2,1)}, bf16[384,3072]{1,0:T(8,128)(2,1)}, u32[]{:S(2)}, u32[]{:S(2)}) %collective-permute-start.27) | collective-permute-done | bytes 2359328 | tf_op jit(solution)/shard_map/ppermute | solution.py:769
  506.4 6.4 add_bitcast_fusion.1
  552.7 13.9 %collective-permute-done.18 = bf16[2,2,2,1,1,24,1152]{6,5,4,3,2,1,0:T(8,128)(2,1)S(1)} collective-permute-done((bf16[2,2,2,1,1,24,1152]{6,5,4,3,2,1,0:T(8,128)(2,1)S(1)}, bf16[2,2,2,1,1,24,1152]{6,5,4,3,2,1,0:T(8,128)(2,1)S(1)}, u32[]{:S(2)}, u32[]{:S(2)}) %collective-permute-start.18) | collective-permute-done | bytes 442400 | tf_op jit(solution)/shard_map/ppermute | solution.py:769
  574.1 6.9 %collective-permute-start.20 = (bf16[1,2,1,1,1,24,1152]{6,5,4,3,2,1,0:T(8,128)(2,1)S(1)}, bf16[1,2,1,1,1,24,1152]{6,5,4,3,2,1,0:T(8,128)(2,1)S(1)}, u32[]{:S(2)}, u32[]{:S(2)}) collective-permute-start(bf16[1,2,1,1,1,24,1152]{6,5,4,3,2,1,0:T(8,128)(2,1)S(1)} %select_convert_fusion.8), channel_id=1, source_target_pairs={{0,4},{1,5},{2,6},{3,7},{4,0},{5,1},{6,2},{7,3},{8,12},{9,13},{10,... | collective-permute-start | bytes 331784 | tf_op jit(solution)/shard_map/ppermute | solution.py:769
  591.4 27.8 %collective-permute-done.15 = bf16[1,2,1,1,1,24,1152]{6,5,4,3,2,1,0:T(8,128)(2,1)S(1)} collective-permute-done((bf16[1,2,1,1,1,24,1152]{6,5,4,3,2,1,0:T(8,128)(2,1)S(1)}, bf16[1,2,1,1,1,24,1152]{6,5,4,3,2,1,0:T(8,128)(2,1)S(1)}, u32[]{:S(2)}, u32[]{:S(2)}) %collective-permute-start.15) | collective-permute-done | bytes 110624 | tf_op jit(solution)/shard_map/ppermute | solution.py:769
  623.8 8.8 %collective-permute-done.21 = bf16[1,1,1,1,1,24,1152]{6,5,4,3,2,1,0:T(8,128)(2,1)S(1)} collective-permute-done((bf16[1,1,1,1,1,24,1152]{6,5,4,3,2,1,0:T(8,128)(2,1)S(1)}, bf16[1,1,1,1,1,24,1152]{6,5,4,3,2,1,0:T(8,128)(2,1)S(1)}, u32[]{:S(2)}, u32[]{:S(2)}) %collective-permute-start.21) | collective-permute-done | bytes 55328 | tf_op jit(solution)/shard_map/ppermute | solution.py:769
  636.2 8.0 %mix.1 = f32[1024,768]{1,0:T(8,128)} custom-call(bf16[1024,768]{1,0:T(8,128)(2,1)} %bitcast.79, bf16[1024,768]{1,0:T(8,128)(2,1)} %bitcast.27.refs_1_, s32[1024,1]{1,0:T(8,128)} %get-tuple-element.72.refs_2_, f32[1024,768]{1,0:T(8,128)} %get-tuple-element.73.refs_3_, f32[1024,1]{1,0:T(8,128)} %get-tuple-element.74.refs_4_), custom_call_target="tpu_custom_call" | custom-call | flops 3221225472 | bytes 9437184 | tf_op jit(solution)/shard_map/mix/pallas_call | solution.py:695
  (238 shorter events, 159.5 us)
Async XLA Ops:
  7.2 103.0 %all-gather.3.cloned.1.call-start = ((), (), s32[]{:S(2)}) async-start(), calls=%async_computation.8 | async-start | bytes 1216512 | tf_op jit(solution)/shard_map/all_gather | solution.py:877
  8.7 24.5 %collective-permute-start.5 = (bf16[1,1,1,1,1,24,1152]{6,5,4,3,2,1,0:T(8,128)(2,1)S(1)}, bf16[1,1,1,1,1,24,1152]{6,5,4,3,2,1,0:T(8,128)(2,1)S(1)}, u32[]{:S(2)}, u32[]{:S(2)}) collective-permute-start(bf16[1,1,1,1,1,24,1152]{6,5,4,3,2,1,0:T(8,128)(2,1)S(1)} %maximum_bitcast_fusion.1), channel_id=1, source_target_pairs={{0,8},{1,9},{2,10},{3,11},{4,12},{5,13},{6,14},{7,15},{8,0},{9,1},... | collective-permute-start | bytes 165896 | tf_op jit(solution)/shard_map/ppermute | solution.py:769
  15.9 19.1 %collective-permute-start = (bf16[1,1,1,1,1,24,1280]{6,5,4,3,2,1,0:T(8,128)(2,1)S(1)}, bf16[1,1,1,1,1,24,1280]{6,5,4,3,2,1,0:T(8,128)(2,1)S(1)}, u32[]{:S(2)}, u32[]{:S(2)}) collective-permute-start(bf16[1,1,1,1,1,24,1280]{6,5,4,3,2,1,0:T(8,128)(2,1)S(1)} %bitcast.84), channel_id=1, source_target_pairs={{0,8},{1,9},{2,10},{3,11},{4,12},{5,13},{6,14},{7,15},{8,0},{9,1},... | collective-permute-start | bytes 184328 | tf_op jit(solution)/shard_map/ppermute | solution.py:769
  119.6 37.0 %all-to-all-start = ((bf16[16,64,768]{2,1,0:T(8,128)(2,1)}), bf16[16,64,768]{2,1,0:T(8,128)(2,1)S(1)}, u32[]{:S(2)}, u32[]{:S(2)}) async-start(bf16[16,64,768]{2,1,0:T(8,128)(2,1)} %bitcast.83), calls=%async_computation | async-start | bytes 3145728 | tf_op jit(solution)/shard_map/all_to_all | solution.py:885
  157.8 68.5 %all-to-all-start.1 = ((bf16[16,128,768]{2,1,0:T(8,128)(2,1)}), bf16[16,128,768]{2,1,0:T(8,128)(2,1)S(1)}, u32[]{:S(2)}, u32[]{:S(2)}) async-start(bf16[16,128,768]{2,1,0:T(8,128)(2,1)} %bitcast.13), calls=%async_computation.1 | async-start | bytes 6291456 | tf_op jit(solution)/shard_map/all_to_all | solution.py:885
  166.9 105.4 %all-gather.5.cloned.1.call-start = ((), (), s32[]{:S(2)}) async-start(), calls=%async_computation.9 | async-start | bytes 7077888 | tf_op jit(solution)/shard_map/all_gather | solution.py:880
  167.7 94.3 %collective-permute-start.11 = (bf16[1,384,3072]{2,1,0:T(8,128)(2,1)}, bf16[1,384,3072]{2,1,0:T(8,128)(2,1)}, u32[]{:S(2)}, u32[]{:S(2)}) collective-permute-start(bf16[1,384,3072]{2,1,0:T(8,128)(2,1)} %param.26), channel_id=1, source_target_pairs={{0,16},{16,0},{1,17},{17,1},{2,18},{18,2},{3,19},{19,3},{4,20},{20... | collective-permute-start | bytes 7077896 | tf_op jit(solution)/shard_map/ppermute | solution.py:769
  226.3 88.6 %all-to-all-start.3 = ((bf16[16,64,768]{2,1,0:T(8,128)(2,1)}), bf16[16,64,768]{2,1,0:T(8,128)(2,1)}, u32[]{:S(2)}, u32[]{:S(2)}) async-start(bf16[16,64,768]{2,1,0:T(8,128)(2,1)} %bitcast.80), calls=%async_computation.3 | async-start | bytes 3145728 | tf_op jit(solution)/shard_map/all_to_all | solution.py:885
  314.9 48.4 %all-to-all-start.2 = ((bf16[16,64,768]{2,1,0:T(8,128)(2,1)}), bf16[16,64,768]{2,1,0:T(8,128)(2,1)S(1)}, u32[]{:S(2)}, u32[]{:S(2)}) async-start(bf16[16,64,768]{2,1,0:T(8,128)(2,1)} %bitcast.81), calls=%async_computation.2 | async-start | bytes 3145728 | tf_op jit(solution)/shard_map/all_to_all | solution.py:885
  363.3 42.2 %all-to-all-start.4 = ((bf16[16,64,768]{2,1,0:T(8,128)(2,1)}), bf16[16,64,768]{2,1,0:T(8,128)(2,1)}, u32[]{:S(2)}, u32[]{:S(2)}) async-start(bf16[16,64,768]{2,1,0:T(8,128)(2,1)} %bitcast.82), calls=%async_computation.4 | async-start | bytes 3145728 | tf_op jit(solution)/shard_map/all_to_all | solution.py:885
  369.5 274.8 %reduce-scatter.2.cloned.1.call-start = ((), (), s32[]{:S(2)}) async-start(), calls=%async_computation.10 | async-start | bytes 2433024 | tf_op jit(solution)/shard_map/reduce_scatter | solution.py:927
  401.6 114.0 %collective-permute-start.28 = (bf16[1536,768]{1,0:T(8,128)(2,1)S(1)}, bf16[1536,768]{1,0:T(8,128)(2,1)}, u32[]{:S(2)}, u32[]{:S(2)}) collective-permute-start(bf16[1536,768]{1,0:T(8,128)(2,1)S(1)} %broadcast_select_fusion), channel_id=1, source_target_pairs={{0,16},{16,0},{1,17},{17,1},{2,18},{18,2},{3,19},{19,3},{4,20},{20... | collective-permute-start | bytes 7077896 | tf_op jit(solution)/shard_map/ppermute | solution.py:769
  404.2 102.2 %collective-permute-start.27 = (bf16[384,3072]{1,0:T(8,128)(2,1)}, bf16[384,3072]{1,0:T(8,128)(2,1)}, u32[]{:S(2)}, u32[]{:S(2)}) collective-permute-start(bf16[384,3072]{1,0:T(8,128)(2,1)} %broadcast_select_fusion.1), channel_id=1, source_target_pairs={{0,16},{16,0},{1,17},{17,1},{2,18},{18,2},{3,19},{19,3},{4,20},{20... | collective-permute-start | bytes 7077896 | tf_op jit(solution)/shard_map/ppermute | solution.py:769
  498.7 14.2 %collective-permute-start.22 = (f32[111,128]{1,0:T(8,128)S(1)}, f32[111,128]{1,0:T(8,128)S(1)}, u32[]{:S(2)}, u32[]{:S(2)}) collective-permute-start(f32[111,128]{1,0:T(8,128)S(1)} %pad_maximum_fusion.11), channel_id=1, source_target_pairs={{0,16},{16,0},{1,17},{17,1},{2,18},{18,2},{3,19},{19,3},{4,20},{20... | collective-permute-start | bytes 170504 | tf_op jit(solution)/shard_map/ppermute | solution.py:769
  531.0 15.2 %collective-permute-start.17 = (bf16[2,2,2,2,1,24,1152]{6,5,4,3,2,1,0:T(8,128)(2,1)}, bf16[2,2,2,2,1,24,1152]{6,5,4,3,2,1,0:T(8,128)(2,1)}, u32[]{:S(2)}, u32[]{:S(2)}) collective-permute-start(bf16[2,2,2,2,1,24,1152]{6,5,4,3,2,1,0:T(8,128)(2,1)} %select_convert_fusion.1), channel_id=1, source_target_pairs={{0,1},{1,0},{2,3},{3,2},{4,5},{5,4},{6,7},{7,6},{8,9},{9,8},{10,11... | collective-permute-start | bytes 2654216 | tf_op jit(solution)/shard_map/ppermute | solution.py:769
  533.3 17.4 %collective-permute-start.12 = (bf16[2,2,2,2,1,24,1152]{6,5,4,3,2,1,0:T(8,128)(2,1)}, bf16[2,2,2,2,1,24,1152]{6,5,4,3,2,1,0:T(8,128)(2,1)}, u32[]{:S(2)}, u32[]{:S(2)}) collective-permute-start(bf16[2,2,2,2,1,24,1152]{6,5,4,3,2,1,0:T(8,128)(2,1)} %select_convert_fusion.2), channel_id=1, source_target_pairs={{0,1},{1,0},{2,3},{3,2},{4,5},{5,4},{6,7},{7,6},{8,9},{9,8},{10,11... | collective-permute-start | bytes 2654216 | tf_op jit(solution)/shard_map/ppermute | solution.py:769
  533.3 47.8 %all-to-all-start.6 = ((bf16[16,64,768]{2,1,0:T(8,128)(2,1)}), bf16[16,64,768]{2,1,0:T(8,128)(2,1)}, u32[]{:S(2)}, u32[]{:S(2)}) async-start(bf16[16,64,768]{2,1,0:T(8,128)(2,1)} %bitcast.75), calls=%async_computation.6 | async-start | bytes 3145728 | tf_op jit(solution)/shard_map/all_to_all | solution.py:885
  548.9 17.8 %collective-permute-start.18 = (bf16[2,2,2,1,1,24,1152]{6,5,4,3,2,1,0:T(8,128)(2,1)S(1)}, bf16[2,2,2,1,1,24,1152]{6,5,4,3,2,1,0:T(8,128)(2,1)S(1)}, u32[]{:S(2)}, u32[]{:S(2)}) collective-permute-start(bf16[2,2,2,1,1,24,1152]{6,5,4,3,2,1,0:T(8,128)(2,1)S(1)} %select_convert_fusion.3), channel_id=1, source_target_pairs={{0,2},{1,3},{2,0},{3,1},{4,6},{5,7},{6,4},{7,5},{8,10},{9,11},{10,... | collective-permute-start | bytes 1327112 | tf_op jit(solution)/shard_map/ppermute | solution.py:769
  552.2 15.2 %collective-permute-start.13 = (bf16[1,2,2,2,1,24,1152]{6,5,4,3,2,1,0:T(8,128)(2,1)S(1)}, bf16[1,2,2,2,1,24,1152]{6,5,4,3,2,1,0:T(8,128)(2,1)S(1)}, u32[]{:S(2)}, u32[]{:S(2)}) collective-permute-start(bf16[1,2,2,2,1,24,1152]{6,5,4,3,2,1,0:T(8,128)(2,1)S(1)} %select_convert_fusion.4), channel_id=1, source_target_pairs={{0,16},{16,0},{1,17},{17,1},{2,18},{18,2},{3,19},{19,3},{4,20},{20... | collective-permute-start | bytes 1327112 | tf_op jit(solution)/shard_map/ppermute | solution.py:769
  574.1 14.9 %collective-permute-start.20 = (bf16[1,2,1,1,1,24,1152]{6,5,4,3,2,1,0:T(8,128)(2,1)S(1)}, bf16[1,2,1,1,1,24,1152]{6,5,4,3,2,1,0:T(8,128)(2,1)S(1)}, u32[]{:S(2)}, u32[]{:S(2)}) collective-permute-start(bf16[1,2,1,1,1,24,1152]{6,5,4,3,2,1,0:T(8,128)(2,1)S(1)} %select_convert_fusion.8), channel_id=1, source_target_pairs={{0,4},{1,5},{2,6},{3,7},{4,0},{5,1},{6,2},{7,3},{8,12},{9,13},{10,... | collective-permute-start | bytes 331784 | tf_op jit(solution)/shard_map/ppermute | solution.py:769
  581.1 54.0 %all-to-all-start.5 = ((bf16[16,64,768]{2,1,0:T(8,128)(2,1)}), bf16[16,64,768]{2,1,0:T(8,128)(2,1)S(1)}, u32[]{:S(2)}, u32[]{:S(2)}) async-start(bf16[16,64,768]{2,1,0:T(8,128)(2,1)} %bitcast.24), calls=%async_computation.5 | async-start | bytes 3145728 | tf_op jit(solution)/shard_map/all_to_all | solution.py:885
  586.9 32.3 %collective-permute-start.15 = (bf16[1,2,1,1,1,24,1152]{6,5,4,3,2,1,0:T(8,128)(2,1)S(1)}, bf16[1,2,1,1,1,24,1152]{6,5,4,3,2,1,0:T(8,128)(2,1)S(1)}, u32[]{:S(2)}, u32[]{:S(2)}) collective-permute-start(bf16[1,2,1,1,1,24,1152]{6,5,4,3,2,1,0:T(8,128)(2,1)S(1)} %select_convert_fusion.9), channel_id=1, source_target_pairs={{0,4},{1,5},{2,6},{3,7},{4,0},{5,1},{6,2},{7,3},{8,12},{9,13},{10,... | collective-permute-start | bytes 331784 | tf_op jit(solution)/shard_map/ppermute | solution.py:769
  589.0 43.7 %collective-permute-start.21 = (bf16[1,1,1,1,1,24,1152]{6,5,4,3,2,1,0:T(8,128)(2,1)S(1)}, bf16[1,1,1,1,1,24,1152]{6,5,4,3,2,1,0:T(8,128)(2,1)S(1)}, u32[]{:S(2)}, u32[]{:S(2)}) collective-permute-start(bf16[1,1,1,1,1,24,1152]{6,5,4,3,2,1,0:T(8,128)(2,1)S(1)} %select_convert_fusion.10), channel_id=1, source_target_pairs={{0,8},{1,9},{2,10},{3,11},{4,12},{5,13},{6,14},{7,15},{8,0},{9,1},... | collective-permute-start | bytes 165896 | tf_op jit(solution)/shard_map/ppermute | solution.py:769
  619.3 14.4 %collective-permute-start.16 = (bf16[1,1,1,1,1,24,1152]{6,5,4,3,2,1,0:T(8,128)(2,1)S(1)}, bf16[1,1,1,1,1,24,1152]{6,5,4,3,2,1,0:T(8,128)(2,1)S(1)}, u32[]{:S(2)}, u32[]{:S(2)}) collective-permute-start(bf16[1,1,1,1,1,24,1152]{6,5,4,3,2,1,0:T(8,128)(2,1)S(1)} %select_convert_fusion.11), channel_id=1, source_target_pairs={{0,8},{1,9},{2,10},{3,11},{4,12},{5,13},{6,14},{7,15},{8,0},{9,1},... | collective-permute-start | bytes 165896 | tf_op jit(solution)/shard_map/ppermute | solution.py:769
  (35 other events, 351.5 us)
Sparse Core Ops, SparseCore 0:
  18.0 54.4 all-gather.2
  169.3 102.9 all-gather.4
  525.4 112.3 reduce-scatter.1
where the time goes:
time: 657 us; the launch traced here: 651 us
  Pallas kernels  267 us (41%)
  waiting for transfers between devices  195 us (30%)
  starting transfers between devices  95.6 us (15%)
  other arithmetic  44 us (7%)
  local copies, waits for them, and re-layouts  31.3 us (5%)
  between operations  15.1 us (2%)
    ppermute x29, waiting for transfers between devices, swap(): lax.ppermute(block, axis, [(place, place ^ bit) for place in range(size)])  100 us
    all_to_all x7, waiting for transfers between devices, exchange(): lax.all_to_all(rows.reshape(experts, -1, D), 'expert', split_axis=0, conc...  88.3 us
    pallas_call x2, Pallas kernels, run_expert(): pl.pallas_call(functools.partial(expert_kernel, experts), grid=(hidden_si...  85 us
    all_to_all x7, starting transfers between devices, exchange(): lax.all_to_all(rows.reshape(experts, -1, D), 'expert', split_axis=0, conc...  52.4 us
    pallas_call x1, Pallas kernels, attend_back(): pl.pallas_call(attend_back_kernel, grid=(pairs,), in_specs=[column, pl.Bl...  49.8 us
    ppermute x29, starting transfers between devices, swap(): lax.ppermute(block, axis, [(place, place ^ bit) for place in range(size)])  43 us
    pallas_call x1, Pallas kernels, attend(): pl.pallas_call(attend_kernel, grid=(pairs,), in_specs=[pl.BlockSpec((TOK,...  37 us
    pallas_call x1, Pallas kernels, expert_weights(): pl.pallas_call(functools.partial(expert_weights_kernel, parts), grid=(hid...  29.3 us
  transfers between devices with their start and end apart: 39, of which 17 were waited for; matrix products, arithmetic and copies ran while one was open for 11% of the time, Pallas kernels for 40%

commit v1 on v0

--- a/solution.py
+++ b/solution.py
@@ -17,7 +17,11 @@
 QBLK = 256
 FF_TILE = 512
 HALVES = 2
-SPLIT = 3 * D // 2
+SIDE = D // 2
+SPLIT = 3 * SIDE
+PAIRS = HEADS // 2
+SIDE_PAIRS = PAIRS // 2
+COST_SHARE = 0.05
 LANES = 128
 
 EPSILON = 1e-06
@@ -40,9 +44,11 @@
     return pltpu.CompilerParams(vmem_limit_bytes=VMEM_LIMIT, dimension_semantics=semantics)
 
 
-def cost(flops, bytes_accessed, transcendentals=0):
+def cost(flops, bytes_accessed, transcendentals=0, share=COST_SHARE):
     return pl.CostEstimate(
-        flops=int(flops), bytes_accessed=int(bytes_accessed), transcendentals=int(transcendentals)
+        flops=int(flops * share),
+        bytes_accessed=int(bytes_accessed * share),
+        transcendentals=int(transcendentals * share),
     )
 
 
@@ -118,10 +124,11 @@
     )(routes, routes.reshape(1, TOK), cotangent)
 
 
-def project_kernel(tokens, gain, left, right, normed, qkv):
+def project_kernel(tokens, gain, left, right, turned, qkv):
     x = tokens[...].astype(F32)
-    low = (x * inverse_rms(x) * gain[...]).astype(BF)
-    normed[...] = low
+    wide = x * inverse_rms(x) * gain[...]
+    low = wide.astype(BF)
+    turned[...] = wide.T.astype(BF)
     qkv[:, :SPLIT] = dot(low, left[...]).astype(BF)
     qkv[:, SPLIT:] = dot(low, right[:, :SPLIT]).astype(BF)
 
@@ -133,9 +140,12 @@
         project_kernel,
         grid=(TOK // block,),
         in_specs=[rows, whole((1, D)), whole(left.shape), whole(right.shape)],
-        out_specs=[rows, pl.BlockSpec((block, 3 * D), lambda r: (r, 0))],
+        out_specs=[
+            pl.BlockSpec((D, block), lambda r: (0, r)),
+            pl.BlockSpec((block, 3 * D), lambda r: (r, 0)),
+        ],
         out_shape=[
-            jax.ShapeDtypeStruct((TOK, D), BF),
+            jax.ShapeDtypeStruct((D, TOK), BF),
             jax.ShapeDtypeStruct((TOK, 3 * D), BF),
         ],
         compiler_params=params(("arbitrary",)),
@@ -230,14 +240,20 @@
 
 
 def attend(qkv, query_features, key_features, band):
-    pairs = HEADS // 2
     return pl.pallas_call(
         attend_kernel,
-        grid=(pairs,),
+        grid=(PAIRS,),
         in_specs=[
-            pl.BlockSpec((TOK, LANES), lambda p: (0, p)),
-            pl.BlockSpec((TOK, LANES), lambda p: (0, p + pairs)),
-            pl.BlockSpec((TOK, LANES), lambda p: (0, p + 2 * pairs)),
+            *(
+                pl.BlockSpec(
+                    (TOK, LANES),
+                    lambda p, kind=kind: (
+                        0,
+                        p // SIDE_PAIRS * (3 * SIDE_PAIRS) + kind * SIDE_PAIRS + p % SIDE_PAIRS,
+                    ),
+                )
+                for kind in range(3)
+            ),
             whole((TOK, LANES)),
             pl.BlockSpec((TOK, LANES), lambda p: (0, p)),
             pl.BlockSpec((2, 1, 4 * LANES), lambda p: (p, 0, 0)),
@@ -263,7 +279,7 @@
 
 def attend_back_kernel(
     q_ref, k_ref, v_ref, do_ref, qx_ref, kx_ref, lse_ref, band_ref,
-    dq_ref, dk_ref, dv_ref, tiles_ref, diag_ref,
+    grad_ref, tiles_ref, diag_ref,
     st, dp, pb, sb, dqt, dkt, dvt, near,
 ):
     low = lax.broadcasted_iota(jnp.int32, (TOK, LANES), 1) < HEAD_DIM
@@ -322,40 +338,48 @@
         for row in range(1, 8):
             diagonal = diagonal + pltpu.roll(folded[row : row + 1], 4 * LANES - row, 1)
         diag_ref[side] = diagonal
-    dq_ref[...] = dqt[...].T.astype(BF)
-    dk_ref[...] = jnp.where(low, dkt[0], dkt[1]).astype(BF)
-    dv_ref[...] = jnp.where(low, dvt[0], dvt[1]).astype(BF)
-
-
-def attend_back(qkv, grad_context, query_features, key_features, lse, band):
-    pairs = HEADS // 2
-    column = pl.BlockSpec((TOK, LANES), lambda p: (0, p))
+    found = (
+        dqt[...].T.astype(BF),
+        jnp.where(low, dkt[0], dkt[1]).astype(BF),
+        jnp.where(low, dvt[0], dvt[1]).astype(BF),
+    )
+    for pair in range(SIDE_PAIRS):
+
+        @pl.when(pl.program_id(0) == pair)
+        def _():
+            for kind in range(3):
+                first = kind * SIDE + pair * LANES
+                grad_ref[:, first : first + LANES] = found[kind]
+
+
+def attend_back(half, qkv, grad_context, query_features, key_features, lse, band):
+    first = half * SIDE_PAIRS
+    column = pl.BlockSpec((TOK, LANES), lambda p: (0, first + p))
     return pl.pallas_call(
         attend_back_kernel,
-        grid=(pairs,),
+        grid=(SIDE_PAIRS,),
         in_specs=[
-            column,
-            pl.BlockSpec((TOK, LANES), lambda p: (0, p + pairs)),
-            pl.BlockSpec((TOK, LANES), lambda p: (0, p + 2 * pairs)),
+            *(
+                pl.BlockSpec(
+                    (TOK, LANES), lambda p, kind=kind: (0, (3 * half + kind) * SIDE_PAIRS + p)
+                )
+                for kind in range(3)
+            ),
             column,
             whole((TOK, LANES)),
             column,
-            pl.BlockSpec((2, 1, TOK), lambda p: (p, 0, 0)),
-            pl.BlockSpec((2, 1, 4 * LANES), lambda p: (p, 0, 0)),
+            pl.BlockSpec((2, 1, TOK), lambda p: (first + p, 0, 0)),
+            pl.BlockSpec((2, 1, 4 * LANES), lambda p: (first + p, 0, 0)),
         ],
         out_specs=[
-            column,
-            column,
-            column,
+            whole((TOK, SPLIT)),
             pl.BlockSpec((2, TILES, LANES), lambda p: (p, 0, 0)),
             pl.BlockSpec((2, 1, 4 * LANES), lambda p: (p, 0, 0)),
         ],
         out_shape=[
-            jax.ShapeDtypeStruct((TOK, D), BF),
-            jax.ShapeDtypeStruct((TOK, D), BF),
-            jax.ShapeDtypeStruct((TOK, D), BF),
-            jax.ShapeDtypeStruct((HEADS, TILES, LANES), F32),
-            jax.ShapeDtypeStruct((HEADS, 1, 4 * LANES), F32),
+            jax.ShapeDtypeStruct((TOK, SPLIT), BF),
+            jax.ShapeDtypeStruct((HEADS // 2, TILES, LANES), F32),
+            jax.ShapeDtypeStruct((HEADS // 2, 1, 4 * LANES), F32),
         ],
         scratch_shapes=[
             pltpu.VMEM((2, TOK, QBLK), F32),
@@ -368,7 +392,7 @@
             pltpu.VMEM((3 * TILE, 4 * LANES), F32),
         ],
         compiler_params=params(("arbitrary",)),
-        cost_estimate=cost(2 * 5 * HEADS * TOK * TOK * 256, 16 * TOK * D, HEADS * TOK * TOK),
+        cost_estimate=cost(5 * HEADS * TOK * TOK * 256, 8 * TOK * D, HEADS * TOK * TOK // 2, share=1),
         name="attend_back",
     )(qkv, qkv, qkv, grad_context, query_features, key_features, lse, band)
 
@@ -605,7 +629,7 @@
         ],
         compiler_params=params(("arbitrary",)),
         cost_estimate=cost(
-            4 * parts * rows * D * hidden_size, 4 * (parts * rows + D) * hidden_size
+            4 * parts * rows * D * hidden_size, 4 * (parts * rows + D) * hidden_size, share=1
         ),
         name="expert_weights",
     )(*xs, *gates, *acts, *dhs, cots)
@@ -676,7 +700,7 @@
             jax.ShapeDtypeStruct((1, D), F32),
         ],
         compiler_params=params(("arbitrary",)),
-        cost_estimate=cost(2 * 2 * TOK * TOK * D + 2 * TOK * D * D, 16 * TOK * D),
+        cost_estimate=cost(2 * 2 * TOK * TOK * D + 2 * TOK * D * D, 16 * TOK * D, share=1),
         name="middle_back",
     )(*backs, slot_col, middle, cot, gain, w_out)
 
@@ -699,19 +723,13 @@
         out_specs=rows,
         out_shape=jax.ShapeDtypeStruct((TOK, D), F32),
         compiler_params=params(("arbitrary",)),
-        cost_estimate=cost(2 * 2 * TOK * TOK * D, 12 * TOK * D),
+        cost_estimate=cost(2 * 2 * TOK * TOK * D, 12 * TOK * D, share=1),
         name="mix",
     )(*backs, slot_col, middle, gate)
 
 
-def tokens_back_kernel(gq, gk, gv, left, right, tokens, gain, grad_middle, grad_tokens, grad_gain):
-    cut = SPLIT - D
-    grad_normed = (
-        dot(gq[...], left[:, :D], 1, 1)
-        + dot(gk[:, :cut], left[:, D:], 1, 1)
-        + dot(gk[:, cut:], right[:, : D - cut], 1, 1)
-        + dot(gv[...], right[:, D - cut : SPLIT], 1, 1)
-    )
+def tokens_back_kernel(g_left, g_right, left, right, tokens, gain, grad_middle, grad_tokens, grad_gain):
+    grad_normed = dot(g_left[...], left[...], 1, 1) + dot(g_right[...], right[:, :SPLIT], 1, 1)
     part, gain_part = rms_back(tokens[...].astype(F32), gain[...], grad_normed)
     grad_tokens[...] = grad_middle[...] + part
 
@@ -724,44 +742,49 @@
         grad_gain[...] += gain_part
 
 
-def tokens_back(gq, gk, gv, left, right, tokens, gain, grad_middle):
+def tokens_back(g_left, g_right, left, right, tokens, gain, grad_middle):
     block = 256
     rows = pl.BlockSpec((block, D), lambda r: (r, 0))
     return pl.pallas_call(
         tokens_back_kernel,
         grid=(TOK // block,),
-        in_specs=[rows, rows, rows, whole(left.shape), whole(right.shape), rows, whole((1, D)), rows],
+        in_specs=[
+            pl.BlockSpec((block, SPLIT), lambda r: (r, 0)),
+            pl.BlockSpec((block, SPLIT), lambda r: (r, 0)),
+            whole(left.shape),
+            whole(right.shape),
+            rows,
+            whole((1, D)),
+            rows,
+        ],
         out_specs=[rows, whole((1, D))],
         out_shape=[
             jax.ShapeDtypeStruct((TOK, D), F32),
             jax.ShapeDtypeStruct((1, D), F32),
         ],
         compiler_params=params(("arbitrary",)),
-        cost_estimate=cost(6 * TOK * D * D, 16 * TOK * D),
+        cost_estimate=cost(6 * TOK * D * D, 16 * TOK * D, share=1),
         name="tokens_back",
-    )(gq, gk, gv, left, right, tokens, gain, grad_middle)
-
-
-def weights_back_kernel(normed, gq, gk, gv, left, right):
-    cut = SPLIT - D
-    turned = normed[...].astype(F32).T.astype(BF)
-    left[:, :D] = dot(turned, gq[...])
-    left[:, D:] = dot(turned, gk[:, :cut])
-    right[:, : D - cut] = dot(turned, gk[:, cut:])
-    right[:, D - cut :] = dot(turned, gv[...])
-
-
-def weights_back(normed, gq, gk, gv):
+    )(g_left, g_right, left, right, tokens, gain, grad_middle)
+
+
+def weights_back_kernel(turned, grads, out):
+    out[...] = dot(turned[...], grads[...])
+
+
+def weights_back(turned, grads):
+    block = 384
+    columns = grads.shape[1]
     return pl.pallas_call(
         weights_back_kernel,
-        out_shape=(
-            jax.ShapeDtypeStruct((D, SPLIT), F32),
-            jax.ShapeDtypeStruct((D, SPLIT), F32),
-        ),
-        compiler_params=params(),
-        cost_estimate=cost(6 * TOK * D * D, 8 * TOK * D + 12 * D * D),
+        grid=(columns // block,),
+        in_specs=[whole(turned.shape), pl.BlockSpec((TOK, block), lambda c: (0, c))],
+        out_specs=pl.BlockSpec((D, block), lambda c: (0, c)),
+        out_shape=jax.ShapeDtypeStruct((D, columns), F32),
+        compiler_params=params(("arbitrary",)),
+        cost_estimate=cost(2 * TOK * D * columns, 2 * TOK * (D + columns) + 4 * D * columns, share=1),
         name="weights_back",
-    )(normed, gq, gk, gv)
+    )(turned, grads)
 
 
 def swap(block, axis, bit):
@@ -805,18 +828,26 @@
     return block.reshape((-1,) + shard.shape[1:])
 
 
-def scatter_sum(total, order):
+def scatter_start(total):
     bits = axis_bits("dp", "expert")
     rows = total.shape[0] >> len(bits)
-    block = total.reshape((2,) * len(bits) + (rows,) + total.shape[1:])
-    for place in reversed(order):
-        axis, bit = bits[place]
-        lower = lax.slice_in_dim(block, 0, 1, axis=place)
-        higher = lax.slice_in_dim(block, 1, 2, axis=place)
-        upper = on_upper(axis, bit)
-        sent = jnp.where(upper, lower, higher).astype(BF)
-        block = jnp.where(upper, higher, lower) + swap(sent, axis, bit).astype(F32)
-    return block.reshape(block.shape[len(bits) :])
+    return total.reshape((2,) * len(bits) + (rows,) + total.shape[1:])
+
+
+def scatter_step(block, place, *others):
+    axis, bit = axis_bits("dp", "expert")[place]
+    lower = lax.slice_in_dim(block, 0, 1, axis=place)
+    higher = lax.slice_in_dim(block, 1, 2, axis=place)
+    upper = on_upper(axis, bit)
+    sent = jnp.where(upper, lower, higher).astype(BF)
+    kept = after(jnp.where(upper, higher, lower), *others)
+    return kept + swap(sent, axis, bit).astype(F32)
+
+
+def scatter_rest(block, order):
+    for place in order:
+        block = scatter_step(block, place)
+    return block.reshape(block.shape[len(axis_bits("dp", "expert")) :])
 
 
 def sum_all(total):
@@ -835,7 +866,7 @@
     )
 
 
-def scatter_dp(total):
+def scatter_dp(total, *others):
     if lax.axis_size("dp") != 2:
         return lax.psum_scatter(
             total[None], "dp", scatter_dimension=1, tiled=True
@@ -844,7 +875,7 @@
     upper = on_upper("dp", 1)
     sent = jnp.where(upper, total[:half], total[half:])
     kept = jnp.where(upper, total[half:], total[:half])
-    return (kept.astype(F32) + swap(sent, "dp", 1).astype(F32))[None]
+    return (after(kept, *others).astype(F32) + swap(sent, "dp", 1).astype(F32))[None]
 
 
 def after(value, *others):
@@ -870,14 +901,14 @@
         ],
         axis=1,
     )
-    cut = SPLIT - D
     first, second = orders()
-    left = gather_rows(jnp.concatenate([w_query, w_key[:, :cut]], axis=1), first)
-    right = gather_rows(jnp.concatenate([w_key[:, cut:], w_value, small], axis=1), second)
+    kinds = (w_query, w_key, w_value)
+    left = gather_rows(jnp.concatenate([w[:, :SIDE] for w in kinds], axis=1), first)
+    right = gather_rows(
+        jnp.concatenate([w[:, SIDE:] for w in kinds] + [small], axis=1), second
+    )
     full_out = lax.all_gather(w_out, everyone, axis=0, tiled=True)
     table = gather_dp(rel_table, 0).astype(F32)
-    w_first = gather_dp(after(expert_in, left, right), 1)[0]
-    w_second = lax.all_gather(after(expert_out, full_out), "dp", axis=1, tiled=True)[0]
 
     slot_col, slot_row, sending_cot = make_slots(routes, cotangent, experts, capacity)
 
@@ -886,7 +917,9 @@
             rows.reshape(experts, -1, D), "expert", split_axis=0, concat_axis=0, tiled=True
         )
 
-    cots = exchange(after(sending_cot, left, right))
+    w_first = gather_dp(after(expert_in, slot_row), 1)[0]
+    w_second = gather_dp(after(expert_out, slot_row), 1)[0]
+    cots = exchange(sending_cot)
 
     extra = right[:, SPLIT:]
     full_router = jnp.where(jnp.arange(lanes)[None, :] < experts, extra, jnp.zeros((), BF))
@@ -894,14 +927,15 @@
     attn_gain = extra[:, experts].astype(F32).reshape(1, D)
     ffn_gain = extra[:, experts + 1].astype(F32).reshape(1, D)
 
-    normed, qkv = project(tokens, attn_gain, left, right)
+    turned, qkv = project(tokens, attn_gain, left, right)
     query_features, key_features = lane_features(seq_ids.reshape(TOK, 1), table)
     band = jnp.sum(band_onehot()[None, :, :] * table.T[:, None, :], axis=2)[:, None, :]
     context, lse = attend(qkv, query_features, key_features, band)
 
     middle, *sending, gate = make_middle(
-        context, tokens, full_out, ffn_gain, full_router, routes, slot_row, experts, capacity
-    )
+        after(context, cots, w_first), tokens, full_out, ffn_gain, full_router, routes, slot_row, experts, capacity
+    )
+    sending[0] = after(sending[0], w_second)
     rows_in = [exchange(part).reshape(-1, D) for part in sending]
     mine = lax.axis_index("expert").astype(jnp.int32).reshape(1, 1)
     acts, dhs, results, grads, gates, router_parts = zip(
@@ -913,30 +947,54 @@
         )
     )
     grads_home = [exchange(part).reshape(-1, D) for part in grads]
-    grad_first, grad_second = expert_weights(rows_in, cots, gates, acts, dhs)
+    grad_first, grad_second = expert_weights(
+        rows_in, cots, (after(gates[0], grads_home[0]), *gates[1:]), acts, dhs
+    )
     results_home = [
         exchange(after(part, *grads_home)).reshape(-1, D) for part in results
     ]
     grads_home[0] = after(grads_home[0], grad_first, grad_second)
-    grad_expert_in = scatter_dp(grad_first)
-    grad_expert_out = scatter_dp(grad_second)
-
     grad_middle, grad_attn, grad_context, grad_gain_f = middle_back(
         grads_home, slot_col, middle, cotangent, ffn_gain, full_out
     )
-    grad_w_out = lax.psum_scatter(
-        dot(context, grad_attn, 0, 0), everyone, scatter_dimension=0, tiled=True
-    )
-    gq, gk, gv, tiles, diagonals = attend_back(
-        qkv, grad_context, query_features, key_features, lse, band
-    )
-    grad_left, grad_right = weights_back(normed, gq, gk, gv)
+    down, down_other = first[::-1], second[::-1]
+    out_block = scatter_step(scatter_start(dot(context, grad_attn, 0, 0)), down_other[0])
+
+    def back(half, *others):
+        return attend_back(
+            half, qkv, after(grad_context, *others), query_features, key_features, lse, band
+        )
+
+    g_left, tiles_left, diagonals_left = back(0)
+    left_block = scatter_start(weights_back(turned, after(g_left, out_block)))
+    g_right, tiles_right, diagonals_right = back(1, left_block, out_block, results_home[0])
+    out_block = scatter_step(out_block, down_other[1], g_right)
+    left_block = scatter_step(left_block, down[0], g_right)
+    grad_expert_out = scatter_dp(grad_second, g_right)
+    grad_right = weights_back(
+        turned, after(g_right, results_home[1], out_block, left_block, grad_expert_out)
+    )
     grad_tokens, grad_gain_a = tokens_back(
-        after(gq, grad_left, grad_right), gk, gv, left, right, tokens, attn_gain, grad_middle
-    )
-    grad_left = scatter_sum(grad_left, first)
-    grad_right = scatter_sum(grad_right, second)
-    mixed = mix(results_home, slot_col, middle, gate)
+        g_left, after(g_right, grad_right), left, right, tokens, attn_gain, grad_middle
+    )
+    mixed = mix(results_home, slot_col, middle, after(gate, grad_tokens))
+    right_block = scatter_step(scatter_start(grad_right), down_other[0], grad_tokens)
+    left_block = scatter_step(left_block, down[1], grad_tokens)
+    out_block = scatter_step(out_block, down_other[2], grad_tokens)
+    near = 2 + len(axis_bits("dp"))
+    for place in down_other[1:near]:
+        right_block = scatter_step(right_block, place)
+    for place in down[2:near]:
+        left_block = scatter_step(left_block, place)
+    for place in down_other[3:near]:
+        out_block = scatter_step(out_block, place)
+    joined = jnp.concatenate([left_block, right_block, out_block], axis=-1)
+    grad_expert_in = scatter_dp(grad_first, joined)
+    dense = scatter_rest(joined, down[near:])
+    grad_left, grad_right = dense[:, :SPLIT], dense[:, SPLIT : 2 * SPLIT]
+    grad_w_out = dense[:, 2 * SPLIT :]
+    tiles = jnp.concatenate([tiles_left, tiles_right], axis=0)
+    diagonals = jnp.concatenate([diagonals_left, diagonals_right], axis=0)
     grad_router = sum(router_parts)[:, :experts]
     grad_table = table_gradient(tiles, diagonals)
 
@@ -963,9 +1021,13 @@
     return (
         mixed,
         grad_tokens,
-        grad_left[:, :D],
-        jnp.concatenate([grad_left[:, D:], grad_right[:, : D - cut]], axis=1),
-        grad_right[:, D - cut :],
+        *(
+            jnp.concatenate(
+                [side[:, kind * SIDE : (kind + 1) * SIDE] for side in (grad_left, grad_right)],
+                axis=1,
+            )
+            for kind in range(3)
+        ),
         grad_w_out,
         own(grad_table.reshape(BUCKETS, HEADS), table_height, lax.axis_index("dp")),
         own(grad_gain_a, shard, number),

time: 657 us -> 634 us (0.965)
  waiting for transfers between devices: 195 us -> 130 us
  blocking collectives: 0 us -> 42.1 us
  starting transfers between devices: 95.6 us -> 77.3 us
  other arithmetic: 44 us -> 56.2 us
  Pallas kernels: 267 us -> 275 us
    all_to_all x7 -> x6, waiting for transfers between devices: 88.3 us -> 0.98 us  [exchange(): lax.all_to_all(rows.reshape(experts, -1, D), 'expert', split_axis=0, conc...]
    all_to_all x0 -> x1, blocking collectives: none -> 42.1 us  [exchange(): lax.all_to_all(rows.reshape(experts, -1, D), 'expert', split_axis=0, conc...]
    ppermute x29 -> x31, waiting for transfers between devices: 100 us -> 129 us  [swap(): lax.ppermute(block, axis, [(place, place ^ bit) for place in range(size)])]
    all_to_all x7 -> x6, starting transfers between devices: 52.4 us -> 38.3 us  [exchange(): lax.all_to_all(rows.reshape(experts, -1, D), 'expert', split_axis=0, conc...]
    pallas_call x4 -> x6, Pallas kernels: 106 us -> 113 us  [the longest x2 53.9 us: attend_back(): pl.pallas_call(attend_back_kernel, grid=(SIDE_PAIRS,), in_specs=[*(pl.Blo...]
    ppermute x29 -> x31, starting transfers between devices: 43 us -> 38.8 us  [swap(): lax.ppermute(block, axis, [(place, place ^ bit) for place in range(size)])]
    unnamed x54 -> x74, local copies, waits for them, and re-layouts: 14.2 us -> 13 us
  transfers between devices with their start and end apart: 39 -> 38, of which waited for: 17 -> 15; matrix products, arithmetic and copies ran while one was open for 11% -> 11% of each run, Pallas kernels for 40% -> 40%
where the time goes in v1:
time: 634 us; the launch traced here: 629 us
  Pallas kernels  275 us (43%)
  waiting for transfers between devices  130 us (21%)
  starting transfers between devices  77.3 us (12%)
  other arithmetic  56.2 us (9%)
  blocking collectives  42.1 us (7%)
  local copies, waits for them, and re-layouts  28.5 us (4%)
  between operations  15.3 us (2%)
    ppermute x31, waiting for transfers between devices, swap(): lax.ppermute(block, axis, [(place, place ^ bit) for place in range(size)])  129 us
    pallas_call x2, Pallas kernels, run_expert(): pl.pallas_call(functools.partial(expert_kernel, experts), grid=(hidden_si...  84.9 us
    pallas_call x2, Pallas kernels, attend_back(): pl.pallas_call(attend_back_kernel, grid=(SIDE_PAIRS,), in_specs=[*(pl.Blo...  53.9 us
    all_to_all x1, blocking collectives, exchange(): lax.all_to_all(rows.reshape(experts, -1, D), 'expert', split_axis=0, conc...  42.1 us
    ppermute x31, starting transfers between devices, swap(): lax.ppermute(block, axis, [(place, place ^ bit) for place in range(size)])  38.8 us
    all_to_all x6, starting transfers between devices, exchange(): lax.all_to_all(rows.reshape(experts, -1, D), 'expert', split_axis=0, conc...  38.3 us
    pallas_call x1, Pallas kernels, attend(): pl.pallas_call(attend_kernel, grid=(PAIRS,), in_specs=[*(pl.BlockSpec((TO...  37 us
    pallas_call x1, Pallas kernels, expert_weights(): pl.pallas_call(functools.partial(expert_weights_kernel, parts), grid=(hid...  29 us
  transfers between devices with their start and end apart: 38, of which 15 were waited for; matrix products, arithmetic and copies ran while one was open for 11% of the time, Pallas kernels for 40%

profile of v1, /device:TPU:0, one launch (start us, length us, event | category | flops | bytes accessed | tf_op | source)
XLA Modules:
  0.0 628.6 jit_solution(17286268365457564921)
XLA Ops:
  18.8 7.8 %slots.1 = (s32[1024,1]{1,0:T(8,128)}, s32[1,1024]{1,0:T(1,128)}, bf16[2048,768]{1,0:T(8,128)(2,1)}) custom-call(s32[1024,1]{1,0:T(8,128)} %copy.48.route_col.refs_5_, s32[1,1024]{1,0:T(1,128)} %bitcast.93, bf16[1024,768]{1,0:T(8,128)(2,1)} %refs_4_.1), custom_call_target="tpu_custom_call" | custom-call | flops 161061280 | bytes 471859 | tf_op jit(solution)/shard_map/slots/pallas_call | solution.py:114
  26.8 6.3 %all-to-all-start = ((bf16[16,128,768]{2,1,0:T(8,128)(2,1)}), bf16[16,128,768]{2,1,0:T(8,128)(2,1)S(1)}, u32[]{:S(2)}, u32[]{:S(2)}) async-start(bf16[16,128,768]{2,1,0:T(8,128)(2,1)} %bitcast.81), calls=%async_computation | async-start | bytes 6291456 | tf_op jit(solution)/shard_map/all_to_all | solution.py:916
  46.3 42.5 %collective-permute-done.6 = bf16[1,2,1,1,1,24,1152]{6,5,4,3,2,1,0:T(8,128)(2,1)S(1)} collective-permute-done((bf16[1,2,1,1,1,24,1152]{6,5,4,3,2,1,0:T(8,128)(2,1)S(1)}, bf16[1,2,1,1,1,24,1152]{6,5,4,3,2,1,0:T(8,128)(2,1)S(1)}, u32[]{:S(2)}, u32[]{:S(2)}) %collective-permute-start.6) | collective-permute-done | bytes 110624 | tf_op jit(solution)/shard_map/ppermute | solution.py:792
  93.2 6.6 %collective-permute-done.7 = bf16[1,2,2,1,1,24,1152]{6,5,4,3,2,1,0:T(8,128)(2,1)S(1)} collective-permute-done((bf16[1,2,2,1,1,24,1152]{6,5,4,3,2,1,0:T(8,128)(2,1)S(1)}, bf16[1,2,2,1,1,24,1152]{6,5,4,3,2,1,0:T(8,128)(2,1)S(1)}, u32[]{:S(2)}, u32[]{:S(2)}) %collective-permute-start.7) | collective-permute-done | bytes 221216 | tf_op jit(solution)/shard_map/ppermute | solution.py:792
  101.5 38.2 %collective-permute-done.2 = bf16[1,2,2,1,1,24,1280]{6,5,4,3,2,1,0:T(8,128)(2,1)S(1)} collective-permute-done((bf16[1,2,2,1,1,24,1280]{6,5,4,3,2,1,0:T(8,128)(2,1)S(1)}, bf16[1,2,2,1,1,24,1280]{6,5,4,3,2,1,0:T(8,128)(2,1)S(1)}, u32[]{:S(2)}, u32[]{:S(2)}) %collective-permute-start.2) | collective-permute-done | bytes 245792 | tf_op jit(solution)/shard_map/ppermute | solution.py:792
  153.9 8.4 %project.1 = (bf16[768,1024]{1,0:T(8,128)(2,1)}, bf16[1024,2304]{1,0:T(8,128)(2,1)}) custom-call(bf16[1024,768]{1,0:T(8,128)(2,1)} %tokens.3, f32[1,768]{1,0:T(1,128)} %reshape.381.gain, bf16[768,1152]{1,0:T(8,128)(2,1)} %bitcast.71, bf16[768,1280]{1,0:T(8,128)(2,1)} %bitcast.67), custom_call_target="tpu_custom_call" | custom-call | flops 181193936 | bytes 471859 | tf_op jit(solution)/shard_map/project/pallas_call | solution.py:139
  162.3 37.0 %attend.1 = (bf16[1024,768]{1,0:T(8,128)(2,1)}, f32[12,1,1024]{2,1,0:T(1,128)}) custom-call(bf16[1024,2304]{1,0:T(8,128)(2,1)} %get-tuple-element.69.q_ref.k_ref.v_ref, bf16[1024,2304]{1,0:T(8,128)(2,1)} %get-tuple-element.69.q_ref.k_ref.v_ref, bf16[1024,2304]{1,0:T(8,128)(2,1)} %get-tuple-element.69.q_ref.k_ref.v_ref, ...), custom_call_target="tpu_custom_call" | custom-call | flops 966367616 | bytes 393216 | tf_op jit(solution)/shard_map/attend/pallas_call | solution.py:243
  210.8 10.6 %middle.1 = (f32[1024,768]{1,0:T(8,128)}, bf16[1024,768]{1,0:T(8,128)(2,1)}, bf16[1024,768]{1,0:T(8,128)(2,1)}, f32[1024,1]{1,0:T(8,128)}) custom-call(bf16[1024,768]{1,0:T(8,128)(2,1)} %get-tuple-element.74.refs_0_, bf16[1024,768]{1,0:T(8,128)(2,1)} %tokens.3, bf16[768,768]{1,0:T(8,128)(2,1)} %all-gather.2.cloned.1.call-done.refs_2_.refs_6_, ...), custom_call_target="tpu_custom_call" | custom-call | flops 221459248 | bytes 629145 | tf_op jit(solution)/shard_map/middle/pallas_call | solution.py:451
  221.3 42.1 %all_to_all.35 = bf16[16,64,768]{2,1,0:T(8,128)(2,1)} all-to-all(bf16[16,64,768]{2,1,0:T(8,128)(2,1)} %bitcast.87), channel_id=1, replica_groups=mesh['dp'=2,'expert'=16] {'expert'}, dimensions={0} | all-to-all | bytes 3145728 | tf_op jit(solution)/shard_map/all_to_all | solution.py:916
  270.5 42.4 %expert.2 = (bf16[1024,3072]{1,0:T(8,128)(2,1)}, bf16[1024,3072]{1,0:T(8,128)(2,1)}, bf16[1024,768]{1,0:T(8,128)(2,1)}, bf16[1024,768]{1,0:T(8,128)(2,1)}, f32[1024,1]{1,0:T(8,128)}, /*index=5*/f32[768,128]{1,0:T(8,128)}) custom-call(bf16[1024,768]{1,0:T(8,128)(2,1)} %bitcast.73, bf16[16,128,768]{2,1,0:T(8,128)(2,1)} %copy-done, ...), custom_call_target="tpu_custom_call" | custom-call | flops 966367616 | bytes 1101004 | tf_op jit(solution)/shard_map/expert/pallas_call | solution.py:535
  312.9 6.6 %all-to-all-start.2 = ((bf16[16,64,768]{2,1,0:T(8,128)(2,1)}), bf16[16,64,768]{2,1,0:T(8,128)(2,1)S(1)}, u32[]{:S(2)}, u32[]{:S(2)}) async-start(bf16[16,64,768]{2,1,0:T(8,128)(2,1)} %bitcast.86), calls=%async_computation.2 | async-start | bytes 3145728 | tf_op jit(solution)/shard_map/all_to_all | solution.py:916
  319.5 42.5 %expert.3 = (bf16[1024,3072]{1,0:T(8,128)(2,1)}, bf16[1024,3072]{1,0:T(8,128)(2,1)}, bf16[1024,768]{1,0:T(8,128)(2,1)}, bf16[1024,768]{1,0:T(8,128)(2,1)}, f32[1024,1]{1,0:T(8,128)}, /*index=5*/f32[768,128]{1,0:T(8,128)}) custom-call(bf16[1024,768]{1,0:T(8,128)(2,1)} %bitcast.75, bf16[16,128,768]{2,1,0:T(8,128)(2,1)} %copy-done, ...), custom_call_target="tpu_custom_call" | custom-call | flops 966367616 | bytes 1101004 | tf_op jit(solution)/shard_map/expert/pallas_call | solution.py:535
  362.1 6.3 %all-to-all-start.4 = ((bf16[16,64,768]{2,1,0:T(8,128)(2,1)}), bf16[16,64,768]{2,1,0:T(8,128)(2,1)S(1)}, u32[]{:S(2)}, u32[]{:S(2)}) async-start(bf16[16,64,768]{2,1,0:T(8,128)(2,1)} %bitcast.85), calls=%async_computation.4 | async-start | bytes 3145728 | tf_op jit(solution)/shard_map/all_to_all | solution.py:916
  370.4 29.0 %expert_weights.1 = (bf16[768,3072]{1,0:T(8,128)(2,1)}, bf16[3072,768]{1,0:T(8,128)(2,1)}) custom-call(bf16[1024,768]{1,0:T(8,128)(2,1)} %bitcast.74, bf16[1024,768]{1,0:T(8,128)(2,1)} %bitcast.76, f32[1024,1]{1,0:T(8,128)} %get-tuple-element.89.refs_2_, f32[1024,1]{1,0:T(8,128)} %get-tuple-element.90.refs_3_, bf16[1024,3072]{1,0:T(8,128)(2,1)} %get-tuple-element.91.refs_4_, ...), custom_call_target="tpu_custom_call" | custom-call | flops 19327352832 | bytes 34603008 | tf_op jit(solution)/shard_map/expert_weights/pallas_call | solution.py:611
  401.5 13.0 %middle_back.1 = (f32[1024,768]{1,0:T(8,128)}, bf16[1024,768]{1,0:T(8,128)(2,1)}, bf16[1024,768]{1,0:T(8,128)(2,1)}, f32[1,768]{1,0:T(1,128)}) custom-call(bf16[1024,768]{1,0:T(8,128)(2,1)} %bitcast.83, bf16[1024,768]{1,0:T(8,128)(2,1)} %bitcast.84, s32[1024,1]{1,0:T(8,128)} %get-tuple-element.85.refs_2_, f32[1024,768]{1,0:T(8,128)} %get-tuple-element.86.refs_3_, ...), custom_call_target="tpu_custom_call" | custom-call | flops 4429185024 | bytes 12582912 | tf_op jit(solution)/shard_map/middle_back/pallas_call | solution.py:684
  425.5 8.9 %all-to-all-start.5 = ((bf16[16,64,768]{2,1,0:T(8,128)(2,1)}), bf16[16,64,768]{2,1,0:T(8,128)(2,1)}, u32[]{:S(2)}, u32[]{:S(2)}) async-start(bf16[16,64,768]{2,1,0:T(8,128)(2,1)} %bitcast.24), calls=%async_computation.5 | async-start | bytes 3145728 | tf_op jit(solution)/shard_map/all_to_all | solution.py:916
  436.5 27.0 %attend_back.2 = (bf16[1024,1152]{1,0:T(8,128)(2,1)}, f32[6,8,128]{2,1,0:T(8,128)}, f32[6,1,512]{2,1,0:T(1,128)}) custom-call(bf16[1024,2304]{1,0:T(8,128)(2,1)} %get-tuple-element.69.q_ref.k_ref.v_ref, bf16[1024,2304]{1,0:T(8,128)(2,1)} %get-tuple-element.69.q_ref.k_ref.v_ref, bf16[1024,2304]{1,0:T(8,128)(2,1)} %get-tuple-element.69.q_ref.k_ref.v_ref, ...), custom_call_target="tpu_custom_call" | custom-call | flops 16106127360 | bytes 6291456 | tf_op jit(solution)/shard_map/attend_back/pallas_call | solution.py:358
  468.9 6.2 weights_back.2
  484.9 26.9 %attend_back.3 = (bf16[1024,1152]{1,0:T(8,128)(2,1)}, f32[6,8,128]{2,1,0:T(8,128)}, f32[6,1,512]{2,1,0:T(1,128)}) custom-call(bf16[1024,2304]{1,0:T(8,128)(2,1)} %get-tuple-element.69.q_ref.k_ref.v_ref, bf16[1024,2304]{1,0:T(8,128)(2,1)} %get-tuple-element.69.q_ref.k_ref.v_ref, bf16[1024,2304]{1,0:T(8,128)(2,1)} %get-tuple-element.69.q_ref.k_ref.v_ref, ...), custom_call_target="tpu_custom_call" | custom-call | flops 16106127360 | bytes 6291456 | tf_op jit(solution)/shard_map/attend_back/pallas_call | solution.py:358
  521.3 6.2 weights_back.3
  534.5 10.1 %tokens_back.1 = (f32[1024,768]{1,0:T(8,128)}, f32[1,768]{1,0:T(1,128)}) custom-call(bf16[1024,1152]{1,0:T(8,128)(2,1)} %get-tuple-element.103.grads.g_left, bf16[1024,1152]{1,0:T(8,128)(2,1)} %get-tuple-element.110.grads.g_right, bf16[768,1152]{1,0:T(8,128)(2,1)} %bitcast.72, bf16[768,1280]{1,0:T(8,128)(2,1)} %bitcast.70, bf16[1024,768]{1,0:T(8,128)(2,1)} %tokens.3, ...), custom_call_target="tpu_custom_call" | custom-call | flops 3623878656 | bytes 12582912 | tf_op jit(solution)/shard_map/tokens_back/pallas_call | solution.py:748
  558.9 8.3 %mix.1 = f32[1024,768]{1,0:T(8,128)} custom-call(bf16[1024,768]{1,0:T(8,128)(2,1)} %bitcast.25.refs_0_, bf16[1024,768]{1,0:T(8,128)(2,1)} %bitcast.27.refs_1_, s32[1024,1]{1,0:T(8,128)} %get-tuple-element.85.refs_2_, f32[1024,768]{1,0:T(8,128)} %get-tuple-element.86.refs_3_, f32[1024,1]{1,0:T(8,128)} %get-tuple-element.113.refs_4_), custom_call_target="tpu_custom_call" | custom-call | flops 3221225472 | bytes 9437184 | tf_op jit(solution)/shard_map/mix/pallas_call | solution.py:719
  578.7 6.0 collective-permute-done.18
  587.8 9.8 %collective-permute-done.20 = bf16[2,2,2,1,1,24,1152]{6,5,4,3,2,1,0:T(8,128)(2,1)S(1)} collective-permute-done((bf16[2,2,2,1,1,24,1152]{6,5,4,3,2,1,0:T(8,128)(2,1)S(1)}, bf16[2,2,2,1,1,24,1152]{6,5,4,3,2,1,0:T(8,128)(2,1)S(1)}, u32[]{:S(2)}, u32[]{:S(2)}) %collective-permute-start.20) | collective-permute-done | bytes 442400 | tf_op jit(solution)/shard_map/ppermute | solution.py:792
  (275 shorter events, 164.6 us)
Async XLA Ops:
  8.7 35.4 %collective-permute-start.5 = (bf16[1,1,1,1,1,24,1152]{6,5,4,3,2,1,0:T(8,128)(2,1)S(1)}, bf16[1,1,1,1,1,24,1152]{6,5,4,3,2,1,0:T(8,128)(2,1)S(1)}, u32[]{:S(2)}, u32[]{:S(2)}) collective-permute-start(bf16[1,1,1,1,1,24,1152]{6,5,4,3,2,1,0:T(8,128)(2,1)S(1)} %maximum_bitcast_fusion.2), channel_id=1, source_target_pairs={{0,8},{1,9},{2,10},{3,11},{4,12},{5,13},{6,14},{7,15},{8,0},{9,1},... | collective-permute-start | bytes 165896 | tf_op jit(solution)/shard_map/ppermute | solution.py:792
  15.2 30.9 %collective-permute-start = (bf16[1,1,1,1,1,24,1280]{6,5,4,3,2,1,0:T(8,128)(2,1)S(1)}, bf16[1,1,1,1,1,24,1280]{6,5,4,3,2,1,0:T(8,128)(2,1)S(1)}, u32[]{:S(2)}, u32[]{:S(2)}) collective-permute-start(bf16[1,1,1,1,1,24,1280]{6,5,4,3,2,1,0:T(8,128)(2,1)S(1)} %bitcast.88), channel_id=1, source_target_pairs={{0,8},{1,9},{2,10},{3,11},{4,12},{5,13},{6,14},{7,15},{8,0},{9,1},... | collective-permute-start | bytes 184328 | tf_op jit(solution)/shard_map/ppermute | solution.py:792
  15.2 22.5 %collective-permute-start.10 = (bf16[16,12]{1,0:T(8,128)(2,1)}, bf16[16,12]{1,0:T(8,128)(2,1)S(1)}, u32[]{:S(2)}, u32[]{:S(2)}) collective-permute-start(bf16[16,12]{1,0:T(8,128)(2,1)} %param.22), channel_id=1, source_target_pairs={{0,16},{16,0},{1,17},{17,1},{2,18},{18,2},{3,19},{19,3},{4,20},{20... | collective-permute-start | bytes 1160 | tf_op jit(solution)/shard_map/ppermute | solution.py:792
  26.6 174.4 %collective-permute-start.11 = (bf16[1,384,3072]{2,1,0:T(8,128)(2,1)}, bf16[1,384,3072]{2,1,0:T(8,128)(2,1)}, u32[]{:S(2)}, u32[]{:S(2)}) collective-permute-start(bf16[1,384,3072]{2,1,0:T(8,128)(2,1)} %param.26), channel_id=1, source_target_pairs={{0,16},{16,0},{1,17},{17,1},{2,18},{18,2},{3,19},{19,3},{4,20},{20... | collective-permute-start | bytes 7077896 | tf_op jit(solution)/shard_map/ppermute | solution.py:792
  26.8 183.9 %all-to-all-start = ((bf16[16,128,768]{2,1,0:T(8,128)(2,1)}), bf16[16,128,768]{2,1,0:T(8,128)(2,1)S(1)}, u32[]{:S(2)}, u32[]{:S(2)}) async-start(bf16[16,128,768]{2,1,0:T(8,128)(2,1)} %bitcast.81), calls=%async_computation | async-start | bytes 6291456 | tf_op jit(solution)/shard_map/all_to_all | solution.py:916
  33.1 177.6 %all-gather.2.cloned.1.call-start = ((), (), s32[]{:S(2)}) async-start(), calls=%async_computation.7 | async-start | bytes 1216512 | tf_op jit(solution)/shard_map/all_gather | solution.py:910
  33.9 172.3 %collective-permute-start.12 = (bf16[1,1536,768]{2,1,0:T(8,128)(2,1)}, bf16[1,1536,768]{2,1,0:T(8,128)(2,1)}, u32[]{:S(2)}, u32[]{:S(2)}) collective-permute-start(bf16[1,1536,768]{2,1,0:T(8,128)(2,1)} %param.27), channel_id=1, source_target_pairs={{0,16},{16,0},{1,17},{17,1},{2,18},{18,2},{3,19},{19,3},{4,20},{20... | collective-permute-start | bytes 7077896 | tf_op jit(solution)/shard_map/ppermute | solution.py:792
  44.1 44.7 %collective-permute-start.6 = (bf16[1,2,1,1,1,24,1152]{6,5,4,3,2,1,0:T(8,128)(2,1)S(1)}, bf16[1,2,1,1,1,24,1152]{6,5,4,3,2,1,0:T(8,128)(2,1)S(1)}, u32[]{:S(2)}, u32[]{:S(2)}) collective-permute-start(bf16[1,2,1,1,1,24,1152]{6,5,4,3,2,1,0:T(8,128)(2,1)S(1)} %pad_maximum_fusion.10), channel_id=1, source_target_pairs={{0,4},{1,5},{2,6},{3,7},{4,0},{5,1},{6,2},{7,3},{8,12},{9,13},{10,... | collective-permute-start | bytes 331784 | tf_op jit(solution)/shard_map/ppermute | solution.py:792
  46.2 45.4 %collective-permute-start.1 = (bf16[1,2,1,1,1,24,1280]{6,5,4,3,2,1,0:T(8,128)(2,1)S(1)}, bf16[1,2,1,1,1,24,1280]{6,5,4,3,2,1,0:T(8,128)(2,1)S(1)}, u32[]{:S(2)}, u32[]{:S(2)}) collective-permute-start(bf16[1,2,1,1,1,24,1280]{6,5,4,3,2,1,0:T(8,128)(2,1)S(1)} %pad_maximum_fusion.9), channel_id=1, source_target_pairs={{0,4},{1,5},{2,6},{3,7},{4,0},{5,1},{6,2},{7,3},{8,12},{9,13},{10,... | collective-permute-start | bytes 368648 | tf_op jit(solution)/shard_map/ppermute | solution.py:792
  91.7 48.0 %collective-permute-start.2 = (bf16[1,2,2,1,1,24,1280]{6,5,4,3,2,1,0:T(8,128)(2,1)S(1)}, bf16[1,2,2,1,1,24,1280]{6,5,4,3,2,1,0:T(8,128)(2,1)S(1)}, u32[]{:S(2)}, u32[]{:S(2)}) collective-permute-start(bf16[1,2,2,1,1,24,1280]{6,5,4,3,2,1,0:T(8,128)(2,1)S(1)} %pad_maximum_fusion.7), channel_id=1, source_target_pairs={{0,16},{16,0},{1,17},{17,1},{2,18},{18,2},{3,19},{19,3},{4,20},{20... | collective-permute-start | bytes 737288 | tf_op jit(solution)/shard_map/ppermute | solution.py:792
  99.9 47.2 %collective-permute-start.8 = (bf16[1,2,2,2,1,24,1152]{6,5,4,3,2,1,0:T(8,128)(2,1)S(1)}, bf16[1,2,2,2,1,24,1152]{6,5,4,3,2,1,0:T(8,128)(2,1)S(1)}, u32[]{:S(2)}, u32[]{:S(2)}) collective-permute-start(bf16[1,2,2,2,1,24,1152]{6,5,4,3,2,1,0:T(8,128)(2,1)S(1)} %pad_maximum_fusion.6), channel_id=1, source_target_pairs={{0,16},{16,0},{1,17},{17,1},{2,18},{18,2},{3,19},{19,3},{4,20},{20... | collective-permute-start | bytes 1327112 | tf_op jit(solution)/shard_map/ppermute | solution.py:792
  263.4 49.5 %all-to-all-start.3 = ((bf16[16,64,768]{2,1,0:T(8,128)(2,1)}), bf16[16,64,768]{2,1,0:T(8,128)(2,1)S(1)}, u32[]{:S(2)}, u32[]{:S(2)}) async-start(bf16[16,64,768]{2,1,0:T(8,128)(2,1)} %bitcast.20), calls=%async_computation.3 | async-start | bytes 3145728 | tf_op jit(solution)/shard_map/all_to_all | solution.py:916
  312.9 49.1 %all-to-all-start.2 = ((bf16[16,64,768]{2,1,0:T(8,128)(2,1)}), bf16[16,64,768]{2,1,0:T(8,128)(2,1)S(1)}, u32[]{:S(2)}, u32[]{:S(2)}) async-start(bf16[16,64,768]{2,1,0:T(8,128)(2,1)} %bitcast.86), calls=%async_computation.2 | async-start | bytes 3145728 | tf_op jit(solution)/shard_map/all_to_all | solution.py:916
  362.1 38.3 %all-to-all-start.4 = ((bf16[16,64,768]{2,1,0:T(8,128)(2,1)}), bf16[16,64,768]{2,1,0:T(8,128)(2,1)S(1)}, u32[]{:S(2)}, u32[]{:S(2)}) async-start(bf16[16,64,768]{2,1,0:T(8,128)(2,1)} %bitcast.85), calls=%async_computation.4 | async-start | bytes 3145728 | tf_op jit(solution)/shard_map/all_to_all | solution.py:916
  424.8 44.0 %collective-permute-start.13 = (bf16[2,2,2,2,1,24,768]{6,5,4,3,2,1,0:T(8,128)(2,1)S(1)}, bf16[2,2,2,2,1,24,768]{6,5,4,3,2,1,0:T(8,128)(2,1)S(1)}, u32[]{:S(2)}, u32[]{:S(2)}) collective-permute-start(bf16[2,2,2,2,1,24,768]{6,5,4,3,2,1,0:T(8,128)(2,1)S(1)} %select_convert_fusion.3), channel_id=1, source_target_pairs={{0,1},{1,0},{2,3},{3,2},{4,5},{5,4},{6,7},{7,6},{8,9},{9,8},{10,11... | collective-permute-start | bytes 1769480 | tf_op jit(solution)/shard_map/ppermute | solution.py:792
  425.5 54.4 %all-to-all-start.5 = ((bf16[16,64,768]{2,1,0:T(8,128)(2,1)}), bf16[16,64,768]{2,1,0:T(8,128)(2,1)}, u32[]{:S(2)}, u32[]{:S(2)}) async-start(bf16[16,64,768]{2,1,0:T(8,128)(2,1)} %bitcast.24), calls=%async_computation.5 | async-start | bytes 3145728 | tf_op jit(solution)/shard_map/all_to_all | solution.py:916
  434.4 81.6 %collective-permute-start.16 = (bf16[1536,768]{1,0:T(8,128)(2,1)}, bf16[1536,768]{1,0:T(8,128)(2,1)}, u32[]{:S(2)}, u32[]{:S(2)}) collective-permute-start(bf16[1536,768]{1,0:T(8,128)(2,1)} %get-tuple-element.157), channel_id=1, source_target_pairs={{0,16},{16,0},{1,17},{17,1},{2,18},{18,2},{3,19},{19,3},{4,20},{20... | collective-permute-start | bytes 7077896 | tf_op jit(solution)/shard_map/ppermute | solution.py:792
  435.0 169.5 %collective-permute-start.30 = (bf16[384,3072]{1,0:T(8,128)(2,1)}, bf16[384,3072]{1,0:T(8,128)(2,1)}, u32[]{:S(2)}, u32[]{:S(2)}) collective-permute-start(bf16[384,3072]{1,0:T(8,128)(2,1)} %get-tuple-element.155), channel_id=1, source_target_pairs={{0,16},{16,0},{1,17},{17,1},{2,18},{18,2},{3,19},{19,3},{4,20},{20... | collective-permute-start | bytes 7077896 | tf_op jit(solution)/shard_map/ppermute | solution.py:792
  477.4 36.2 %collective-permute-start.15 = (bf16[2,2,2,2,1,24,1152]{6,5,4,3,2,1,0:T(8,128)(2,1)S(1)}, bf16[2,2,2,2,1,24,1152]{6,5,4,3,2,1,0:T(8,128)(2,1)}, u32[]{:S(2)}, u32[]{:S(2)}) collective-permute-start(bf16[2,2,2,2,1,24,1152]{6,5,4,3,2,1,0:T(8,128)(2,1)S(1)} %select_convert_fusion.2), channel_id=1, source_target_pairs={{0,1},{1,0},{2,3},{3,2},{4,5},{5,4},{6,7},{7,6},{8,9},{9,8},{10,11... | collective-permute-start | bytes 2654216 | tf_op jit(solution)/shard_map/ppermute | solution.py:792
  477.6 34.2 %collective-permute-start.14 = (bf16[2,2,2,1,1,24,768]{6,5,4,3,2,1,0:T(8,128)(2,1)S(1)}, bf16[2,2,2,1,1,24,768]{6,5,4,3,2,1,0:T(8,128)(2,1)}, u32[]{:S(2)}, u32[]{:S(2)}) collective-permute-start(bf16[2,2,2,1,1,24,768]{6,5,4,3,2,1,0:T(8,128)(2,1)S(1)} %select_convert_fusion.7), channel_id=1, source_target_pairs={{0,2},{1,3},{2,0},{3,1},{4,6},{5,7},{6,4},{7,5},{8,10},{9,11},{10,... | collective-permute-start | bytes 884744 | tf_op jit(solution)/shard_map/ppermute | solution.py:792
  479.9 41.4 %all-to-all-start.6 = ((bf16[16,64,768]{2,1,0:T(8,128)(2,1)}), bf16[16,64,768]{2,1,0:T(8,128)(2,1)}, u32[]{:S(2)}, u32[]{:S(2)}) async-start(bf16[16,64,768]{2,1,0:T(8,128)(2,1)} %bitcast.82), calls=%async_computation.6 | async-start | bytes 3145728 | tf_op jit(solution)/shard_map/all_to_all | solution.py:916
  555.2 21.8 %collective-permute-start.17 = (bf16[1,2,2,2,1,24,1152]{6,5,4,3,2,1,0:T(8,128)(2,1)}, bf16[1,2,2,2,1,24,1152]{6,5,4,3,2,1,0:T(8,128)(2,1)S(1)}, u32[]{:S(2)}, u32[]{:S(2)}) collective-permute-start(bf16[1,2,2,2,1,24,1152]{6,5,4,3,2,1,0:T(8,128)(2,1)} %select_convert_fusion.5), channel_id=1, source_target_pairs={{0,16},{16,0},{1,17},{17,1},{2,18},{18,2},{3,19},{19,3},{4,20},{20... | collective-permute-start | bytes 1327112 | tf_op jit(solution)/shard_map/ppermute | solution.py:792
  555.8 29.0 %collective-permute-start.19 = (bf16[2,2,2,2,1,24,1152]{6,5,4,3,2,1,0:T(8,128)(2,1)}, bf16[2,2,2,2,1,24,1152]{6,5,4,3,2,1,0:T(8,128)(2,1)}, u32[]{:S(2)}, u32[]{:S(2)}) collective-permute-start(bf16[2,2,2,2,1,24,1152]{6,5,4,3,2,1,0:T(8,128)(2,1)} %select_convert_fusion.1), channel_id=1, source_target_pairs={{0,1},{1,0},{2,3},{3,2},{4,5},{5,4},{6,7},{7,6},{8,9},{9,8},{10,11... | collective-permute-start | bytes 2654216 | tf_op jit(solution)/shard_map/ppermute | solution.py:792
  555.8 15.8 %collective-permute-start.22 = (bf16[1,2,2,1,1,24,768]{6,5,4,3,2,1,0:T(8,128)(2,1)S(1)}, bf16[1,2,2,1,1,24,768]{6,5,4,3,2,1,0:T(8,128)(2,1)S(1)}, u32[]{:S(2)}, u32[]{:S(2)}) collective-permute-start(bf16[1,2,2,1,1,24,768]{6,5,4,3,2,1,0:T(8,128)(2,1)S(1)} %select_convert_fusion.12), channel_id=1, source_target_pairs={{0,16},{16,0},{1,17},{17,1},{2,18},{18,2},{3,19},{19,3},{4,20},{20... | collective-permute-start | bytes 442376 | tf_op jit(solution)/shard_map/ppermute | solution.py:792
  (44 other events, 306.8 us)
Sparse Core Ops, SparseCore 0:
  36.9 85.4 all-gather.1

commit v2 on v1

--- a/solution.py
+++ b/solution.py
@@ -130,7 +130,7 @@
     low = wide.astype(BF)
     turned[...] = wide.T.astype(BF)
     qkv[:, :SPLIT] = dot(low, left[...]).astype(BF)
-    qkv[:, SPLIT:] = dot(low, right[:, :SPLIT]).astype(BF)
+    qkv[:, SPLIT:] = dot(low, right[...]).astype(BF)
 
 
 def project(tokens, gain, left, right):
@@ -139,7 +139,7 @@
     return pl.pallas_call(
         project_kernel,
         grid=(TOK // block,),
-        in_specs=[rows, whole((1, D)), whole(left.shape), whole(right.shape)],
+        in_specs=[rows, whole((1, D)), whole((D, SPLIT)), whole((D, SPLIT))],
         out_specs=[
             pl.BlockSpec((D, block), lambda r: (0, r)),
             pl.BlockSpec((block, 3 * D), lambda r: (r, 0)),
@@ -418,8 +418,10 @@
     )
 
 
-def middle_kernel(context, tokens, w_out, gain, router, route_col, slot_row, experts,
-                  middle, sending_low, sending_high, gate, normed):
+def middle_kernel(context, tokens, out_left, out_right, gain, router, route_col, slot_row, experts,
+                  middle, sending_low, sending_high, gate, normed, w_out):
+    w_out[:, :SIDE] = out_left[...]
+    w_out[:, SIDE:] = out_right[...]
     for first in range(0, TOK, 256):
         at = slice(first, first + 256)
         mid = tokens[at, :].astype(F32) + dot(context[at, :], w_out[...])
@@ -442,25 +444,43 @@
     return raised / jnp.sum(raised, axis=1, keepdims=True)
 
 
-def make_middle(context, tokens, w_out, gain, router, routes, slot_row, experts, capacity):
+def make_middle(context, tokens, left, right, gain, router, routes, slot_row, experts, capacity):
     total = experts * capacity
 
     def kernel(*refs):
-        middle_kernel(*refs[:7], experts, *refs[7:])
-
+        middle_kernel(*refs[:8], experts, *refs[8:])
+
+    out_half = pl.BlockSpec((D, SIDE), lambda r: (0, 3))
     return pl.pallas_call(
         kernel,
+        grid=(1,),
+        in_specs=[
+            whole((TOK, D)),
+            whole((TOK, D)),
+            out_half,
+            out_half,
+            whole((1, D)),
+            whole(router.shape),
+            whole((TOK, 1)),
+            whole((1, TOK)),
+        ],
+        out_specs=(
+            whole((TOK, D)),
+            whole((total // 2, D)),
+            whole((total // 2, D)),
+            whole((TOK, 1)),
+        ),
         out_shape=(
             jax.ShapeDtypeStruct((TOK, D), F32),
             jax.ShapeDtypeStruct((total // 2, D), BF),
             jax.ShapeDtypeStruct((total // 2, D), BF),
             jax.ShapeDtypeStruct((TOK, 1), F32),
         ),
-        scratch_shapes=[pltpu.VMEM((TOK, D), BF)],
+        scratch_shapes=[pltpu.VMEM((TOK, D), BF), pltpu.VMEM((D, D), BF)],
         compiler_params=params(),
         cost_estimate=cost(2 * total * TOK * D + 2 * TOK * D * D, 12 * TOK * D + 2 * total * D),
         name="middle",
-    )(context, tokens, w_out, gain, router, routes, slot_row)
+    )(context, tokens, left, right, gain, router, routes, slot_row)
 
 
 def gelu_parts(v):
@@ -569,10 +589,16 @@
     )(x, c, w_first, w_second, router, router_t, mine)
 
 
-def expert_weights_kernel(parts, *refs):
+def expert_weights_kernel(parts, side, *refs):
+    if side is not None:
+        side, refs = refs[0], refs[1:]
     xs, gates = refs[:parts], refs[parts : 2 * parts]
     acts, dhs = refs[2 * parts : 3 * parts], refs[3 * parts : 4 * parts]
-    cots, grad_first, grad_second, x_t, c_t = refs[4 * parts :]
+    cots = refs[4 * parts]
+    if side is None:
+        grad_first, grad_second, x_t, c_t = refs[4 * parts + 1 :]
+    else:
+        kept_first, sent_first, kept_second, sent_second, x_t, c_t, whole_first = refs[4 * parts + 1 :]
     rows = xs[0].shape[0]
     share = cots.shape[1] // parts
     chunk = 256
@@ -599,40 +625,74 @@
         two = dot(c_t[:, at], acts[part][...])
         first_sum = one if first_sum is None else first_sum + one
         second_sum = two if second_sum is None else second_sum + two
-    grad_first[...] = first_sum.astype(BF)
-    grad_second[...] = second_sum.T.astype(BF)
-
-
-def expert_weights(xs, cots, gates, acts, dhs):
+    if side is None:
+        grad_first[...] = first_sum.astype(BF)
+        grad_second[...] = second_sum.T.astype(BF)
+        return
+    mine = side[0]
+    half = D // 2
+    whole_first[...] = first_sum.astype(BF)
+    kept_first[...] = whole_first[pl.ds(pl.multiple_of(mine * half, half), half), :]
+    sent_first[...] = whole_first[pl.ds(pl.multiple_of((1 - mine) * half, half), half), :]
+    here = pl.program_id(0) // (pl.num_programs(0) // 2) == mine
+
+    @pl.when(here)
+    def _():
+        kept_second[...] = second_sum.T.astype(BF)
+
+    @pl.when(jnp.logical_not(here))
+    def _():
+        sent_second[...] = second_sum.T.astype(BF)
+
+
+def expert_weights(xs, cots, gates, acts, dhs, side):
     parts = len(xs)
     rows = xs[0].shape[0]
     hidden_size = acts[0].shape[1]
-    tile = pl.BlockSpec((rows, FF_TILE), lambda f: (0, f))
-    return pl.pallas_call(
-        functools.partial(expert_weights_kernel, parts),
-        grid=(hidden_size // FF_TILE,),
-        in_specs=[whole((rows, D))] * parts
+    steps = hidden_size // FF_TILE
+    in_specs = (
+        [whole((rows, D))] * parts
         + [whole((rows, 1))] * parts
-        + [tile] * (2 * parts)
-        + [whole(cots.shape)],
-        out_specs=[
+        + [pl.BlockSpec((rows, FF_TILE), lambda f, *_: (0, f))] * (2 * parts)
+        + [whole(cots.shape)]
+    )
+    scratch = [pltpu.VMEM((D, parts * rows), BF), pltpu.VMEM((D, parts * rows), BF)]
+    if side is None:
+        out_specs = [
             pl.BlockSpec((D, FF_TILE), lambda f: (0, f)),
             pl.BlockSpec((FF_TILE, D), lambda f: (f, 0)),
-        ],
-        out_shape=[
-            jax.ShapeDtypeStruct((D, hidden_size), BF),
-            jax.ShapeDtypeStruct((hidden_size, D), BF),
-        ],
-        scratch_shapes=[
-            pltpu.VMEM((D, parts * rows), BF),
-            pltpu.VMEM((D, parts * rows), BF),
-        ],
+        ]
+        shapes = [(D, hidden_size), (hidden_size, D)]
+    else:
+        columns = pl.BlockSpec((D // 2, FF_TILE), lambda f, s: (0, f))
+
+        def rows_of(place):
+            def index(f, s):
+                start = jnp.where(s[0] == 1, place, 1 - place) * (steps // 2)
+                return (jnp.clip(f - start, 0, steps // 2 - 1), 0)
+
+            return pl.BlockSpec((FF_TILE, D), index)
+
+        out_specs = [columns, columns, rows_of(1), rows_of(0)]
+        shapes = [(D // 2, hidden_size)] * 2 + [(hidden_size // 2, D)] * 2
+        scratch = scratch + [pltpu.VMEM((D, FF_TILE), BF)]
+    prefetched = () if side is None else (side,)
+    return pl.pallas_call(
+        functools.partial(expert_weights_kernel, parts, side is not None or None),
+        grid_spec=pltpu.PrefetchScalarGridSpec(
+            num_scalar_prefetch=len(prefetched),
+            grid=(steps,),
+            in_specs=in_specs,
+            out_specs=out_specs,
+            scratch_shapes=scratch,
+        ),
+        out_shape=[jax.ShapeDtypeStruct(shape, BF) for shape in shapes],
         compiler_params=params(("arbitrary",)),
         cost_estimate=cost(
             4 * parts * rows * D * hidden_size, 4 * (parts * rows + D) * hidden_size, share=1
         ),
         name="expert_weights",
-    )(*xs, *gates, *acts, *dhs, cots)
+    )(*prefetched, *xs, *gates, *acts, *dhs, cots)
 
 
 def rms_back(values, factor, grad):
@@ -659,7 +719,16 @@
 
 def middle_back_kernel(parts, *refs):
     backs = refs[:parts]
-    slot_col, middle, cot, gain, w_out, grad_middle, grad_attn, grad_context, grad_gain = refs[parts:]
+    (
+        slot_col, middle, cot, gain, out_left, out_right,
+        grad_middle, grad_attn, grad_context, grad_gain, w_out,
+    ) = refs[parts:]
+
+    @pl.when(pl.program_id(0) == 0)
+    def _():
+        w_out[:, :SIDE] = out_left[...]
+        w_out[:, SIDE:] = out_right[...]
+
     grad_normed = undispatch(slot_col[...], backs)
     part, gain_part = rms_back(middle[...], gain[...], grad_normed)
     grad = cot[...].astype(F32) + part
@@ -677,7 +746,7 @@
         grad_gain[...] += gain_part
 
 
-def middle_back(backs, slot_col, middle, cot, gain, w_out):
+def middle_back(backs, slot_col, middle, cot, gain, left, right):
     parts = len(backs)
     block = 256
     rows = pl.BlockSpec((block, D), lambda r: (r, 0))
@@ -690,9 +759,11 @@
             rows,
             rows,
             whole((1, D)),
-            whole((D, D)),
+            pl.BlockSpec((D, SIDE), lambda r: (0, 3)),
+            pl.BlockSpec((D, SIDE), lambda r: (0, 3)),
         ],
         out_specs=[rows, rows, rows, whole((1, D))],
+        scratch_shapes=[pltpu.VMEM((D, D), BF)],
         out_shape=[
             jax.ShapeDtypeStruct((TOK, D), F32),
             jax.ShapeDtypeStruct((TOK, D), BF),
@@ -702,7 +773,7 @@
         compiler_params=params(("arbitrary",)),
         cost_estimate=cost(2 * 2 * TOK * TOK * D + 2 * TOK * D * D, 16 * TOK * D, share=1),
         name="middle_back",
-    )(*backs, slot_col, middle, cot, gain, w_out)
+    )(*backs, slot_col, middle, cot, gain, left, right)
 
 
 def mix_kernel(parts, *refs):
@@ -729,7 +800,7 @@
 
 
 def tokens_back_kernel(g_left, g_right, left, right, tokens, gain, grad_middle, grad_tokens, grad_gain):
-    grad_normed = dot(g_left[...], left[...], 1, 1) + dot(g_right[...], right[:, :SPLIT], 1, 1)
+    grad_normed = dot(g_left[...], left[...], 1, 1) + dot(g_right[...], right[...], 1, 1)
     part, gain_part = rms_back(tokens[...].astype(F32), gain[...], grad_normed)
     grad_tokens[...] = grad_middle[...] + part
 
@@ -751,8 +822,8 @@
         in_specs=[
             pl.BlockSpec((block, SPLIT), lambda r: (r, 0)),
             pl.BlockSpec((block, SPLIT), lambda r: (r, 0)),
-            whole(left.shape),
-            whole(right.shape),
+            whole((D, SPLIT)),
+            whole((D, SPLIT)),
             rows,
             whole((1, D)),
             rows,
@@ -815,11 +886,13 @@
     return (rest + along + dp + [core], rest + dp + along + [core])
 
 
-def gather_rows(shard, order):
+def gather_rows(shard, order, *before_dp):
     bits = axis_bits("dp", "expert")
     block = shard.reshape((1,) * len(bits) + shard.shape)
     for place in order:
         axis, bit = bits[place]
+        if axis == "dp" and before_dp:
+            block = after(block, *before_dp)
         other = swap(block, axis, bit)
         upper = on_upper(axis, bit)
         block = jnp.concatenate(
@@ -856,25 +929,23 @@
     return total
 
 
-def gather_dp(block, axis):
+def gather_dp(block, axis, other=None):
     if lax.axis_size("dp") != 2:
         return lax.all_gather(block, "dp", axis=axis, tiled=True)
-    other = swap(block, "dp", 1)
+    if other is None:
+        other = swap(block, "dp", 1)
     upper = on_upper("dp", 1)
     return jnp.concatenate(
         [jnp.where(upper, other, block), jnp.where(upper, block, other)], axis=axis
     )
 
 
-def scatter_dp(total, *others):
-    if lax.axis_size("dp") != 2:
+def scatter_dp(halves, *others):
+    if len(halves) == 1:
         return lax.psum_scatter(
-            total[None], "dp", scatter_dimension=1, tiled=True
+            halves[0][None], "dp", scatter_dimension=1, tiled=True
         ).astype(F32)
-    half = total.shape[0] // 2
-    upper = on_upper("dp", 1)
-    sent = jnp.where(upper, total[:half], total[half:])
-    kept = jnp.where(upper, total[half:], total[:half])
+    kept, sent = halves
     return (after(kept, *others).astype(F32) + swap(sent, "dp", 1).astype(F32))[None]
 
 
@@ -890,7 +961,6 @@
     capacity = 2 * TOK // experts
     shard = w_query.shape[0]
     lanes = -(-(experts + 2) // LANES) * LANES
-    everyone = ("dp", "expert")
 
     small = jnp.concatenate(
         [
@@ -902,13 +972,18 @@
         axis=1,
     )
     first, second = orders()
-    kinds = (w_query, w_key, w_value)
-    left = gather_rows(jnp.concatenate([w[:, :SIDE] for w in kinds], axis=1), first)
+    kinds = (w_query, w_key, w_value, w_out)
+    paired = lax.axis_size("dp") == 2
+    own_first, own_second = expert_in[0], expert_out[0]
+    first_cut, second_cut = own_first.shape[1] // 2, own_second.shape[0] // 2
+    early = [swap(own_first[:, :first_cut], "dp", 1)] if paired else []
+    table = gather_dp(rel_table, 0)
+    left = gather_rows(
+        jnp.concatenate([w[:, :SIDE] for w in kinds], axis=1), first, table, *early
+    )
     right = gather_rows(
-        jnp.concatenate([w[:, SIDE:] for w in kinds] + [small], axis=1), second
-    )
-    full_out = lax.all_gather(w_out, everyone, axis=0, tiled=True)
-    table = gather_dp(rel_table, 0).astype(F32)
+        jnp.concatenate([w[:, SIDE:] for w in kinds] + [small], axis=1), second, table, *early
+    )
 
     slot_col, slot_row, sending_cot = make_slots(routes, cotangent, experts, capacity)
 
@@ -917,25 +992,34 @@
             rows.reshape(experts, -1, D), "expert", split_axis=0, concat_axis=0, tiled=True
         )
 
-    w_first = gather_dp(after(expert_in, slot_row), 1)[0]
-    w_second = gather_dp(after(expert_out, slot_row), 1)[0]
-    cots = exchange(sending_cot)
-
-    extra = right[:, SPLIT:]
+    cots = exchange(after(sending_cot, left, right))
+    if paired:
+        early.append(swap(after(own_first[:, first_cut:], left, right), "dp", 1))
+        early.append(swap(after(own_second[:second_cut], left, right), "dp", 1))
+        late = swap(after(own_second[second_cut:], *early), "dp", 1)
+        other_first = jnp.concatenate(early[:2], axis=1)
+        other_second = jnp.concatenate([early[2], late], axis=0)
+    else:
+        other_first = other_second = None
+    w_first = gather_dp(own_first, 0, other_first)
+    w_second = gather_dp(own_second, 0, other_second)
+
+    extra = right[:, SPLIT + SIDE :]
     full_router = jnp.where(jnp.arange(lanes)[None, :] < experts, extra, jnp.zeros((), BF))
     router_t = full_router.T
     attn_gain = extra[:, experts].astype(F32).reshape(1, D)
     ffn_gain = extra[:, experts + 1].astype(F32).reshape(1, D)
 
     turned, qkv = project(tokens, attn_gain, left, right)
+    table = table.astype(F32)
     query_features, key_features = lane_features(seq_ids.reshape(TOK, 1), table)
     band = jnp.sum(band_onehot()[None, :, :] * table.T[:, None, :], axis=2)[:, None, :]
     context, lse = attend(qkv, query_features, key_features, band)
 
     middle, *sending, gate = make_middle(
-        after(context, cots, w_first), tokens, full_out, ffn_gain, full_router, routes, slot_row, experts, capacity
-    )
-    sending[0] = after(sending[0], w_second)
+        context, tokens, left, right, ffn_gain, full_router, routes, slot_row, experts, capacity
+    )
+    sending[0] = after(sending[0], cots, *early)
     rows_in = [exchange(part).reshape(-1, D) for part in sending]
     mine = lax.axis_index("expert").astype(jnp.int32).reshape(1, 1)
     acts, dhs, results, grads, gates, router_parts = zip(
@@ -947,15 +1031,22 @@
         )
     )
     grads_home = [exchange(part).reshape(-1, D) for part in grads]
-    grad_first, grad_second = expert_weights(
-        rows_in, cots, (after(gates[0], grads_home[0]), *gates[1:]), acts, dhs
-    )
+    weight_parts = expert_weights(
+        rows_in,
+        cots,
+        (after(gates[0], grads_home[0]), *gates[1:]),
+        acts,
+        dhs,
+        lax.axis_index("dp").astype(jnp.int32).reshape(1) if paired else None,
+    )
+    half = len(weight_parts) // 2
+    grad_first, grad_second = weight_parts[:half], weight_parts[half:]
     results_home = [
         exchange(after(part, *grads_home)).reshape(-1, D) for part in results
     ]
-    grads_home[0] = after(grads_home[0], grad_first, grad_second)
+    grads_home[0] = after(grads_home[0], *weight_parts)
     grad_middle, grad_attn, grad_context, grad_gain_f = middle_back(
-        grads_home, slot_col, middle, cotangent, ffn_gain, full_out
+        grads_home, slot_col, middle, cotangent, ffn_gain, left, right
     )
     down, down_other = first[::-1], second[::-1]
     out_block = scatter_step(scatter_start(dot(context, grad_attn, 0, 0)), down_other[0])

time: 634 us -> 560 us (0.88)
  blocking collectives: 42.1 us -> 0 us
  waiting for transfers between devices: 130 us -> 95.1 us
  between operations: 15.3 us -> 2.04 us
  starting transfers between devices: 77.3 us -> 86.8 us
  local copies, waits for them, and re-layouts: 28.5 us -> 36.8 us
    ppermute x31 -> x33, waiting for transfers between devices: 129 us -> 68.8 us  [swap(): lax.ppermute(block, axis, [(place, place ^ bit) for place in range(size)])]
    all_to_all x1 -> x0, blocking collectives: 42.1 us -> none  [exchange(): lax.all_to_all(rows.reshape(experts, -1, D), 'expert', split_axis=0, conc...]
    all_to_all x6 -> x7, waiting for transfers between devices: 0.98 us -> 26.3 us  [exchange(): lax.all_to_all(rows.reshape(experts, -1, D), 'expert', split_axis=0, conc...]
    all_to_all x6 -> x7, starting transfers between devices: 38.3 us -> 46 us  [exchange(): lax.all_to_all(rows.reshape(experts, -1, D), 'expert', split_axis=0, conc...]
    ppermute x31 -> x33, starting transfers between devices: 38.8 us -> 40.9 us  [swap(): lax.ppermute(block, axis, [(place, place ^ bit) for place in range(size)])]
    unnamed x74 -> x78, local copies, waits for them, and re-layouts: 13 us -> 14.2 us
  transfers between devices with their start and end apart: 38 -> 40, of which waited for: 15 -> 16; matrix products, arithmetic and copies ran while one was open for 11% -> 14% of each run, Pallas kernels for 40% -> 48%
where the time goes in v2:
time: 560 us; the launch traced here: 553 us
  Pallas kernels  276 us (49%)
  waiting for transfers between devices  95.1 us (17%)
  starting transfers between devices  86.8 us (16%)
  other arithmetic  52.1 us (9%)
  local copies, waits for them, and re-layouts  36.8 us (7%)
    pallas_call x2, Pallas kernels, run_expert(): pl.pallas_call(functools.partial(expert_kernel, experts), grid=(hidden_si...  84.9 us
    ppermute x33, waiting for transfers between devices, swap(): lax.ppermute(block, axis, [(place, place ^ bit) for place in range(size)])  68.8 us
    pallas_call x2, Pallas kernels, attend_back(): pl.pallas_call(attend_back_kernel, grid=(SIDE_PAIRS,), in_specs=[*(pl.Blo...  53.9 us
    all_to_all x7, starting transfers between devices, exchange(): lax.all_to_all(rows.reshape(experts, -1, D), 'expert', split_axis=0, conc...  46 us
    ppermute x33, starting transfers between devices, swap(): lax.ppermute(block, axis, [(place, place ^ bit) for place in range(size)])  40.9 us
    pallas_call x1, Pallas kernels, attend(): pl.pallas_call(attend_kernel, grid=(PAIRS,), in_specs=[*(pl.BlockSpec((TO...  37 us
    pallas_call x1, Pallas kernels, expert_weights(): pl.pallas_call(functools.partial(expert_weights_kernel, parts, side is no...  31.2 us
    all_to_all x7, waiting for transfers between devices, exchange(): lax.all_to_all(rows.reshape(experts, -1, D), 'expert', split_axis=0, conc...  26.3 us
  transfers between devices with their start and end apart: 40, of which 16 were waited for; matrix products, arithmetic and copies ran while one was open for 14% of the time, Pallas kernels for 48%

profile of v2, /device:TPU:0, one launch (start us, length us, event | category | flops | bytes accessed | tf_op | source)
XLA Modules:
  0.0 552.9 jit_solution(12039649662462277575)
XLA Ops:
  23.0 14.9 %collective-permute-done.3 = bf16[384,1536]{1,0:T(8,128)(2,1)S(1)} collective-permute-done((bf16[384,1536]{1,0:T(8,128)(2,1)S(1)}, bf16[384,1536]{1,0:T(8,128)(2,1)S(1)}, u32[]{:S(2)}, u32[]{:S(2)}) %collective-permute-start.3) | collective-permute-done | bytes 1179680 | tf_op jit(solution)/shard_map/ppermute | solution.py:863
  40.1 8.2 %collective-permute-done.4 = bf16[1,2,2,1,1,24,1664]{6,5,4,3,2,1,0:T(8,128)(2,1)S(1)} collective-permute-done((bf16[1,2,2,1,1,24,1664]{6,5,4,3,2,1,0:T(8,128)(2,1)S(1)}, bf16[1,2,2,1,1,24,1664]{6,5,4,3,2,1,0:T(8,128)(2,1)S(1)}, u32[]{:S(2)}, u32[]{:S(2)}) %collective-permute-start.4) | collective-permute-done | bytes 319520 | tf_op jit(solution)/shard_map/ppermute | solution.py:863
  50.0 8.2 %collective-permute-done.10 = bf16[1,2,2,2,1,24,1536]{6,5,4,3,2,1,0:T(8,128)(2,1)S(1)} collective-permute-done((bf16[1,2,2,2,1,24,1536]{6,5,4,3,2,1,0:T(8,128)(2,1)S(1)}, bf16[1,2,2,2,1,24,1536]{6,5,4,3,2,1,0:T(8,128)(2,1)S(1)}, u32[]{:S(2)}, u32[]{:S(2)}) %collective-permute-start.10) | collective-permute-done | bytes 589856 | tf_op jit(solution)/shard_map/ppermute | solution.py:863
  62.4 7.8 %slots.1 = (s32[1024,1]{1,0:T(8,128)}, s32[1,1024]{1,0:T(1,128)}, bf16[2048,768]{1,0:T(8,128)(2,1)}) custom-call(s32[1024,1]{1,0:T(8,128)} %copy.49.route_col.refs_6_, s32[1,1024]{1,0:T(1,128)} %bitcast.104, bf16[1024,768]{1,0:T(8,128)(2,1)} %refs_4_.1), custom_call_target="tpu_custom_call" | custom-call | flops 161061280 | bytes 471859 | tf_op jit(solution)/shard_map/slots/pallas_call | solution.py:114
  93.0 8.3 %project.1 = (bf16[768,1024]{1,0:T(8,128)(2,1)}, bf16[1024,2304]{1,0:T(8,128)(2,1)}) custom-call(bf16[1024,768]{1,0:T(8,128)(2,1)} %tokens.3, f32[1,768]{1,0:T(1,128)} %reshape.387.gain, bf16[768,1536]{1,0:T(8,128)(2,1)} %bitcast.76, bf16[768,1664]{1,0:T(8,128)(2,1)} %bitcast.70), custom_call_target="tpu_custom_call" | custom-call | flops 181193936 | bytes 471859 | tf_op jit(solution)/shard_map/project/pallas_call | solution.py:139
  101.4 37.0 %attend.1 = (bf16[1024,768]{1,0:T(8,128)(2,1)}, f32[12,1,1024]{2,1,0:T(1,128)}) custom-call(bf16[1024,2304]{1,0:T(8,128)(2,1)} %get-tuple-element.76.q_ref.k_ref.v_ref, bf16[1024,2304]{1,0:T(8,128)(2,1)} %get-tuple-element.76.q_ref.k_ref.v_ref, bf16[1024,2304]{1,0:T(8,128)(2,1)} %get-tuple-element.76.q_ref.k_ref.v_ref, ...), custom_call_target="tpu_custom_call" | custom-call | flops 966367616 | bytes 393216 | tf_op jit(solution)/shard_map/attend/pallas_call | solution.py:243
  140.0 9.5 %middle.1 = (f32[1024,768]{1,0:T(8,128)}, bf16[1024,768]{1,0:T(8,128)(2,1)}, bf16[1024,768]{1,0:T(8,128)(2,1)}, f32[1024,1]{1,0:T(8,128)}) custom-call(bf16[1024,768]{1,0:T(8,128)(2,1)} %get-tuple-element.77.refs_0_, bf16[1024,768]{1,0:T(8,128)(2,1)} %tokens.3, bf16[768,1536]{1,0:T(8,128)(2,1)} %bitcast.77, bf16[768,1664]{1,0:T(8,128)(2,1)} %bitcast.72, ...), custom_call_target="tpu_custom_call" | custom-call | flops 221459248 | bytes 629145 | tf_op jit(solution)/shard_map/middle/pallas_call | solution.py:454
  149.5 6.2 %all-to-all-start.1 = ((bf16[16,64,768]{2,1,0:T(8,128)(2,1)}), bf16[16,64,768]{2,1,0:T(8,128)(2,1)S(1)}, u32[]{:S(2)}, u32[]{:S(2)}) async-start(bf16[16,64,768]{2,1,0:T(8,128)(2,1)} %bitcast.97), calls=%async_computation.1 | async-start | bytes 3145728 | tf_op jit(solution)/shard_map/all_to_all | solution.py:991
  161.4 26.3 %all-to-all-done.1 = bf16[16,64,768]{2,1,0:T(8,128)(2,1)S(1)} async-done(((bf16[16,64,768]{2,1,0:T(8,128)(2,1)}), bf16[16,64,768]{2,1,0:T(8,128)(2,1)S(1)}, u32[]{:S(2)}, u32[]{:S(2)}) %all-to-all-start.1) | async-done | bytes 1572896 | tf_op jit(solution)/shard_map/all_to_all | solution.py:991
  187.7 9.4 %all-to-all-start.3 = ((bf16[16,64,768]{2,1,0:T(8,128)(2,1)}), bf16[16,64,768]{2,1,0:T(8,128)(2,1)S(1)}, u32[]{:S(2)}, u32[]{:S(2)}) async-start(bf16[16,64,768]{2,1,0:T(8,128)(2,1)} %bitcast.94), calls=%async_computation.3 | async-start | bytes 3145728 | tf_op jit(solution)/shard_map/all_to_all | solution.py:991
  208.7 42.4 %expert.2 = (bf16[1024,3072]{1,0:T(8,128)(2,1)}, bf16[1024,3072]{1,0:T(8,128)(2,1)}, bf16[1024,768]{1,0:T(8,128)(2,1)}, bf16[1024,768]{1,0:T(8,128)(2,1)}, f32[1024,1]{1,0:T(8,128)}, /*index=5*/f32[768,128]{1,0:T(8,128)}) custom-call(bf16[1024,768]{1,0:T(8,128)(2,1)} %bitcast.85, bf16[16,128,768]{2,1,0:T(8,128)(2,1)} %all-to-all-done.c3.refs_9_, ...), custom_call_target="tpu_custom_call" | custom-call | flops 966367616 | bytes 1101004 | tf_op jit(solution)/shard_map/expert/pallas_call | solution.py:555
  251.1 6.6 %all-to-all-start.2 = ((bf16[16,64,768]{2,1,0:T(8,128)(2,1)}), bf16[16,64,768]{2,1,0:T(8,128)(2,1)S(1)}, u32[]{:S(2)}, u32[]{:S(2)}) async-start(bf16[16,64,768]{2,1,0:T(8,128)(2,1)} %bitcast.98), calls=%async_computation.2 | async-start | bytes 3145728 | tf_op jit(solution)/shard_map/all_to_all | solution.py:991
  257.7 42.6 %expert.3 = (bf16[1024,3072]{1,0:T(8,128)(2,1)}, bf16[1024,3072]{1,0:T(8,128)(2,1)}, bf16[1024,768]{1,0:T(8,128)(2,1)}, bf16[1024,768]{1,0:T(8,128)(2,1)}, f32[1024,1]{1,0:T(8,128)}, /*index=5*/f32[768,128]{1,0:T(8,128)}) custom-call(bf16[1024,768]{1,0:T(8,128)(2,1)} %bitcast.87, bf16[16,128,768]{2,1,0:T(8,128)(2,1)} %all-to-all-done.c3.refs_9_, ...), custom_call_target="tpu_custom_call" | custom-call | flops 966367616 | bytes 1101004 | tf_op jit(solution)/shard_map/expert/pallas_call | solution.py:555
  300.3 6.3 %all-to-all-start.4 = ((bf16[16,64,768]{2,1,0:T(8,128)(2,1)}), bf16[16,64,768]{2,1,0:T(8,128)(2,1)S(1)}, u32[]{:S(2)}, u32[]{:S(2)}) async-start(bf16[16,64,768]{2,1,0:T(8,128)(2,1)} %bitcast.96), calls=%async_computation.4 | async-start | bytes 3145728 | tf_op jit(solution)/shard_map/all_to_all | solution.py:991
  309.1 31.2 %expert_weights.1 = (bf16[384,3072]{1,0:T(8,128)(2,1)}, bf16[384,3072]{1,0:T(8,128)(2,1)}, bf16[1536,768]{1,0:T(8,128)(2,1)}, bf16[1536,768]{1,0:T(8,128)(2,1)}) custom-call(s32[1]{0:T(128)} %bitcast.30.refs_0_, bf16[1024,768]{1,0:T(8,128)(2,1)} %bitcast.86, bf16[1024,768]{1,0:T(8,128)(2,1)} %bitcast.88, f32[1024,1]{1,0:T(8,128)} %get-tuple-element.97.refs_3_, ...), custom_call_target="tpu_custom_call" | custom-call | flops 19327352832 | bytes 34603008 | tf_op jit(solution)/shard_map/expert_weights/pallas_call | solution.py:680
  341.5 13.1 %middle_back.1 = (f32[1024,768]{1,0:T(8,128)}, bf16[1024,768]{1,0:T(8,128)(2,1)}, bf16[1024,768]{1,0:T(8,128)(2,1)}, f32[1,768]{1,0:T(1,128)}) custom-call(bf16[1024,768]{1,0:T(8,128)(2,1)} %bitcast.93, bf16[1024,768]{1,0:T(8,128)(2,1)} %bitcast.95, s32[1024,1]{1,0:T(8,128)} %get-tuple-element.93.refs_2_, f32[1024,768]{1,0:T(8,128)} %get-tuple-element.94.refs_3_, ...), custom_call_target="tpu_custom_call" | custom-call | flops 4429185024 | bytes 12582912 | tf_op jit(solution)/shard_map/middle_back/pallas_call | solution.py:753
  359.8 7.8 %all-to-all-start.5 = ((bf16[16,64,768]{2,1,0:T(8,128)(2,1)}), bf16[16,64,768]{2,1,0:T(8,128)(2,1)}, u32[]{:S(2)}, u32[]{:S(2)}) async-start(bf16[16,64,768]{2,1,0:T(8,128)(2,1)} %bitcast.26), calls=%async_computation.5 | async-start | bytes 3145728 | tf_op jit(solution)/shard_map/all_to_all | solution.py:991
  367.5 27.0 %attend_back.2 = (bf16[1024,1152]{1,0:T(8,128)(2,1)}, f32[6,8,128]{2,1,0:T(8,128)}, f32[6,1,512]{2,1,0:T(1,128)}) custom-call(bf16[1024,2304]{1,0:T(8,128)(2,1)} %get-tuple-element.76.q_ref.k_ref.v_ref, bf16[1024,2304]{1,0:T(8,128)(2,1)} %get-tuple-element.76.q_ref.k_ref.v_ref, bf16[1024,2304]{1,0:T(8,128)(2,1)} %get-tuple-element.76.q_ref.k_ref.v_ref, ...), custom_call_target="tpu_custom_call" | custom-call | flops 16106127360 | bytes 6291456 | tf_op jit(solution)/shard_map/attend_back/pallas_call | solution.py:358
  399.8 6.2 %weights_back.2 = f32[768,1152]{1,0:T(8,128)} custom-call(bf16[768,1024]{1,0:T(8,128)(2,1)} %get-tuple-element.111.turned, bf16[1024,1152]{1,0:T(8,128)(2,1)} %get-tuple-element.113.grads.g_left), custom_call_target="tpu_custom_call" | custom-call | flops 1811939328 | bytes 7471104 | tf_op jit(solution)/shard_map/weights_back/pallas_call | solution.py:849
  415.9 27.0 %attend_back.3 = (bf16[1024,1152]{1,0:T(8,128)(2,1)}, f32[6,8,128]{2,1,0:T(8,128)}, f32[6,1,512]{2,1,0:T(1,128)}) custom-call(bf16[1024,2304]{1,0:T(8,128)(2,1)} %get-tuple-element.76.q_ref.k_ref.v_ref, bf16[1024,2304]{1,0:T(8,128)(2,1)} %get-tuple-element.76.q_ref.k_ref.v_ref, bf16[1024,2304]{1,0:T(8,128)(2,1)} %get-tuple-element.76.q_ref.k_ref.v_ref, ...), custom_call_target="tpu_custom_call" | custom-call | flops 16106127360 | bytes 6291456 | tf_op jit(solution)/shard_map/attend_back/pallas_call | solution.py:358
  452.4 6.2 %weights_back.3 = f32[768,1152]{1,0:T(8,128)} custom-call(bf16[768,1024]{1,0:T(8,128)(2,1)} %get-tuple-element.111.turned, bf16[1024,1152]{1,0:T(8,128)(2,1)} %get-tuple-element.120.grads.g_right), custom_call_target="tpu_custom_call" | custom-call | flops 1811939328 | bytes 7471104 | tf_op jit(solution)/shard_map/weights_back/pallas_call | solution.py:849
  465.6 10.0 %tokens_back.1 = (f32[1024,768]{1,0:T(8,128)}, f32[1,768]{1,0:T(1,128)}) custom-call(bf16[1024,1152]{1,0:T(8,128)(2,1)} %get-tuple-element.113.grads.g_left, bf16[1024,1152]{1,0:T(8,128)(2,1)} %get-tuple-element.120.grads.g_right, bf16[768,1536]{1,0:T(8,128)(2,1)} %bitcast.79, bf16[768,1664]{1,0:T(8,128)(2,1)} %bitcast.75, bf16[1024,768]{1,0:T(8,128)(2,1)} %tokens.3, ...), custom_call_target="tpu_custom_call" | custom-call | flops 3623878656 | bytes 12582912 | tf_op jit(solution)/shard_map/tokens_back/pallas_call | solution.py:819
  489.5 8.3 %mix.1 = f32[1024,768]{1,0:T(8,128)} custom-call(bf16[1024,768]{1,0:T(8,128)(2,1)} %bitcast.27.refs_0_, bf16[1024,768]{1,0:T(8,128)(2,1)} %bitcast.29.refs_1_, s32[1024,1]{1,0:T(8,128)} %get-tuple-element.93.refs_2_, f32[1024,768]{1,0:T(8,128)} %get-tuple-element.94.refs_3_, f32[1024,1]{1,0:T(8,128)} %get-tuple-element.123.refs_4_), custom_call_target="tpu_custom_call" | custom-call | flops 3221225472 | bytes 9437184 | tf_op jit(solution)/shard_map/mix/pallas_call | solution.py:790
  518.4 9.8 %collective-permute-done.22 = bf16[2,2,2,1,1,24,1152]{6,5,4,3,2,1,0:T(8,128)(2,1)S(1)} collective-permute-done((bf16[2,2,2,1,1,24,1152]{6,5,4,3,2,1,0:T(8,128)(2,1)S(1)}, bf16[2,2,2,1,1,24,1152]{6,5,4,3,2,1,0:T(8,128)(2,1)S(1)}, u32[]{:S(2)}, u32[]{:S(2)}) %collective-permute-start.22) | collective-permute-done | bytes 442400 | tf_op jit(solution)/shard_map/ppermute | solution.py:863
  (282 shorter events, 170.8 us)
Async XLA Ops:
  10.7 27.1 %collective-permute-start.3 = (bf16[384,1536]{1,0:T(8,128)(2,1)S(1)}, bf16[384,1536]{1,0:T(8,128)(2,1)S(1)}, u32[]{:S(2)}, u32[]{:S(2)}) collective-permute-start(bf16[384,1536]{1,0:T(8,128)(2,1)S(1)} %get-tuple-element.173), channel_id=1, source_target_pairs={{0,16},{16,0},{1,17},{17,1},{2,18},{18,2},{3,19},{19,3},{4,20},{20... | collective-permute-start | bytes 3538952 | tf_op jit(solution)/shard_map/ppermute | solution.py:863
  19.7 18.7 %collective-permute-start.9 = (bf16[1,2,2,1,1,24,1536]{6,5,4,3,2,1,0:T(8,128)(2,1)S(1)}, bf16[1,2,2,1,1,24,1536]{6,5,4,3,2,1,0:T(8,128)(2,1)S(1)}, u32[]{:S(2)}, u32[]{:S(2)}) collective-permute-start(bf16[1,2,2,1,1,24,1536]{6,5,4,3,2,1,0:T(8,128)(2,1)S(1)} %pad_maximum_fusion.10), channel_id=1, source_target_pairs={{0,2},{1,3},{2,0},{3,1},{4,6},{5,7},{6,4},{7,5},{8,10},{9,11},{10,... | collective-permute-start | bytes 884744 | tf_op jit(solution)/shard_map/ppermute | solution.py:863
  38.5 19.8 %collective-permute-start.10 = (bf16[1,2,2,2,1,24,1536]{6,5,4,3,2,1,0:T(8,128)(2,1)S(1)}, bf16[1,2,2,2,1,24,1536]{6,5,4,3,2,1,0:T(8,128)(2,1)S(1)}, u32[]{:S(2)}, u32[]{:S(2)}) collective-permute-start(bf16[1,2,2,2,1,24,1536]{6,5,4,3,2,1,0:T(8,128)(2,1)S(1)} %pad_maximum_fusion.8), channel_id=1, source_target_pairs={{0,16},{16,0},{1,17},{17,1},{2,18},{18,2},{3,19},{19,3},{4,20},{20... | collective-permute-start | bytes 1769480 | tf_op jit(solution)/shard_map/ppermute | solution.py:863
  48.5 11.1 %collective-permute-start.5 = (bf16[2,2,2,1,1,24,1664]{6,5,4,3,2,1,0:T(8,128)(2,1)S(1)}, bf16[2,2,2,1,1,24,1664]{6,5,4,3,2,1,0:T(8,128)(2,1)S(1)}, u32[]{:S(2)}, u32[]{:S(2)}) collective-permute-start(bf16[2,2,2,1,1,24,1664]{6,5,4,3,2,1,0:T(8,128)(2,1)S(1)} %pad_maximum_fusion.7), channel_id=1, source_target_pairs={{0,2},{1,3},{2,0},{3,1},{4,6},{5,7},{6,4},{7,5},{8,10},{9,11},{10,... | collective-permute-start | bytes 1916936 | tf_op jit(solution)/shard_map/ppermute | solution.py:863
  60.9 12.3 %collective-permute-start.6 = (bf16[2,2,2,2,1,24,1664]{6,5,4,3,2,1,0:T(8,128)(2,1)}, bf16[2,2,2,2,1,24,1664]{6,5,4,3,2,1,0:T(8,128)(2,1)}, u32[]{:S(2)}, u32[]{:S(2)}) collective-permute-start(bf16[2,2,2,2,1,24,1664]{6,5,4,3,2,1,0:T(8,128)(2,1)} %pad_maximum_fusion.4), channel_id=1, source_target_pairs={{0,1},{1,0},{2,3},{3,2},{4,5},{5,4},{6,7},{7,6},{8,9},{9,8},{10,11... | collective-permute-start | bytes 3833864 | tf_op jit(solution)/shard_map/ppermute | solution.py:863
  75.1 74.3 %all-to-all-start = ((bf16[16,128,768]{2,1,0:T(8,128)(2,1)}), bf16[16,128,768]{2,1,0:T(8,128)(2,1)}, u32[]{:S(2)}, u32[]{:S(2)}) async-start(bf16[16,128,768]{2,1,0:T(8,128)(2,1)} %bitcast.91), calls=%async_computation | async-start | bytes 6291456 | tf_op jit(solution)/shard_map/all_to_all | solution.py:991
  84.3 65.1 %collective-permute-start.12 = (bf16[384,1536]{1,0:T(8,128)(2,1)}, bf16[384,1536]{1,0:T(8,128)(2,1)}, u32[]{:S(2)}, u32[]{:S(2)}) collective-permute-start(bf16[384,1536]{1,0:T(8,128)(2,1)} %get-tuple-element.82), channel_id=1, source_target_pairs={{0,16},{16,0},{1,17},{17,1},{2,18},{18,2},{3,19},{19,3},{4,20},{20... | collective-permute-start | bytes 3538952 | tf_op jit(solution)/shard_map/ppermute | solution.py:863
  84.8 64.6 %collective-permute-start.13 = (bf16[768,768]{1,0:T(8,128)(2,1)}, bf16[768,768]{1,0:T(8,128)(2,1)}, u32[]{:S(2)}, u32[]{:S(2)}) collective-permute-start(bf16[768,768]{1,0:T(8,128)(2,1)} %get-tuple-element.83), channel_id=1, source_target_pairs={{0,16},{16,0},{1,17},{17,1},{2,18},{18,2},{3,19},{19,3},{4,20},{20... | collective-permute-start | bytes 3538952 | tf_op jit(solution)/shard_map/ppermute | solution.py:863
  149.5 38.2 %all-to-all-start.1 = ((bf16[16,64,768]{2,1,0:T(8,128)(2,1)}), bf16[16,64,768]{2,1,0:T(8,128)(2,1)S(1)}, u32[]{:S(2)}, u32[]{:S(2)}) async-start(bf16[16,64,768]{2,1,0:T(8,128)(2,1)} %bitcast.97), calls=%async_computation.1 | async-start | bytes 3145728 | tf_op jit(solution)/shard_map/all_to_all | solution.py:991
  158.6 45.0 %collective-permute-start.14 = (bf16[768,768]{1,0:T(8,128)(2,1)}, bf16[768,768]{1,0:T(8,128)(2,1)}, u32[]{:S(2)}, u32[]{:S(2)}) collective-permute-start(bf16[768,768]{1,0:T(8,128)(2,1)} %get-tuple-element.85), channel_id=1, source_target_pairs={{0,16},{16,0},{1,17},{17,1},{2,18},{18,2},{3,19},{19,3},{4,20},{20... | collective-permute-start | bytes 3538952 | tf_op jit(solution)/shard_map/ppermute | solution.py:863
  187.7 63.4 %all-to-all-start.3 = ((bf16[16,64,768]{2,1,0:T(8,128)(2,1)}), bf16[16,64,768]{2,1,0:T(8,128)(2,1)S(1)}, u32[]{:S(2)}, u32[]{:S(2)}) async-start(bf16[16,64,768]{2,1,0:T(8,128)(2,1)} %bitcast.94), calls=%async_computation.3 | async-start | bytes 3145728 | tf_op jit(solution)/shard_map/all_to_all | solution.py:991
  251.1 49.2 %all-to-all-start.2 = ((bf16[16,64,768]{2,1,0:T(8,128)(2,1)}), bf16[16,64,768]{2,1,0:T(8,128)(2,1)S(1)}, u32[]{:S(2)}, u32[]{:S(2)}) async-start(bf16[16,64,768]{2,1,0:T(8,128)(2,1)} %bitcast.98), calls=%async_computation.2 | async-start | bytes 3145728 | tf_op jit(solution)/shard_map/all_to_all | solution.py:991
  300.3 40.0 %all-to-all-start.4 = ((bf16[16,64,768]{2,1,0:T(8,128)(2,1)}), bf16[16,64,768]{2,1,0:T(8,128)(2,1)S(1)}, u32[]{:S(2)}, u32[]{:S(2)}) async-start(bf16[16,64,768]{2,1,0:T(8,128)(2,1)} %bitcast.96), calls=%async_computation.4 | async-start | bytes 3145728 | tf_op jit(solution)/shard_map/all_to_all | solution.py:991
  357.7 89.4 %collective-permute-start.18 = (bf16[1536,768]{1,0:T(8,128)(2,1)}, bf16[1536,768]{1,0:T(8,128)(2,1)}, u32[]{:S(2)}, u32[]{:S(2)}) collective-permute-start(bf16[1536,768]{1,0:T(8,128)(2,1)} %get-tuple-element.106), channel_id=1, source_target_pairs={{0,16},{16,0},{1,17},{17,1},{2,18},{18,2},{3,19},{19,3},{4,20},{20... | collective-permute-start | bytes 7077896 | tf_op jit(solution)/shard_map/ppermute | solution.py:863
  358.2 176.9 %collective-permute-start.32 = (bf16[384,3072]{1,0:T(8,128)(2,1)}, bf16[384,3072]{1,0:T(8,128)(2,1)}, u32[]{:S(2)}, u32[]{:S(2)}) collective-permute-start(bf16[384,3072]{1,0:T(8,128)(2,1)} %get-tuple-element.104), channel_id=1, source_target_pairs={{0,16},{16,0},{1,17},{17,1},{2,18},{18,2},{3,19},{19,3},{4,20},{20... | collective-permute-start | bytes 7077896 | tf_op jit(solution)/shard_map/ppermute | solution.py:863
  359.7 39.9 %collective-permute-start.15 = (bf16[2,2,2,2,1,24,768]{6,5,4,3,2,1,0:T(8,128)(2,1)S(1)}, bf16[2,2,2,2,1,24,768]{6,5,4,3,2,1,0:T(8,128)(2,1)S(1)}, u32[]{:S(2)}, u32[]{:S(2)}) collective-permute-start(bf16[2,2,2,2,1,24,768]{6,5,4,3,2,1,0:T(8,128)(2,1)S(1)} %select_convert_fusion.3), channel_id=1, source_target_pairs={{0,1},{1,0},{2,3},{3,2},{4,5},{5,4},{6,7},{7,6},{8,9},{9,8},{10,11... | collective-permute-start | bytes 1769480 | tf_op jit(solution)/shard_map/ppermute | solution.py:863
  359.8 51.2 %all-to-all-start.5 = ((bf16[16,64,768]{2,1,0:T(8,128)(2,1)}), bf16[16,64,768]{2,1,0:T(8,128)(2,1)}, u32[]{:S(2)}, u32[]{:S(2)}) async-start(bf16[16,64,768]{2,1,0:T(8,128)(2,1)} %bitcast.26), calls=%async_computation.5 | async-start | bytes 3145728 | tf_op jit(solution)/shard_map/all_to_all | solution.py:991
  408.3 36.4 %collective-permute-start.17 = (bf16[2,2,2,2,1,24,1152]{6,5,4,3,2,1,0:T(8,128)(2,1)S(1)}, bf16[2,2,2,2,1,24,1152]{6,5,4,3,2,1,0:T(8,128)(2,1)}, u32[]{:S(2)}, u32[]{:S(2)}) collective-permute-start(bf16[2,2,2,2,1,24,1152]{6,5,4,3,2,1,0:T(8,128)(2,1)S(1)} %select_convert_fusion.2), channel_id=1, source_target_pairs={{0,1},{1,0},{2,3},{3,2},{4,5},{5,4},{6,7},{7,6},{8,9},{9,8},{10,11... | collective-permute-start | bytes 2654216 | tf_op jit(solution)/shard_map/ppermute | solution.py:863
  408.9 33.9 %collective-permute-start.16 = (bf16[2,2,2,1,1,24,768]{6,5,4,3,2,1,0:T(8,128)(2,1)S(1)}, bf16[2,2,2,1,1,24,768]{6,5,4,3,2,1,0:T(8,128)(2,1)}, u32[]{:S(2)}, u32[]{:S(2)}) collective-permute-start(bf16[2,2,2,1,1,24,768]{6,5,4,3,2,1,0:T(8,128)(2,1)S(1)} %select_convert_fusion.7), channel_id=1, source_target_pairs={{0,2},{1,3},{2,0},{3,1},{4,6},{5,7},{6,4},{7,5},{8,10},{9,11},{10,... | collective-permute-start | bytes 884744 | tf_op jit(solution)/shard_map/ppermute | solution.py:863
  410.9 41.5 %all-to-all-start.6 = ((bf16[16,64,768]{2,1,0:T(8,128)(2,1)}), bf16[16,64,768]{2,1,0:T(8,128)(2,1)}, u32[]{:S(2)}, u32[]{:S(2)}) async-start(bf16[16,64,768]{2,1,0:T(8,128)(2,1)} %bitcast.92), calls=%async_computation.6 | async-start | bytes 3145728 | tf_op jit(solution)/shard_map/all_to_all | solution.py:991
  485.2 22.4 %collective-permute-start.19 = (bf16[1,2,2,2,1,24,1152]{6,5,4,3,2,1,0:T(8,128)(2,1)}, bf16[1,2,2,2,1,24,1152]{6,5,4,3,2,1,0:T(8,128)(2,1)S(1)}, u32[]{:S(2)}, u32[]{:S(2)}) collective-permute-start(bf16[1,2,2,2,1,24,1152]{6,5,4,3,2,1,0:T(8,128)(2,1)} %select_convert_fusion.5), channel_id=1, source_target_pairs={{0,16},{16,0},{1,17},{17,1},{2,18},{18,2},{3,19},{19,3},{4,20},{20... | collective-permute-start | bytes 1327112 | tf_op jit(solution)/shard_map/ppermute | solution.py:863
  485.8 29.5 %collective-permute-start.21 = (bf16[2,2,2,2,1,24,1152]{6,5,4,3,2,1,0:T(8,128)(2,1)}, bf16[2,2,2,2,1,24,1152]{6,5,4,3,2,1,0:T(8,128)(2,1)}, u32[]{:S(2)}, u32[]{:S(2)}) collective-permute-start(bf16[2,2,2,2,1,24,1152]{6,5,4,3,2,1,0:T(8,128)(2,1)} %select_convert_fusion.1), channel_id=1, source_target_pairs={{0,1},{1,0},{2,3},{3,2},{4,5},{5,4},{6,7},{7,6},{8,9},{9,8},{10,11... | collective-permute-start | bytes 2654216 | tf_op jit(solution)/shard_map/ppermute | solution.py:863
  485.8 16.3 %collective-permute-start.24 = (bf16[1,2,2,1,1,24,768]{6,5,4,3,2,1,0:T(8,128)(2,1)S(1)}, bf16[1,2,2,1,1,24,768]{6,5,4,3,2,1,0:T(8,128)(2,1)S(1)}, u32[]{:S(2)}, u32[]{:S(2)}) collective-permute-start(bf16[1,2,2,1,1,24,768]{6,5,4,3,2,1,0:T(8,128)(2,1)S(1)} %select_convert_fusion.12), channel_id=1, source_target_pairs={{0,16},{16,0},{1,17},{17,1},{2,18},{18,2},{3,19},{19,3},{4,20},{20... | collective-permute-start | bytes 442376 | tf_op jit(solution)/shard_map/ppermute | solution.py:863
  516.8 11.5 %collective-permute-start.22 = (bf16[2,2,2,1,1,24,1152]{6,5,4,3,2,1,0:T(8,128)(2,1)S(1)}, bf16[2,2,2,1,1,24,1152]{6,5,4,3,2,1,0:T(8,128)(2,1)S(1)}, u32[]{:S(2)}, u32[]{:S(2)}) collective-permute-start(bf16[2,2,2,1,1,24,1152]{6,5,4,3,2,1,0:T(8,128)(2,1)S(1)} %select_convert_fusion.4), channel_id=1, source_target_pairs={{0,2},{1,3},{2,0},{3,1},{4,6},{5,7},{6,4},{7,5},{8,10},{9,11},{10,... | collective-permute-start | bytes 1327112 | tf_op jit(solution)/shard_map/ppermute | solution.py:863
  (47 other events, 300.3 us)

commit v3 on v2

--- a/solution.py
+++ b/solution.py
@@ -16,6 +16,8 @@
 TILES = TOK // TILE
 QBLK = 256
 FF_TILE = 512
+EXPERT_TILE = 512
+EXPERT_ROWS = 1024
 HALVES = 2
 SIDE = D // 2
 SPLIT = 3 * SIDE
@@ -392,7 +394,7 @@
             pltpu.VMEM((3 * TILE, 4 * LANES), F32),
         ],
         compiler_params=params(("arbitrary",)),
-        cost_estimate=cost(5 * HEADS * TOK * TOK * 256, 8 * TOK * D, HEADS * TOK * TOK // 2, share=1),
+        cost_estimate=cost(5 * HEADS * TOK * TOK * 256, 8 * TOK * D, HEADS * TOK * TOK // 2, share=0.3),
         name="attend_back",
     )(qkv, qkv, qkv, grad_context, query_features, key_features, lse, band)
 
@@ -496,40 +498,38 @@
     return v * phi, phi + v * (bell * 0.3989422804014327)
 
 
-def expert_kernel(experts, x, c3, w_first, w_second, router, router_t, mine,
-                  act_ref, dh_ref, result, grad_x, gate_ref, grad_router, acc_r, acc_x):
+def expert_kernel(experts, x, c3, w_first, w_second, router, router_t, mine, *refs):
+    act_ref, dh_ref, result, grad_x, gate_ref, grad_router, acc_r, acc_x = refs[-8:]
     step = pl.program_id(0)
     rows = x.shape[0]
-    chunk = 256
-    per = chunk // c3.shape[1]
+    chunk = EXPERT_ROWS
+    share = c3.shape[1]
+    per = chunk // share
+
+    @pl.when(step == 0)
+    def _():
+        acc_r[...] = jnp.zeros_like(acc_r)
+        acc_x[...] = jnp.zeros_like(acc_x)
+
     for first in range(0, rows, chunk):
         at = slice(first, first + chunk)
+        sources = slice(first // share, first // share + per)
         hidden = dot(x[at, :], w_first[...])
-        cot = c3[first // chunk * per : (first // chunk + 1) * per].reshape(chunk, D)
-        grad_act = dot(cot, w_second[...], 1, 1)
+        grad_act = dot(c3[sources].reshape(chunk, D), w_second[...], 1, 1)
         act, slope = gelu_parts(hidden)
         act = act.astype(BF)
         grad_hidden = (grad_act * slope).astype(BF)
         act_ref[at, :] = act
         dh_ref[at, :] = grad_hidden
-        part_r = dot(act, w_second[...])
-        part_x = dot(grad_hidden, w_first[...], 1, 1)
-
-        @pl.when(step == 0)
-        def _():
-            acc_r[at, :] = part_r
-            acc_x[at, :] = part_x
-
-        @pl.when(step > 0)
-        def _():
-            acc_r[at, :] += part_r
-            acc_x[at, :] += part_x
+        acc_r[at, :] += dot(act, w_second[...])
+        acc_x[at, :] += dot(grad_hidden, w_first[...], 1, 1)
 
     @pl.when(step == pl.num_programs(0) - 1)
     def _():
         total_router = jnp.zeros(grad_router.shape, F32)
         for first in range(0, rows, chunk):
             at = slice(first, first + chunk)
+            sources = slice(first // share, first // share + per)
             rounded = acc_r[at, :].astype(BF)
             result[at, :] = rounded
             probs = router_softmax(x[at, :], router[...], experts)
@@ -537,7 +537,7 @@
             here = lane == mine[0, 0]
             gate = jnp.sum(jnp.where(here, probs, 0.0), axis=1, keepdims=True)
             grad_gate = jnp.sum(
-                c3[first // chunk * per : (first // chunk + 1) * per].reshape(chunk, D).astype(F32) * rounded.astype(F32), axis=1, keepdims=True
+                c3[sources].reshape(chunk, D).astype(F32) * rounded.astype(F32), axis=1, keepdims=True
             )
             grad_logits = (
                 probs * (jnp.where(here, grad_gate, 0.0) - gate * grad_gate)
@@ -552,21 +552,23 @@
     rows = x.shape[0]
     hidden_size = w_first.shape[1]
     lanes = router.shape[1]
+    sources, capacity = c.shape[:2]
+    half = pl.BlockSpec((sources, capacity // HALVES, D), lambda f: (0, part, 0))
     return pl.pallas_call(
         functools.partial(expert_kernel, experts),
-        grid=(hidden_size // FF_TILE,),
+        grid=(hidden_size // EXPERT_TILE,),
         in_specs=[
             whole((rows, D)),
-            pl.BlockSpec((c.shape[0], c.shape[1] // HALVES, D), lambda f: (0, part, 0)),
-            pl.BlockSpec((D, FF_TILE), lambda f: (0, f)),
-            pl.BlockSpec((FF_TILE, D), lambda f: (f, 0)),
+            half,
+            pl.BlockSpec((D, EXPERT_TILE), lambda f: (0, f)),
+            pl.BlockSpec((EXPERT_TILE, D), lambda f: (f, 0)),
             whole((D, lanes)),
             whole((lanes, D)),
             pl.BlockSpec(memory_space=pltpu.SMEM),
         ],
         out_specs=[
-            pl.BlockSpec((rows, FF_TILE), lambda f: (0, f)),
-            pl.BlockSpec((rows, FF_TILE), lambda f: (0, f)),
+            pl.BlockSpec((rows, EXPERT_TILE), lambda f: (0, f)),
+            pl.BlockSpec((rows, EXPERT_TILE), lambda f: (0, f)),
             whole((rows, D)),
             whole((rows, D)),
             whole((rows, 1)),
@@ -689,7 +691,7 @@
         out_shape=[jax.ShapeDtypeStruct(shape, BF) for shape in shapes],
         compiler_params=params(("arbitrary",)),
         cost_estimate=cost(
-            4 * parts * rows * D * hidden_size, 4 * (parts * rows + D) * hidden_size, share=1
+            4 * parts * rows * D * hidden_size, 4 * (parts * rows + D) * hidden_size
         ),
         name="expert_weights",
     )(*prefetched, *xs, *gates, *acts, *dhs, cots)
@@ -771,7 +773,7 @@
             jax.ShapeDtypeStruct((1, D), F32),
         ],
         compiler_params=params(("arbitrary",)),
-        cost_estimate=cost(2 * 2 * TOK * TOK * D + 2 * TOK * D * D, 16 * TOK * D, share=1),
+        cost_estimate=cost(2 * 2 * TOK * TOK * D + 2 * TOK * D * D, 16 * TOK * D),
         name="middle_back",
     )(*backs, slot_col, middle, cot, gain, left, right)
 
@@ -794,7 +796,7 @@
         out_specs=rows,
         out_shape=jax.ShapeDtypeStruct((TOK, D), F32),
         compiler_params=params(("arbitrary",)),
-        cost_estimate=cost(2 * 2 * TOK * TOK * D, 12 * TOK * D, share=1),
+        cost_estimate=cost(2 * 2 * TOK * TOK * D, 12 * TOK * D),
         name="mix",
     )(*backs, slot_col, middle, gate)
 
@@ -834,28 +836,41 @@
             jax.ShapeDtypeStruct((1, D), F32),
         ],
         compiler_params=params(("arbitrary",)),
-        cost_estimate=cost(6 * TOK * D * D, 16 * TOK * D, share=1),
+        cost_estimate=cost(6 * TOK * D * D, 16 * TOK * D),
         name="tokens_back",
     )(g_left, g_right, left, right, tokens, gain, grad_middle)
 
 
-def weights_back_kernel(turned, grads, out):
-    out[...] = dot(turned[...], grads[...])
-
-
-def weights_back(turned, grads):
-    block = 384
-    columns = grads.shape[1]
+def weights_back_kernel(turned, grads, context, grad_attn, out):
+    last = pl.num_programs(0) - 1
+
+    @pl.when(pl.program_id(0) < last)
+    def _():
+        out[...] = dot(turned[...], grads[...])
+
+    @pl.when(pl.program_id(0) == last)
+    def _():
+        out[...] = dot(context[...], grad_attn[...], 0, 0)
+
+
+def weights_back(half, turned, grads, context, grad_attn):
+    steps = grads.shape[1] // SIDE
+    columns = (steps + 1) * SIDE
     return pl.pallas_call(
         weights_back_kernel,
-        grid=(columns // block,),
-        in_specs=[whole(turned.shape), pl.BlockSpec((TOK, block), lambda c: (0, c))],
-        out_specs=pl.BlockSpec((D, block), lambda c: (0, c)),
+        grid=(steps + 1,),
+        in_specs=[
+            whole(turned.shape),
+            pl.BlockSpec((TOK, SIDE), lambda c: (0, jnp.minimum(c, steps - 1))),
+            whole((TOK, D)),
+            pl.BlockSpec((TOK, SIDE), lambda c: (0, half)),
+        ],
+        out_specs=pl.BlockSpec((D, SIDE), lambda c: (0, c)),
         out_shape=jax.ShapeDtypeStruct((D, columns), F32),
         compiler_params=params(("arbitrary",)),
-        cost_estimate=cost(2 * TOK * D * columns, 2 * TOK * (D + columns) + 4 * D * columns, share=1),
+        cost_estimate=cost(2 * TOK * D * columns, 2 * TOK * (D + columns) + 4 * D * columns),
         name="weights_back",
-    )(turned, grads)
+    )(turned, grads, context, grad_attn)
 
 
 def swap(block, axis, bit):
@@ -940,13 +955,19 @@
     )
 
 
-def scatter_dp(halves, *others):
+def receive_dp(halves):
     if len(halves) == 1:
-        return lax.psum_scatter(
-            halves[0][None], "dp", scatter_dimension=1, tiled=True
-        ).astype(F32)
+        return (lax.psum_scatter(halves[0], "dp", scatter_dimension=0, tiled=True),)
     kept, sent = halves
-    return (after(kept, *others).astype(F32) + swap(sent, "dp", 1).astype(F32))[None]
+    return (kept, swap(sent, "dp", 1))
+
+
+def add_dp(parts, *others):
+    kept, *received = parts
+    total = after(kept, *others).astype(F32)
+    for part in received:
+        total = total + part.astype(F32)
+    return total[None]
 
 
 def after(value, *others):
@@ -975,17 +996,25 @@
     kinds = (w_query, w_key, w_value, w_out)
     paired = lax.axis_size("dp") == 2
     own_first, own_second = expert_in[0], expert_out[0]
-    first_cut, second_cut = own_first.shape[1] // 2, own_second.shape[0] // 2
-    early = [swap(own_first[:, :first_cut], "dp", 1)] if paired else []
+    first_cut, second_cut = own_first.shape[1] // 3, own_second.shape[0] // 2
     table = gather_dp(rel_table, 0)
+    if paired:
+        early = [swap(own_first[:, :first_cut], "dp", 1)]
+        waiting = [own_first[:, first_cut:], own_second[:second_cut], own_second[second_cut:]]
+    else:
+        early, waiting = [], []
+    slot_col, slot_row, sending_cot = make_slots(routes, cotangent, experts, capacity)
+    wide_table = table.astype(F32)
+    query_features, key_features = lane_features(seq_ids.reshape(TOK, 1), wide_table)
+    band = jnp.sum(band_onehot()[None, :, :] * wide_table.T[:, None, :], axis=2)[:, None, :]
     left = gather_rows(
-        jnp.concatenate([w[:, :SIDE] for w in kinds], axis=1), first, table, *early
+        jnp.concatenate([w[:, :SIDE] for w in kinds], axis=1),
+        first,
+        sending_cot, query_features, key_features, band, *early, *waiting,
     )
     right = gather_rows(
-        jnp.concatenate([w[:, SIDE:] for w in kinds] + [small], axis=1), second, table, *early
-    )
-
-    slot_col, slot_row, sending_cot = make_slots(routes, cotangent, experts, capacity)
+        jnp.concatenate([w[:, SIDE:] for w in kinds] + [small], axis=1), second, *early
+    )
 
     def exchange(rows):
         return lax.all_to_all(
@@ -994,9 +1023,9 @@
 
     cots = exchange(after(sending_cot, left, right))
     if paired:
-        early.append(swap(after(own_first[:, first_cut:], left, right), "dp", 1))
-        early.append(swap(after(own_second[:second_cut], left, right), "dp", 1))
-        late = swap(after(own_second[second_cut:], *early), "dp", 1)
+        early.append(swap(after(waiting[0], left, right), "dp", 1))
+        early.append(swap(after(waiting[1], left, right), "dp", 1))
+        late = swap(after(waiting[2], *early), "dp", 1)
         other_first = jnp.concatenate(early[:2], axis=1)
         other_second = jnp.concatenate([early[2], late], axis=0)
     else:
@@ -1011,15 +1040,13 @@
     ffn_gain = extra[:, experts + 1].astype(F32).reshape(1, D)
 
     turned, qkv = project(tokens, attn_gain, left, right)
-    table = table.astype(F32)
-    query_features, key_features = lane_features(seq_ids.reshape(TOK, 1), table)
-    band = jnp.sum(band_onehot()[None, :, :] * table.T[:, None, :], axis=2)[:, None, :]
     context, lse = attend(qkv, query_features, key_features, band)
 
     middle, *sending, gate = make_middle(
         context, tokens, left, right, ffn_gain, full_router, routes, slot_row, experts, capacity
     )
     sending[0] = after(sending[0], cots, *early)
+    sending[1] = after(sending[1], w_first, w_second)
     rows_in = [exchange(part).reshape(-1, D) for part in sending]
     mine = lax.axis_index("expert").astype(jnp.int32).reshape(1, 1)
     acts, dhs, results, grads, gates, router_parts = zip(
@@ -1041,15 +1068,15 @@
     )
     half = len(weight_parts) // 2
     grad_first, grad_second = weight_parts[:half], weight_parts[half:]
-    results_home = [
-        exchange(after(part, *grads_home)).reshape(-1, D) for part in results
-    ]
+    results_home = []
+    for part in results:
+        part = after(part, *grads_home, *weight_parts, *results_home)
+        results_home.append(exchange(part).reshape(-1, D))
     grads_home[0] = after(grads_home[0], *weight_parts)
     grad_middle, grad_attn, grad_context, grad_gain_f = middle_back(
         grads_home, slot_col, middle, cotangent, ffn_gain, left, right
     )
     down, down_other = first[::-1], second[::-1]
-    out_block = scatter_step(scatter_start(dot(context, grad_attn, 0, 0)), down_other[0])
 
     def back(half, *others):
         return attend_back(
@@ -1057,33 +1084,32 @@
         )
 
     g_left, tiles_left, diagonals_left = back(0)
-    left_block = scatter_start(weights_back(turned, after(g_left, out_block)))
-    g_right, tiles_right, diagonals_right = back(1, left_block, out_block, results_home[0])
-    out_block = scatter_step(out_block, down_other[1], g_right)
-    left_block = scatter_step(left_block, down[0], g_right)
-    grad_expert_out = scatter_dp(grad_second, g_right)
+    left_block = scatter_start(weights_back(0, turned, g_left, context, grad_attn))
+    g_right, tiles_right, diagonals_right = back(1, left_block, results_home[0])
+    left_block = after(left_block, results_home[0])
+    first_halves, second_halves = receive_dp(grad_first), receive_dp(grad_second)
     grad_right = weights_back(
-        turned, after(g_right, results_home[1], out_block, left_block, grad_expert_out)
-    )
+        1, turned, after(g_right, results_home[1]), context, grad_attn
+    )
+    left_block = scatter_step(left_block, down[0], grad_right)
+    right_block = scatter_step(scatter_start(grad_right), down_other[0], second_halves[-1])
+    left_block = scatter_step(left_block, down[1], grad_right)
     grad_tokens, grad_gain_a = tokens_back(
-        g_left, after(g_right, grad_right), left, right, tokens, attn_gain, grad_middle
+        g_left, after(g_right, right_block), left, right, tokens, attn_gain, grad_middle
     )
     mixed = mix(results_home, slot_col, middle, after(gate, grad_tokens))
-    right_block = scatter_step(scatter_start(grad_right), down_other[0], grad_tokens)
-    left_block = scatter_step(left_block, down[1], grad_tokens)
-    out_block = scatter_step(out_block, down_other[2], grad_tokens)
+    right_block = scatter_step(right_block, down_other[1], mixed, first_halves[-1])
     near = 2 + len(axis_bits("dp"))
-    for place in down_other[1:near]:
+    for place in down[2:near]:
+        left_block = scatter_step(left_block, place, mixed)
+    along = (left_block, right_block)
+    for place in down_other[2:near]:
         right_block = scatter_step(right_block, place)
-    for place in down[2:near]:
-        left_block = scatter_step(left_block, place)
-    for place in down_other[3:near]:
-        out_block = scatter_step(out_block, place)
-    joined = jnp.concatenate([left_block, right_block, out_block], axis=-1)
-    grad_expert_in = scatter_dp(grad_first, joined)
+    joined = jnp.concatenate([left_block, right_block], axis=-1)
+    grad_expert_in = add_dp(first_halves, joined)
+    grad_expert_out = add_dp(second_halves, joined)
     dense = scatter_rest(joined, down[near:])
-    grad_left, grad_right = dense[:, :SPLIT], dense[:, SPLIT : 2 * SPLIT]
-    grad_w_out = dense[:, 2 * SPLIT :]
+    grad_left, grad_right = dense[:, : SPLIT + SIDE], dense[:, SPLIT + SIDE :]
     tiles = jnp.concatenate([tiles_left, tiles_right], axis=0)
     diagonals = jnp.concatenate([diagonals_left, diagonals_right], axis=0)
     grad_router = sum(router_parts)[:, :experts]
@@ -1094,7 +1120,7 @@
         jnp.concatenate(
             [
                 part.reshape(-1, LANES)
-                for part in (grad_router, grad_gain_a, grad_gain_f, grad_table)
+                for part in (grad_router, after(grad_gain_a, *along), grad_gain_f, grad_table)
             ],
             axis=0,
         )
@@ -1117,9 +1143,8 @@
                 [side[:, kind * SIDE : (kind + 1) * SIDE] for side in (grad_left, grad_right)],
                 axis=1,
             )
-            for kind in range(3)
+            for kind in range(4)
         ),
-        grad_w_out,
         own(grad_table.reshape(BUCKETS, HEADS), table_height, lax.axis_index("dp")),
         own(grad_gain_a, shard, number),
         own(grad_gain_f, shard, number),

time: 560 us -> 528 us (0.943)
  waiting for transfers between devices: 95.1 us -> 78.9 us
  Pallas kernels: 276 us -> 264 us
  starting transfers between devices: 86.8 us -> 93.9 us
    pallas_call x2, Pallas kernels: 84.9 us -> 69 us  [run_expert(): pl.pallas_call(functools.partial(expert_kernel, experts), grid=(hidden_si...]
    all_to_all x7, waiting for transfers between devices: 26.3 us -> 13 us  [exchange(): lax.all_to_all(rows.reshape(experts, -1, D), 'expert', split_axis=0, conc...]
    all_to_all x7, starting transfers between devices: 46 us -> 53.3 us  [exchange(): lax.all_to_all(rows.reshape(experts, -1, D), 'expert', split_axis=0, conc...]
    unnamed x78 -> x76, local copies, waits for them, and re-layouts: 14.2 us -> 9.4 us
    ppermute x33 -> x30, waiting for transfers between devices: 68.8 us -> 65.8 us  [swap(): lax.ppermute(block, axis, [(place, place ^ bit) for place in range(size)])]
    ppermute x33 -> x30, starting transfers between devices: 40.9 us -> 40.5 us  [swap(): lax.ppermute(block, axis, [(place, place ^ bit) for place in range(size)])]
  transfers between devices with their start and end apart: 40 -> 37, of which waited for: 16 -> 18; matrix products, arithmetic and copies ran while one was open for 14% -> 14% of each run, Pallas kernels for 48% -> 51%
where the time goes in v3:
time: 528 us; the launch traced here: 519 us
  Pallas kernels  264 us (50%)
  starting transfers between devices  93.9 us (18%)
  waiting for transfers between devices  78.9 us (15%)
  other arithmetic  48.6 us (9%)
  local copies, waits for them, and re-layouts  31.7 us (6%)
    pallas_call x2, Pallas kernels, run_expert(): pl.pallas_call(functools.partial(expert_kernel, experts), grid=(hidden_si...  69 us
    ppermute x30, waiting for transfers between devices, swap(): lax.ppermute(block, axis, [(place, place ^ bit) for place in range(size)])  65.8 us
    pallas_call x2, Pallas kernels, attend_back(): pl.pallas_call(attend_back_kernel, grid=(SIDE_PAIRS,), in_specs=[*(pl.Blo...  53.8 us
    all_to_all x7, starting transfers between devices, exchange(): lax.all_to_all(rows.reshape(experts, -1, D), 'expert', split_axis=0, conc...  53.3 us
    ppermute x30, starting transfers between devices, swap(): lax.ppermute(block, axis, [(place, place ^ bit) for place in range(size)])  40.5 us
    pallas_call x1, Pallas kernels, attend(): pl.pallas_call(attend_kernel, grid=(PAIRS,), in_specs=[*(pl.BlockSpec((TO...  36.8 us
    pallas_call x1, Pallas kernels, expert_weights(): pl.pallas_call(functools.partial(expert_weights_kernel, parts, side is no...  31.3 us
    pallas_call x2, Pallas kernels, weights_back(): pl.pallas_call(weights_back_kernel, grid=(steps + 1,), in_specs=[whole(tu...  16.1 us
  transfers between devices with their start and end apart: 37, of which 18 were waited for; matrix products, arithmetic and copies ran while one was open for 14% of the time, Pallas kernels for 51%

profile of v3, /device:TPU:0, one launch (start us, length us, event | category | flops | bytes accessed | tf_op | source)
XLA Modules:
  0.0 519.2 jit_solution(5501597293064706791)
XLA Ops:
  20.3 7.8 %slots.1 = (s32[1024,1]{1,0:T(8,128)}, s32[1,1024]{1,0:T(1,128)}, bf16[2048,768]{1,0:T(8,128)(2,1)}) custom-call(s32[1024,1]{1,0:T(8,128)} %copy.47.route_col.refs_6_, s32[1,1024]{1,0:T(1,128)} %bitcast.102, bf16[1024,768]{1,0:T(8,128)(2,1)} %refs_4_.1), custom_call_target="tpu_custom_call" | custom-call | flops 161061280 | bytes 471859 | tf_op jit(solution)/shard_map/slots/pallas_call | solution.py:116
  56.6 8.0 %collective-permute-done.10 = bf16[1,2,2,2,1,24,1536]{6,5,4,3,2,1,0:T(8,128)(2,1)S(1)} collective-permute-done((bf16[1,2,2,2,1,24,1536]{6,5,4,3,2,1,0:T(8,128)(2,1)S(1)}, bf16[1,2,2,2,1,24,1536]{6,5,4,3,2,1,0:T(8,128)(2,1)S(1)}, u32[]{:S(2)}, u32[]{:S(2)}) %collective-permute-start.10) | collective-permute-done | bytes 589856 | tf_op jit(solution)/shard_map/ppermute | solution.py:878
  84.3 8.3 %project.1 = (bf16[768,1024]{1,0:T(8,128)(2,1)}, bf16[1024,2304]{1,0:T(8,128)(2,1)}) custom-call(bf16[1024,768]{1,0:T(8,128)(2,1)} %tokens.3, f32[1,768]{1,0:T(1,128)} %reshape.383.gain, bf16[768,1536]{1,0:T(8,128)(2,1)} %bitcast.73, bf16[768,1664]{1,0:T(8,128)(2,1)} %bitcast.67), custom_call_target="tpu_custom_call" | custom-call | flops 181193936 | bytes 471859 | tf_op jit(solution)/shard_map/project/pallas_call | solution.py:141
  92.7 36.8 %attend.1 = (bf16[1024,768]{1,0:T(8,128)(2,1)}, f32[12,1,1024]{2,1,0:T(1,128)}) custom-call(bf16[1024,2304]{1,0:T(8,128)(2,1)} %get-tuple-element.79.q_ref.k_ref.v_ref, bf16[1024,2304]{1,0:T(8,128)(2,1)} %get-tuple-element.79.q_ref.k_ref.v_ref, bf16[1024,2304]{1,0:T(8,128)(2,1)} %get-tuple-element.79.q_ref.k_ref.v_ref, ...), custom_call_target="tpu_custom_call" | custom-call | flops 966367616 | bytes 393216 | tf_op jit(solution)/shard_map/attend/pallas_call | solution.py:245
  131.1 9.4 %middle.1 = (f32[1024,768]{1,0:T(8,128)}, bf16[1024,768]{1,0:T(8,128)(2,1)}, bf16[1024,768]{1,0:T(8,128)(2,1)}, f32[1024,1]{1,0:T(8,128)}) custom-call(bf16[1024,768]{1,0:T(8,128)(2,1)} %get-tuple-element.80.refs_0_.context, bf16[1024,768]{1,0:T(8,128)(2,1)} %tokens.3, bf16[768,1536]{1,0:T(8,128)(2,1)} %bitcast.74, bf16[768,1664]{1,0:T(8,128)(2,1)} %bitcast.69, ...), custom_call_target="tpu_custom_call" | custom-call | flops 221459248 | bytes 629145 | tf_op jit(solution)/shard_map/middle/pallas_call | solution.py:456
  144.8 9.9 %all-to-all-start.1 = ((bf16[16,64,768]{2,1,0:T(8,128)(2,1)}), bf16[16,64,768]{2,1,0:T(8,128)(2,1)S(1)}, u32[]{:S(2)}, u32[]{:S(2)}) async-start(bf16[16,64,768]{2,1,0:T(8,128)(2,1)} %bitcast.15), calls=%async_computation.1 | async-start | bytes 3145728 | tf_op jit(solution)/shard_map/all_to_all | solution.py:1020
  162.0 9.0 %collective-permute-done.14 = bf16[768,768]{1,0:T(8,128)(2,1)S(1)} collective-permute-done((bf16[768,768]{1,0:T(8,128)(2,1)}, bf16[768,768]{1,0:T(8,128)(2,1)S(1)}, u32[]{:S(2)}, u32[]{:S(2)}) %collective-permute-start.14) | collective-permute-done | bytes 1179680 | tf_op jit(solution)/shard_map/ppermute | solution.py:878
  174.3 12.3 %all-to-all-done.1 = bf16[16,64,768]{2,1,0:T(8,128)(2,1)S(1)} async-done(((bf16[16,64,768]{2,1,0:T(8,128)(2,1)}), bf16[16,64,768]{2,1,0:T(8,128)(2,1)S(1)}, u32[]{:S(2)}, u32[]{:S(2)}) %all-to-all-start.1) | async-done | bytes 1572896 | tf_op jit(solution)/shard_map/all_to_all | solution.py:1020
  186.6 9.1 %all-to-all-start.3 = ((bf16[16,64,768]{2,1,0:T(8,128)(2,1)}), bf16[16,64,768]{2,1,0:T(8,128)(2,1)S(1)}, u32[]{:S(2)}, u32[]{:S(2)}) async-start(bf16[16,64,768]{2,1,0:T(8,128)(2,1)} %bitcast.94), calls=%async_computation.3 | async-start | bytes 3145728 | tf_op jit(solution)/shard_map/all_to_all | solution.py:1020
  197.5 34.4 %expert.2 = (bf16[1024,3072]{1,0:T(8,128)(2,1)}, bf16[1024,3072]{1,0:T(8,128)(2,1)}, bf16[1024,768]{1,0:T(8,128)(2,1)}, bf16[1024,768]{1,0:T(8,128)(2,1)}, f32[1024,1]{1,0:T(8,128)}, /*index=5*/f32[768,128]{1,0:T(8,128)}) custom-call(bf16[1024,768]{1,0:T(8,128)(2,1)} %bitcast.83, bf16[16,128,768]{2,1,0:T(8,128)(2,1)} %all-to-all-done.c3.refs_9_, ...), custom_call_target="tpu_custom_call" | custom-call | flops 966367616 | bytes 1101004 | tf_op jit(solution)/shard_map/expert/pallas_call | solution.py:557
  232.0 6.4 %all-to-all-start.2 = ((bf16[16,64,768]{2,1,0:T(8,128)(2,1)}), bf16[16,64,768]{2,1,0:T(8,128)(2,1)S(1)}, u32[]{:S(2)}, u32[]{:S(2)}) async-start(bf16[16,64,768]{2,1,0:T(8,128)(2,1)} %bitcast.96), calls=%async_computation.2 | async-start | bytes 3145728 | tf_op jit(solution)/shard_map/all_to_all | solution.py:1020
  238.4 34.6 %expert.3 = (bf16[1024,3072]{1,0:T(8,128)(2,1)}, bf16[1024,3072]{1,0:T(8,128)(2,1)}, bf16[1024,768]{1,0:T(8,128)(2,1)}, bf16[1024,768]{1,0:T(8,128)(2,1)}, f32[1024,1]{1,0:T(8,128)}, /*index=5*/f32[768,128]{1,0:T(8,128)}) custom-call(bf16[1024,768]{1,0:T(8,128)(2,1)} %bitcast.85, bf16[16,128,768]{2,1,0:T(8,128)(2,1)} %all-to-all-done.c3.refs_9_, ...), custom_call_target="tpu_custom_call" | custom-call | flops 966367616 | bytes 1101004 | tf_op jit(solution)/shard_map/expert/pallas_call | solution.py:557
  273.0 6.5 %all-to-all-start.4 = ((bf16[16,64,768]{2,1,0:T(8,128)(2,1)}), bf16[16,64,768]{2,1,0:T(8,128)(2,1)S(1)}, u32[]{:S(2)}, u32[]{:S(2)}) async-start(bf16[16,64,768]{2,1,0:T(8,128)(2,1)} %bitcast.95), calls=%async_computation.4 | async-start | bytes 3145728 | tf_op jit(solution)/shard_map/all_to_all | solution.py:1020
  279.5 31.3 %expert_weights.1 = (bf16[384,3072]{1,0:T(8,128)(2,1)}, bf16[384,3072]{1,0:T(8,128)(2,1)}, bf16[1536,768]{1,0:T(8,128)(2,1)}, bf16[1536,768]{1,0:T(8,128)(2,1)}) custom-call(s32[1]{0:T(128)} %bitcast.26.refs_0_, bf16[1024,768]{1,0:T(8,128)(2,1)} %bitcast.84, bf16[1024,768]{1,0:T(8,128)(2,1)} %bitcast.86, f32[1024,1]{1,0:T(8,128)} %get-tuple-element.94.refs_3_, ...), custom_call_target="tpu_custom_call" | custom-call | flops 966367616 | bytes 1730150 | tf_op jit(solution)/shard_map/expert_weights/pallas_call | solution.py:682
  311.5 9.3 %all-to-all-start.5 = ((bf16[16,64,768]{2,1,0:T(8,128)(2,1)}), bf16[16,64,768]{2,1,0:T(8,128)(2,1)S(1)}, u32[]{:S(2)}, u32[]{:S(2)}) async-start(bf16[16,64,768]{2,1,0:T(8,128)(2,1)} %bitcast.93), calls=%async_computation.5 | async-start | bytes 3145728 | tf_op jit(solution)/shard_map/all_to_all | solution.py:1020
  325.3 12.9 %middle_back.1 = (f32[1024,768]{1,0:T(8,128)}, bf16[1024,768]{1,0:T(8,128)(2,1)}, bf16[1024,768]{1,0:T(8,128)(2,1)}, f32[1,768]{1,0:T(1,128)}) custom-call(bf16[1024,768]{1,0:T(8,128)(2,1)} %bitcast.90, bf16[1024,768]{1,0:T(8,128)(2,1)} %bitcast.91, s32[1024,1]{1,0:T(8,128)} %get-tuple-element.107.refs_2_, f32[1024,768]{1,0:T(8,128)} %get-tuple-element.108.refs_3_, ...), custom_call_target="tpu_custom_call" | custom-call | flops 221459248 | bytes 629145 | tf_op jit(solution)/shard_map/middle_back/pallas_call | solution.py:755
  339.5 27.0 %attend_back.2 = (bf16[1024,1152]{1,0:T(8,128)(2,1)}, f32[6,8,128]{2,1,0:T(8,128)}, f32[6,1,512]{2,1,0:T(1,128)}) custom-call(bf16[1024,2304]{1,0:T(8,128)(2,1)} %get-tuple-element.79.q_ref.k_ref.v_ref, bf16[1024,2304]{1,0:T(8,128)(2,1)} %get-tuple-element.79.q_ref.k_ref.v_ref, bf16[1024,2304]{1,0:T(8,128)(2,1)} %get-tuple-element.79.q_ref.k_ref.v_ref, ...), custom_call_target="tpu_custom_call" | custom-call | flops 4831838208 | bytes 1887436 | tf_op jit(solution)/shard_map/attend_back/pallas_call | solution.py:360
  366.5 7.9 %weights_back.2 = f32[768,1536]{1,0:T(8,128)} custom-call(bf16[768,1024]{1,0:T(8,128)(2,1)} %get-tuple-element.114.turned, bf16[1024,1152]{1,0:T(8,128)(2,1)} %get-tuple-element.113.grads.g_left, bf16[1024,768]{1,0:T(8,128)(2,1)} %get-tuple-element.80.refs_0_.context, bf16[1024,768]{1,0:T(8,128)(2,1)} %get-tuple-element.115.grad_attn), custom_call_target="tpu_custom_call" | custom-call | flops 120795952 | bytes 471859 | tf_op jit(solution)/shard_map/weights_back/pallas_call | solution.py:859
  385.6 26.9 %attend_back.3 = (bf16[1024,1152]{1,0:T(8,128)(2,1)}, f32[6,8,128]{2,1,0:T(8,128)}, f32[6,1,512]{2,1,0:T(1,128)}) custom-call(bf16[1024,2304]{1,0:T(8,128)(2,1)} %get-tuple-element.79.q_ref.k_ref.v_ref, bf16[1024,2304]{1,0:T(8,128)(2,1)} %get-tuple-element.79.q_ref.k_ref.v_ref, bf16[1024,2304]{1,0:T(8,128)(2,1)} %get-tuple-element.79.q_ref.k_ref.v_ref, ...), custom_call_target="tpu_custom_call" | custom-call | flops 4831838208 | bytes 1887436 | tf_op jit(solution)/shard_map/attend_back/pallas_call | solution.py:360
  420.9 8.1 %weights_back.3 = f32[768,1536]{1,0:T(8,128)} custom-call(bf16[768,1024]{1,0:T(8,128)(2,1)} %get-tuple-element.114.turned, bf16[1024,1152]{1,0:T(8,128)(2,1)} %get-tuple-element.120.grads.g_right, bf16[1024,768]{1,0:T(8,128)(2,1)} %get-tuple-element.80.refs_0_.context, bf16[1024,768]{1,0:T(8,128)(2,1)} %get-tuple-element.115.grad_attn), custom_call_target="tpu_custom_call" | custom-call | flops 120795952 | bytes 471859 | tf_op jit(solution)/shard_map/weights_back/pallas_call | solution.py:859
  432.3 12.6 %collective-permute-done.18 = bf16[1,2,2,2,1,24,1536]{6,5,4,3,2,1,0:T(8,128)(2,1)S(1)} collective-permute-done((bf16[1,2,2,2,1,24,1536]{6,5,4,3,2,1,0:T(8,128)(2,1)S(1)}, bf16[1,2,2,2,1,24,1536]{6,5,4,3,2,1,0:T(8,128)(2,1)S(1)}, u32[]{:S(2)}, u32[]{:S(2)}) %collective-permute-start.18) | collective-permute-done | bytes 589856 | tf_op jit(solution)/shard_map/ppermute | solution.py:878
  447.9 10.0 %tokens_back.1 = (f32[1024,768]{1,0:T(8,128)}, f32[1,768]{1,0:T(1,128)}) custom-call(bf16[1024,1152]{1,0:T(8,128)(2,1)} %get-tuple-element.113.grads.g_left, bf16[1024,1152]{1,0:T(8,128)(2,1)} %get-tuple-element.120.grads.g_right, bf16[768,1536]{1,0:T(8,128)(2,1)} %bitcast.76, bf16[768,1664]{1,0:T(8,128)(2,1)} %bitcast.72, bf16[1024,768]{1,0:T(8,128)(2,1)} %tokens.3, ...), custom_call_target="tpu_custom_call" | custom-call | flops 181193936 | bytes 629145 | tf_op jit(solution)/shard_map/tokens_back/pallas_call | solution.py:821
  457.9 8.0 %mix.1 = f32[1024,768]{1,0:T(8,128)} custom-call(bf16[1024,768]{1,0:T(8,128)(2,1)} %bitcast.89, bf16[1024,768]{1,0:T(8,128)(2,1)} %bitcast.30.refs_1_, s32[1024,1]{1,0:T(8,128)} %get-tuple-element.107.refs_2_, f32[1024,768]{1,0:T(8,128)} %get-tuple-element.108.refs_3_, f32[1024,1]{1,0:T(8,128)} %get-tuple-element.123.refs_4_), custom_call_target="tpu_custom_call" | custom-call | flops 161061280 | bytes 471859 | tf_op jit(solution)/shard_map/mix/pallas_call | solution.py:792
  509.6 6.6 %collective-permute-done.24 = bf16[1,1,1,1,1,24,3072]{6,5,4,3,2,1,0:T(8,128)(2,1)S(1)} collective-permute-done((bf16[1,1,1,1,1,24,3072]{6,5,4,3,2,1,0:T(8,128)(2,1)S(1)}, bf16[1,1,1,1,1,24,3072]{6,5,4,3,2,1,0:T(8,128)(2,1)S(1)}, u32[]{:S(2)}, u32[]{:S(2)}) %collective-permute-start.24) | collective-permute-done | bytes 147488 | tf_op jit(solution)/shard_map/ppermute | solution.py:878
  (265 shorter events, 164.1 us)
Async XLA Ops:
  2.4 32.7 %collective-permute-start.6 = (bf16[1,1,1,1,1,24,1536]{6,5,4,3,2,1,0:T(8,128)(2,1)S(1)}, bf16[1,1,1,1,1,24,1536]{6,5,4,3,2,1,0:T(8,128)(2,1)}, u32[]{:S(2)}, u32[]{:S(2)}) collective-permute-start(bf16[1,1,1,1,1,24,1536]{6,5,4,3,2,1,0:T(8,128)(2,1)S(1)} %maximum_bitcast_fusion), channel_id=1, source_target_pairs={{0,8},{1,9},{2,10},{3,11},{4,12},{5,13},{6,14},{7,15},{8,0},{9,1},... | collective-permute-start | bytes 221192 | tf_op jit(solution)/shard_map/ppermute | solution.py:878
  6.5 22.7 %collective-permute-start.9 = (bf16[16,12]{1,0:T(8,128)(2,1)}, bf16[16,12]{1,0:T(8,128)(2,1)}, u32[]{:S(2)}, u32[]{:S(2)}) collective-permute-start(bf16[16,12]{1,0:T(8,128)(2,1)} %param.22), channel_id=1, source_target_pairs={{0,16},{16,0},{1,17},{17,1},{2,18},{18,2},{3,19},{19,3},{4,20},{20... | collective-permute-start | bytes 1160 | tf_op jit(solution)/shard_map/ppermute | solution.py:878
  10.1 34.3 %collective-permute-start.2 = (bf16[384,1024]{1,0:T(8,128)(2,1)}, bf16[384,1024]{1,0:T(8,128)(2,1)S(1)}, u32[]{:S(2)}, u32[]{:S(2)}) collective-permute-start(bf16[384,1024]{1,0:T(8,128)(2,1)} %slice.290), channel_id=1, source_target_pairs={{0,16},{16,0},{1,17},{17,1},{2,18},{18,2},{3,19},{19,3},{4,20},{20... | collective-permute-start | bytes 2359304 | tf_op jit(solution)/shard_map/ppermute | solution.py:878
  13.0 25.0 %collective-permute-start = (bf16[1,1,1,1,1,24,1664]{6,5,4,3,2,1,0:T(8,128)(2,1)S(1)}, bf16[1,1,1,1,1,24,1664]{6,5,4,3,2,1,0:T(8,128)(2,1)S(1)}, u32[]{:S(2)}, u32[]{:S(2)}) collective-permute-start(bf16[1,1,1,1,1,24,1664]{6,5,4,3,2,1,0:T(8,128)(2,1)S(1)} %bitcast.97), channel_id=1, source_target_pairs={{0,8},{1,9},{2,10},{3,11},{4,12},{5,13},{6,14},{7,15},{8,0},{9,1},... | collective-permute-start | bytes 239624 | tf_op jit(solution)/shard_map/ppermute | solution.py:878
  49.6 15.0 %collective-permute-start.10 = (bf16[1,2,2,2,1,24,1536]{6,5,4,3,2,1,0:T(8,128)(2,1)S(1)}, bf16[1,2,2,2,1,24,1536]{6,5,4,3,2,1,0:T(8,128)(2,1)S(1)}, u32[]{:S(2)}, u32[]{:S(2)}) collective-permute-start(bf16[1,2,2,2,1,24,1536]{6,5,4,3,2,1,0:T(8,128)(2,1)S(1)} %pad_maximum_fusion.8), channel_id=1, source_target_pairs={{0,16},{16,0},{1,17},{17,1},{2,18},{18,2},{3,19},{19,3},{4,20},{20... | collective-permute-start | bytes 1769480 | tf_op jit(solution)/shard_map/ppermute | solution.py:878
  55.1 10.7 %collective-permute-start.4 = (bf16[2,2,2,1,1,24,1664]{6,5,4,3,2,1,0:T(8,128)(2,1)S(1)}, bf16[2,2,2,1,1,24,1664]{6,5,4,3,2,1,0:T(8,128)(2,1)S(1)}, u32[]{:S(2)}, u32[]{:S(2)}) collective-permute-start(bf16[2,2,2,1,1,24,1664]{6,5,4,3,2,1,0:T(8,128)(2,1)S(1)} %pad_maximum_fusion.7), channel_id=1, source_target_pairs={{0,2},{1,3},{2,0},{3,1},{4,6},{5,7},{6,4},{7,5},{8,10},{9,11},{10,... | collective-permute-start | bytes 1916936 | tf_op jit(solution)/shard_map/ppermute | solution.py:878
  74.0 70.8 %all-to-all-start = ((bf16[16,128,768]{2,1,0:T(8,128)(2,1)}), bf16[16,128,768]{2,1,0:T(8,128)(2,1)}, u32[]{:S(2)}, u32[]{:S(2)}) async-start(bf16[16,128,768]{2,1,0:T(8,128)(2,1)} %bitcast.92), calls=%async_computation | async-start | bytes 6291456 | tf_op jit(solution)/shard_map/all_to_all | solution.py:1020
  79.8 63.4 %collective-permute-start.12 = (bf16[384,2048]{1,0:T(8,128)(2,1)}, bf16[384,2048]{1,0:T(8,128)(2,1)}, u32[]{:S(2)}, u32[]{:S(2)}) collective-permute-start(bf16[384,2048]{1,0:T(8,128)(2,1)} %slice.294), channel_id=1, source_target_pairs={{0,16},{16,0},{1,17},{17,1},{2,18},{18,2},{3,19},{19,3},{4,20},{20... | collective-permute-start | bytes 4718600 | tf_op jit(solution)/shard_map/ppermute | solution.py:878
  81.4 60.8 %collective-permute-start.13 = (bf16[768,768]{1,0:T(8,128)(2,1)}, bf16[768,768]{1,0:T(8,128)(2,1)S(1)}, u32[]{:S(2)}, u32[]{:S(2)}) collective-permute-start(bf16[768,768]{1,0:T(8,128)(2,1)} %get-tuple-element.85), channel_id=1, source_target_pairs={{0,16},{16,0},{1,17},{17,1},{2,18},{18,2},{3,19},{19,3},{4,20},{20... | collective-permute-start | bytes 3538952 | tf_op jit(solution)/shard_map/ppermute | solution.py:878
  143.3 27.8 %collective-permute-start.14 = (bf16[768,768]{1,0:T(8,128)(2,1)}, bf16[768,768]{1,0:T(8,128)(2,1)S(1)}, u32[]{:S(2)}, u32[]{:S(2)}) collective-permute-start(bf16[768,768]{1,0:T(8,128)(2,1)} %get-tuple-element.87), channel_id=1, source_target_pairs={{0,16},{16,0},{1,17},{17,1},{2,18},{18,2},{3,19},{19,3},{4,20},{20... | collective-permute-start | bytes 3538952 | tf_op jit(solution)/shard_map/ppermute | solution.py:878
  144.8 41.8 %all-to-all-start.1 = ((bf16[16,64,768]{2,1,0:T(8,128)(2,1)}), bf16[16,64,768]{2,1,0:T(8,128)(2,1)S(1)}, u32[]{:S(2)}, u32[]{:S(2)}) async-start(bf16[16,64,768]{2,1,0:T(8,128)(2,1)} %bitcast.15), calls=%async_computation.1 | async-start | bytes 3145728 | tf_op jit(solution)/shard_map/all_to_all | solution.py:1020
  186.6 45.3 %all-to-all-start.3 = ((bf16[16,64,768]{2,1,0:T(8,128)(2,1)}), bf16[16,64,768]{2,1,0:T(8,128)(2,1)S(1)}, u32[]{:S(2)}, u32[]{:S(2)}) async-start(bf16[16,64,768]{2,1,0:T(8,128)(2,1)} %bitcast.94), calls=%async_computation.3 | async-start | bytes 3145728 | tf_op jit(solution)/shard_map/all_to_all | solution.py:1020
  232.0 41.0 %all-to-all-start.2 = ((bf16[16,64,768]{2,1,0:T(8,128)(2,1)}), bf16[16,64,768]{2,1,0:T(8,128)(2,1)S(1)}, u32[]{:S(2)}, u32[]{:S(2)}) async-start(bf16[16,64,768]{2,1,0:T(8,128)(2,1)} %bitcast.96), calls=%async_computation.2 | async-start | bytes 3145728 | tf_op jit(solution)/shard_map/all_to_all | solution.py:1020
  273.0 38.5 %all-to-all-start.4 = ((bf16[16,64,768]{2,1,0:T(8,128)(2,1)}), bf16[16,64,768]{2,1,0:T(8,128)(2,1)S(1)}, u32[]{:S(2)}, u32[]{:S(2)}) async-start(bf16[16,64,768]{2,1,0:T(8,128)(2,1)} %bitcast.95), calls=%async_computation.4 | async-start | bytes 3145728 | tf_op jit(solution)/shard_map/all_to_all | solution.py:1020
  311.5 63.4 %all-to-all-start.5 = ((bf16[16,64,768]{2,1,0:T(8,128)(2,1)}), bf16[16,64,768]{2,1,0:T(8,128)(2,1)S(1)}, u32[]{:S(2)}, u32[]{:S(2)}) async-start(bf16[16,64,768]{2,1,0:T(8,128)(2,1)} %bitcast.93), calls=%async_computation.5 | async-start | bytes 3145728 | tf_op jit(solution)/shard_map/all_to_all | solution.py:1020
  323.3 108.6 %collective-permute-start.15 = (bf16[1536,768]{1,0:T(8,128)(2,1)}, bf16[1536,768]{1,0:T(8,128)(2,1)}, u32[]{:S(2)}, u32[]{:S(2)}) collective-permute-start(bf16[1536,768]{1,0:T(8,128)(2,1)} %get-tuple-element.103), channel_id=1, source_target_pairs={{0,16},{16,0},{1,17},{17,1},{2,18},{18,2},{3,19},{19,3},{4,20},{20... | collective-permute-start | bytes 7077896 | tf_op jit(solution)/shard_map/ppermute | solution.py:878
  324.8 141.2 %collective-permute-start.20 = (bf16[384,3072]{1,0:T(8,128)(2,1)}, bf16[384,3072]{1,0:T(8,128)(2,1)}, u32[]{:S(2)}, u32[]{:S(2)}) collective-permute-start(bf16[384,3072]{1,0:T(8,128)(2,1)} %get-tuple-element.101), channel_id=1, source_target_pairs={{0,16},{16,0},{1,17},{17,1},{2,18},{18,2},{3,19},{19,3},{4,20},{20... | collective-permute-start | bytes 7077896 | tf_op jit(solution)/shard_map/ppermute | solution.py:878
  374.9 46.0 %all-to-all-start.6 = ((bf16[16,64,768]{2,1,0:T(8,128)(2,1)}), bf16[16,64,768]{2,1,0:T(8,128)(2,1)}, u32[]{:S(2)}, u32[]{:S(2)}) async-start(bf16[16,64,768]{2,1,0:T(8,128)(2,1)} %bitcast.29), calls=%async_computation.6 | async-start | bytes 3145728 | tf_op jit(solution)/shard_map/all_to_all | solution.py:1020
  385.0 44.0 %collective-permute-start.17 = (bf16[2,2,2,2,1,24,1536]{6,5,4,3,2,1,0:T(8,128)(2,1)}, bf16[2,2,2,2,1,24,1536]{6,5,4,3,2,1,0:T(8,128)(2,1)S(1)}, u32[]{:S(2)}, u32[]{:S(2)}) collective-permute-start(bf16[2,2,2,2,1,24,1536]{6,5,4,3,2,1,0:T(8,128)(2,1)} %select_convert_fusion.1), channel_id=1, source_target_pairs={{0,1},{1,0},{2,3},{3,2},{4,5},{5,4},{6,7},{7,6},{8,9},{9,8},{10,11... | collective-permute-start | bytes 3538952 | tf_op jit(solution)/shard_map/ppermute | solution.py:878
  429.5 15.4 %collective-permute-start.18 = (bf16[1,2,2,2,1,24,1536]{6,5,4,3,2,1,0:T(8,128)(2,1)S(1)}, bf16[1,2,2,2,1,24,1536]{6,5,4,3,2,1,0:T(8,128)(2,1)S(1)}, u32[]{:S(2)}, u32[]{:S(2)}) collective-permute-start(bf16[1,2,2,2,1,24,1536]{6,5,4,3,2,1,0:T(8,128)(2,1)S(1)} %select_convert_fusion.4), channel_id=1, source_target_pairs={{0,16},{16,0},{1,17},{17,1},{2,18},{18,2},{3,19},{19,3},{4,20},{20... | collective-permute-start | bytes 1769480 | tf_op jit(solution)/shard_map/ppermute | solution.py:878
  432.1 15.1 %collective-permute-start.16 = (bf16[2,2,2,2,1,24,1536]{6,5,4,3,2,1,0:T(8,128)(2,1)S(1)}, bf16[2,2,2,2,1,24,1536]{6,5,4,3,2,1,0:T(8,128)(2,1)S(1)}, u32[]{:S(2)}, u32[]{:S(2)}) collective-permute-start(bf16[2,2,2,2,1,24,1536]{6,5,4,3,2,1,0:T(8,128)(2,1)S(1)} %select_convert_fusion.2), channel_id=1, source_target_pairs={{0,1},{1,0},{2,3},{3,2},{4,5},{5,4},{6,7},{7,6},{8,9},{9,8},{10,11... | collective-permute-start | bytes 3538952 | tf_op jit(solution)/shard_map/ppermute | solution.py:878
  445.1 20.9 %collective-permute-start.19 = (bf16[1,2,2,1,1,24,1536]{6,5,4,3,2,1,0:T(8,128)(2,1)S(1)}, bf16[1,2,2,1,1,24,1536]{6,5,4,3,2,1,0:T(8,128)(2,1)S(1)}, u32[]{:S(2)}, u32[]{:S(2)}) collective-permute-start(bf16[1,2,2,1,1,24,1536]{6,5,4,3,2,1,0:T(8,128)(2,1)S(1)} %select_convert_fusion.7), channel_id=1, source_target_pairs={{0,2},{1,3},{2,0},{3,1},{4,6},{5,7},{6,4},{7,5},{8,10},{9,11},{10,... | collective-permute-start | bytes 884744 | tf_op jit(solution)/shard_map/ppermute | solution.py:878
  447.7 18.9 %collective-permute-start.21 = (bf16[2,2,2,1,1,24,1536]{6,5,4,3,2,1,0:T(8,128)(2,1)S(1)}, bf16[2,2,2,1,1,24,1536]{6,5,4,3,2,1,0:T(8,128)(2,1)S(1)}, u32[]{:S(2)}, u32[]{:S(2)}) collective-permute-start(bf16[2,2,2,1,1,24,1536]{6,5,4,3,2,1,0:T(8,128)(2,1)S(1)} %select_convert_fusion.3), channel_id=1, source_target_pairs={{0,2},{1,3},{2,0},{3,1},{4,6},{5,7},{6,4},{7,5},{8,10},{9,11},{10,... | collective-permute-start | bytes 1769480 | tf_op jit(solution)/shard_map/ppermute | solution.py:878
  494.5 11.8 %collective-permute-start.23 = (bf16[1,2,1,1,1,24,3072]{6,5,4,3,2,1,0:T(8,128)(2,1)S(1)}, bf16[1,2,1,1,1,24,3072]{6,5,4,3,2,1,0:T(8,128)(2,1)S(1)}, u32[]{:S(2)}, u32[]{:S(2)}) collective-permute-start(bf16[1,2,1,1,1,24,3072]{6,5,4,3,2,1,0:T(8,128)(2,1)S(1)} %select_convert_fusion.5), channel_id=1, source_target_pairs={{0,4},{1,5},{2,6},{3,7},{4,0},{5,1},{6,2},{7,3},{8,12},{9,13},{10,... | collective-permute-start | bytes 884744 | tf_op jit(solution)/shard_map/ppermute | solution.py:878
  (43 other events, 403.5 us)

commit v4 on v3

--- a/solution.py
+++ b/solution.py
@@ -801,18 +801,11 @@
     )(*backs, slot_col, middle, gate)
 
 
-def tokens_back_kernel(g_left, g_right, left, right, tokens, gain, grad_middle, grad_tokens, grad_gain):
+def tokens_back_kernel(g_left, g_right, left, right, tokens, gain, grad_middle, grad_tokens):
     grad_normed = dot(g_left[...], left[...], 1, 1) + dot(g_right[...], right[...], 1, 1)
-    part, gain_part = rms_back(tokens[...].astype(F32), gain[...], grad_normed)
-    grad_tokens[...] = grad_middle[...] + part
-
-    @pl.when(pl.program_id(0) == 0)
-    def _():
-        grad_gain[...] = gain_part
-
-    @pl.when(pl.program_id(0) > 0)
-    def _():
-        grad_gain[...] += gain_part
+    grad_tokens[...] = grad_middle[...] + rms_back(
+        tokens[...].astype(F32), gain[...], grad_normed
+    )[0]
 
 
 def tokens_back(g_left, g_right, left, right, tokens, gain, grad_middle):
@@ -830,11 +823,8 @@
             whole((1, D)),
             rows,
         ],
-        out_specs=[rows, whole((1, D))],
-        out_shape=[
-            jax.ShapeDtypeStruct((TOK, D), F32),
-            jax.ShapeDtypeStruct((1, D), F32),
-        ],
+        out_specs=rows,
+        out_shape=jax.ShapeDtypeStruct((TOK, D), F32),
         compiler_params=params(("arbitrary",)),
         cost_estimate=cost(6 * TOK * D * D, 16 * TOK * D),
         name="tokens_back",
@@ -901,19 +891,21 @@
     return (rest + along + dp + [core], rest + dp + along + [core])
 
 
-def gather_rows(shard, order, *before_dp):
-    bits = axis_bits("dp", "expert")
-    block = shard.reshape((1,) * len(bits) + shard.shape)
-    for place in order:
-        axis, bit = bits[place]
-        if axis == "dp" and before_dp:
-            block = after(block, *before_dp)
-        other = swap(block, axis, bit)
-        upper = on_upper(axis, bit)
-        block = jnp.concatenate(
-            [jnp.where(upper, other, block), jnp.where(upper, block, other)], axis=place
-        )
-    return block.reshape((-1,) + shard.shape[1:])
+def gather_start(shard):
+    return shard.reshape((1,) * len(axis_bits("dp", "expert")) + shard.shape)
+
+
+def gather_step(block, place):
+    axis, bit = axis_bits("dp", "expert")[place]
+    other = swap(block, axis, bit)
+    upper = on_upper(axis, bit)
+    return jnp.concatenate(
+        [jnp.where(upper, other, block), jnp.where(upper, block, other)], axis=place
+    )
+
+
+def gather_end(block):
+    return block.reshape((-1, block.shape[-1]))
 
 
 def scatter_start(total):
@@ -938,9 +930,10 @@
     return block.reshape(block.shape[len(axis_bits("dp", "expert")) :])
 
 
-def sum_all(total):
-    for axis, bit in axis_bits("dp", "expert"):
-        total = total + swap(total, axis, bit)
+def sum_all(total, beside):
+    for number, (axis, bit) in enumerate(axis_bits("dp", "expert")):
+        kept = after(total, beside[number]) if number < len(beside) else total
+        total = kept + swap(total, axis, bit)
     return total
 
 
@@ -996,25 +989,32 @@
     kinds = (w_query, w_key, w_value, w_out)
     paired = lax.axis_size("dp") == 2
     own_first, own_second = expert_in[0], expert_out[0]
-    first_cut, second_cut = own_first.shape[1] // 3, own_second.shape[0] // 2
+    second_cut = own_second.shape[0] // 2
     table = gather_dp(rel_table, 0)
-    if paired:
-        early = [swap(own_first[:, :first_cut], "dp", 1)]
-        waiting = [own_first[:, first_cut:], own_second[:second_cut], own_second[second_cut:]]
-    else:
-        early, waiting = [], []
-    slot_col, slot_row, sending_cot = make_slots(routes, cotangent, experts, capacity)
+    early = [swap(own_second[:second_cut], "dp", 1)] if paired else []
+    left = gather_start(jnp.concatenate([w[:, :SIDE] for w in kinds], axis=1))
+    right = gather_start(jnp.concatenate([w[:, SIDE:] for w in kinds] + [small], axis=1))
+    dp_bits = len(axis_bits("dp"))
+    rest = len(first) - dp_bits - 2
+    left, right = gather_step(left, first[0]), gather_step(right, second[0])
+    slot_col, slot_row, sending_cot = make_slots(
+        after(routes, left), cotangent, experts, capacity
+    )
+    for at in range(1, rest):
+        left, right = gather_step(left, first[at]), gather_step(right, second[at])
     wide_table = table.astype(F32)
     query_features, key_features = lane_features(seq_ids.reshape(TOK, 1), wide_table)
     band = jnp.sum(band_onehot()[None, :, :] * wide_table.T[:, None, :], axis=2)[:, None, :]
-    left = gather_rows(
-        jnp.concatenate([w[:, :SIDE] for w in kinds], axis=1),
-        first,
-        sending_cot, query_features, key_features, band, *early, *waiting,
-    )
-    right = gather_rows(
-        jnp.concatenate([w[:, SIDE:] for w in kinds] + [small], axis=1), second, *early
-    )
+    left = gather_step(left, first[rest])
+    right = after(right, query_features, key_features, band, *early)
+    for place in second[rest : rest + dp_bits]:
+        right = gather_step(right, place)
+    left = after(left, sending_cot)
+    for place in first[rest + 1 :]:
+        left = gather_step(left, place)
+    for place in second[rest + dp_bits :]:
+        right = gather_step(right, place)
+    left, right = gather_end(left), gather_end(right)
 
     def exchange(rows):
         return lax.all_to_all(
@@ -1023,11 +1023,10 @@
 
     cots = exchange(after(sending_cot, left, right))
     if paired:
-        early.append(swap(after(waiting[0], left, right), "dp", 1))
-        early.append(swap(after(waiting[1], left, right), "dp", 1))
-        late = swap(after(waiting[2], *early), "dp", 1)
-        other_first = jnp.concatenate(early[:2], axis=1)
-        other_second = jnp.concatenate([early[2], late], axis=0)
+        other_first = swap(after(own_first, left, right), "dp", 1)
+        late = swap(after(own_second[second_cut:], other_first), "dp", 1)
+        other_second = jnp.concatenate([*early, late], axis=0)
+        early.append(other_first)
     else:
         other_first = other_second = None
     w_first = gather_dp(own_first, 0, other_first)
@@ -1076,7 +1075,7 @@
     grad_middle, grad_attn, grad_context, grad_gain_f = middle_back(
         grads_home, slot_col, middle, cotangent, ffn_gain, left, right
     )
-    down, down_other = first[::-1], second[::-1]
+    down, down_other = second[::-1], first[::-1]
 
     def back(half, *others):
         return attend_back(
@@ -1093,40 +1092,47 @@
     )
     left_block = scatter_step(left_block, down[0], grad_right)
     right_block = scatter_step(scatter_start(grad_right), down_other[0], second_halves[-1])
-    left_block = scatter_step(left_block, down[1], grad_right)
-    grad_tokens, grad_gain_a = tokens_back(
+    grad_tokens = tokens_back(
         g_left, after(g_right, right_block), left, right, tokens, attn_gain, grad_middle
     )
     mixed = mix(results_home, slot_col, middle, after(gate, grad_tokens))
+    beside = [left_block]
+    left_block = scatter_step(left_block, down[1], mixed)
+    beside.append(left_block)
     right_block = scatter_step(right_block, down_other[1], mixed, first_halves[-1])
     near = 2 + len(axis_bits("dp"))
     for place in down[2:near]:
-        left_block = scatter_step(left_block, place, mixed)
-    along = (left_block, right_block)
+        left_block = scatter_step(left_block, place)
+    beside.append(left_block)
     for place in down_other[2:near]:
         right_block = scatter_step(right_block, place)
     joined = jnp.concatenate([left_block, right_block], axis=-1)
     grad_expert_in = add_dp(first_halves, joined)
     grad_expert_out = add_dp(second_halves, joined)
-    dense = scatter_rest(joined, down[near:])
+    joined = scatter_step(joined, down[near])
+    beside.append(joined)
+    dense = scatter_rest(joined, down[near + 1 :])
     grad_left, grad_right = dense[:, : SPLIT + SIDE], dense[:, SPLIT + SIDE :]
     tiles = jnp.concatenate([tiles_left, tiles_right], axis=0)
     diagonals = jnp.concatenate([diagonals_left, diagonals_right], axis=0)
     grad_router = sum(router_parts)[:, :experts]
     grad_table = table_gradient(tiles, diagonals)
 
-    sizes = (D * experts, D, D, BUCKETS * HEADS)
+    own_weights = jnp.concatenate(
+        [w[:, :SIDE] for w in kinds[:3]] + [w[:, SIDE:] for w in kinds[:3]], axis=1
+    ).astype(F32)
+    own_grads = jnp.concatenate([grad_left[:, :SPLIT], grad_right[:, :SPLIT]], axis=1)
+    grad_gain_a = jnp.sum(own_weights * own_grads, axis=1) / gain_attn.astype(F32)
+
+    sizes = (D * experts, D, BUCKETS * HEADS)
     sums = sum_all(
         jnp.concatenate(
-            [
-                part.reshape(-1, LANES)
-                for part in (grad_router, after(grad_gain_a, *along), grad_gain_f, grad_table)
-            ],
-            axis=0,
-        )
+            [part.reshape(-1, LANES) for part in (grad_router, grad_gain_f, grad_table)], axis=0
+        ),
+        beside,
     ).reshape(-1)
     ends = [sum(sizes[: at + 1]) for at in range(len(sizes))]
-    grad_router, grad_gain_a, grad_gain_f, grad_table = (
+    grad_router, grad_gain_f, grad_table = (
         sums[end - size : end] for end, size in zip(ends, sizes)
     )
     number = lax.axis_index("dp") * experts + lax.axis_index("expert")
@@ -1146,7 +1152,7 @@
             for kind in range(4)
         ),
         own(grad_table.reshape(BUCKETS, HEADS), table_height, lax.axis_index("dp")),
-        own(grad_gain_a, shard, number),
+        grad_gain_a,
         own(grad_gain_f, shard, number),
         own(grad_router.reshape(D, experts), shard, number),
         grad_expert_in,

time: 528 us -> 526 us (level)
    all_to_all x7, waiting for transfers between devices: 13 us -> 0.86 us  [exchange(): lax.all_to_all(rows.reshape(experts, -1, D), 'expert', split_axis=0, conc...]
    ppermute x30 -> x29, waiting for transfers between devices: 65.8 us -> 77.9 us  [swap(): lax.ppermute(block, axis, [(place, place ^ bit) for place in range(size)])]
    ppermute x30 -> x29, starting transfers between devices: 40.5 us -> 30 us  [swap(): lax.ppermute(block, axis, [(place, place ^ bit) for place in range(size)])]
    unnamed x76 -> x66, local copies, waits for them, and re-layouts: 9.4 us -> 16.3 us
    all_to_all x7, starting transfers between devices: 53.3 us -> 60 us  [exchange(): lax.all_to_all(rows.reshape(experts, -1, D), 'expert', split_axis=0, conc...]
    slice x5 -> x2, local copies, waits for them, and re-layouts: 8.27 us -> 2.83 us  [the longest x1 2.81 us: body(): late = swap(after(own_second[second_cut:], other_first), 'dp', 1)]
  transfers between devices with their start and end apart: 37 -> 36, of which waited for: 18 -> 12; matrix products, arithmetic and copies ran while one was open for 14% -> 13% of each run, Pallas kernels for 51% -> 51%
where the time goes in v4:
time: 526 us; the launch traced here: 517 us
  Pallas kernels  264 us (50%)
  starting transfers between devices  90.1 us (17%)
  waiting for transfers between devices  78.8 us (15%)
  other arithmetic  52.2 us (10%)
  local copies, waits for them, and re-layouts  30.7 us (6%)
    ppermute x29, waiting for transfers between devices, swap(): lax.ppermute(block, axis, [(place, place ^ bit) for place in range(size)])  77.9 us
    pallas_call x2, Pallas kernels, run_expert(): pl.pallas_call(functools.partial(expert_kernel, experts), grid=(hidden_si...  69.1 us
    all_to_all x7, starting transfers between devices, exchange(): lax.all_to_all(rows.reshape(experts, -1, D), 'expert', split_axis=0, conc...  60 us
    pallas_call x2, Pallas kernels, attend_back(): pl.pallas_call(attend_back_kernel, grid=(SIDE_PAIRS,), in_specs=[*(pl.Blo...  53.9 us
    pallas_call x1, Pallas kernels, attend(): pl.pallas_call(attend_kernel, grid=(PAIRS,), in_specs=[*(pl.BlockSpec((TO...  36.8 us
    pallas_call x1, Pallas kernels, expert_weights(): pl.pallas_call(functools.partial(expert_weights_kernel, parts, side is no...  31.1 us
    ppermute x29, starting transfers between devices, swap(): lax.ppermute(block, axis, [(place, place ^ bit) for place in range(size)])  30 us
    unnamed x66, local copies, waits for them, and re-layouts  16.3 us
  transfers between devices with their start and end apart: 36, of which 12 were waited for; matrix products, arithmetic and copies ran while one was open for 13% of the time, Pallas kernels for 51%

profile of v4, /device:TPU:0, one launch (start us, length us, event | category | flops | bytes accessed | tf_op | source)
XLA Modules:
  0.0 517.1 jit_solution(14768061091492124696)
XLA Ops:
  29.5 7.8 %slots.1 = (s32[1024,1]{1,0:T(8,128)}, s32[1,1024]{1,0:T(1,128)}, bf16[2048,768]{1,0:T(8,128)(2,1)}) custom-call(s32[1024,1]{1,0:T(8,128)} %copy.48.route_col, s32[1,1024]{1,0:T(1,128)} %bitcast.93, bf16[1024,768]{1,0:T(8,128)(2,1)} %refs_4_.1), custom_call_target="tpu_custom_call" | custom-call | flops 161061280 | bytes 471859 | tf_op jit(solution)/shard_map/slots/pallas_call | solution.py:116
  49.1 8.2 %collective-permute-done.4 = bf16[1,2,2,1,1,24,1664]{6,5,4,3,2,1,0:T(8,128)(2,1)S(1)} collective-permute-done((bf16[1,2,2,1,1,24,1664]{6,5,4,3,2,1,0:T(8,128)(2,1)S(1)}, bf16[1,2,2,1,1,24,1664]{6,5,4,3,2,1,0:T(8,128)(2,1)S(1)}, u32[]{:S(2)}, u32[]{:S(2)}) %collective-permute-start.4) | collective-permute-done | bytes 319520 | tf_op jit(solution)/shard_map/ppermute | solution.py:868
  59.0 8.0 %collective-permute-done.10 = bf16[1,2,2,2,1,24,1536]{6,5,4,3,2,1,0:T(8,128)(2,1)S(1)} collective-permute-done((bf16[1,2,2,2,1,24,1536]{6,5,4,3,2,1,0:T(8,128)(2,1)S(1)}, bf16[1,2,2,2,1,24,1536]{6,5,4,3,2,1,0:T(8,128)(2,1)S(1)}, u32[]{:S(2)}, u32[]{:S(2)}) %collective-permute-start.10) | collective-permute-done | bytes 589856 | tf_op jit(solution)/shard_map/ppermute | solution.py:868
  85.8 8.3 %project.1 = (bf16[768,1024]{1,0:T(8,128)(2,1)}, bf16[1024,2304]{1,0:T(8,128)(2,1)}) custom-call(bf16[1024,768]{1,0:T(8,128)(2,1)} %tokens.3, f32[1,768]{1,0:T(1,128)} %reshape.378.gain, bf16[768,1536]{1,0:T(8,128)(2,1)} %bitcast.70, bf16[768,1664]{1,0:T(8,128)(2,1)} %bitcast.64), custom_call_target="tpu_custom_call" | custom-call | flops 181193936 | bytes 471859 | tf_op jit(solution)/shard_map/project/pallas_call | solution.py:141
  94.2 36.8 %attend.1 = (bf16[1024,768]{1,0:T(8,128)(2,1)}, f32[12,1,1024]{2,1,0:T(1,128)}) custom-call(bf16[1024,2304]{1,0:T(8,128)(2,1)} %get-tuple-element.80.q_ref.k_ref.v_ref, bf16[1024,2304]{1,0:T(8,128)(2,1)} %get-tuple-element.80.q_ref.k_ref.v_ref, bf16[1024,2304]{1,0:T(8,128)(2,1)} %get-tuple-element.80.q_ref.k_ref.v_ref, ...), custom_call_target="tpu_custom_call" | custom-call | flops 966367616 | bytes 393216 | tf_op jit(solution)/shard_map/attend/pallas_call | solution.py:245
  132.6 9.5 %middle.1 = (f32[1024,768]{1,0:T(8,128)}, bf16[1024,768]{1,0:T(8,128)(2,1)}, bf16[1024,768]{1,0:T(8,128)(2,1)}, f32[1024,1]{1,0:T(8,128)}) custom-call(bf16[1024,768]{1,0:T(8,128)(2,1)} %get-tuple-element.81.refs_0_.context, bf16[1024,768]{1,0:T(8,128)(2,1)} %tokens.3, bf16[768,1536]{1,0:T(8,128)(2,1)} %bitcast.71, bf16[768,1664]{1,0:T(8,128)(2,1)} %bitcast.66, ...), custom_call_target="tpu_custom_call" | custom-call | flops 221459248 | bytes 629145 | tf_op jit(solution)/shard_map/middle/pallas_call | solution.py:456
  142.2 15.9 %all-to-all-start.1 = ((bf16[16,64,768]{2,1,0:T(8,128)(2,1)}), bf16[16,64,768]{2,1,0:T(8,128)(2,1)S(1)}, u32[]{:S(2)}, u32[]{:S(2)}) async-start(bf16[16,64,768]{2,1,0:T(8,128)(2,1)} %bitcast.89), calls=%async_computation.1 | async-start | bytes 3145728 | tf_op jit(solution)/shard_map/all_to_all | solution.py:1020
  164.3 22.6 %collective-permute-done.13 = bf16[768,768]{1,0:T(8,128)(2,1)S(1)} collective-permute-done((bf16[768,768]{1,0:T(8,128)(2,1)}, bf16[768,768]{1,0:T(8,128)(2,1)S(1)}, u32[]{:S(2)}, u32[]{:S(2)}) %collective-permute-start.13) | collective-permute-done | bytes 1179680 | tf_op jit(solution)/shard_map/ppermute | solution.py:868
  190.1 9.1 %all-to-all-start.3 = ((bf16[16,64,768]{2,1,0:T(8,128)(2,1)}), bf16[16,64,768]{2,1,0:T(8,128)(2,1)S(1)}, u32[]{:S(2)}, u32[]{:S(2)}) async-start(bf16[16,64,768]{2,1,0:T(8,128)(2,1)} %bitcast.88), calls=%async_computation.3 | async-start | bytes 3145728 | tf_op jit(solution)/shard_map/all_to_all | solution.py:1020
  201.0 34.5 %expert.2 = (bf16[1024,3072]{1,0:T(8,128)(2,1)}, bf16[1024,3072]{1,0:T(8,128)(2,1)}, bf16[1024,768]{1,0:T(8,128)(2,1)}, bf16[1024,768]{1,0:T(8,128)(2,1)}, f32[1024,1]{1,0:T(8,128)}, /*index=5*/f32[768,128]{1,0:T(8,128)}) custom-call(bf16[1024,768]{1,0:T(8,128)(2,1)} %bitcast.78, bf16[16,128,768]{2,1,0:T(8,128)(2,1)} %all-to-all-done.c3.refs_9_, ...), custom_call_target="tpu_custom_call" | custom-call | flops 966367616 | bytes 1101004 | tf_op jit(solution)/shard_map/expert/pallas_call | solution.py:557
  241.7 34.6 %expert.3 = (bf16[1024,3072]{1,0:T(8,128)(2,1)}, bf16[1024,3072]{1,0:T(8,128)(2,1)}, bf16[1024,768]{1,0:T(8,128)(2,1)}, bf16[1024,768]{1,0:T(8,128)(2,1)}, f32[1024,1]{1,0:T(8,128)}, /*index=5*/f32[768,128]{1,0:T(8,128)}) custom-call(bf16[1024,768]{1,0:T(8,128)(2,1)} %bitcast.80, bf16[16,128,768]{2,1,0:T(8,128)(2,1)} %all-to-all-done.c3.refs_9_, ...), custom_call_target="tpu_custom_call" | custom-call | flops 966367616 | bytes 1101004 | tf_op jit(solution)/shard_map/expert/pallas_call | solution.py:557
  282.7 31.1 %expert_weights.1 = (bf16[384,3072]{1,0:T(8,128)(2,1)}, bf16[384,3072]{1,0:T(8,128)(2,1)}, bf16[1536,768]{1,0:T(8,128)(2,1)}, bf16[1536,768]{1,0:T(8,128)(2,1)}) custom-call(s32[1]{0:T(128)} %bitcast.26.refs_0_, bf16[1024,768]{1,0:T(8,128)(2,1)} %bitcast.79, bf16[1024,768]{1,0:T(8,128)(2,1)} %bitcast.81, f32[1024,1]{1,0:T(8,128)} %get-tuple-element.94.refs_3_, ...), custom_call_target="tpu_custom_call" | custom-call | flops 966367616 | bytes 1730150 | tf_op jit(solution)/shard_map/expert_weights/pallas_call | solution.py:682
  314.7 9.3 %all-to-all-start.5 = ((bf16[16,64,768]{2,1,0:T(8,128)(2,1)}), bf16[16,64,768]{2,1,0:T(8,128)(2,1)S(1)}, u32[]{:S(2)}, u32[]{:S(2)}) async-start(bf16[16,64,768]{2,1,0:T(8,128)(2,1)} %bitcast.87), calls=%async_computation.5 | async-start | bytes 3145728 | tf_op jit(solution)/shard_map/all_to_all | solution.py:1020
  328.5 12.9 %middle_back.1 = (f32[1024,768]{1,0:T(8,128)}, bf16[1024,768]{1,0:T(8,128)(2,1)}, bf16[1024,768]{1,0:T(8,128)(2,1)}, f32[1,768]{1,0:T(1,128)}) custom-call(bf16[1024,768]{1,0:T(8,128)(2,1)} %bitcast.83, bf16[1024,768]{1,0:T(8,128)(2,1)} %bitcast.84, s32[1024,1]{1,0:T(8,128)} %get-tuple-element.107.refs_2_, f32[1024,768]{1,0:T(8,128)} %get-tuple-element.108.refs_3_, ...), custom_call_target="tpu_custom_call" | custom-call | flops 221459248 | bytes 629145 | tf_op jit(solution)/shard_map/middle_back/pallas_call | solution.py:755
  342.2 27.0 %attend_back.2 = (bf16[1024,1152]{1,0:T(8,128)(2,1)}, f32[6,8,128]{2,1,0:T(8,128)}, f32[6,1,512]{2,1,0:T(1,128)}) custom-call(bf16[1024,2304]{1,0:T(8,128)(2,1)} %get-tuple-element.80.q_ref.k_ref.v_ref, bf16[1024,2304]{1,0:T(8,128)(2,1)} %get-tuple-element.80.q_ref.k_ref.v_ref, bf16[1024,2304]{1,0:T(8,128)(2,1)} %get-tuple-element.80.q_ref.k_ref.v_ref, ...), custom_call_target="tpu_custom_call" | custom-call | flops 4831838208 | bytes 1887436 | tf_op jit(solution)/shard_map/attend_back/pallas_call | solution.py:360
  369.2 7.9 %weights_back.2 = f32[768,1536]{1,0:T(8,128)} custom-call(bf16[768,1024]{1,0:T(8,128)(2,1)} %get-tuple-element.114.turned, bf16[1024,1152]{1,0:T(8,128)(2,1)} %get-tuple-element.113.grads.g_left, bf16[1024,768]{1,0:T(8,128)(2,1)} %get-tuple-element.81.refs_0_.context, bf16[1024,768]{1,0:T(8,128)(2,1)} %get-tuple-element.115.grad_attn), custom_call_target="tpu_custom_call" | custom-call | flops 120795952 | bytes 471859 | tf_op jit(solution)/shard_map/weights_back/pallas_call | solution.py:849
  381.7 6.7 %all-to-all-start.6 = ((bf16[16,64,768]{2,1,0:T(8,128)(2,1)}), bf16[16,64,768]{2,1,0:T(8,128)(2,1)}, u32[]{:S(2)}, u32[]{:S(2)}) async-start(bf16[16,64,768]{2,1,0:T(8,128)(2,1)} %bitcast.29), calls=%async_computation.6 | async-start | bytes 3145728 | tf_op jit(solution)/shard_map/all_to_all | solution.py:1020
  388.5 26.9 %attend_back.3 = (bf16[1024,1152]{1,0:T(8,128)(2,1)}, f32[6,8,128]{2,1,0:T(8,128)}, f32[6,1,512]{2,1,0:T(1,128)}) custom-call(bf16[1024,2304]{1,0:T(8,128)(2,1)} %get-tuple-element.80.q_ref.k_ref.v_ref, bf16[1024,2304]{1,0:T(8,128)(2,1)} %get-tuple-element.80.q_ref.k_ref.v_ref, bf16[1024,2304]{1,0:T(8,128)(2,1)} %get-tuple-element.80.q_ref.k_ref.v_ref, ...), custom_call_target="tpu_custom_call" | custom-call | flops 4831838208 | bytes 1887436 | tf_op jit(solution)/shard_map/attend_back/pallas_call | solution.py:360
  425.2 7.9 %weights_back.3 = f32[768,1536]{1,0:T(8,128)} custom-call(bf16[768,1024]{1,0:T(8,128)(2,1)} %get-tuple-element.114.turned, bf16[1024,1152]{1,0:T(8,128)(2,1)} %get-tuple-element.120.grads.g_right, bf16[1024,768]{1,0:T(8,128)(2,1)} %get-tuple-element.81.refs_0_.context, bf16[1024,768]{1,0:T(8,128)(2,1)} %get-tuple-element.115.grad_attn), custom_call_target="tpu_custom_call" | custom-call | flops 120795952 | bytes 471859 | tf_op jit(solution)/shard_map/weights_back/pallas_call | solution.py:849
  444.4 10.1 %tokens_back.1 = f32[1024,768]{1,0:T(8,128)} custom-call(bf16[1024,1152]{1,0:T(8,128)(2,1)} %get-tuple-element.113.grads.g_left, bf16[1024,1152]{1,0:T(8,128)(2,1)} %get-tuple-element.120.grads.g_right, bf16[768,1536]{1,0:T(8,128)(2,1)} %bitcast.73, bf16[768,1664]{1,0:T(8,128)(2,1)} %bitcast.69, bf16[1024,768]{1,0:T(8,128)(2,1)} %tokens.3, ...), custom_call_target="tpu_custom_call" | custom-call | flops 181193936 | bytes 629145 | tf_op jit(solution)/shard_map/tokens_back/pallas_call | solution.py:814
  454.5 8.0 %mix.1 = f32[1024,768]{1,0:T(8,128)} custom-call(bf16[1024,768]{1,0:T(8,128)(2,1)} %bitcast.82, bf16[1024,768]{1,0:T(8,128)(2,1)} %bitcast.30.refs_1_, s32[1024,1]{1,0:T(8,128)} %get-tuple-element.107.refs_2_, f32[1024,768]{1,0:T(8,128)} %get-tuple-element.108.refs_3_, f32[1024,1]{1,0:T(8,128)} %get-tuple-element.122.refs_4_), custom_call_target="tpu_custom_call" | custom-call | flops 161061280 | bytes 471859 | tf_op jit(solution)/shard_map/mix/pallas_call | solution.py:792
  473.5 10.2 %collective-permute-done.20 = bf16[1,2,2,2,1,24,1536]{6,5,4,3,2,1,0:T(8,128)(2,1)S(1)} collective-permute-done((bf16[1,2,2,2,1,24,1536]{6,5,4,3,2,1,0:T(8,128)(2,1)S(1)}, bf16[1,2,2,2,1,24,1536]{6,5,4,3,2,1,0:T(8,128)(2,1)S(1)}, u32[]{:S(2)}, u32[]{:S(2)}) %collective-permute-start.20) | collective-permute-done | bytes 589856 | tf_op jit(solution)/shard_map/ppermute | solution.py:868
  484.6 6.6 %collective-permute-done.21 = bf16[1,2,2,1,1,24,1536]{6,5,4,3,2,1,0:T(8,128)(2,1)S(1)} collective-permute-done((bf16[1,2,2,1,1,24,1536]{6,5,4,3,2,1,0:T(8,128)(2,1)S(1)}, bf16[1,2,2,1,1,24,1536]{6,5,4,3,2,1,0:T(8,128)(2,1)S(1)}, u32[]{:S(2)}, u32[]{:S(2)}) %collective-permute-start.21) | collective-permute-done | bytes 294944 | tf_op jit(solution)/shard_map/ppermute | solution.py:868
  505.7 7.0 %collective-permute-done.23 = bf16[1,1,1,1,1,24,3072]{6,5,4,3,2,1,0:T(8,128)(2,1)S(1)} collective-permute-done((bf16[1,1,1,1,1,24,3072]{6,5,4,3,2,1,0:T(8,128)(2,1)S(1)}, bf16[1,1,1,1,1,24,3072]{6,5,4,3,2,1,0:T(8,128)(2,1)S(1)}, u32[]{:S(2)}, u32[]{:S(2)}) %collective-permute-start.23) | collective-permute-done | bytes 147488 | tf_op jit(solution)/shard_map/ppermute | solution.py:868
  (250 shorter events, 148.3 us)
Async XLA Ops:
  8.7 17.8 %collective-permute-start.7 = (bf16[1,1,1,1,1,24,1536]{6,5,4,3,2,1,0:T(8,128)(2,1)S(1)}, bf16[1,1,1,1,1,24,1536]{6,5,4,3,2,1,0:T(8,128)(2,1)S(1)}, u32[]{:S(2)}, u32[]{:S(2)}) collective-permute-start(bf16[1,1,1,1,1,24,1536]{6,5,4,3,2,1,0:T(8,128)(2,1)S(1)} %maximum_bitcast_fusion), channel_id=1, source_target_pairs={{0,8},{1,9},{2,10},{3,11},{4,12},{5,13},{6,14},{7,15},{8,0},{9,1},... | collective-permute-start | bytes 221192 | tf_op jit(solution)/shard_map/ppermute | solution.py:868
  15.2 22.1 %collective-permute-start = (bf16[1,1,1,1,1,24,1664]{6,5,4,3,2,1,0:T(8,128)(2,1)S(1)}, bf16[1,1,1,1,1,24,1664]{6,5,4,3,2,1,0:T(8,128)(2,1)S(1)}, u32[]{:S(2)}, u32[]{:S(2)}) collective-permute-start(bf16[1,1,1,1,1,24,1664]{6,5,4,3,2,1,0:T(8,128)(2,1)S(1)} %bitcast.92), channel_id=1, source_target_pairs={{0,8},{1,9},{2,10},{3,11},{4,12},{5,13},{6,14},{7,15},{8,0},{9,1},... | collective-permute-start | bytes 239624 | tf_op jit(solution)/shard_map/ppermute | solution.py:868
  19.9 26.9 %collective-permute-start.3 = (bf16[768,768]{1,0:T(8,128)(2,1)S(1)}, bf16[768,768]{1,0:T(8,128)(2,1)S(1)}, u32[]{:S(2)}, u32[]{:S(2)}) collective-permute-start(bf16[768,768]{1,0:T(8,128)(2,1)S(1)} %get-tuple-element.175), channel_id=1, source_target_pairs={{0,16},{16,0},{1,17},{17,1},{2,18},{18,2},{3,19},{19,3},{4,20},{20... | collective-permute-start | bytes 3538952 | tf_op jit(solution)/shard_map/ppermute | solution.py:868
  26.6 11.0 %collective-permute-start.8 = (bf16[1,2,1,1,1,24,1536]{6,5,4,3,2,1,0:T(8,128)(2,1)S(1)}, bf16[1,2,1,1,1,24,1536]{6,5,4,3,2,1,0:T(8,128)(2,1)S(1)}, u32[]{:S(2)}, u32[]{:S(2)}) collective-permute-start(bf16[1,2,1,1,1,24,1536]{6,5,4,3,2,1,0:T(8,128)(2,1)S(1)} %pad_maximum_fusion.12), channel_id=1, source_target_pairs={{0,4},{1,5},{2,6},{3,7},{4,0},{5,1},{6,2},{7,3},{8,12},{9,13},{10,... | collective-permute-start | bytes 442376 | tf_op jit(solution)/shard_map/ppermute | solution.py:868
  47.5 19.5 %collective-permute-start.10 = (bf16[1,2,2,2,1,24,1536]{6,5,4,3,2,1,0:T(8,128)(2,1)S(1)}, bf16[1,2,2,2,1,24,1536]{6,5,4,3,2,1,0:T(8,128)(2,1)S(1)}, u32[]{:S(2)}, u32[]{:S(2)}) collective-permute-start(bf16[1,2,2,2,1,24,1536]{6,5,4,3,2,1,0:T(8,128)(2,1)S(1)} %pad_maximum_fusion.8), channel_id=1, source_target_pairs={{0,16},{16,0},{1,17},{17,1},{2,18},{18,2},{3,19},{19,3},{4,20},{20... | collective-permute-start | bytes 1769480 | tf_op jit(solution)/shard_map/ppermute | solution.py:868
  57.5 10.8 %collective-permute-start.5 = (bf16[2,2,2,1,1,24,1664]{6,5,4,3,2,1,0:T(8,128)(2,1)S(1)}, bf16[2,2,2,1,1,24,1664]{6,5,4,3,2,1,0:T(8,128)(2,1)S(1)}, u32[]{:S(2)}, u32[]{:S(2)}) collective-permute-start(bf16[2,2,2,1,1,24,1664]{6,5,4,3,2,1,0:T(8,128)(2,1)S(1)} %pad_maximum_fusion.7), channel_id=1, source_target_pairs={{0,2},{1,3},{2,0},{3,1},{4,6},{5,7},{6,4},{7,5},{8,10},{9,11},{10,... | collective-permute-start | bytes 1916936 | tf_op jit(solution)/shard_map/ppermute | solution.py:868
  76.4 65.8 %all-to-all-start = ((bf16[16,128,768]{2,1,0:T(8,128)(2,1)}), bf16[16,128,768]{2,1,0:T(8,128)(2,1)}, u32[]{:S(2)}, u32[]{:S(2)}) async-start(bf16[16,128,768]{2,1,0:T(8,128)(2,1)} %bitcast.85), calls=%async_computation | async-start | bytes 6291456 | tf_op jit(solution)/shard_map/all_to_all | solution.py:1020
  82.7 59.4 %collective-permute-start.12 = (bf16[384,3072]{1,0:T(8,128)(2,1)}, bf16[384,3072]{1,0:T(8,128)(2,1)}, u32[]{:S(2)}, u32[]{:S(2)}) collective-permute-start(bf16[384,3072]{1,0:T(8,128)(2,1)} %bitcast.86), channel_id=1, source_target_pairs={{0,16},{16,0},{1,17},{17,1},{2,18},{18,2},{3,19},{19,3},{4,20},{20... | collective-permute-start | bytes 7077896 | tf_op jit(solution)/shard_map/ppermute | solution.py:868
  142.2 48.0 %all-to-all-start.1 = ((bf16[16,64,768]{2,1,0:T(8,128)(2,1)}), bf16[16,64,768]{2,1,0:T(8,128)(2,1)S(1)}, u32[]{:S(2)}, u32[]{:S(2)}) async-start(bf16[16,64,768]{2,1,0:T(8,128)(2,1)} %bitcast.89), calls=%async_computation.1 | async-start | bytes 3145728 | tf_op jit(solution)/shard_map/all_to_all | solution.py:1020
  158.2 28.6 %collective-permute-start.13 = (bf16[768,768]{1,0:T(8,128)(2,1)}, bf16[768,768]{1,0:T(8,128)(2,1)S(1)}, u32[]{:S(2)}, u32[]{:S(2)}) collective-permute-start(bf16[768,768]{1,0:T(8,128)(2,1)} %get-tuple-element.87), channel_id=1, source_target_pairs={{0,16},{16,0},{1,17},{17,1},{2,18},{18,2},{3,19},{19,3},{4,20},{20... | collective-permute-start | bytes 3538952 | tf_op jit(solution)/shard_map/ppermute | solution.py:868
  190.1 45.3 %all-to-all-start.3 = ((bf16[16,64,768]{2,1,0:T(8,128)(2,1)}), bf16[16,64,768]{2,1,0:T(8,128)(2,1)S(1)}, u32[]{:S(2)}, u32[]{:S(2)}) async-start(bf16[16,64,768]{2,1,0:T(8,128)(2,1)} %bitcast.88), calls=%async_computation.3 | async-start | bytes 3145728 | tf_op jit(solution)/shard_map/all_to_all | solution.py:1020
  235.5 40.8 %all-to-all-start.2 = ((bf16[16,64,768]{2,1,0:T(8,128)(2,1)}), bf16[16,64,768]{2,1,0:T(8,128)(2,1)S(1)}, u32[]{:S(2)}, u32[]{:S(2)}) async-start(bf16[16,64,768]{2,1,0:T(8,128)(2,1)} %bitcast.91), calls=%async_computation.2 | async-start | bytes 3145728 | tf_op jit(solution)/shard_map/all_to_all | solution.py:1020
  276.3 38.4 %all-to-all-start.4 = ((bf16[16,64,768]{2,1,0:T(8,128)(2,1)}), bf16[16,64,768]{2,1,0:T(8,128)(2,1)S(1)}, u32[]{:S(2)}, u32[]{:S(2)}) async-start(bf16[16,64,768]{2,1,0:T(8,128)(2,1)} %bitcast.90), calls=%async_computation.4 | async-start | bytes 3145728 | tf_op jit(solution)/shard_map/all_to_all | solution.py:1020
  314.7 62.8 %all-to-all-start.5 = ((bf16[16,64,768]{2,1,0:T(8,128)(2,1)}), bf16[16,64,768]{2,1,0:T(8,128)(2,1)S(1)}, u32[]{:S(2)}, u32[]{:S(2)}) async-start(bf16[16,64,768]{2,1,0:T(8,128)(2,1)} %bitcast.87), calls=%async_computation.5 | async-start | bytes 3145728 | tf_op jit(solution)/shard_map/all_to_all | solution.py:1020
  326.5 114.1 %collective-permute-start.14 = (bf16[1536,768]{1,0:T(8,128)(2,1)}, bf16[1536,768]{1,0:T(8,128)(2,1)}, u32[]{:S(2)}, u32[]{:S(2)}) collective-permute-start(bf16[1536,768]{1,0:T(8,128)(2,1)} %get-tuple-element.103), channel_id=1, source_target_pairs={{0,16},{16,0},{1,17},{17,1},{2,18},{18,2},{3,19},{19,3},{4,20},{20... | collective-permute-start | bytes 7077896 | tf_op jit(solution)/shard_map/ppermute | solution.py:868
  327.0 138.2 %collective-permute-start.19 = (bf16[384,3072]{1,0:T(8,128)(2,1)}, bf16[384,3072]{1,0:T(8,128)(2,1)}, u32[]{:S(2)}, u32[]{:S(2)}) collective-permute-start(bf16[384,3072]{1,0:T(8,128)(2,1)} %get-tuple-element.101), channel_id=1, source_target_pairs={{0,16},{16,0},{1,17},{17,1},{2,18},{18,2},{3,19},{19,3},{4,20},{20... | collective-permute-start | bytes 7077896 | tf_op jit(solution)/shard_map/ppermute | solution.py:868
  381.7 54.3 %collective-permute-start.16 = (bf16[2,2,2,2,1,24,1536]{6,5,4,3,2,1,0:T(8,128)(2,1)}, bf16[2,2,2,2,1,24,1536]{6,5,4,3,2,1,0:T(8,128)(2,1)S(1)}, u32[]{:S(2)}, u32[]{:S(2)}) collective-permute-start(bf16[2,2,2,2,1,24,1536]{6,5,4,3,2,1,0:T(8,128)(2,1)} %select_convert_fusion.1), channel_id=1, source_target_pairs={{0,1},{1,0},{2,3},{3,2},{4,5},{5,4},{6,7},{7,6},{8,9},{9,8},{10,11... | collective-permute-start | bytes 3538952 | tf_op jit(solution)/shard_map/ppermute | solution.py:868
  381.7 43.5 %all-to-all-start.6 = ((bf16[16,64,768]{2,1,0:T(8,128)(2,1)}), bf16[16,64,768]{2,1,0:T(8,128)(2,1)}, u32[]{:S(2)}, u32[]{:S(2)}) async-start(bf16[16,64,768]{2,1,0:T(8,128)(2,1)} %bitcast.29), calls=%async_computation.6 | async-start | bytes 3145728 | tf_op jit(solution)/shard_map/all_to_all | solution.py:1020
  424.7 15.9 %collective-permute-start.24 = (f32[105,128]{1,0:T(8,128)}, f32[105,128]{1,0:T(8,128)}, u32[]{:S(2)}, u32[]{:S(2)}) collective-permute-start(f32[105,128]{1,0:T(8,128)} %pad_maximum_fusion.17), channel_id=1, source_target_pairs={{0,16},{16,0},{1,17},{17,1},{2,18},{18,2},{3,19},{19,3},{4,20},{20... | collective-permute-start | bytes 161288 | tf_op jit(solution)/shard_map/ppermute | solution.py:868
  438.6 24.0 %collective-permute-start.17 = (bf16[2,2,2,1,1,24,1536]{6,5,4,3,2,1,0:T(8,128)(2,1)S(1)}, bf16[2,2,2,1,1,24,1536]{6,5,4,3,2,1,0:T(8,128)(2,1)S(1)}, u32[]{:S(2)}, u32[]{:S(2)}) collective-permute-start(bf16[2,2,2,1,1,24,1536]{6,5,4,3,2,1,0:T(8,128)(2,1)S(1)} %select_convert_fusion.4), channel_id=1, source_target_pairs={{0,2},{1,3},{2,0},{3,1},{4,6},{5,7},{6,4},{7,5},{8,10},{9,11},{10,... | collective-permute-start | bytes 1769480 | tf_op jit(solution)/shard_map/ppermute | solution.py:868
  441.5 23.7 %collective-permute-start.25 = (f32[105,128]{1,0:T(8,128)S(1)}, f32[105,128]{1,0:T(8,128)S(1)}, u32[]{:S(2)}, u32[]{:S(2)}) collective-permute-start(f32[105,128]{1,0:T(8,128)S(1)} %add.317), channel_id=1, source_target_pairs={{0,8},{1,9},{2,10},{3,11},{4,12},{5,13},{6,14},{7,15},{8,0},{9,1},... | collective-permute-start | bytes 161288 | tf_op jit(solution)/shard_map/ppermute | solution.py:868
  464.5 19.2 %collective-permute-start.20 = (bf16[1,2,2,2,1,24,1536]{6,5,4,3,2,1,0:T(8,128)(2,1)S(1)}, bf16[1,2,2,2,1,24,1536]{6,5,4,3,2,1,0:T(8,128)(2,1)S(1)}, u32[]{:S(2)}, u32[]{:S(2)}) collective-permute-start(bf16[1,2,2,2,1,24,1536]{6,5,4,3,2,1,0:T(8,128)(2,1)S(1)} %select_convert_fusion.3), channel_id=1, source_target_pairs={{0,16},{16,0},{1,17},{17,1},{2,18},{18,2},{3,19},{19,3},{4,20},{20... | collective-permute-start | bytes 1769480 | tf_op jit(solution)/shard_map/ppermute | solution.py:868
  472.9 29.4 %collective-permute-start.27 = (f32[105,128]{1,0:T(8,128)S(1)}, f32[105,128]{1,0:T(8,128)S(1)}, u32[]{:S(2)}, u32[]{:S(2)}) collective-permute-start(f32[105,128]{1,0:T(8,128)S(1)} %add.319), channel_id=1, source_target_pairs={{0,2},{1,3},{2,0},{3,1},{4,6},{5,7},{6,4},{7,5},{8,10},{9,11},{10,... | collective-permute-start | bytes 161288 | tf_op jit(solution)/shard_map/ppermute | solution.py:868
  491.3 10.8 %collective-permute-start.22 = (bf16[1,2,1,1,1,24,3072]{6,5,4,3,2,1,0:T(8,128)(2,1)S(1)}, bf16[1,2,1,1,1,24,3072]{6,5,4,3,2,1,0:T(8,128)(2,1)S(1)}, u32[]{:S(2)}, u32[]{:S(2)}) collective-permute-start(bf16[1,2,1,1,1,24,3072]{6,5,4,3,2,1,0:T(8,128)(2,1)S(1)} %select_convert_fusion.5), channel_id=1, source_target_pairs={{0,4},{1,5},{2,6},{3,7},{4,0},{5,1},{6,2},{7,3},{8,12},{9,13},{10,... | collective-permute-start | bytes 884744 | tf_op jit(solution)/shard_map/ppermute | solution.py:868
  (35 other events, 372.8 us)

commit v5 on v4

--- a/solution.py
+++ b/solution.py
@@ -204,40 +204,69 @@
     return pltpu.roll(wide, 0, 1, stride=1, stride_axis=0)[:, :TILE]
 
 
+def add_band(st, slot, block, band):
+    for part in range(QBLK // TILE):
+        tile = block * (QBLK // TILE) + part
+        first, last = near_rows(tile)
+        at = (slot, slice(first * TILE, last * TILE), slice(part * TILE, (part + 1) * TILE))
+        st[at] += band[(first - tile + 1) * TILE : (last - tile + 1) * TILE]
+
+
 def attend_kernel(q_ref, k_ref, v_ref, qx_ref, kx_ref, band_ref, out_ref, lse_ref, st, pb, ot):
     low = lax.broadcasted_iota(jnp.int32, (TOK, LANES), 1) < HEAD_DIM
     v_t = v_ref[...].astype(F32).T.astype(BF)
+    sides = []
     for side in range(2):
         own = low if side == 0 else ~low
-        queries = jnp.where(own, q_ref[...], qx_ref[...])
-        keys = jnp.where(own, k_ref[...], kx_ref[...])
-        band = spread_band(band_ref[side])
-        for block in range(TOK // QBLK):
-            rows = slice(block * QBLK, (block + 1) * QBLK)
-            slot = block % 2
-            st[slot] = dot(keys, queries[rows], 1, 1)
-            for part in range(QBLK // TILE):
-                tile = block * (QBLK // TILE) + part
-                first, last = near_rows(tile)
-                at = (slot, slice(first * TILE, last * TILE), slice(part * TILE, (part + 1) * TILE))
-                st[at] += band[(first - tile + 1) * TILE : (last - tile + 1) * TILE]
-            top = jnp.max(st[slot, 0:TILE], axis=0, keepdims=True)
-            for chunk in range(1, TILES):
-                top = jnp.maximum(
-                    top,
-                    jnp.max(
-                        st[slot, chunk * TILE : (chunk + 1) * TILE], axis=0, keepdims=True
-                    ),
-                )
-            total = jnp.zeros((1, QBLK), F32)
-            for chunk in range(TILES):
-                at = slice(chunk * TILE, (chunk + 1) * TILE)
-                raised = jnp.exp(st[slot, at] - top)
-                total = total + jnp.sum(raised, axis=0, keepdims=True)
-                pb[slot, at] = raised.astype(BF)
-            half = slice(side * HEAD_DIM, (side + 1) * HEAD_DIM)
-            ot[half, rows] = dot(v_t[half], pb[slot]) * (1.0 / total)
-            lse_ref[side, :, rows] = top + jnp.log(total)
+        sides.append(
+            (
+                jnp.where(own, q_ref[...], qx_ref[...]),
+                jnp.where(own, k_ref[...], kx_ref[...]),
+                spread_band(band_ref[side]),
+            )
+        )
+    work = [(side, block) for side in range(2) for block in range(TOK // QBLK)]
+
+    def score(number):
+        side, block = work[number]
+        queries, keys, band = sides[side]
+        st[number % 2] = dot(keys, queries[block * QBLK : (block + 1) * QBLK], 1, 1)
+
+    def finish(number):
+        side, block = work[number]
+        slot = number % 2
+        rows = slice(block * QBLK, (block + 1) * QBLK)
+        add_band(st, slot, block, sides[side][2])
+        top = jnp.max(st[slot, 0:TILE], axis=0, keepdims=True)
+        for chunk in range(1, TILES):
+            top = jnp.maximum(
+                top,
+                jnp.max(st[slot, chunk * TILE : (chunk + 1) * TILE], axis=0, keepdims=True),
+            )
+        total = jnp.zeros((1, QBLK), F32)
+        for chunk in range(TILES):
+            at = slice(chunk * TILE, (chunk + 1) * TILE)
+            raised = jnp.exp(st[slot, at] - top)
+            total = total + jnp.sum(raised, axis=0, keepdims=True)
+            pb[slot, at] = raised.astype(BF)
+        lse_ref[side, :, rows] = top + jnp.log(total)
+        return total
+
+    def mix_values(number, total):
+        side, block = work[number]
+        half = slice(side * HEAD_DIM, (side + 1) * HEAD_DIM)
+        rows = slice(block * QBLK, (block + 1) * QBLK)
+        ot[half, rows] = dot(v_t[half], pb[number % 2]) * (1.0 / total)
+
+    score(0)
+    waiting = None
+    for number in range(len(work)):
+        if number + 1 < len(work):
+            score(number + 1)
+        if waiting is not None:
+            mix_values(number - 1, waiting)
+        waiting = finish(number)
+    mix_values(len(work) - 1, waiting)
     out_ref[...] = ot[...].T.astype(BF)
 
 
@@ -286,56 +315,83 @@
 ):
     low = lax.broadcasted_iota(jnp.int32, (TOK, LANES), 1) < HEAD_DIM
     k_t = k_ref[...].astype(F32).T.astype(BF)
+    sides = []
     for side in range(2):
         own = low if side == 0 else ~low
-        queries = jnp.where(own, q_ref[...], qx_ref[...])
-        keys = jnp.where(own, k_ref[...], kx_ref[...])
-        values = jnp.where(own, v_ref[...], jnp.zeros((), BF))
-        band = spread_band(band_ref[side])
-        near[...] = jnp.zeros_like(near)
+        sides.append(
+            (
+                jnp.where(own, q_ref[...], qx_ref[...]),
+                jnp.where(own, k_ref[...], kx_ref[...]),
+                jnp.where(own, v_ref[...], jnp.zeros((), BF)),
+                spread_band(band_ref[side]),
+            )
+        )
+    near[...] = jnp.zeros_like(near)
+    work = [(side, block) for side in range(2) for block in range(TOK // QBLK)]
+
+    def rows_of(block):
+        return slice(block * QBLK, (block + 1) * QBLK)
+
+    def score(number):
+        side, block = work[number]
+        queries, keys, values, _ = sides[side]
+        st[number % 2] = dot(keys, queries[rows_of(block)], 1, 1)
+        dp[number % 2] = dot(values, do_ref[rows_of(block), :], 1, 1)
+
+    def finish(number):
+        side, block = work[number]
+        slot = number % 2
+        add_band(st, slot, block, sides[side][3])
+        lse = lse_ref[side, :, rows_of(block)]
+        spread = jnp.zeros((1, QBLK), F32)
+        for chunk in range(TILES):
+            at = slice(chunk * TILE, (chunk + 1) * TILE)
+            weights = jnp.exp(st[slot, at] - lse)
+            st[slot, at] = weights
+            pb[slot, at] = weights.astype(BF)
+            spread = spread + jnp.sum(weights * dp[slot, at], axis=0, keepdims=True)
+        for chunk in range(TILES):
+            at = slice(chunk * TILE, (chunk + 1) * TILE)
+            sb[slot, at] = (st[slot, at] * (dp[slot, at] - spread)).astype(BF)
+        for part in range(QBLK // TILE):
+            tile = block * (QBLK // TILE) + part
+            first, last = near_rows(tile)
+            at = (slot, slice(first * TILE, last * TILE), slice(part * TILE, (part + 1) * TILE))
+            near[side, (first - tile + 1) * TILE : (last - tile + 1) * TILE, :TILE] += sb[
+                at
+            ].astype(F32)
+
+    def multiply(number):
+        side, block = work[number]
+        slot = number % 2
+        rows = rows_of(block)
         half = slice(side * HEAD_DIM, (side + 1) * HEAD_DIM)
-        for block in range(TOK // QBLK):
-            rows = slice(block * QBLK, (block + 1) * QBLK)
-            slot = block % 2
-            st[slot] = dot(keys, queries[rows], 1, 1)
-            dp[slot] = dot(values, do_ref[rows, :], 1, 1)
-            for part in range(QBLK // TILE):
-                tile = block * (QBLK // TILE) + part
-                first, last = near_rows(tile)
-                at = (slot, slice(first * TILE, last * TILE), slice(part * TILE, (part + 1) * TILE))
-                st[at] += band[(first - tile + 1) * TILE : (last - tile + 1) * TILE]
-            lse = lse_ref[side, :, rows]
-            spread = jnp.zeros((1, QBLK), F32)
-            for chunk in range(TILES):
-                at = slice(chunk * TILE, (chunk + 1) * TILE)
-                weights = jnp.exp(st[slot, at] - lse)
-                st[slot, at] = weights
-                pb[slot, at] = weights.astype(BF)
-                spread = spread + jnp.sum(weights * dp[slot, at], axis=0, keepdims=True)
-            for chunk in range(TILES):
-                at = slice(chunk * TILE, (chunk + 1) * TILE)
-                sb[slot, at] = (st[slot, at] * (dp[slot, at] - spread)).astype(BF)
-            for part in range(QBLK // TILE):
-                tile = block * (QBLK // TILE) + part
-                first, last = near_rows(tile)
-                at = (slot, slice(first * TILE, last * TILE), slice(part * TILE, (part + 1) * TILE))
-                near[(first - tile + 1) * TILE : (last - tile + 1) * TILE, :TILE] += sb[at].astype(F32)
-            dv = dot(pb[slot], do_ref[rows, :])
-            dk = dot(sb[slot], queries[rows])
-            if block == 0:
-                dvt[side] = dv
-                dkt[side] = dk
-            else:
-                dvt[side] += dv
-                dkt[side] += dk
-            dqt[half, rows] = dot(k_t[half], sb[slot])
+        dv = dot(pb[slot], do_ref[rows, :])
+        dk = dot(sb[slot], sides[side][0][rows])
+        if block == 0:
+            dvt[side] = dv
+            dkt[side] = dk
+        else:
+            dvt[side] += dv
+            dkt[side] += dk
+        dqt[half, rows] = dot(k_t[half], sb[slot])
+
+    score(0)
+    for number in range(len(work)):
+        if number + 1 < len(work):
+            score(number + 1)
+        if number > 0:
+            multiply(number - 1)
+        finish(number)
+    multiply(len(work) - 1)
+    for side in range(2):
         for tile in range(TILES):
             tiles_ref[side, tile : tile + 1, :] = jnp.sum(
                 dkt[side, tile * TILE : (tile + 1) * TILE], axis=0, keepdims=True
             )
-        folded = near[0:8, :]
+        folded = near[side, 0:8, :]
         for first in range(8, 3 * TILE, 8):
-            folded = folded + pltpu.roll(near[first : first + 8, :], 4 * LANES - first, 1)
+            folded = folded + pltpu.roll(near[side, first : first + 8, :], 4 * LANES - first, 1)
         diagonal = folded[0:1]
         for row in range(1, 8):
             diagonal = diagonal + pltpu.roll(folded[row : row + 1], 4 * LANES - row, 1)
@@ -391,7 +447,7 @@
             pltpu.VMEM((LANES, TOK), F32),
             pltpu.VMEM((2, TOK, LANES), F32),
             pltpu.VMEM((2, TOK, LANES), F32),
-            pltpu.VMEM((3 * TILE, 4 * LANES), F32),
+            pltpu.VMEM((2, 3 * TILE, 4 * LANES), F32),
         ],
         compiler_params=params(("arbitrary",)),
         cost_estimate=cost(5 * HEADS * TOK * TOK * 256, 8 * TOK * D, HEADS * TOK * TOK // 2, share=0.3),
@@ -796,7 +852,7 @@
         out_specs=rows,
         out_shape=jax.ShapeDtypeStruct((TOK, D), F32),
         compiler_params=params(("arbitrary",)),
-        cost_estimate=cost(2 * 2 * TOK * TOK * D, 12 * TOK * D),
+        cost_estimate=cost(2 * 2 * TOK * TOK * D, 12 * TOK * D, share=1),
         name="mix",
     )(*backs, slot_col, middle, gate)
 
@@ -826,7 +882,7 @@
         out_specs=rows,
         out_shape=jax.ShapeDtypeStruct((TOK, D), F32),
         compiler_params=params(("arbitrary",)),
-        cost_estimate=cost(6 * TOK * D * D, 16 * TOK * D),
+        cost_estimate=cost(6 * TOK * D * D, 16 * TOK * D, share=1),
         name="tokens_back",
     )(g_left, g_right, left, right, tokens, gain, grad_middle)
 
@@ -990,31 +1046,41 @@
     paired = lax.axis_size("dp") == 2
     own_first, own_second = expert_in[0], expert_out[0]
     second_cut = own_second.shape[0] // 2
+    early = [swap(own_second[:second_cut], "dp", 1)] if paired else []
+    ahead = [own_second[:second_cut]] if paired else []
+    left = gather_start(
+        jnp.concatenate([after(w_query[:, :SIDE], *ahead)] + [w[:, :SIDE] for w in kinds[1:]], axis=1)
+    )
+    right = gather_start(
+        jnp.concatenate(
+            [after(w_query[:, SIDE:], *ahead)] + [w[:, SIDE:] for w in kinds[1:]] + [small], axis=1
+        )
+    )
     table = gather_dp(rel_table, 0)
-    early = [swap(own_second[:second_cut], "dp", 1)] if paired else []
-    left = gather_start(jnp.concatenate([w[:, :SIDE] for w in kinds], axis=1))
-    right = gather_start(jnp.concatenate([w[:, SIDE:] for w in kinds] + [small], axis=1))
     dp_bits = len(axis_bits("dp"))
     rest = len(first) - dp_bits - 2
-    left, right = gather_step(left, first[0]), gather_step(right, second[0])
+    for at in range(rest):
+        left, right = gather_step(left, first[at]), gather_step(right, second[at])
+    left, right = lax.optimization_barrier((left, right, *early))[:2]
     slot_col, slot_row, sending_cot = make_slots(
         after(routes, left), cotangent, experts, capacity
     )
-    for at in range(1, rest):
-        left, right = gather_step(left, first[at]), gather_step(right, second[at])
-    wide_table = table.astype(F32)
-    query_features, key_features = lane_features(seq_ids.reshape(TOK, 1), wide_table)
-    band = jnp.sum(band_onehot()[None, :, :] * wide_table.T[:, None, :], axis=2)[:, None, :]
     left = gather_step(left, first[rest])
-    right = after(right, query_features, key_features, band, *early)
     for place in second[rest : rest + dp_bits]:
         right = gather_step(right, place)
+    wide_table = after(table, right).astype(F32)
+    query_features, key_features = lane_features(
+        after(seq_ids, right).reshape(TOK, 1), wide_table
+    )
+    band = jnp.sum(band_onehot()[None, :, :] * wide_table.T[:, None, :], axis=2)[:, None, :]
+    for place in first[rest + 1 : -1]:
+        left = gather_step(left, place)
+    for place in second[rest + dp_bits : -1]:
+        right = gather_step(right, place)
     left = after(left, sending_cot)
-    for place in first[rest + 1 :]:
-        left = gather_step(left, place)
-    for place in second[rest + dp_bits :]:
-        right = gather_step(right, place)
-    left, right = gather_end(left), gather_end(right)
+    right = after(right, query_features, key_features, band)
+    left = gather_end(gather_step(left, first[-1]))
+    right = gather_end(gather_step(right, second[-1]))
 
     def exchange(rows):
         return lax.all_to_all(
@@ -1095,17 +1161,17 @@
     grad_tokens = tokens_back(
         g_left, after(g_right, right_block), left, right, tokens, attn_gain, grad_middle
     )
-    mixed = mix(results_home, slot_col, middle, after(gate, grad_tokens))
     beside = [left_block]
-    left_block = scatter_step(left_block, down[1], mixed)
+    left_block = scatter_step(left_block, down[1], grad_tokens)
+    right_block = scatter_step(right_block, down_other[1], grad_tokens)
     beside.append(left_block)
-    right_block = scatter_step(right_block, down_other[1], mixed, first_halves[-1])
+    mixed = mix(results_home, slot_col, middle, after(gate, left_block, right_block))
     near = 2 + len(axis_bits("dp"))
     for place in down[2:near]:
-        left_block = scatter_step(left_block, place)
+        left_block = scatter_step(left_block, place, mixed, first_halves[-1])
     beside.append(left_block)
     for place in down_other[2:near]:
-        right_block = scatter_step(right_block, place)
+        right_block = scatter_step(right_block, place, mixed)
     joined = jnp.concatenate([left_block, right_block], axis=-1)
     grad_expert_in = add_dp(first_halves, joined)
     grad_expert_out = add_dp(second_halves, joined)
@@ -1118,11 +1184,14 @@
     grad_router = sum(router_parts)[:, :experts]
     grad_table = table_gradient(tiles, diagonals)
 
-    own_weights = jnp.concatenate(
-        [w[:, :SIDE] for w in kinds[:3]] + [w[:, SIDE:] for w in kinds[:3]], axis=1
-    ).astype(F32)
-    own_grads = jnp.concatenate([grad_left[:, :SPLIT], grad_right[:, :SPLIT]], axis=1)
-    grad_gain_a = jnp.sum(own_weights * own_grads, axis=1) / gain_attn.astype(F32)
+    grad_weights = [
+        jnp.concatenate(
+            [side[:, kind * SIDE : (kind + 1) * SIDE] for side in (grad_left, grad_right)], axis=1
+        )
+        for kind in range(4)
+    ]
+    products = sum(w.astype(F32) * grad for w, grad in zip(kinds[:3], grad_weights[:3]))
+    grad_gain_a = jnp.sum(products, axis=1) / gain_attn.astype(F32)
 
     sizes = (D * experts, D, BUCKETS * HEADS)
     sums = sum_all(
@@ -1144,13 +1213,7 @@
     return (
         mixed,
         grad_tokens,
-        *(
-            jnp.concatenate(
-                [side[:, kind * SIDE : (kind + 1) * SIDE] for side in (grad_left, grad_right)],
-                axis=1,
-            )
-            for kind in range(4)
-        ),
+        *grad_weights,
         own(grad_table.reshape(BUCKETS, HEADS), table_height, lax.axis_index("dp")),
         grad_gain_a,
         own(grad_gain_f, shard, number),

time: 526 us -> 490 us (0.932)
  Pallas kernels: 264 us -> 240 us
  local copies, waits for them, and re-layouts: 30.7 us -> 20.9 us
    pallas_call x1, Pallas kernels: 36.8 us -> 21.8 us  [attend(): pl.pallas_call(attend_kernel, grid=(PAIRS,), in_specs=[*(pl.BlockSpec((TO...]
    pallas_call x2, Pallas kernels: 53.9 us -> 45.7 us  [attend_back(): pl.pallas_call(attend_back_kernel, grid=(SIDE_PAIRS,), in_specs=[*(pl.Blo...]
    unnamed x66 -> x81, local copies, waits for them, and re-layouts: 16.3 us -> 9.08 us
    all_to_all x7, waiting for transfers between devices: 0.86 us -> 6.29 us  [exchange(): lax.all_to_all(rows.reshape(experts, -1, D), 'expert', split_axis=0, conc...]
  transfers between devices with their start and end apart: 36 -> 36, of which waited for: 12 -> 16; matrix products, arithmetic and copies ran while one was open for 13% -> 13% of each run, Pallas kernels for 51% -> 50%
where the time goes in v5:
time: 490 us; the launch traced here: 482 us
  Pallas kernels  240 us (49%)
  starting transfers between devices  88.5 us (18%)
  waiting for transfers between devices  80.8 us (16%)
  other arithmetic  49.4 us (10%)
  local copies, waits for them, and re-layouts  20.9 us (4%)
    ppermute x29, waiting for transfers between devices, swap(): lax.ppermute(block, axis, [(place, place ^ bit) for place in range(size)])  74.6 us
    pallas_call x2, Pallas kernels, run_expert(): pl.pallas_call(functools.partial(expert_kernel, experts), grid=(hidden_si...  69 us
    all_to_all x7, starting transfers between devices, exchange(): lax.all_to_all(rows.reshape(experts, -1, D), 'expert', split_axis=0, conc...  58.6 us
    pallas_call x2, Pallas kernels, attend_back(): pl.pallas_call(attend_back_kernel, grid=(SIDE_PAIRS,), in_specs=[*(pl.Blo...  45.7 us
    pallas_call x1, Pallas kernels, expert_weights(): pl.pallas_call(functools.partial(expert_weights_kernel, parts, side is no...  31.1 us
    ppermute x29, starting transfers between devices, swap(): lax.ppermute(block, axis, [(place, place ^ bit) for place in range(size)])  29.9 us
    pallas_call x1, Pallas kernels, attend(): pl.pallas_call(attend_kernel, grid=(PAIRS,), in_specs=[*(pl.BlockSpec((TO...  21.8 us
    pallas_call x2, Pallas kernels, weights_back(): pl.pallas_call(weights_back_kernel, grid=(steps + 1,), in_specs=[whole(tu...  15.9 us
  transfers between devices with their start and end apart: 36, of which 16 were waited for; matrix products, arithmetic and copies ran while one was open for 13% of the time, Pallas kernels for 50%

profile of v5, /device:TPU:0, one launch (start us, length us, event | category | flops | bytes accessed | tf_op | source)
XLA Modules:
  0.0 481.9 jit_solution(3756965841391692489)
XLA Ops:
  10.4 6.5 %collective-permute-done = bf16[1,1,1,1,1,24,1536]{6,5,4,3,2,1,0:T(8,128)(2,1)S(1)} collective-permute-done((bf16[1,1,1,1,1,24,1536]{6,5,4,3,2,1,0:T(8,128)(2,1)S(1)}, bf16[1,1,1,1,1,24,1536]{6,5,4,3,2,1,0:T(8,128)(2,1)S(1)}, u32[]{:S(2)}, u32[]{:S(2)}) %collective-permute-start) | collective-permute-done | bytes 73760 | tf_op jit(solution)/shard_map/ppermute | solution.py:924
  25.9 6.6 %collective-permute-done.4 = bf16[768,768]{1,0:T(8,128)(2,1)S(1)} collective-permute-done((bf16[768,768]{1,0:T(8,128)(2,1)S(1)}, bf16[768,768]{1,0:T(8,128)(2,1)S(1)}, u32[]{:S(2)}, u32[]{:S(2)}) %collective-permute-start.4) | collective-permute-done | bytes 1179680 | tf_op jit(solution)/shard_map/ppermute | solution.py:924
  36.8 7.8 %slots.1 = (s32[1024,1]{1,0:T(8,128)}, s32[1,1024]{1,0:T(1,128)}, bf16[2048,768]{1,0:T(8,128)(2,1)}) custom-call(s32[1024,1]{1,0:T(8,128)} %copy.48.route_col, s32[1,1024]{1,0:T(1,128)} %bitcast.93, bf16[1024,768]{1,0:T(8,128)(2,1)} %refs_4_.1), custom_call_target="tpu_custom_call" | custom-call | flops 161061280 | bytes 471859 | tf_op jit(solution)/shard_map/slots/pallas_call | solution.py:116
  52.0 7.5 %collective-permute-done.10 = bf16[1,2,2,2,1,24,1536]{6,5,4,3,2,1,0:T(8,128)(2,1)} collective-permute-done((bf16[1,2,2,2,1,24,1536]{6,5,4,3,2,1,0:T(8,128)(2,1)}, bf16[1,2,2,2,1,24,1536]{6,5,4,3,2,1,0:T(8,128)(2,1)}, u32[]{:S(2)}, u32[]{:S(2)}) %collective-permute-start.10) | collective-permute-done | bytes 589856 | tf_op jit(solution)/shard_map/ppermute | solution.py:924
  77.2 8.3 %project.1 = (bf16[768,1024]{1,0:T(8,128)(2,1)}, bf16[1024,2304]{1,0:T(8,128)(2,1)}) custom-call(bf16[1024,768]{1,0:T(8,128)(2,1)} %tokens.3, f32[1,768]{1,0:T(1,128)} %reshape.378.gain, bf16[768,1536]{1,0:T(8,128)(2,1)} %bitcast.70, bf16[768,1664]{1,0:T(8,128)(2,1)} %bitcast.64), custom_call_target="tpu_custom_call" | custom-call | flops 181193936 | bytes 471859 | tf_op jit(solution)/shard_map/project/pallas_call | solution.py:141
  85.5 21.8 %attend.1 = (bf16[1024,768]{1,0:T(8,128)(2,1)}, f32[12,1,1024]{2,1,0:T(1,128)}) custom-call(bf16[1024,2304]{1,0:T(8,128)(2,1)} %get-tuple-element.94.q_ref.k_ref.v_ref, bf16[1024,2304]{1,0:T(8,128)(2,1)} %get-tuple-element.94.q_ref.k_ref.v_ref, bf16[1024,2304]{1,0:T(8,128)(2,1)} %get-tuple-element.94.q_ref.k_ref.v_ref, ...), custom_call_target="tpu_custom_call" | custom-call | flops 966367616 | bytes 393216 | tf_op jit(solution)/shard_map/attend/pallas_call | solution.py:274
  108.9 9.5 %middle.1 = (f32[1024,768]{1,0:T(8,128)}, bf16[1024,768]{1,0:T(8,128)(2,1)}, bf16[1024,768]{1,0:T(8,128)(2,1)}, f32[1024,1]{1,0:T(8,128)}) custom-call(bf16[1024,768]{1,0:T(8,128)(2,1)} %get-tuple-element.95.refs_0_.context, bf16[1024,768]{1,0:T(8,128)(2,1)} %tokens.3, bf16[768,1536]{1,0:T(8,128)(2,1)} %bitcast.71, bf16[768,1664]{1,0:T(8,128)(2,1)} %bitcast.66, ...), custom_call_target="tpu_custom_call" | custom-call | flops 221459248 | bytes 629145 | tf_op jit(solution)/shard_map/middle/pallas_call | solution.py:512
  118.4 9.7 %collective-permute-done.12 = bf16[384,3072]{1,0:T(8,128)(2,1)} collective-permute-done((bf16[384,3072]{1,0:T(8,128)(2,1)}, bf16[384,3072]{1,0:T(8,128)(2,1)}, u32[]{:S(2)}, u32[]{:S(2)}) %collective-permute-start.12) | collective-permute-done | bytes 2359328 | tf_op jit(solution)/shard_map/ppermute | solution.py:924
  133.5 15.4 %all-to-all-start.1 = ((bf16[16,64,768]{2,1,0:T(8,128)(2,1)}), bf16[16,64,768]{2,1,0:T(8,128)(2,1)S(1)}, u32[]{:S(2)}, u32[]{:S(2)}) async-start(bf16[16,64,768]{2,1,0:T(8,128)(2,1)} %bitcast.89), calls=%async_computation.1 | async-start | bytes 3145728 | tf_op jit(solution)/shard_map/all_to_all | solution.py:1086
  155.1 22.5 %collective-permute-done.13 = bf16[768,768]{1,0:T(8,128)(2,1)S(1)} collective-permute-done((bf16[768,768]{1,0:T(8,128)(2,1)}, bf16[768,768]{1,0:T(8,128)(2,1)S(1)}, u32[]{:S(2)}, u32[]{:S(2)}) %collective-permute-start.13) | collective-permute-done | bytes 1179680 | tf_op jit(solution)/shard_map/ppermute | solution.py:924
  180.9 9.5 %all-to-all-start.3 = ((bf16[16,64,768]{2,1,0:T(8,128)(2,1)}), bf16[16,64,768]{2,1,0:T(8,128)(2,1)S(1)}, u32[]{:S(2)}, u32[]{:S(2)}) async-start(bf16[16,64,768]{2,1,0:T(8,128)(2,1)} %bitcast.88), calls=%async_computation.3 | async-start | bytes 3145728 | tf_op jit(solution)/shard_map/all_to_all | solution.py:1086
  192.2 34.5 %expert.2 = (bf16[1024,3072]{1,0:T(8,128)(2,1)}, bf16[1024,3072]{1,0:T(8,128)(2,1)}, bf16[1024,768]{1,0:T(8,128)(2,1)}, bf16[1024,768]{1,0:T(8,128)(2,1)}, f32[1024,1]{1,0:T(8,128)}, /*index=5*/f32[768,128]{1,0:T(8,128)}) custom-call(bf16[1024,768]{1,0:T(8,128)(2,1)} %bitcast.78, bf16[16,128,768]{2,1,0:T(8,128)(2,1)} %all-to-all-done.c3.refs_9_, ...), custom_call_target="tpu_custom_call" | custom-call | flops 966367616 | bytes 1101004 | tf_op jit(solution)/shard_map/expert/pallas_call | solution.py:613
  232.9 34.5 %expert.3 = (bf16[1024,3072]{1,0:T(8,128)(2,1)}, bf16[1024,3072]{1,0:T(8,128)(2,1)}, bf16[1024,768]{1,0:T(8,128)(2,1)}, bf16[1024,768]{1,0:T(8,128)(2,1)}, f32[1024,1]{1,0:T(8,128)}, /*index=5*/f32[768,128]{1,0:T(8,128)}) custom-call(bf16[1024,768]{1,0:T(8,128)(2,1)} %bitcast.80, bf16[16,128,768]{2,1,0:T(8,128)(2,1)} %all-to-all-done.c3.refs_9_, ...), custom_call_target="tpu_custom_call" | custom-call | flops 966367616 | bytes 1101004 | tf_op jit(solution)/shard_map/expert/pallas_call | solution.py:613
  267.3 6.6 %all-to-all-start.4 = ((bf16[16,64,768]{2,1,0:T(8,128)(2,1)}), bf16[16,64,768]{2,1,0:T(8,128)(2,1)S(1)}, u32[]{:S(2)}, u32[]{:S(2)}) async-start(bf16[16,64,768]{2,1,0:T(8,128)(2,1)} %bitcast.90), calls=%async_computation.4 | async-start | bytes 3145728 | tf_op jit(solution)/shard_map/all_to_all | solution.py:1086
  273.9 31.1 %expert_weights.1 = (bf16[384,3072]{1,0:T(8,128)(2,1)}, bf16[384,3072]{1,0:T(8,128)(2,1)}, bf16[1536,768]{1,0:T(8,128)(2,1)}, bf16[1536,768]{1,0:T(8,128)(2,1)}) custom-call(s32[1]{0:T(128)} %bitcast.26.refs_0_, bf16[1024,768]{1,0:T(8,128)(2,1)} %bitcast.79, bf16[1024,768]{1,0:T(8,128)(2,1)} %bitcast.81, f32[1024,1]{1,0:T(8,128)} %get-tuple-element.108.refs_3_, ...), custom_call_target="tpu_custom_call" | custom-call | flops 966367616 | bytes 1730150 | tf_op jit(solution)/shard_map/expert_weights/pallas_call | solution.py:738
  305.9 9.3 %all-to-all-start.5 = ((bf16[16,64,768]{2,1,0:T(8,128)(2,1)}), bf16[16,64,768]{2,1,0:T(8,128)(2,1)S(1)}, u32[]{:S(2)}, u32[]{:S(2)}) async-start(bf16[16,64,768]{2,1,0:T(8,128)(2,1)} %bitcast.87), calls=%async_computation.5 | async-start | bytes 3145728 | tf_op jit(solution)/shard_map/all_to_all | solution.py:1086
  319.7 12.9 %middle_back.1 = (f32[1024,768]{1,0:T(8,128)}, bf16[1024,768]{1,0:T(8,128)(2,1)}, bf16[1024,768]{1,0:T(8,128)(2,1)}, f32[1,768]{1,0:T(1,128)}) custom-call(bf16[1024,768]{1,0:T(8,128)(2,1)} %bitcast.82, bf16[1024,768]{1,0:T(8,128)(2,1)} %bitcast.83, s32[1024,1]{1,0:T(8,128)} %get-tuple-element.121.refs_2_, f32[1024,768]{1,0:T(8,128)} %get-tuple-element.122.refs_3_, ...), custom_call_target="tpu_custom_call" | custom-call | flops 221459248 | bytes 629145 | tf_op jit(solution)/shard_map/middle_back/pallas_call | solution.py:811
  333.3 22.9 %attend_back.2 = (bf16[1024,1152]{1,0:T(8,128)(2,1)}, f32[6,8,128]{2,1,0:T(8,128)}, f32[6,1,512]{2,1,0:T(1,128)}) custom-call(bf16[1024,2304]{1,0:T(8,128)(2,1)} %get-tuple-element.94.q_ref.k_ref.v_ref, bf16[1024,2304]{1,0:T(8,128)(2,1)} %get-tuple-element.94.q_ref.k_ref.v_ref, bf16[1024,2304]{1,0:T(8,128)(2,1)} %get-tuple-element.94.q_ref.k_ref.v_ref, ...), custom_call_target="tpu_custom_call" | custom-call | flops 4831838208 | bytes 1887436 | tf_op jit(solution)/shard_map/attend_back/pallas_call | solution.py:416
  356.3 7.9 %weights_back.2 = f32[768,1536]{1,0:T(8,128)} custom-call(bf16[768,1024]{1,0:T(8,128)(2,1)} %get-tuple-element.124.turned, bf16[1024,1152]{1,0:T(8,128)(2,1)} %get-tuple-element.128.grads.g_left, bf16[1024,768]{1,0:T(8,128)(2,1)} %get-tuple-element.95.refs_0_.context, bf16[1024,768]{1,0:T(8,128)(2,1)} %get-tuple-element.129.grad_attn), custom_call_target="tpu_custom_call" | custom-call | flops 120795952 | bytes 471859 | tf_op jit(solution)/shard_map/weights_back/pallas_call | solution.py:905
  375.2 22.8 %attend_back.3 = (bf16[1024,1152]{1,0:T(8,128)(2,1)}, f32[6,8,128]{2,1,0:T(8,128)}, f32[6,1,512]{2,1,0:T(1,128)}) custom-call(bf16[1024,2304]{1,0:T(8,128)(2,1)} %get-tuple-element.94.q_ref.k_ref.v_ref, bf16[1024,2304]{1,0:T(8,128)(2,1)} %get-tuple-element.94.q_ref.k_ref.v_ref, bf16[1024,2304]{1,0:T(8,128)(2,1)} %get-tuple-element.94.q_ref.k_ref.v_ref, ...), custom_call_target="tpu_custom_call" | custom-call | flops 4831838208 | bytes 1887436 | tf_op jit(solution)/shard_map/attend_back/pallas_call | solution.py:416
  407.9 7.9 %weights_back.3 = f32[768,1536]{1,0:T(8,128)} custom-call(bf16[768,1024]{1,0:T(8,128)(2,1)} %get-tuple-element.124.turned, bf16[1024,1152]{1,0:T(8,128)(2,1)} %get-tuple-element.136.grads.g_right, bf16[1024,768]{1,0:T(8,128)(2,1)} %get-tuple-element.95.refs_0_.context, bf16[1024,768]{1,0:T(8,128)(2,1)} %get-tuple-element.129.grad_attn), custom_call_target="tpu_custom_call" | custom-call | flops 120795952 | bytes 471859 | tf_op jit(solution)/shard_map/weights_back/pallas_call | solution.py:905
  428.4 10.1 %tokens_back.1 = f32[1024,768]{1,0:T(8,128)} custom-call(bf16[1024,1152]{1,0:T(8,128)(2,1)} %get-tuple-element.128.grads.g_left, bf16[1024,1152]{1,0:T(8,128)(2,1)} %get-tuple-element.136.grads.g_right, bf16[768,1536]{1,0:T(8,128)(2,1)} %bitcast.73, bf16[768,1664]{1,0:T(8,128)(2,1)} %bitcast.69, bf16[1024,768]{1,0:T(8,128)(2,1)} %tokens.3, ...), custom_call_target="tpu_custom_call" | custom-call | flops 3623878656 | bytes 12582912 | tf_op jit(solution)/shard_map/tokens_back/pallas_call | solution.py:870
  443.0 8.0 %mix.1 = f32[1024,768]{1,0:T(8,128)} custom-call(bf16[1024,768]{1,0:T(8,128)(2,1)} %bitcast.86, bf16[1024,768]{1,0:T(8,128)(2,1)} %bitcast.30.refs_1_, s32[1024,1]{1,0:T(8,128)} %get-tuple-element.121.refs_2_, f32[1024,768]{1,0:T(8,128)} %get-tuple-element.122.refs_3_, f32[1024,1]{1,0:T(8,128)} %get-tuple-element.140.refs_4_), custom_call_target="tpu_custom_call" | custom-call | flops 3221225472 | bytes 9437184 | tf_op jit(solution)/shard_map/mix/pallas_call | solution.py:848
  472.6 7.0 %collective-permute-done.23 = bf16[1,1,1,1,1,24,3072]{6,5,4,3,2,1,0:T(8,128)(2,1)S(1)} collective-permute-done((bf16[1,1,1,1,1,24,3072]{6,5,4,3,2,1,0:T(8,128)(2,1)S(1)}, bf16[1,1,1,1,1,24,3072]{6,5,4,3,2,1,0:T(8,128)(2,1)S(1)}, u32[]{:S(2)}, u32[]{:S(2)}) %collective-permute-start.23) | collective-permute-done | bytes 147488 | tf_op jit(solution)/shard_map/ppermute | solution.py:924
  (264 shorter events, 139.3 us)
Async XLA Ops:
  3.6 29.0 %collective-permute-start.4 = (bf16[768,768]{1,0:T(8,128)(2,1)S(1)}, bf16[768,768]{1,0:T(8,128)(2,1)S(1)}, u32[]{:S(2)}, u32[]{:S(2)}) collective-permute-start(bf16[768,768]{1,0:T(8,128)(2,1)S(1)} %get-tuple-element.195), channel_id=1, source_target_pairs={{0,16},{16,0},{1,17},{17,1},{2,18},{18,2},{3,19},{19,3},{4,20},{20... | collective-permute-start | bytes 3538952 | tf_op jit(solution)/shard_map/ppermute | solution.py:924
  10.0 24.3 %collective-permute-start.7 = (bf16[16,12]{1,0:T(8,128)(2,1)S(1)}, bf16[16,12]{1,0:T(8,128)(2,1)S(1)}, u32[]{:S(2)}, u32[]{:S(2)}) collective-permute-start(bf16[16,12]{1,0:T(8,128)(2,1)S(1)} %copy-done.27), channel_id=1, source_target_pairs={{0,16},{16,0},{1,17},{17,1},{2,18},{18,2},{3,19},{19,3},{4,20},{20... | collective-permute-start | bytes 1160 | tf_op jit(solution)/shard_map/ppermute | solution.py:924
  32.6 12.1 %collective-permute-start.9 = (bf16[1,2,2,1,1,24,1536]{6,5,4,3,2,1,0:T(8,128)(2,1)S(1)}, bf16[1,2,2,1,1,24,1536]{6,5,4,3,2,1,0:T(8,128)(2,1)S(1)}, u32[]{:S(2)}, u32[]{:S(2)}) collective-permute-start(bf16[1,2,2,1,1,24,1536]{6,5,4,3,2,1,0:T(8,128)(2,1)S(1)} %pad_maximum_fusion.10), channel_id=1, source_target_pairs={{0,2},{1,3},{2,0},{3,1},{4,6},{5,7},{6,4},{7,5},{8,10},{9,11},{10,... | collective-permute-start | bytes 884744 | tf_op jit(solution)/shard_map/ppermute | solution.py:924
  45.6 13.9 %collective-permute-start.10 = (bf16[1,2,2,2,1,24,1536]{6,5,4,3,2,1,0:T(8,128)(2,1)}, bf16[1,2,2,2,1,24,1536]{6,5,4,3,2,1,0:T(8,128)(2,1)}, u32[]{:S(2)}, u32[]{:S(2)}) collective-permute-start(bf16[1,2,2,2,1,24,1536]{6,5,4,3,2,1,0:T(8,128)(2,1)} %pad_maximum_fusion.8), channel_id=1, source_target_pairs={{0,16},{16,0},{1,17},{17,1},{2,18},{18,2},{3,19},{19,3},{4,20},{20... | collective-permute-start | bytes 1769480 | tf_op jit(solution)/shard_map/ppermute | solution.py:924
  46.2 15.4 %collective-permute-start.6 = (bf16[2,2,2,1,1,24,1664]{6,5,4,3,2,1,0:T(8,128)(2,1)S(1)}, bf16[2,2,2,1,1,24,1664]{6,5,4,3,2,1,0:T(8,128)(2,1)S(1)}, u32[]{:S(2)}, u32[]{:S(2)}) collective-permute-start(bf16[2,2,2,1,1,24,1664]{6,5,4,3,2,1,0:T(8,128)(2,1)S(1)} %pad_maximum_fusion.7), channel_id=1, source_target_pairs={{0,2},{1,3},{2,0},{3,1},{4,6},{5,7},{6,4},{7,5},{8,10},{9,11},{10,... | collective-permute-start | bytes 1916936 | tf_op jit(solution)/shard_map/ppermute | solution.py:924
  68.7 64.8 %all-to-all-start = ((bf16[16,128,768]{2,1,0:T(8,128)(2,1)}), bf16[16,128,768]{2,1,0:T(8,128)(2,1)}, u32[]{:S(2)}, u32[]{:S(2)}) async-start(bf16[16,128,768]{2,1,0:T(8,128)(2,1)} %bitcast.84), calls=%async_computation | async-start | bytes 6291456 | tf_op jit(solution)/shard_map/all_to_all | solution.py:1086
  74.1 54.0 %collective-permute-start.12 = (bf16[384,3072]{1,0:T(8,128)(2,1)}, bf16[384,3072]{1,0:T(8,128)(2,1)}, u32[]{:S(2)}, u32[]{:S(2)}) collective-permute-start(bf16[384,3072]{1,0:T(8,128)(2,1)} %bitcast.85), channel_id=1, source_target_pairs={{0,16},{16,0},{1,17},{17,1},{2,18},{18,2},{3,19},{19,3},{4,20},{20... | collective-permute-start | bytes 7077896 | tf_op jit(solution)/shard_map/ppermute | solution.py:924
  133.5 47.4 %all-to-all-start.1 = ((bf16[16,64,768]{2,1,0:T(8,128)(2,1)}), bf16[16,64,768]{2,1,0:T(8,128)(2,1)S(1)}, u32[]{:S(2)}, u32[]{:S(2)}) async-start(bf16[16,64,768]{2,1,0:T(8,128)(2,1)} %bitcast.89), calls=%async_computation.1 | async-start | bytes 3145728 | tf_op jit(solution)/shard_map/all_to_all | solution.py:1086
  149.0 28.6 %collective-permute-start.13 = (bf16[768,768]{1,0:T(8,128)(2,1)}, bf16[768,768]{1,0:T(8,128)(2,1)S(1)}, u32[]{:S(2)}, u32[]{:S(2)}) collective-permute-start(bf16[768,768]{1,0:T(8,128)(2,1)} %get-tuple-element.101), channel_id=1, source_target_pairs={{0,16},{16,0},{1,17},{17,1},{2,18},{18,2},{3,19},{19,3},{4,20},{20... | collective-permute-start | bytes 3538952 | tf_op jit(solution)/shard_map/ppermute | solution.py:924
  180.9 45.8 %all-to-all-start.3 = ((bf16[16,64,768]{2,1,0:T(8,128)(2,1)}), bf16[16,64,768]{2,1,0:T(8,128)(2,1)S(1)}, u32[]{:S(2)}, u32[]{:S(2)}) async-start(bf16[16,64,768]{2,1,0:T(8,128)(2,1)} %bitcast.88), calls=%async_computation.3 | async-start | bytes 3145728 | tf_op jit(solution)/shard_map/all_to_all | solution.py:1086
  226.7 40.6 %all-to-all-start.2 = ((bf16[16,64,768]{2,1,0:T(8,128)(2,1)}), bf16[16,64,768]{2,1,0:T(8,128)(2,1)S(1)}, u32[]{:S(2)}, u32[]{:S(2)}) async-start(bf16[16,64,768]{2,1,0:T(8,128)(2,1)} %bitcast.91), calls=%async_computation.2 | async-start | bytes 3145728 | tf_op jit(solution)/shard_map/all_to_all | solution.py:1086
  267.3 38.6 %all-to-all-start.4 = ((bf16[16,64,768]{2,1,0:T(8,128)(2,1)}), bf16[16,64,768]{2,1,0:T(8,128)(2,1)S(1)}, u32[]{:S(2)}, u32[]{:S(2)}) async-start(bf16[16,64,768]{2,1,0:T(8,128)(2,1)} %bitcast.90), calls=%async_computation.4 | async-start | bytes 3145728 | tf_op jit(solution)/shard_map/all_to_all | solution.py:1086
  305.9 58.7 %all-to-all-start.5 = ((bf16[16,64,768]{2,1,0:T(8,128)(2,1)}), bf16[16,64,768]{2,1,0:T(8,128)(2,1)S(1)}, u32[]{:S(2)}, u32[]{:S(2)}) async-start(bf16[16,64,768]{2,1,0:T(8,128)(2,1)} %bitcast.87), calls=%async_computation.5 | async-start | bytes 3145728 | tf_op jit(solution)/shard_map/all_to_all | solution.py:1086
  317.7 103.5 %collective-permute-start.15 = (bf16[1536,768]{1,0:T(8,128)(2,1)}, bf16[1536,768]{1,0:T(8,128)(2,1)}, u32[]{:S(2)}, u32[]{:S(2)}) collective-permute-start(bf16[1536,768]{1,0:T(8,128)(2,1)} %get-tuple-element.117), channel_id=1, source_target_pairs={{0,16},{16,0},{1,17},{17,1},{2,18},{18,2},{3,19},{19,3},{4,20},{20... | collective-permute-start | bytes 7077896 | tf_op jit(solution)/shard_map/ppermute | solution.py:924
  318.2 132.8 %collective-permute-start.19 = (bf16[384,3072]{1,0:T(8,128)(2,1)}, bf16[384,3072]{1,0:T(8,128)(2,1)}, u32[]{:S(2)}, u32[]{:S(2)}) collective-permute-start(bf16[384,3072]{1,0:T(8,128)(2,1)} %get-tuple-element.115), channel_id=1, source_target_pairs={{0,16},{16,0},{1,17},{17,1},{2,18},{18,2},{3,19},{19,3},{4,20},{20... | collective-permute-start | bytes 7077896 | tf_op jit(solution)/shard_map/ppermute | solution.py:924
  364.6 43.2 %all-to-all-start.6 = ((bf16[16,64,768]{2,1,0:T(8,128)(2,1)}), bf16[16,64,768]{2,1,0:T(8,128)(2,1)}, u32[]{:S(2)}, u32[]{:S(2)}) async-start(bf16[16,64,768]{2,1,0:T(8,128)(2,1)} %bitcast.29), calls=%async_computation.6 | async-start | bytes 3145728 | tf_op jit(solution)/shard_map/all_to_all | solution.py:1086
  374.7 43.8 %collective-permute-start.14 = (bf16[2,2,2,2,1,24,1536]{6,5,4,3,2,1,0:T(8,128)(2,1)}, bf16[2,2,2,2,1,24,1536]{6,5,4,3,2,1,0:T(8,128)(2,1)S(1)}, u32[]{:S(2)}, u32[]{:S(2)}) collective-permute-start(bf16[2,2,2,2,1,24,1536]{6,5,4,3,2,1,0:T(8,128)(2,1)} %select_convert_fusion.2), channel_id=1, source_target_pairs={{0,1},{1,0},{2,3},{3,2},{4,5},{5,4},{6,7},{7,6},{8,9},{9,8},{10,11... | collective-permute-start | bytes 3538952 | tf_op jit(solution)/shard_map/ppermute | solution.py:924
  407.4 16.1 %collective-permute-start.24 = (f32[105,128]{1,0:T(8,128)}, f32[105,128]{1,0:T(8,128)}, u32[]{:S(2)}, u32[]{:S(2)}) collective-permute-start(f32[105,128]{1,0:T(8,128)} %pad_maximum_fusion.17), channel_id=1, source_target_pairs={{0,16},{16,0},{1,17},{17,1},{2,18},{18,2},{3,19},{19,3},{4,20},{20... | collective-permute-start | bytes 161288 | tf_op jit(solution)/shard_map/ppermute | solution.py:924
  421.2 17.5 %collective-permute-start.17 = (bf16[2,2,2,1,1,24,1536]{6,5,4,3,2,1,0:T(8,128)(2,1)S(1)}, bf16[2,2,2,1,1,24,1536]{6,5,4,3,2,1,0:T(8,128)(2,1)S(1)}, u32[]{:S(2)}, u32[]{:S(2)}) collective-permute-start(bf16[2,2,2,1,1,24,1536]{6,5,4,3,2,1,0:T(8,128)(2,1)S(1)} %select_convert_fusion.4), channel_id=1, source_target_pairs={{0,2},{1,3},{2,0},{3,1},{4,6},{5,7},{6,4},{7,5},{8,10},{9,11},{10,... | collective-permute-start | bytes 1769480 | tf_op jit(solution)/shard_map/ppermute | solution.py:924
  424.3 15.9 %collective-permute-start.25 = (f32[105,128]{1,0:T(8,128)S(1)}, f32[105,128]{1,0:T(8,128)S(1)}, u32[]{:S(2)}, u32[]{:S(2)}) collective-permute-start(f32[105,128]{1,0:T(8,128)S(1)} %add.323), channel_id=1, source_target_pairs={{0,8},{1,9},{2,10},{3,11},{4,12},{5,13},{6,14},{7,15},{8,0},{9,1},... | collective-permute-start | bytes 161288 | tf_op jit(solution)/shard_map/ppermute | solution.py:924
  427.5 15.3 %collective-permute-start.18 = (bf16[1,2,2,2,1,24,1536]{6,5,4,3,2,1,0:T(8,128)(2,1)S(1)}, bf16[1,2,2,2,1,24,1536]{6,5,4,3,2,1,0:T(8,128)(2,1)S(1)}, u32[]{:S(2)}, u32[]{:S(2)}) collective-permute-start(bf16[1,2,2,2,1,24,1536]{6,5,4,3,2,1,0:T(8,128)(2,1)S(1)} %select_convert_fusion.3), channel_id=1, source_target_pairs={{0,16},{16,0},{1,17},{17,1},{2,18},{18,2},{3,19},{19,3},{4,20},{20... | collective-permute-start | bytes 1769480 | tf_op jit(solution)/shard_map/ppermute | solution.py:924
  438.9 14.5 %collective-permute-start.20 = (bf16[1,2,2,1,1,24,1536]{6,5,4,3,2,1,0:T(8,128)(2,1)S(1)}, bf16[1,2,2,1,1,24,1536]{6,5,4,3,2,1,0:T(8,128)(2,1)S(1)}, u32[]{:S(2)}, u32[]{:S(2)}) collective-permute-start(bf16[1,2,2,1,1,24,1536]{6,5,4,3,2,1,0:T(8,128)(2,1)S(1)} %select_convert_fusion.7), channel_id=1, source_target_pairs={{0,16},{16,0},{1,17},{17,1},{2,18},{18,2},{3,19},{19,3},{4,20},{20... | collective-permute-start | bytes 884744 | tf_op jit(solution)/shard_map/ppermute | solution.py:924
  440.2 13.4 %collective-permute-start.26 = (f32[105,128]{1,0:T(8,128)S(1)}, f32[105,128]{1,0:T(8,128)S(1)}, u32[]{:S(2)}, u32[]{:S(2)}) collective-permute-start(f32[105,128]{1,0:T(8,128)S(1)} %add.324), channel_id=1, source_target_pairs={{0,4},{1,5},{2,6},{3,7},{4,0},{5,1},{6,2},{7,3},{8,12},{9,13},{10,... | collective-permute-start | bytes 161288 | tf_op jit(solution)/shard_map/ppermute | solution.py:924
  453.6 15.5 %collective-permute-start.27 = (f32[105,128]{1,0:T(8,128)S(1)}, f32[105,128]{1,0:T(8,128)S(1)}, u32[]{:S(2)}, u32[]{:S(2)}) collective-permute-start(f32[105,128]{1,0:T(8,128)S(1)} %add.325), channel_id=1, source_target_pairs={{0,2},{1,3},{2,0},{3,1},{4,6},{5,7},{6,4},{7,5},{8,10},{9,11},{10,... | collective-permute-start | bytes 161288 | tf_op jit(solution)/shard_map/ppermute | solution.py:924
  (45 other events, 482.4 us)

commit v6 on v5

--- a/solution.py
+++ b/solution.py
@@ -74,7 +74,7 @@
     return part * (experts * share) + route * share + (rank - part * share)
 
 
-def slots_kernel(experts, capacity, route_col, route_row, cot, slot_col, slot_row, sending):
+def slots_kernel(experts, capacity, route_col, route_row, cot, slot_col, flat_col, slot_row, sending):
     padded = -(-experts // LANES) * LANES
     picked = (
         lax.broadcasted_iota(jnp.int32, (TOK, padded), 1) == route_col[...]
@@ -93,6 +93,7 @@
     counts = dot(from_t, picked) * picked.astype(F32)
     rank = jnp.sum(counts, axis=1, keepdims=True).astype(jnp.int32) - 1
     slot_col[...] = place_in_buffers(route_col[...], rank, experts, capacity)
+    flat_col[...] = route_col[...] * capacity + rank
     counts_t = dot(picked_t, upto) * picked_t.astype(F32)
     rank_row = jnp.sum(counts_t, axis=0, keepdims=True).astype(jnp.int32) - 1
     slot_row[...] = place_in_buffers(route_row[...], rank_row, experts, capacity)
@@ -116,6 +117,7 @@
     return pl.pallas_call(
         functools.partial(slots_kernel, experts, capacity),
         out_shape=(
+            jax.ShapeDtypeStruct((TOK, 1), jnp.int32),
             jax.ShapeDtypeStruct((TOK, 1), jnp.int32),
             jax.ShapeDtypeStruct((1, TOK), jnp.int32),
             jax.ShapeDtypeStruct((total, D), BF),
@@ -587,7 +589,7 @@
             at = slice(first, first + chunk)
             sources = slice(first // share, first // share + per)
             rounded = acc_r[at, :].astype(BF)
-            result[at, :] = rounded
+            result[sources] = rounded.reshape(per, share, D)
             probs = router_softmax(x[at, :], router[...], experts)
             lane = lax.broadcasted_iota(jnp.int32, probs.shape, 1)
             here = lane == mine[0, 0]
@@ -604,12 +606,13 @@
         grad_router[...] = total_router
 
 
-def run_expert(part, x, c, w_first, w_second, router, router_t, mine, experts):
+def run_expert(part, x, c, w_first, w_second, router, router_t, mine, experts, results=None):
     rows = x.shape[0]
     hidden_size = w_first.shape[1]
     lanes = router.shape[1]
     sources, capacity = c.shape[:2]
     half = pl.BlockSpec((sources, capacity // HALVES, D), lambda f: (0, part, 0))
+    chained = () if results is None else (results,)
     return pl.pallas_call(
         functools.partial(expert_kernel, experts),
         grid=(hidden_size // EXPERT_TILE,),
@@ -621,11 +624,12 @@
             whole((D, lanes)),
             whole((lanes, D)),
             pl.BlockSpec(memory_space=pltpu.SMEM),
-        ],
+        ]
+        + [pl.BlockSpec(memory_space=pl.ANY)] * len(chained),
         out_specs=[
             pl.BlockSpec((rows, EXPERT_TILE), lambda f: (0, f)),
             pl.BlockSpec((rows, EXPERT_TILE), lambda f: (0, f)),
-            whole((rows, D)),
+            half,
             whole((rows, D)),
             whole((rows, 1)),
             whole((D, lanes)),
@@ -633,18 +637,19 @@
         out_shape=[
             jax.ShapeDtypeStruct((rows, hidden_size), BF),
             jax.ShapeDtypeStruct((rows, hidden_size), BF),
-            jax.ShapeDtypeStruct((rows, D), BF),
+            jax.ShapeDtypeStruct(c.shape, BF),
             jax.ShapeDtypeStruct((rows, D), BF),
             jax.ShapeDtypeStruct((rows, 1), F32),
             jax.ShapeDtypeStruct((D, lanes), F32),
         ],
         scratch_shapes=[pltpu.VMEM((rows, D), F32), pltpu.VMEM((rows, D), F32)],
+        input_output_aliases={7: 2} if chained else {},
         compiler_params=params(("arbitrary",)),
         cost_estimate=cost(
             8 * rows * D * hidden_size, 4 * rows * hidden_size + 4 * D * hidden_size
         ),
         name="expert",
-    )(x, c, w_first, w_second, router, router_t, mine)
+    )(x, c, w_first, w_second, router, router_t, mine, *chained)
 
 
 def expert_weights_kernel(parts, side, *refs):
@@ -887,36 +892,46 @@
     )(g_left, g_right, left, right, tokens, gain, grad_middle)
 
 
-def weights_back_kernel(turned, grads, context, grad_attn, out):
-    last = pl.num_programs(0) - 1
-
-    @pl.when(pl.program_id(0) < last)
+def weights_back_kernel(steps, turned, grads, *refs):
+    if len(refs) == 1:
+        refs[0][...] = dot(turned[...], grads[...])
+        return
+    context, grad_attn, out = refs
+
+    @pl.when(pl.program_id(0) < steps)
     def _():
         out[...] = dot(turned[...], grads[...])
 
-    @pl.when(pl.program_id(0) == last)
+    @pl.when(pl.program_id(0) >= steps)
     def _():
         out[...] = dot(context[...], grad_attn[...], 0, 0)
 
 
-def weights_back(half, turned, grads, context, grad_attn):
+def weights_back(turned, grads, *others):
     steps = grads.shape[1] // SIDE
-    columns = (steps + 1) * SIDE
+    more = others[1].shape[1] // SIDE if others else 0
+    columns = (steps + more) * SIDE
     return pl.pallas_call(
-        weights_back_kernel,
-        grid=(steps + 1,),
+        functools.partial(weights_back_kernel, steps),
+        grid=(steps + more,),
         in_specs=[
             whole(turned.shape),
             pl.BlockSpec((TOK, SIDE), lambda c: (0, jnp.minimum(c, steps - 1))),
-            whole((TOK, D)),
-            pl.BlockSpec((TOK, SIDE), lambda c: (0, half)),
-        ],
+        ]
+        + (
+            [
+                whole((TOK, D)),
+                pl.BlockSpec((TOK, SIDE), lambda c: (0, jnp.maximum(c - steps, 0))),
+            ]
+            if others
+            else []
+        ),
         out_specs=pl.BlockSpec((D, SIDE), lambda c: (0, c)),
         out_shape=jax.ShapeDtypeStruct((D, columns), F32),
         compiler_params=params(("arbitrary",)),
         cost_estimate=cost(2 * TOK * D * columns, 2 * TOK * (D + columns) + 4 * D * columns),
         name="weights_back",
-    )(turned, grads, context, grad_attn)
+    )(turned, grads, *others)
 
 
 def swap(block, axis, bit):
@@ -1062,7 +1077,7 @@
     for at in range(rest):
         left, right = gather_step(left, first[at]), gather_step(right, second[at])
     left, right = lax.optimization_barrier((left, right, *early))[:2]
-    slot_col, slot_row, sending_cot = make_slots(
+    slot_col, flat_col, slot_row, sending_cot = make_slots(
         after(routes, left), cotangent, experts, capacity
     )
     left = gather_step(left, first[rest])
@@ -1089,8 +1104,10 @@
 
     cots = exchange(after(sending_cot, left, right))
     if paired:
+        third_cut = second_cut + second_cut // 3
         other_first = swap(after(own_first, left, right), "dp", 1)
-        late = swap(after(own_second[second_cut:], other_first), "dp", 1)
+        early.append(swap(after(own_second[second_cut:third_cut], left, right), "dp", 1))
+        late = swap(after(own_second[third_cut:], other_first), "dp", 1)
         other_second = jnp.concatenate([*early, late], axis=0)
         early.append(other_first)
     else:
@@ -1114,14 +1131,13 @@
     sending[1] = after(sending[1], w_first, w_second)
     rows_in = [exchange(part).reshape(-1, D) for part in sending]
     mine = lax.axis_index("expert").astype(jnp.int32).reshape(1, 1)
-    acts, dhs, results, grads, gates, router_parts = zip(
-        *(
-            run_expert(
-                part, rows, cots, w_first, w_second, full_router, router_t, mine, experts
-            )
-            for part, rows in enumerate(rows_in)
+    runs, results = [], None
+    for part, rows in enumerate(rows_in):
+        act, dh, results, *others = run_expert(
+            part, rows, cots, w_first, w_second, full_router, router_t, mine, experts, results
         )
-    )
+        runs.append((act, dh, *others))
+    acts, dhs, grads, gates, router_parts = zip(*runs)
     grads_home = [exchange(part).reshape(-1, D) for part in grads]
     weight_parts = expert_weights(
         rows_in,
@@ -1133,10 +1149,7 @@
     )
     half = len(weight_parts) // 2
     grad_first, grad_second = weight_parts[:half], weight_parts[half:]
-    results_home = []
-    for part in results:
-        part = after(part, *grads_home, *weight_parts, *results_home)
-        results_home.append(exchange(part).reshape(-1, D))
+    results_home = exchange(after(results, *grads_home, *weight_parts)).reshape(-1, D)
     grads_home[0] = after(grads_home[0], *weight_parts)
     grad_middle, grad_attn, grad_context, grad_gain_f = middle_back(
         grads_home, slot_col, middle, cotangent, ffn_gain, left, right
@@ -1149,13 +1162,10 @@
         )
 
     g_left, tiles_left, diagonals_left = back(0)
-    left_block = scatter_start(weights_back(0, turned, g_left, context, grad_attn))
-    g_right, tiles_right, diagonals_right = back(1, left_block, results_home[0])
-    left_block = after(left_block, results_home[0])
+    left_block = scatter_start(weights_back(turned, g_left, context, grad_attn))
+    g_right, tiles_right, diagonals_right = back(1, left_block)
     first_halves, second_halves = receive_dp(grad_first), receive_dp(grad_second)
-    grad_right = weights_back(
-        1, turned, after(g_right, results_home[1]), context, grad_attn
-    )
+    grad_right = weights_back(turned, after(g_right, results_home))
     left_block = scatter_step(left_block, down[0], grad_right)
     right_block = scatter_step(scatter_start(grad_right), down_other[0], second_halves[-1])
     grad_tokens = tokens_back(
@@ -1165,7 +1175,7 @@
     left_block = scatter_step(left_block, down[1], grad_tokens)
     right_block = scatter_step(right_block, down_other[1], grad_tokens)
     beside.append(left_block)
-    mixed = mix(results_home, slot_col, middle, after(gate, left_block, right_block))
+    mixed = mix([results_home], flat_col, middle, after(gate, left_block, right_block))
     near = 2 + len(axis_bits("dp"))
     for place in down[2:near]:
         left_block = scatter_step(left_block, place, mixed, first_halves[-1])
@@ -1178,7 +1188,7 @@
     joined = scatter_step(joined, down[near])
     beside.append(joined)
     dense = scatter_rest(joined, down[near + 1 :])
-    grad_left, grad_right = dense[:, : SPLIT + SIDE], dense[:, SPLIT + SIDE :]
+    grad_left, grad_w_out, grad_right = jnp.split(dense, (SPLIT, SPLIT + D), axis=1)
     tiles = jnp.concatenate([tiles_left, tiles_right], axis=0)
     diagonals = jnp.concatenate([diagonals_left, diagonals_right], axis=0)
     grad_router = sum(router_parts)[:, :experts]
@@ -1188,9 +1198,9 @@
         jnp.concatenate(
             [side[:, kind * SIDE : (kind + 1) * SIDE] for side in (grad_left, grad_right)], axis=1
         )
-        for kind in range(4)
+        for kind in range(3)
     ]
-    products = sum(w.astype(F32) * grad for w, grad in zip(kinds[:3], grad_weights[:3]))
+    products = sum(w.astype(F32) * grad for w, grad in zip(kinds[:3], grad_weights))
     grad_gain_a = jnp.sum(products, axis=1) / gain_attn.astype(F32)
 
     sizes = (D * experts, D, BUCKETS * HEADS)
@@ -1214,6 +1224,7 @@
         mixed,
         grad_tokens,
         *grad_weights,
+        grad_w_out,
         own(grad_table.reshape(BUCKETS, HEADS), table_height, lax.axis_index("dp")),
         grad_gain_a,
         own(grad_gain_f, shard, number),

time: 490 us -> 495 us (1.010)
  waiting for transfers between devices: 80.8 us -> 88.1 us
  starting transfers between devices: 88.5 us -> 83.2 us
    all_to_all x7 -> x6, starting transfers between devices: 58.6 us -> 49.3 us  [exchange(): lax.all_to_all(rows.reshape(experts, -1, D), 'expert', split_axis=0, conc...]
    ppermute x29 -> x30, waiting for transfers between devices: 74.6 us -> 79.4 us  [swap(): lax.ppermute(block, axis, [(place, place ^ bit) for place in range(size)])]
    unnamed x81 -> x86, local copies, waits for them, and re-layouts: 9.08 us -> 13.1 us
    ppermute x29 -> x30, starting transfers between devices: 29.9 us -> 33.8 us  [swap(): lax.ppermute(block, axis, [(place, place ^ bit) for place in range(size)])]
  transfers between devices with their start and end apart: 36 -> 36, of which waited for: 16 -> 15; matrix products, arithmetic and copies ran while one was open for 13% -> 14% of each run, Pallas kernels for 50% -> 49%
where the time goes in v6:
time: 495 us; the launch traced here: 487 us
  Pallas kernels  240 us (48%)
  waiting for transfers between devices  88.1 us (18%)
  starting transfers between devices  83.2 us (17%)
  other arithmetic  47.5 us (10%)
  local copies, waits for them, and re-layouts  25.7 us (5%)
    ppermute x30, waiting for transfers between devices, swap(): lax.ppermute(block, axis, [(place, place ^ bit) for place in range(size)])  79.4 us
    pallas_call x2, Pallas kernels, run_expert(): pl.pallas_call(functools.partial(expert_kernel, experts), grid=(hidden_si...  68.9 us
    all_to_all x6, starting transfers between devices, exchange(): lax.all_to_all(rows.reshape(experts, -1, D), 'expert', split_axis=0, conc...  49.3 us
    pallas_call x2, Pallas kernels, attend_back(): pl.pallas_call(attend_back_kernel, grid=(SIDE_PAIRS,), in_specs=[*(pl.Blo...  45.9 us
    ppermute x30, starting transfers between devices, swap(): lax.ppermute(block, axis, [(place, place ^ bit) for place in range(size)])  33.8 us
    pallas_call x1, Pallas kernels, expert_weights(): pl.pallas_call(functools.partial(expert_weights_kernel, parts, side is no...  31.2 us
    pallas_call x1, Pallas kernels, attend(): pl.pallas_call(attend_kernel, grid=(PAIRS,), in_specs=[*(pl.BlockSpec((TO...  21.8 us
    pallas_call x2, Pallas kernels, weights_back(): pl.pallas_call(functools.partial(weights_back_kernel, steps), grid=(steps...  15.8 us
  transfers between devices with their start and end apart: 36, of which 15 were waited for; matrix products, arithmetic and copies ran while one was open for 14% of the time, Pallas kernels for 49%

profile of v6, /device:TPU:0, one launch (start us, length us, event | category | flops | bytes accessed | tf_op | source)
XLA Modules:
  0.0 486.9 jit_solution(897169446673253006)
XLA Ops:
  9.0 6.5 %collective-permute-done = bf16[1,1,1,1,1,24,1536]{6,5,4,3,2,1,0:T(8,128)(2,1)S(1)} collective-permute-done((bf16[1,1,1,1,1,24,1536]{6,5,4,3,2,1,0:T(8,128)(2,1)S(1)}, bf16[1,1,1,1,1,24,1536]{6,5,4,3,2,1,0:T(8,128)(2,1)S(1)}, u32[]{:S(2)}, u32[]{:S(2)}) %collective-permute-start) | collective-permute-done | bytes 73760 | tf_op jit(solution)/shard_map/ppermute | solution.py:939
  24.6 6.6 %collective-permute-done.4 = bf16[768,768]{1,0:T(8,128)(2,1)S(1)} collective-permute-done((bf16[768,768]{1,0:T(8,128)(2,1)S(1)}, bf16[768,768]{1,0:T(8,128)(2,1)S(1)}, u32[]{:S(2)}, u32[]{:S(2)}) %collective-permute-start.4) | collective-permute-done | bytes 1179680 | tf_op jit(solution)/shard_map/ppermute | solution.py:939
  35.5 7.8 %slots.1 = (s32[1024,1]{1,0:T(8,128)}, s32[1024,1]{1,0:T(8,128)}, s32[1,1024]{1,0:T(1,128)}, bf16[2048,768]{1,0:T(8,128)(2,1)}) custom-call(s32[1024,1]{1,0:T(8,128)} %copy.49.route_col, s32[1,1024]{1,0:T(1,128)} %bitcast.92, bf16[1024,768]{1,0:T(8,128)(2,1)} %refs_4_.1), custom_call_target="tpu_custom_call" | custom-call | flops 161061280 | bytes 471859 | tf_op jit(solution)/shard_map/slots/pallas_call | solution.py:117
  50.6 7.5 %collective-permute-done.10 = bf16[1,2,2,2,1,24,1536]{6,5,4,3,2,1,0:T(8,128)(2,1)} collective-permute-done((bf16[1,2,2,2,1,24,1536]{6,5,4,3,2,1,0:T(8,128)(2,1)}, bf16[1,2,2,2,1,24,1536]{6,5,4,3,2,1,0:T(8,128)(2,1)}, u32[]{:S(2)}, u32[]{:S(2)}) %collective-permute-start.10) | collective-permute-done | bytes 589856 | tf_op jit(solution)/shard_map/ppermute | solution.py:939
  80.0 8.3 %project.1 = (bf16[768,1024]{1,0:T(8,128)(2,1)}, bf16[1024,2304]{1,0:T(8,128)(2,1)}) custom-call(bf16[1024,768]{1,0:T(8,128)(2,1)} %tokens.3, f32[1,768]{1,0:T(1,128)} %reshape.367.gain, bf16[768,1536]{1,0:T(8,128)(2,1)} %bitcast.69, bf16[768,1664]{1,0:T(8,128)(2,1)} %bitcast.63), custom_call_target="tpu_custom_call" | custom-call | flops 181193936 | bytes 471859 | tf_op jit(solution)/shard_map/project/pallas_call | solution.py:143
  88.3 21.8 %attend.1 = (bf16[1024,768]{1,0:T(8,128)(2,1)}, f32[12,1,1024]{2,1,0:T(1,128)}) custom-call(bf16[1024,2304]{1,0:T(8,128)(2,1)} %get-tuple-element.94.q_ref.k_ref.v_ref, bf16[1024,2304]{1,0:T(8,128)(2,1)} %get-tuple-element.94.q_ref.k_ref.v_ref, bf16[1024,2304]{1,0:T(8,128)(2,1)} %get-tuple-element.94.q_ref.k_ref.v_ref, ...), custom_call_target="tpu_custom_call" | custom-call | flops 966367616 | bytes 393216 | tf_op jit(solution)/shard_map/attend/pallas_call | solution.py:276
  111.7 9.5 %middle.1 = (f32[1024,768]{1,0:T(8,128)}, bf16[1024,768]{1,0:T(8,128)(2,1)}, bf16[1024,768]{1,0:T(8,128)(2,1)}, f32[1024,1]{1,0:T(8,128)}) custom-call(bf16[1024,768]{1,0:T(8,128)(2,1)} %get-tuple-element.95.refs_0_, bf16[1024,768]{1,0:T(8,128)(2,1)} %tokens.3, bf16[768,1536]{1,0:T(8,128)(2,1)} %bitcast.70, bf16[768,1664]{1,0:T(8,128)(2,1)} %bitcast.65, ...), custom_call_target="tpu_custom_call" | custom-call | flops 221459248 | bytes 629145 | tf_op jit(solution)/shard_map/middle/pallas_call | solution.py:514
  121.2 14.3 %collective-permute-done.13 = bf16[256,768]{1,0:T(8,128)(2,1)} collective-permute-done((bf16[256,768]{1,0:T(8,128)(2,1)S(1)}, bf16[256,768]{1,0:T(8,128)(2,1)}, u32[]{:S(2)}, u32[]{:S(2)}) %collective-permute-start.13) | collective-permute-done | bytes 393248 | tf_op jit(solution)/shard_map/ppermute | solution.py:939
  135.6 12.4 %all-to-all-start.2 = ((bf16[16,64,768]{2,1,0:T(8,128)(2,1)}), bf16[16,64,768]{2,1,0:T(8,128)(2,1)S(1)}, u32[]{:S(2)}, u32[]{:S(2)}) async-start(bf16[16,64,768]{2,1,0:T(8,128)(2,1)} %bitcast.88), calls=%async_computation.2 | async-start | bytes 3145728 | tf_op jit(solution)/shard_map/all_to_all | solution.py:1101
  154.6 14.6 %collective-permute-done.14 = bf16[512,768]{1,0:T(8,128)(2,1)S(1)} collective-permute-done((bf16[512,768]{1,0:T(8,128)(2,1)S(1)}, bf16[512,768]{1,0:T(8,128)(2,1)S(1)}, u32[]{:S(2)}, u32[]{:S(2)}) %collective-permute-start.14) | collective-permute-done | bytes 786464 | tf_op jit(solution)/shard_map/ppermute | solution.py:939
  172.1 7.8 %all-to-all-done.2 = bf16[16,64,768]{2,1,0:T(8,128)(2,1)S(1)} async-done(((bf16[16,64,768]{2,1,0:T(8,128)(2,1)}), bf16[16,64,768]{2,1,0:T(8,128)(2,1)S(1)}, u32[]{:S(2)}, u32[]{:S(2)}) %all-to-all-start.2) | async-done | bytes 1572896 | tf_op jit(solution)/shard_map/all_to_all | solution.py:1101
  179.9 9.1 %all-to-all-start = ((bf16[16,64,768]{2,1,0:T(8,128)(2,1)}), bf16[16,64,768]{2,1,0:T(8,128)(2,1)S(1)}, u32[]{:S(2)}, u32[]{:S(2)}) async-start(bf16[16,64,768]{2,1,0:T(8,128)(2,1)} %bitcast.87), calls=%async_computation | async-start | bytes 3145728 | tf_op jit(solution)/shard_map/all_to_all | solution.py:1101
  190.8 34.5 %expert.2 = (bf16[1024,3072]{1,0:T(8,128)(2,1)}, bf16[1024,3072]{1,0:T(8,128)(2,1)}, bf16[16,128,768]{2,1,0:T(8,128)(2,1)}, bf16[1024,768]{1,0:T(8,128)(2,1)}, f32[1024,1]{1,0:T(8,128)}, /*index=5*/f32[768,128]{1,0:T(8,128)}) custom-call(bf16[1024,768]{1,0:T(8,128)(2,1)} %bitcast.81, bf16[16,128,768]{2,1,0:T(8,128)(2,1)} %all-to-all-done.1.c3.refs_9_, ...), custom_call_target="tpu_custom_call" | custom-call | flops 966367616 | bytes 1101004 | tf_op jit(solution)/shard_map/expert/pallas_call | solution.py:616
  231.3 34.5 %expert.3 = (bf16[1024,3072]{1,0:T(8,128)(2,1)}, bf16[1024,3072]{1,0:T(8,128)(2,1)}, bf16[16,128,768]{2,1,0:T(8,128)(2,1)}, bf16[1024,768]{1,0:T(8,128)(2,1)}, f32[1024,1]{1,0:T(8,128)}, /*index=5*/f32[768,128]{1,0:T(8,128)}) custom-call(bf16[1024,768]{1,0:T(8,128)(2,1)} %bitcast.79, ...), custom_call_target="tpu_custom_call", output_to_operand_aliasing={{2}: (7, {})} | custom-call | flops 966367616 | bytes 1101004 | tf_op jit(solution)/shard_map/expert/pallas_call | solution.py:616
  265.8 6.6 %all-to-all-start.4 = ((bf16[16,64,768]{2,1,0:T(8,128)(2,1)}), bf16[16,64,768]{2,1,0:T(8,128)(2,1)S(1)}, u32[]{:S(2)}, u32[]{:S(2)}) async-start(bf16[16,64,768]{2,1,0:T(8,128)(2,1)} %bitcast.89), calls=%async_computation.4 | async-start | bytes 3145728 | tf_op jit(solution)/shard_map/all_to_all | solution.py:1101
  272.4 31.2 %expert_weights.1 = (bf16[384,3072]{1,0:T(8,128)(2,1)}, bf16[384,3072]{1,0:T(8,128)(2,1)}, bf16[1536,768]{1,0:T(8,128)(2,1)}, bf16[1536,768]{1,0:T(8,128)(2,1)}) custom-call(s32[1]{0:T(128)} %bitcast.27.refs_0_, bf16[1024,768]{1,0:T(8,128)(2,1)} %bitcast.82, bf16[1024,768]{1,0:T(8,128)(2,1)} %bitcast.80, f32[1024,1]{1,0:T(8,128)} %get-tuple-element.110.refs_3_, ...), custom_call_target="tpu_custom_call" | custom-call | flops 966367616 | bytes 1730150 | tf_op jit(solution)/shard_map/expert_weights/pallas_call | solution.py:743
  305.5 9.6 %all-to-all-start.5 = ((bf16[16,128,768]{2,1,0:T(8,128)(2,1)}), bf16[16,128,768]{2,1,0:T(8,128)(2,1)}, u32[]{:S(2)}, u32[]{:S(2)}) async-start(bf16[16,128,768]{2,1,0:T(8,128)(2,1)} %get-tuple-element.120), calls=%async_computation.5 | async-start | bytes 6291456 | tf_op jit(solution)/shard_map/all_to_all | solution.py:1101
  318.5 13.0 %middle_back.1 = (f32[1024,768]{1,0:T(8,128)}, bf16[1024,768]{1,0:T(8,128)(2,1)}, bf16[1024,768]{1,0:T(8,128)(2,1)}, f32[1,768]{1,0:T(1,128)}) custom-call(bf16[1024,768]{1,0:T(8,128)(2,1)} %bitcast.83, bf16[1024,768]{1,0:T(8,128)(2,1)} %bitcast.84, s32[1024,1]{1,0:T(8,128)} %get-tuple-element.126.refs_2_, f32[1024,768]{1,0:T(8,128)} %get-tuple-element.122.refs_3_.refs_2_, ...), custom_call_target="tpu_custom_call" | custom-call | flops 221459248 | bytes 629145 | tf_op jit(solution)/shard_map/middle_back/pallas_call | solution.py:816
  331.5 22.9 %attend_back.2 = (bf16[1024,1152]{1,0:T(8,128)(2,1)}, f32[6,8,128]{2,1,0:T(8,128)}, f32[6,1,512]{2,1,0:T(1,128)}) custom-call(bf16[1024,2304]{1,0:T(8,128)(2,1)} %get-tuple-element.94.q_ref.k_ref.v_ref, bf16[1024,2304]{1,0:T(8,128)(2,1)} %get-tuple-element.94.q_ref.k_ref.v_ref, bf16[1024,2304]{1,0:T(8,128)(2,1)} %get-tuple-element.94.q_ref.k_ref.v_ref, ...), custom_call_target="tpu_custom_call" | custom-call | flops 4831838208 | bytes 1887436 | tf_op jit(solution)/shard_map/attend_back/pallas_call | solution.py:418
  354.3 9.6 %weights_back.2 = f32[768,1920]{1,0:T(8,128)} custom-call(bf16[768,1024]{1,0:T(8,128)(2,1)} %get-tuple-element.124.turned, bf16[1024,1152]{1,0:T(8,128)(2,1)} %get-tuple-element.129.grads.g_left, bf16[1024,768]{1,0:T(8,128)(2,1)} %get-tuple-element.95.refs_0_, bf16[1024,768]{1,0:T(8,128)(2,1)} %get-tuple-element.130.refs_1_), custom_call_target="tpu_custom_call" | custom-call | flops 150994944 | bytes 570163 | tf_op jit(solution)/shard_map/weights_back/pallas_call | solution.py:914
  368.3 23.1 %attend_back.3 = (bf16[1024,1152]{1,0:T(8,128)(2,1)}, f32[6,8,128]{2,1,0:T(8,128)}, f32[6,1,512]{2,1,0:T(1,128)}) custom-call(bf16[1024,2304]{1,0:T(8,128)(2,1)} %get-tuple-element.94.q_ref.k_ref.v_ref, bf16[1024,2304]{1,0:T(8,128)(2,1)} %get-tuple-element.94.q_ref.k_ref.v_ref, bf16[1024,2304]{1,0:T(8,128)(2,1)} %get-tuple-element.94.q_ref.k_ref.v_ref, ...), custom_call_target="tpu_custom_call" | custom-call | flops 4831838208 | bytes 1887436 | tf_op jit(solution)/shard_map/attend_back/pallas_call | solution.py:418
  425.2 9.9 %tokens_back.1 = f32[1024,768]{1,0:T(8,128)} custom-call(bf16[1024,1152]{1,0:T(8,128)(2,1)} %get-tuple-element.129.grads.g_left, bf16[1024,1152]{1,0:T(8,128)(2,1)} %get-tuple-element.136.grads.g_right, bf16[768,1536]{1,0:T(8,128)(2,1)} %bitcast.72, bf16[768,1664]{1,0:T(8,128)(2,1)} %bitcast.68, bf16[1024,768]{1,0:T(8,128)(2,1)} %tokens.3, ...), custom_call_target="tpu_custom_call" | custom-call | flops 3623878656 | bytes 12582912 | tf_op jit(solution)/shard_map/tokens_back/pallas_call | solution.py:875
  441.2 9.2 %collective-permute-done.19 = bf16[1,2,2,2,1,24,1152]{6,5,4,3,2,1,0:T(8,128)(2,1)S(1)} collective-permute-done((bf16[1,2,2,2,1,24,1152]{6,5,4,3,2,1,0:T(8,128)(2,1)S(1)}, bf16[1,2,2,2,1,24,1152]{6,5,4,3,2,1,0:T(8,128)(2,1)S(1)}, u32[]{:S(2)}, u32[]{:S(2)}) %collective-permute-start.19) | collective-permute-done | bytes 442400 | tf_op jit(solution)/shard_map/ppermute | solution.py:939
  450.5 8.2 %mix.1 = f32[1024,768]{1,0:T(8,128)} custom-call(bf16[2048,768]{1,0:T(8,128)(2,1)} %bitcast.28.refs_0_, s32[1024,1]{1,0:T(8,128)} %get-tuple-element.121.refs_1_, f32[1024,768]{1,0:T(8,128)} %get-tuple-element.122.refs_3_.refs_2_, f32[1024,1]{1,0:T(8,128)} %get-tuple-element.140.refs_3_), custom_call_target="tpu_custom_call" | custom-call | flops 3221225472 | bytes 9437184 | tf_op jit(solution)/shard_map/mix/pallas_call | solution.py:853
  (272 shorter events, 146.8 us)
Async XLA Ops:
  2.1 29.0 %collective-permute-start.4 = (bf16[768,768]{1,0:T(8,128)(2,1)S(1)}, bf16[768,768]{1,0:T(8,128)(2,1)S(1)}, u32[]{:S(2)}, u32[]{:S(2)}) collective-permute-start(bf16[768,768]{1,0:T(8,128)(2,1)S(1)} %slice_bitcast_fusion), channel_id=1, source_target_pairs={{0,16},{16,0},{1,17},{17,1},{2,18},{18,2},{3,19},{19,3},{4,20},{20... | collective-permute-start | bytes 3538952 | tf_op jit(solution)/shard_map/ppermute | solution.py:939
  8.6 24.3 %collective-permute-start.7 = (bf16[16,12]{1,0:T(8,128)(2,1)S(1)}, bf16[16,12]{1,0:T(8,128)(2,1)S(1)}, u32[]{:S(2)}, u32[]{:S(2)}) collective-permute-start(bf16[16,12]{1,0:T(8,128)(2,1)S(1)} %copy-done.26), channel_id=1, source_target_pairs={{0,16},{16,0},{1,17},{17,1},{2,18},{18,2},{3,19},{19,3},{4,20},{20... | collective-permute-start | bytes 1160 | tf_op jit(solution)/shard_map/ppermute | solution.py:939
  31.2 12.1 %collective-permute-start.9 = (bf16[1,2,2,1,1,24,1536]{6,5,4,3,2,1,0:T(8,128)(2,1)S(1)}, bf16[1,2,2,1,1,24,1536]{6,5,4,3,2,1,0:T(8,128)(2,1)S(1)}, u32[]{:S(2)}, u32[]{:S(2)}) collective-permute-start(bf16[1,2,2,1,1,24,1536]{6,5,4,3,2,1,0:T(8,128)(2,1)S(1)} %pad_maximum_fusion.10), channel_id=1, source_target_pairs={{0,2},{1,3},{2,0},{3,1},{4,6},{5,7},{6,4},{7,5},{8,10},{9,11},{10,... | collective-permute-start | bytes 884744 | tf_op jit(solution)/shard_map/ppermute | solution.py:939
  44.2 13.9 %collective-permute-start.10 = (bf16[1,2,2,2,1,24,1536]{6,5,4,3,2,1,0:T(8,128)(2,1)}, bf16[1,2,2,2,1,24,1536]{6,5,4,3,2,1,0:T(8,128)(2,1)}, u32[]{:S(2)}, u32[]{:S(2)}) collective-permute-start(bf16[1,2,2,2,1,24,1536]{6,5,4,3,2,1,0:T(8,128)(2,1)} %pad_maximum_fusion.8), channel_id=1, source_target_pairs={{0,16},{16,0},{1,17},{17,1},{2,18},{18,2},{3,19},{19,3},{4,20},{20... | collective-permute-start | bytes 1769480 | tf_op jit(solution)/shard_map/ppermute | solution.py:939
  44.9 15.4 %collective-permute-start.6 = (bf16[2,2,2,1,1,24,1664]{6,5,4,3,2,1,0:T(8,128)(2,1)S(1)}, bf16[2,2,2,1,1,24,1664]{6,5,4,3,2,1,0:T(8,128)(2,1)S(1)}, u32[]{:S(2)}, u32[]{:S(2)}) collective-permute-start(bf16[2,2,2,1,1,24,1664]{6,5,4,3,2,1,0:T(8,128)(2,1)S(1)} %pad_maximum_fusion.7), channel_id=1, source_target_pairs={{0,2},{1,3},{2,0},{3,1},{4,6},{5,7},{6,4},{7,5},{8,10},{9,11},{10,... | collective-permute-start | bytes 1916936 | tf_op jit(solution)/shard_map/ppermute | solution.py:939
  67.4 68.2 %all-to-all-start.1 = ((bf16[16,128,768]{2,1,0:T(8,128)(2,1)}), bf16[16,128,768]{2,1,0:T(8,128)(2,1)}, u32[]{:S(2)}, u32[]{:S(2)}) async-start(bf16[16,128,768]{2,1,0:T(8,128)(2,1)} %bitcast.85), calls=%async_computation.1 | async-start | bytes 6291456 | tf_op jit(solution)/shard_map/all_to_all | solution.py:1101
  73.1 62.5 %collective-permute-start.12 = (bf16[384,3072]{1,0:T(8,128)(2,1)}, bf16[384,3072]{1,0:T(8,128)(2,1)}, u32[]{:S(2)}, u32[]{:S(2)}) collective-permute-start(bf16[384,3072]{1,0:T(8,128)(2,1)} %bitcast.86), channel_id=1, source_target_pairs={{0,16},{16,0},{1,17},{17,1},{2,18},{18,2},{3,19},{19,3},{4,20},{20... | collective-permute-start | bytes 7077896 | tf_op jit(solution)/shard_map/ppermute | solution.py:939
  76.9 58.6 %collective-permute-start.13 = (bf16[256,768]{1,0:T(8,128)(2,1)S(1)}, bf16[256,768]{1,0:T(8,128)(2,1)}, u32[]{:S(2)}, u32[]{:S(2)}) collective-permute-start(bf16[256,768]{1,0:T(8,128)(2,1)S(1)} %slice_bitcast_fusion.2), channel_id=1, source_target_pairs={{0,16},{16,0},{1,17},{17,1},{2,18},{18,2},{3,19},{19,3},{4,20},{20... | collective-permute-start | bytes 1179656 | tf_op jit(solution)/shard_map/ppermute | solution.py:939
  135.6 44.3 %all-to-all-start.2 = ((bf16[16,64,768]{2,1,0:T(8,128)(2,1)}), bf16[16,64,768]{2,1,0:T(8,128)(2,1)S(1)}, u32[]{:S(2)}, u32[]{:S(2)}) async-start(bf16[16,64,768]{2,1,0:T(8,128)(2,1)} %bitcast.88), calls=%async_computation.2 | async-start | bytes 3145728 | tf_op jit(solution)/shard_map/all_to_all | solution.py:1101
  149.2 19.9 %collective-permute-start.14 = (bf16[512,768]{1,0:T(8,128)(2,1)S(1)}, bf16[512,768]{1,0:T(8,128)(2,1)S(1)}, u32[]{:S(2)}, u32[]{:S(2)}) collective-permute-start(bf16[512,768]{1,0:T(8,128)(2,1)S(1)} %slice_bitcast_fusion.1), channel_id=1, source_target_pairs={{0,16},{16,0},{1,17},{17,1},{2,18},{18,2},{3,19},{19,3},{4,20},{20... | collective-permute-start | bytes 2359304 | tf_op jit(solution)/shard_map/ppermute | solution.py:939
  179.9 45.4 %all-to-all-start = ((bf16[16,64,768]{2,1,0:T(8,128)(2,1)}), bf16[16,64,768]{2,1,0:T(8,128)(2,1)S(1)}, u32[]{:S(2)}, u32[]{:S(2)}) async-start(bf16[16,64,768]{2,1,0:T(8,128)(2,1)} %bitcast.87), calls=%async_computation | async-start | bytes 3145728 | tf_op jit(solution)/shard_map/all_to_all | solution.py:1101
  225.3 40.5 %all-to-all-start.3 = ((bf16[16,64,768]{2,1,0:T(8,128)(2,1)}), bf16[16,64,768]{2,1,0:T(8,128)(2,1)S(1)}, u32[]{:S(2)}, u32[]{:S(2)}) async-start(bf16[16,64,768]{2,1,0:T(8,128)(2,1)} %bitcast.90), calls=%async_computation.3 | async-start | bytes 3145728 | tf_op jit(solution)/shard_map/all_to_all | solution.py:1101
  265.8 38.5 %all-to-all-start.4 = ((bf16[16,64,768]{2,1,0:T(8,128)(2,1)}), bf16[16,64,768]{2,1,0:T(8,128)(2,1)S(1)}, u32[]{:S(2)}, u32[]{:S(2)}) async-start(bf16[16,64,768]{2,1,0:T(8,128)(2,1)} %bitcast.89), calls=%async_computation.4 | async-start | bytes 3145728 | tf_op jit(solution)/shard_map/all_to_all | solution.py:1101
  305.5 99.5 %all-to-all-start.5 = ((bf16[16,128,768]{2,1,0:T(8,128)(2,1)}), bf16[16,128,768]{2,1,0:T(8,128)(2,1)}, u32[]{:S(2)}, u32[]{:S(2)}) async-start(bf16[16,128,768]{2,1,0:T(8,128)(2,1)} %get-tuple-element.120), calls=%async_computation.5 | async-start | bytes 6291456 | tf_op jit(solution)/shard_map/all_to_all | solution.py:1101
  316.4 101.7 %collective-permute-start.16 = (bf16[1536,768]{1,0:T(8,128)(2,1)}, bf16[1536,768]{1,0:T(8,128)(2,1)S(1)}, u32[]{:S(2)}, u32[]{:S(2)}) collective-permute-start(bf16[1536,768]{1,0:T(8,128)(2,1)} %get-tuple-element.119), channel_id=1, source_target_pairs={{0,16},{16,0},{1,17},{17,1},{2,18},{18,2},{3,19},{19,3},{4,20},{20... | collective-permute-start | bytes 7077896 | tf_op jit(solution)/shard_map/ppermute | solution.py:939
  317.0 141.7 %collective-permute-start.20 = (bf16[384,3072]{1,0:T(8,128)(2,1)}, bf16[384,3072]{1,0:T(8,128)(2,1)}, u32[]{:S(2)}, u32[]{:S(2)}) collective-permute-start(bf16[384,3072]{1,0:T(8,128)(2,1)} %get-tuple-element.117), channel_id=1, source_target_pairs={{0,16},{16,0},{1,17},{17,1},{2,18},{18,2},{3,19},{19,3},{4,20},{20... | collective-permute-start | bytes 7077896 | tf_op jit(solution)/shard_map/ppermute | solution.py:939
  368.3 47.6 %collective-permute-start.15 = (bf16[2,2,2,2,1,24,1920]{6,5,4,3,2,1,0:T(8,128)(2,1)}, bf16[2,2,2,2,1,24,1920]{6,5,4,3,2,1,0:T(8,128)(2,1)}, u32[]{:S(2)}, u32[]{:S(2)}) collective-permute-start(bf16[2,2,2,2,1,24,1920]{6,5,4,3,2,1,0:T(8,128)(2,1)} %select_convert_fusion.1), channel_id=1, source_target_pairs={{0,1},{1,0},{2,3},{3,2},{4,5},{5,4},{6,7},{7,6},{8,9},{9,8},{10,11... | collective-permute-start | bytes 4423688 | tf_op jit(solution)/shard_map/ppermute | solution.py:939
  404.4 17.7 %collective-permute-start.25 = (f32[105,128]{1,0:T(8,128)S(1)}, f32[105,128]{1,0:T(8,128)S(1)}, u32[]{:S(2)}, u32[]{:S(2)}) collective-permute-start(f32[105,128]{1,0:T(8,128)S(1)} %pad_maximum_fusion.16), channel_id=1, source_target_pairs={{0,16},{16,0},{1,17},{17,1},{2,18},{18,2},{3,19},{19,3},{4,20},{20... | collective-permute-start | bytes 161288 | tf_op jit(solution)/shard_map/ppermute | solution.py:939
  418.1 18.9 %collective-permute-start.18 = (bf16[2,2,2,1,1,24,1920]{6,5,4,3,2,1,0:T(8,128)(2,1)S(1)}, bf16[2,2,2,1,1,24,1920]{6,5,4,3,2,1,0:T(8,128)(2,1)S(1)}, u32[]{:S(2)}, u32[]{:S(2)}) collective-permute-start(bf16[2,2,2,1,1,24,1920]{6,5,4,3,2,1,0:T(8,128)(2,1)S(1)} %select_convert_fusion.3), channel_id=1, source_target_pairs={{0,2},{1,3},{2,0},{3,1},{4,6},{5,7},{6,4},{7,5},{8,10},{9,11},{10,... | collective-permute-start | bytes 2211848 | tf_op jit(solution)/shard_map/ppermute | solution.py:939
  422.1 17.2 %collective-permute-start.26 = (f32[105,128]{1,0:T(8,128)S(1)}, f32[105,128]{1,0:T(8,128)S(1)}, u32[]{:S(2)}, u32[]{:S(2)}) collective-permute-start(f32[105,128]{1,0:T(8,128)S(1)} %add.323), channel_id=1, source_target_pairs={{0,8},{1,9},{2,10},{3,11},{4,12},{5,13},{6,14},{7,15},{8,0},{9,1},... | collective-permute-start | bytes 161288 | tf_op jit(solution)/shard_map/ppermute | solution.py:939
  437.2 13.1 %collective-permute-start.19 = (bf16[1,2,2,2,1,24,1152]{6,5,4,3,2,1,0:T(8,128)(2,1)S(1)}, bf16[1,2,2,2,1,24,1152]{6,5,4,3,2,1,0:T(8,128)(2,1)S(1)}, u32[]{:S(2)}, u32[]{:S(2)}) collective-permute-start(bf16[1,2,2,2,1,24,1152]{6,5,4,3,2,1,0:T(8,128)(2,1)S(1)} %select_convert_fusion.4), channel_id=1, source_target_pairs={{0,16},{16,0},{1,17},{17,1},{2,18},{18,2},{3,19},{19,3},{4,20},{20... | collective-permute-start | bytes 1327112 | tf_op jit(solution)/shard_map/ppermute | solution.py:939
  438.8 21.8 %collective-permute-start.21 = (bf16[1,2,2,1,1,24,1920]{6,5,4,3,2,1,0:T(8,128)(2,1)S(1)}, bf16[1,2,2,1,1,24,1920]{6,5,4,3,2,1,0:T(8,128)(2,1)S(1)}, u32[]{:S(2)}, u32[]{:S(2)}) collective-permute-start(bf16[1,2,2,1,1,24,1920]{6,5,4,3,2,1,0:T(8,128)(2,1)S(1)} %select_convert_fusion.5), channel_id=1, source_target_pairs={{0,16},{16,0},{1,17},{17,1},{2,18},{18,2},{3,19},{19,3},{4,20},{20... | collective-permute-start | bytes 1105928 | tf_op jit(solution)/shard_map/ppermute | solution.py:939
  439.3 21.4 %collective-permute-start.27 = (f32[105,128]{1,0:T(8,128)S(1)}, f32[105,128]{1,0:T(8,128)S(1)}, u32[]{:S(2)}, u32[]{:S(2)}) collective-permute-start(f32[105,128]{1,0:T(8,128)S(1)} %add.324), channel_id=1, source_target_pairs={{0,4},{1,5},{2,6},{3,7},{4,0},{5,1},{6,2},{7,3},{8,12},{9,13},{10,... | collective-permute-start | bytes 161288 | tf_op jit(solution)/shard_map/ppermute | solution.py:939
  460.8 13.6 %collective-permute-start.28 = (f32[105,128]{1,0:T(8,128)S(1)}, f32[105,128]{1,0:T(8,128)S(1)}, u32[]{:S(2)}, u32[]{:S(2)}) collective-permute-start(f32[105,128]{1,0:T(8,128)S(1)} %add.325), channel_id=1, source_target_pairs={{0,2},{1,3},{2,0},{3,1},{4,6},{5,7},{6,4},{7,5},{8,10},{9,11},{10,... | collective-permute-start | bytes 161288 | tf_op jit(solution)/shard_map/ppermute | solution.py:939
  (47 other events, 480.3 us)

commit v7 on v5

--- a/solution.py
+++ b/solution.py
@@ -1158,23 +1158,23 @@
     )
     left_block = scatter_step(left_block, down[0], grad_right)
     right_block = scatter_step(scatter_start(grad_right), down_other[0], second_halves[-1])
+    beside = [left_block]
+    left_block = scatter_step(left_block, down[1])
     grad_tokens = tokens_back(
-        g_left, after(g_right, right_block), left, right, tokens, attn_gain, grad_middle
-    )
-    beside = [left_block]
-    left_block = scatter_step(left_block, down[1], grad_tokens)
+        g_left, after(g_right, right_block, left_block), left, right, tokens, attn_gain, grad_middle
+    )
     right_block = scatter_step(right_block, down_other[1], grad_tokens)
-    beside.append(left_block)
-    mixed = mix(results_home, slot_col, middle, after(gate, left_block, right_block))
+    beside.append(right_block)
     near = 2 + len(axis_bits("dp"))
     for place in down[2:near]:
-        left_block = scatter_step(left_block, place, mixed, first_halves[-1])
+        left_block = scatter_step(left_block, place, right_block, first_halves[-1])
     beside.append(left_block)
     for place in down_other[2:near]:
-        right_block = scatter_step(right_block, place, mixed)
+        right_block = scatter_step(right_block, place)
     joined = jnp.concatenate([left_block, right_block], axis=-1)
     grad_expert_in = add_dp(first_halves, joined)
     grad_expert_out = add_dp(second_halves, joined)
+    mixed = mix(results_home, slot_col, middle, after(gate, joined))
     joined = scatter_step(joined, down[near])
     beside.append(joined)
     dense = scatter_rest(joined, down[near + 1 :])

time: 490 us -> 506 us (1.033)
  waiting for transfers between devices: 80.8 us -> 94.1 us
  starting transfers between devices: 88.5 us -> 94.8 us
    ppermute x29, waiting for transfers between devices: 74.6 us -> 87.9 us  [swap(): lax.ppermute(block, axis, [(place, place ^ bit) for place in range(size)])]
    ppermute x29, starting transfers between devices: 29.9 us -> 36.2 us  [swap(): lax.ppermute(block, axis, [(place, place ^ bit) for place in range(size)])]
  transfers between devices with their start and end apart: 36 -> 36, of which waited for: 16 -> 17; matrix products, arithmetic and copies ran while one was open for 13% -> 12% of each run, Pallas kernels for 50% -> 48%
where the time goes in v7:
time: 506 us; the launch traced here: 498 us
  Pallas kernels  240 us (47%)
  starting transfers between devices  94.8 us (19%)
  waiting for transfers between devices  94.1 us (19%)
  other arithmetic  47.7 us (9%)
  local copies, waits for them, and re-layouts  19.1 us (4%)
    ppermute x29, waiting for transfers between devices, swap(): lax.ppermute(block, axis, [(place, place ^ bit) for place in range(size)])  87.9 us
    pallas_call x2, Pallas kernels, run_expert(): pl.pallas_call(functools.partial(expert_kernel, experts), grid=(hidden_si...  69.1 us
    all_to_all x7, starting transfers between devices, exchange(): lax.all_to_all(rows.reshape(experts, -1, D), 'expert', split_axis=0, conc...  58.7 us
    pallas_call x2, Pallas kernels, attend_back(): pl.pallas_call(attend_back_kernel, grid=(SIDE_PAIRS,), in_specs=[*(pl.Blo...  45.7 us
    ppermute x29, starting transfers between devices, swap(): lax.ppermute(block, axis, [(place, place ^ bit) for place in range(size)])  36.2 us
    pallas_call x1, Pallas kernels, expert_weights(): pl.pallas_call(functools.partial(expert_weights_kernel, parts, side is no...  31.2 us
    pallas_call x1, Pallas kernels, attend(): pl.pallas_call(attend_kernel, grid=(PAIRS,), in_specs=[*(pl.BlockSpec((TO...  21.7 us
    pallas_call x2, Pallas kernels, weights_back(): pl.pallas_call(weights_back_kernel, grid=(steps + 1,), in_specs=[whole(tu...  15.9 us
  transfers between devices with their start and end apart: 36, of which 17 were waited for; matrix products, arithmetic and copies ran while one was open for 12% of the time, Pallas kernels for 48%

profile of v7, /device:TPU:0, one launch (start us, length us, event | category | flops | bytes accessed | tf_op | source)
XLA Modules:
  0.0 498.1 jit_solution(16932895801959014646)
XLA Ops:
  25.9 6.6 %collective-permute-done.4 = bf16[768,768]{1,0:T(8,128)(2,1)S(1)} collective-permute-done((bf16[768,768]{1,0:T(8,128)(2,1)S(1)}, bf16[768,768]{1,0:T(8,128)(2,1)S(1)}, u32[]{:S(2)}, u32[]{:S(2)}) %collective-permute-start.4) | collective-permute-done | bytes 1179680 | tf_op jit(solution)/shard_map/ppermute | solution.py:924
  36.9 7.8 %slots.1 = (s32[1024,1]{1,0:T(8,128)}, s32[1,1024]{1,0:T(1,128)}, bf16[2048,768]{1,0:T(8,128)(2,1)}) custom-call(s32[1024,1]{1,0:T(8,128)} %copy.48.route_col, s32[1,1024]{1,0:T(1,128)} %bitcast.93, bf16[1024,768]{1,0:T(8,128)(2,1)} %refs_4_.1), custom_call_target="tpu_custom_call" | custom-call | flops 161061280 | bytes 471859 | tf_op jit(solution)/shard_map/slots/pallas_call | solution.py:116
  52.0 7.5 %collective-permute-done.10 = bf16[1,2,2,2,1,24,1536]{6,5,4,3,2,1,0:T(8,128)(2,1)} collective-permute-done((bf16[1,2,2,2,1,24,1536]{6,5,4,3,2,1,0:T(8,128)(2,1)}, bf16[1,2,2,2,1,24,1536]{6,5,4,3,2,1,0:T(8,128)(2,1)}, u32[]{:S(2)}, u32[]{:S(2)}) %collective-permute-start.10) | collective-permute-done | bytes 589856 | tf_op jit(solution)/shard_map/ppermute | solution.py:924
  77.2 8.3 %project.1 = (bf16[768,1024]{1,0:T(8,128)(2,1)}, bf16[1024,2304]{1,0:T(8,128)(2,1)}) custom-call(bf16[1024,768]{1,0:T(8,128)(2,1)} %tokens.3, f32[1,768]{1,0:T(1,128)} %reshape.378.gain, bf16[768,1536]{1,0:T(8,128)(2,1)} %bitcast.70, bf16[768,1664]{1,0:T(8,128)(2,1)} %bitcast.64), custom_call_target="tpu_custom_call" | custom-call | flops 181193936 | bytes 471859 | tf_op jit(solution)/shard_map/project/pallas_call | solution.py:141
  85.5 21.7 %attend.1 = (bf16[1024,768]{1,0:T(8,128)(2,1)}, f32[12,1,1024]{2,1,0:T(1,128)}) custom-call(bf16[1024,2304]{1,0:T(8,128)(2,1)} %get-tuple-element.92.q_ref.k_ref.v_ref, bf16[1024,2304]{1,0:T(8,128)(2,1)} %get-tuple-element.92.q_ref.k_ref.v_ref, bf16[1024,2304]{1,0:T(8,128)(2,1)} %get-tuple-element.92.q_ref.k_ref.v_ref, ...), custom_call_target="tpu_custom_call" | custom-call | flops 966367616 | bytes 393216 | tf_op jit(solution)/shard_map/attend/pallas_call | solution.py:274
  108.9 9.5 %middle.1 = (f32[1024,768]{1,0:T(8,128)}, bf16[1024,768]{1,0:T(8,128)(2,1)}, bf16[1024,768]{1,0:T(8,128)(2,1)}, f32[1024,1]{1,0:T(8,128)}) custom-call(bf16[1024,768]{1,0:T(8,128)(2,1)} %get-tuple-element.93.refs_0_.context, bf16[1024,768]{1,0:T(8,128)(2,1)} %tokens.3, bf16[768,1536]{1,0:T(8,128)(2,1)} %bitcast.71, bf16[768,1664]{1,0:T(8,128)(2,1)} %bitcast.66, ...), custom_call_target="tpu_custom_call" | custom-call | flops 221459248 | bytes 629145 | tf_op jit(solution)/shard_map/middle/pallas_call | solution.py:512
  118.4 9.8 %collective-permute-done.12 = bf16[384,3072]{1,0:T(8,128)(2,1)} collective-permute-done((bf16[384,3072]{1,0:T(8,128)(2,1)}, bf16[384,3072]{1,0:T(8,128)(2,1)}, u32[]{:S(2)}, u32[]{:S(2)}) %collective-permute-start.12) | collective-permute-done | bytes 2359328 | tf_op jit(solution)/shard_map/ppermute | solution.py:924
  133.5 15.4 %all-to-all-start.1 = ((bf16[16,64,768]{2,1,0:T(8,128)(2,1)}), bf16[16,64,768]{2,1,0:T(8,128)(2,1)S(1)}, u32[]{:S(2)}, u32[]{:S(2)}) async-start(bf16[16,64,768]{2,1,0:T(8,128)(2,1)} %bitcast.89), calls=%async_computation.1 | async-start | bytes 3145728 | tf_op jit(solution)/shard_map/all_to_all | solution.py:1086
  155.1 22.5 %collective-permute-done.13 = bf16[768,768]{1,0:T(8,128)(2,1)S(1)} collective-permute-done((bf16[768,768]{1,0:T(8,128)(2,1)}, bf16[768,768]{1,0:T(8,128)(2,1)S(1)}, u32[]{:S(2)}, u32[]{:S(2)}) %collective-permute-start.13) | collective-permute-done | bytes 1179680 | tf_op jit(solution)/shard_map/ppermute | solution.py:924
  180.9 9.5 %all-to-all-start.3 = ((bf16[16,64,768]{2,1,0:T(8,128)(2,1)}), bf16[16,64,768]{2,1,0:T(8,128)(2,1)S(1)}, u32[]{:S(2)}, u32[]{:S(2)}) async-start(bf16[16,64,768]{2,1,0:T(8,128)(2,1)} %bitcast.88), calls=%async_computation.3 | async-start | bytes 3145728 | tf_op jit(solution)/shard_map/all_to_all | solution.py:1086
  192.2 34.5 %expert.2 = (bf16[1024,3072]{1,0:T(8,128)(2,1)}, bf16[1024,3072]{1,0:T(8,128)(2,1)}, bf16[1024,768]{1,0:T(8,128)(2,1)}, bf16[1024,768]{1,0:T(8,128)(2,1)}, f32[1024,1]{1,0:T(8,128)}, /*index=5*/f32[768,128]{1,0:T(8,128)}) custom-call(bf16[1024,768]{1,0:T(8,128)(2,1)} %bitcast.78, bf16[16,128,768]{2,1,0:T(8,128)(2,1)} %all-to-all-done.c3.refs_9_, ...), custom_call_target="tpu_custom_call" | custom-call | flops 966367616 | bytes 1101004 | tf_op jit(solution)/shard_map/expert/pallas_call | solution.py:613
  232.9 34.6 %expert.3 = (bf16[1024,3072]{1,0:T(8,128)(2,1)}, bf16[1024,3072]{1,0:T(8,128)(2,1)}, bf16[1024,768]{1,0:T(8,128)(2,1)}, bf16[1024,768]{1,0:T(8,128)(2,1)}, f32[1024,1]{1,0:T(8,128)}, /*index=5*/f32[768,128]{1,0:T(8,128)}) custom-call(bf16[1024,768]{1,0:T(8,128)(2,1)} %bitcast.80, bf16[16,128,768]{2,1,0:T(8,128)(2,1)} %all-to-all-done.c3.refs_9_, ...), custom_call_target="tpu_custom_call" | custom-call | flops 966367616 | bytes 1101004 | tf_op jit(solution)/shard_map/expert/pallas_call | solution.py:613
  267.5 6.5 %all-to-all-start.4 = ((bf16[16,64,768]{2,1,0:T(8,128)(2,1)}), bf16[16,64,768]{2,1,0:T(8,128)(2,1)S(1)}, u32[]{:S(2)}, u32[]{:S(2)}) async-start(bf16[16,64,768]{2,1,0:T(8,128)(2,1)} %bitcast.90), calls=%async_computation.4 | async-start | bytes 3145728 | tf_op jit(solution)/shard_map/all_to_all | solution.py:1086
  273.9 31.2 %expert_weights.1 = (bf16[384,3072]{1,0:T(8,128)(2,1)}, bf16[384,3072]{1,0:T(8,128)(2,1)}, bf16[1536,768]{1,0:T(8,128)(2,1)}, bf16[1536,768]{1,0:T(8,128)(2,1)}) custom-call(s32[1]{0:T(128)} %bitcast.26.refs_0_, bf16[1024,768]{1,0:T(8,128)(2,1)} %bitcast.79, bf16[1024,768]{1,0:T(8,128)(2,1)} %bitcast.81, f32[1024,1]{1,0:T(8,128)} %get-tuple-element.106.refs_3_, ...), custom_call_target="tpu_custom_call" | custom-call | flops 966367616 | bytes 1730150 | tf_op jit(solution)/shard_map/expert_weights/pallas_call | solution.py:738
  305.9 9.3 %all-to-all-start.5 = ((bf16[16,64,768]{2,1,0:T(8,128)(2,1)}), bf16[16,64,768]{2,1,0:T(8,128)(2,1)S(1)}, u32[]{:S(2)}, u32[]{:S(2)}) async-start(bf16[16,64,768]{2,1,0:T(8,128)(2,1)} %bitcast.87), calls=%async_computation.5 | async-start | bytes 3145728 | tf_op jit(solution)/shard_map/all_to_all | solution.py:1086
  319.7 12.9 %middle_back.1 = (f32[1024,768]{1,0:T(8,128)}, bf16[1024,768]{1,0:T(8,128)(2,1)}, bf16[1024,768]{1,0:T(8,128)(2,1)}, f32[1,768]{1,0:T(1,128)}) custom-call(bf16[1024,768]{1,0:T(8,128)(2,1)} %bitcast.82, bf16[1024,768]{1,0:T(8,128)(2,1)} %bitcast.83, s32[1024,1]{1,0:T(8,128)} %get-tuple-element.119.refs_2_, f32[1024,768]{1,0:T(8,128)} %get-tuple-element.120.refs_3_, ...), custom_call_target="tpu_custom_call" | custom-call | flops 221459248 | bytes 629145 | tf_op jit(solution)/shard_map/middle_back/pallas_call | solution.py:811
  333.4 22.9 %attend_back.2 = (bf16[1024,1152]{1,0:T(8,128)(2,1)}, f32[6,8,128]{2,1,0:T(8,128)}, f32[6,1,512]{2,1,0:T(1,128)}) custom-call(bf16[1024,2304]{1,0:T(8,128)(2,1)} %get-tuple-element.92.q_ref.k_ref.v_ref, bf16[1024,2304]{1,0:T(8,128)(2,1)} %get-tuple-element.92.q_ref.k_ref.v_ref, bf16[1024,2304]{1,0:T(8,128)(2,1)} %get-tuple-element.92.q_ref.k_ref.v_ref, ...), custom_call_target="tpu_custom_call" | custom-call | flops 4831838208 | bytes 1887436 | tf_op jit(solution)/shard_map/attend_back/pallas_call | solution.py:416
  356.3 7.9 %weights_back.2 = f32[768,1536]{1,0:T(8,128)} custom-call(bf16[768,1024]{1,0:T(8,128)(2,1)} %get-tuple-element.122.turned, bf16[1024,1152]{1,0:T(8,128)(2,1)} %get-tuple-element.126.grads.g_left, bf16[1024,768]{1,0:T(8,128)(2,1)} %get-tuple-element.93.refs_0_.context, bf16[1024,768]{1,0:T(8,128)(2,1)} %get-tuple-element.127.grad_attn), custom_call_target="tpu_custom_call" | custom-call | flops 120795952 | bytes 471859 | tf_op jit(solution)/shard_map/weights_back/pallas_call | solution.py:905
  368.8 6.5 %all-to-all-start.6 = ((bf16[16,64,768]{2,1,0:T(8,128)(2,1)}), bf16[16,64,768]{2,1,0:T(8,128)(2,1)}, u32[]{:S(2)}, u32[]{:S(2)}) async-start(bf16[16,64,768]{2,1,0:T(8,128)(2,1)} %bitcast.29), calls=%async_computation.6 | async-start | bytes 3145728 | tf_op jit(solution)/shard_map/all_to_all | solution.py:1086
  375.4 22.8 %attend_back.3 = (bf16[1024,1152]{1,0:T(8,128)(2,1)}, f32[6,8,128]{2,1,0:T(8,128)}, f32[6,1,512]{2,1,0:T(1,128)}) custom-call(bf16[1024,2304]{1,0:T(8,128)(2,1)} %get-tuple-element.92.q_ref.k_ref.v_ref, bf16[1024,2304]{1,0:T(8,128)(2,1)} %get-tuple-element.92.q_ref.k_ref.v_ref, bf16[1024,2304]{1,0:T(8,128)(2,1)} %get-tuple-element.92.q_ref.k_ref.v_ref, ...), custom_call_target="tpu_custom_call" | custom-call | flops 4831838208 | bytes 1887436 | tf_op jit(solution)/shard_map/attend_back/pallas_call | solution.py:416
  408.0 7.9 %weights_back.3 = f32[768,1536]{1,0:T(8,128)} custom-call(bf16[768,1024]{1,0:T(8,128)(2,1)} %get-tuple-element.122.turned, bf16[1024,1152]{1,0:T(8,128)(2,1)} %get-tuple-element.134.grads.g_right, bf16[1024,768]{1,0:T(8,128)(2,1)} %get-tuple-element.93.refs_0_.context, bf16[1024,768]{1,0:T(8,128)(2,1)} %get-tuple-element.127.grad_attn), custom_call_target="tpu_custom_call" | custom-call | flops 120795952 | bytes 471859 | tf_op jit(solution)/shard_map/weights_back/pallas_call | solution.py:905
  435.6 10.1 %tokens_back.1 = f32[1024,768]{1,0:T(8,128)} custom-call(bf16[1024,1152]{1,0:T(8,128)(2,1)} %get-tuple-element.126.grads.g_left, bf16[1024,1152]{1,0:T(8,128)(2,1)} %get-tuple-element.134.grads.g_right, bf16[768,1536]{1,0:T(8,128)(2,1)} %bitcast.73, bf16[768,1664]{1,0:T(8,128)(2,1)} %bitcast.69, bf16[1024,768]{1,0:T(8,128)(2,1)} %tokens.3, ...), custom_call_target="tpu_custom_call" | custom-call | flops 3623878656 | bytes 12582912 | tf_op jit(solution)/shard_map/tokens_back/pallas_call | solution.py:870
  445.8 8.8 %collective-permute-done.18 = bf16[1,2,2,2,1,24,1536]{6,5,4,3,2,1,0:T(8,128)(2,1)S(1)} collective-permute-done((bf16[1,2,2,2,1,24,1536]{6,5,4,3,2,1,0:T(8,128)(2,1)S(1)}, bf16[1,2,2,2,1,24,1536]{6,5,4,3,2,1,0:T(8,128)(2,1)S(1)}, u32[]{:S(2)}, u32[]{:S(2)}) %collective-permute-start.18) | collective-permute-done | bytes 589856 | tf_op jit(solution)/shard_map/ppermute | solution.py:924
  477.6 8.0 %mix.1 = f32[1024,768]{1,0:T(8,128)} custom-call(bf16[1024,768]{1,0:T(8,128)(2,1)} %bitcast.86, bf16[1024,768]{1,0:T(8,128)(2,1)} %bitcast.30.refs_1_, s32[1024,1]{1,0:T(8,128)} %get-tuple-element.119.refs_2_, f32[1024,768]{1,0:T(8,128)} %get-tuple-element.120.refs_3_, f32[1024,1]{1,0:T(8,128)} %get-tuple-element.138.refs_4_), custom_call_target="tpu_custom_call" | custom-call | flops 3221225472 | bytes 9437184 | tf_op jit(solution)/shard_map/mix/pallas_call | solution.py:848
  (262 shorter events, 153.5 us)
Async XLA Ops:
  3.6 29.0 %collective-permute-start.4 = (bf16[768,768]{1,0:T(8,128)(2,1)S(1)}, bf16[768,768]{1,0:T(8,128)(2,1)S(1)}, u32[]{:S(2)}, u32[]{:S(2)}) collective-permute-start(bf16[768,768]{1,0:T(8,128)(2,1)S(1)} %get-tuple-element.191), channel_id=1, source_target_pairs={{0,16},{16,0},{1,17},{17,1},{2,18},{18,2},{3,19},{19,3},{4,20},{20... | collective-permute-start | bytes 3538952 | tf_op jit(solution)/shard_map/ppermute | solution.py:924
  10.0 24.3 %collective-permute-start.7 = (bf16[16,12]{1,0:T(8,128)(2,1)S(1)}, bf16[16,12]{1,0:T(8,128)(2,1)S(1)}, u32[]{:S(2)}, u32[]{:S(2)}) collective-permute-start(bf16[16,12]{1,0:T(8,128)(2,1)S(1)} %copy-done.27), channel_id=1, source_target_pairs={{0,16},{16,0},{1,17},{17,1},{2,18},{18,2},{3,19},{19,3},{4,20},{20... | collective-permute-start | bytes 1160 | tf_op jit(solution)/shard_map/ppermute | solution.py:924
  45.6 13.9 %collective-permute-start.10 = (bf16[1,2,2,2,1,24,1536]{6,5,4,3,2,1,0:T(8,128)(2,1)}, bf16[1,2,2,2,1,24,1536]{6,5,4,3,2,1,0:T(8,128)(2,1)}, u32[]{:S(2)}, u32[]{:S(2)}) collective-permute-start(bf16[1,2,2,2,1,24,1536]{6,5,4,3,2,1,0:T(8,128)(2,1)} %pad_maximum_fusion.8), channel_id=1, source_target_pairs={{0,16},{16,0},{1,17},{17,1},{2,18},{18,2},{3,19},{19,3},{4,20},{20... | collective-permute-start | bytes 1769480 | tf_op jit(solution)/shard_map/ppermute | solution.py:924
  46.2 15.4 %collective-permute-start.6 = (bf16[2,2,2,1,1,24,1664]{6,5,4,3,2,1,0:T(8,128)(2,1)S(1)}, bf16[2,2,2,1,1,24,1664]{6,5,4,3,2,1,0:T(8,128)(2,1)S(1)}, u32[]{:S(2)}, u32[]{:S(2)}) collective-permute-start(bf16[2,2,2,1,1,24,1664]{6,5,4,3,2,1,0:T(8,128)(2,1)S(1)} %pad_maximum_fusion.7), channel_id=1, source_target_pairs={{0,2},{1,3},{2,0},{3,1},{4,6},{5,7},{6,4},{7,5},{8,10},{9,11},{10,... | collective-permute-start | bytes 1916936 | tf_op jit(solution)/shard_map/ppermute | solution.py:924
  68.8 64.8 %all-to-all-start = ((bf16[16,128,768]{2,1,0:T(8,128)(2,1)}), bf16[16,128,768]{2,1,0:T(8,128)(2,1)}, u32[]{:S(2)}, u32[]{:S(2)}) async-start(bf16[16,128,768]{2,1,0:T(8,128)(2,1)} %bitcast.84), calls=%async_computation | async-start | bytes 6291456 | tf_op jit(solution)/shard_map/all_to_all | solution.py:1086
  74.1 54.0 %collective-permute-start.12 = (bf16[384,3072]{1,0:T(8,128)(2,1)}, bf16[384,3072]{1,0:T(8,128)(2,1)}, u32[]{:S(2)}, u32[]{:S(2)}) collective-permute-start(bf16[384,3072]{1,0:T(8,128)(2,1)} %bitcast.85), channel_id=1, source_target_pairs={{0,16},{16,0},{1,17},{17,1},{2,18},{18,2},{3,19},{19,3},{4,20},{20... | collective-permute-start | bytes 7077896 | tf_op jit(solution)/shard_map/ppermute | solution.py:924
  133.5 47.4 %all-to-all-start.1 = ((bf16[16,64,768]{2,1,0:T(8,128)(2,1)}), bf16[16,64,768]{2,1,0:T(8,128)(2,1)S(1)}, u32[]{:S(2)}, u32[]{:S(2)}) async-start(bf16[16,64,768]{2,1,0:T(8,128)(2,1)} %bitcast.89), calls=%async_computation.1 | async-start | bytes 3145728 | tf_op jit(solution)/shard_map/all_to_all | solution.py:1086
  149.1 28.6 %collective-permute-start.13 = (bf16[768,768]{1,0:T(8,128)(2,1)}, bf16[768,768]{1,0:T(8,128)(2,1)S(1)}, u32[]{:S(2)}, u32[]{:S(2)}) collective-permute-start(bf16[768,768]{1,0:T(8,128)(2,1)} %get-tuple-element.99), channel_id=1, source_target_pairs={{0,16},{16,0},{1,17},{17,1},{2,18},{18,2},{3,19},{19,3},{4,20},{20... | collective-permute-start | bytes 3538952 | tf_op jit(solution)/shard_map/ppermute | solution.py:924
  180.9 45.8 %all-to-all-start.3 = ((bf16[16,64,768]{2,1,0:T(8,128)(2,1)}), bf16[16,64,768]{2,1,0:T(8,128)(2,1)S(1)}, u32[]{:S(2)}, u32[]{:S(2)}) async-start(bf16[16,64,768]{2,1,0:T(8,128)(2,1)} %bitcast.88), calls=%async_computation.3 | async-start | bytes 3145728 | tf_op jit(solution)/shard_map/all_to_all | solution.py:1086
  226.7 40.7 %all-to-all-start.2 = ((bf16[16,64,768]{2,1,0:T(8,128)(2,1)}), bf16[16,64,768]{2,1,0:T(8,128)(2,1)S(1)}, u32[]{:S(2)}, u32[]{:S(2)}) async-start(bf16[16,64,768]{2,1,0:T(8,128)(2,1)} %bitcast.91), calls=%async_computation.2 | async-start | bytes 3145728 | tf_op jit(solution)/shard_map/all_to_all | solution.py:1086
  267.5 38.5 %all-to-all-start.4 = ((bf16[16,64,768]{2,1,0:T(8,128)(2,1)}), bf16[16,64,768]{2,1,0:T(8,128)(2,1)S(1)}, u32[]{:S(2)}, u32[]{:S(2)}) async-start(bf16[16,64,768]{2,1,0:T(8,128)(2,1)} %bitcast.90), calls=%async_computation.4 | async-start | bytes 3145728 | tf_op jit(solution)/shard_map/all_to_all | solution.py:1086
  305.9 58.7 %all-to-all-start.5 = ((bf16[16,64,768]{2,1,0:T(8,128)(2,1)}), bf16[16,64,768]{2,1,0:T(8,128)(2,1)S(1)}, u32[]{:S(2)}, u32[]{:S(2)}) async-start(bf16[16,64,768]{2,1,0:T(8,128)(2,1)} %bitcast.87), calls=%async_computation.5 | async-start | bytes 3145728 | tf_op jit(solution)/shard_map/all_to_all | solution.py:1086
  317.7 101.6 %collective-permute-start.16 = (bf16[1536,768]{1,0:T(8,128)(2,1)}, bf16[1536,768]{1,0:T(8,128)(2,1)}, u32[]{:S(2)}, u32[]{:S(2)}) collective-permute-start(bf16[1536,768]{1,0:T(8,128)(2,1)} %get-tuple-element.115), channel_id=1, source_target_pairs={{0,16},{16,0},{1,17},{17,1},{2,18},{18,2},{3,19},{19,3},{4,20},{20... | collective-permute-start | bytes 7077896 | tf_op jit(solution)/shard_map/ppermute | solution.py:924
  318.2 136.6 %collective-permute-start.19 = (bf16[384,3072]{1,0:T(8,128)(2,1)}, bf16[384,3072]{1,0:T(8,128)(2,1)}, u32[]{:S(2)}, u32[]{:S(2)}) collective-permute-start(bf16[384,3072]{1,0:T(8,128)(2,1)} %get-tuple-element.113), channel_id=1, source_target_pairs={{0,16},{16,0},{1,17},{17,1},{2,18},{18,2},{3,19},{19,3},{4,20},{20... | collective-permute-start | bytes 7077896 | tf_op jit(solution)/shard_map/ppermute | solution.py:924
  368.8 47.2 %collective-permute-start.14 = (bf16[2,2,2,2,1,24,1536]{6,5,4,3,2,1,0:T(8,128)(2,1)}, bf16[2,2,2,2,1,24,1536]{6,5,4,3,2,1,0:T(8,128)(2,1)S(1)}, u32[]{:S(2)}, u32[]{:S(2)}) collective-permute-start(bf16[2,2,2,2,1,24,1536]{6,5,4,3,2,1,0:T(8,128)(2,1)} %select_convert_fusion.2), channel_id=1, source_target_pairs={{0,1},{1,0},{2,3},{3,2},{4,5},{5,4},{6,7},{7,6},{8,9},{9,8},{10,11... | collective-permute-start | bytes 3538952 | tf_op jit(solution)/shard_map/ppermute | solution.py:924
  368.8 39.2 %all-to-all-start.6 = ((bf16[16,64,768]{2,1,0:T(8,128)(2,1)}), bf16[16,64,768]{2,1,0:T(8,128)(2,1)}, u32[]{:S(2)}, u32[]{:S(2)}) async-start(bf16[16,64,768]{2,1,0:T(8,128)(2,1)} %bitcast.29), calls=%async_computation.6 | async-start | bytes 3145728 | tf_op jit(solution)/shard_map/all_to_all | solution.py:1086
  404.7 18.7 %collective-permute-start.24 = (f32[105,128]{1,0:T(8,128)}, f32[105,128]{1,0:T(8,128)}, u32[]{:S(2)}, u32[]{:S(2)}) collective-permute-start(f32[105,128]{1,0:T(8,128)} %pad_maximum_fusion.17), channel_id=1, source_target_pairs={{0,16},{16,0},{1,17},{17,1},{2,18},{18,2},{3,19},{19,3},{4,20},{20... | collective-permute-start | bytes 161288 | tf_op jit(solution)/shard_map/ppermute | solution.py:924
  416.4 16.2 %collective-permute-start.15 = (bf16[2,2,2,1,1,24,1536]{6,5,4,3,2,1,0:T(8,128)(2,1)S(1)}, bf16[2,2,2,1,1,24,1536]{6,5,4,3,2,1,0:T(8,128)(2,1)S(1)}, u32[]{:S(2)}, u32[]{:S(2)}) collective-permute-start(bf16[2,2,2,1,1,24,1536]{6,5,4,3,2,1,0:T(8,128)(2,1)S(1)} %select_convert_fusion.4), channel_id=1, source_target_pairs={{0,2},{1,3},{2,0},{3,1},{4,6},{5,7},{6,4},{7,5},{8,10},{9,11},{10,... | collective-permute-start | bytes 1769480 | tf_op jit(solution)/shard_map/ppermute | solution.py:924
  419.2 14.6 %collective-permute-start.17 = (bf16[2,2,2,2,1,24,1536]{6,5,4,3,2,1,0:T(8,128)(2,1)S(1)}, bf16[2,2,2,2,1,24,1536]{6,5,4,3,2,1,0:T(8,128)(2,1)S(1)}, u32[]{:S(2)}, u32[]{:S(2)}) collective-permute-start(bf16[2,2,2,2,1,24,1536]{6,5,4,3,2,1,0:T(8,128)(2,1)S(1)} %select_convert_fusion.1), channel_id=1, source_target_pairs={{0,1},{1,0},{2,3},{3,2},{4,5},{5,4},{6,7},{7,6},{8,9},{9,8},{10,11... | collective-permute-start | bytes 3538952 | tf_op jit(solution)/shard_map/ppermute | solution.py:924
  424.3 32.2 %collective-permute-start.25 = (f32[105,128]{1,0:T(8,128)S(1)}, f32[105,128]{1,0:T(8,128)S(1)}, u32[]{:S(2)}, u32[]{:S(2)}) collective-permute-start(f32[105,128]{1,0:T(8,128)S(1)} %add.323), channel_id=1, source_target_pairs={{0,8},{1,9},{2,10},{3,11},{4,12},{5,13},{6,14},{7,15},{8,0},{9,1},... | collective-permute-start | bytes 161288 | tf_op jit(solution)/shard_map/ppermute | solution.py:924
  432.9 28.2 %collective-permute-start.20 = (bf16[1,2,2,1,1,24,1536]{6,5,4,3,2,1,0:T(8,128)(2,1)S(1)}, bf16[1,2,2,1,1,24,1536]{6,5,4,3,2,1,0:T(8,128)(2,1)S(1)}, u32[]{:S(2)}, u32[]{:S(2)}) collective-permute-start(bf16[1,2,2,1,1,24,1536]{6,5,4,3,2,1,0:T(8,128)(2,1)S(1)} %select_convert_fusion.7), channel_id=1, source_target_pairs={{0,16},{16,0},{1,17},{17,1},{2,18},{18,2},{3,19},{19,3},{4,20},{20... | collective-permute-start | bytes 884744 | tf_op jit(solution)/shard_map/ppermute | solution.py:924
  434.3 20.3 %collective-permute-start.18 = (bf16[1,2,2,2,1,24,1536]{6,5,4,3,2,1,0:T(8,128)(2,1)S(1)}, bf16[1,2,2,2,1,24,1536]{6,5,4,3,2,1,0:T(8,128)(2,1)S(1)}, u32[]{:S(2)}, u32[]{:S(2)}) collective-permute-start(bf16[1,2,2,2,1,24,1536]{6,5,4,3,2,1,0:T(8,128)(2,1)S(1)} %select_convert_fusion.3), channel_id=1, source_target_pairs={{0,16},{16,0},{1,17},{17,1},{2,18},{18,2},{3,19},{19,3},{4,20},{20... | collective-permute-start | bytes 1769480 | tf_op jit(solution)/shard_map/ppermute | solution.py:924
  463.3 22.5 %collective-permute-start.27 = (f32[105,128]{1,0:T(8,128)S(1)}, f32[105,128]{1,0:T(8,128)S(1)}, u32[]{:S(2)}, u32[]{:S(2)}) collective-permute-start(f32[105,128]{1,0:T(8,128)S(1)} %add.325), channel_id=1, source_target_pairs={{0,2},{1,3},{2,0},{3,1},{4,6},{5,7},{6,4},{7,5},{8,10},{9,11},{10,... | collective-permute-start | bytes 161288 | tf_op jit(solution)/shard_map/ppermute | solution.py:924
  464.0 21.7 %collective-permute-start.22 = (bf16[1,2,1,1,1,24,3072]{6,5,4,3,2,1,0:T(8,128)(2,1)S(1)}, bf16[1,2,1,1,1,24,3072]{6,5,4,3,2,1,0:T(8,128)(2,1)S(1)}, u32[]{:S(2)}, u32[]{:S(2)}) collective-permute-start(bf16[1,2,1,1,1,24,3072]{6,5,4,3,2,1,0:T(8,128)(2,1)S(1)} %select_convert_fusion.5), channel_id=1, source_target_pairs={{0,4},{1,5},{2,6},{3,7},{4,0},{5,1},{6,2},{7,3},{8,12},{9,13},{10,... | collective-permute-start | bytes 884744 | tf_op jit(solution)/shard_map/ppermute | solution.py:924
  (44 other events, 491.0 us)

commit v8 on v5

--- a/solution.py
+++ b/solution.py
@@ -1061,7 +1061,7 @@
     rest = len(first) - dp_bits - 2
     for at in range(rest):
         left, right = gather_step(left, first[at]), gather_step(right, second[at])
-    left, right = lax.optimization_barrier((left, right, *early))[:2]
+    left, right = lax.optimization_barrier((left, right, table, *early))[:2]
     slot_col, slot_row, sending_cot = make_slots(
         after(routes, left), cotangent, experts, capacity
     )
@@ -1077,6 +1077,7 @@
         left = gather_step(left, place)
     for place in second[rest + dp_bits : -1]:
         right = gather_step(right, place)
+    ready = (left, right)
     left = after(left, sending_cot)
     right = after(right, query_features, key_features, band)
     left = gather_end(gather_step(left, first[-1]))
@@ -1087,9 +1088,9 @@
             rows.reshape(experts, -1, D), "expert", split_axis=0, concat_axis=0, tiled=True
         )
 
-    cots = exchange(after(sending_cot, left, right))
+    cots = exchange(after(sending_cot, *ready))
     if paired:
-        other_first = swap(after(own_first, left, right), "dp", 1)
+        other_first = swap(after(own_first, *ready), "dp", 1)
         late = swap(after(own_second[second_cut:], other_first), "dp", 1)
         other_second = jnp.concatenate([*early, late], axis=0)
         early.append(other_first)

time: 490 us -> 489 us (level)
    ppermute x29, waiting for transfers between devices: 74.6 us -> 81.2 us  [swap(): lax.ppermute(block, axis, [(place, place ^ bit) for place in range(size)])]
    all_to_all x7, waiting for transfers between devices: 6.29 us -> 0.92 us  [exchange(): lax.all_to_all(rows.reshape(experts, -1, D), 'expert', split_axis=0, conc...]
  transfers between devices with their start and end apart: 36 -> 36, of which waited for: 16 -> 13; matrix products, arithmetic and copies ran while one was open for 13% -> 13% of each run, Pallas kernels for 50% -> 50%
where the time goes in v8:
time: 489 us; the launch traced here: 483 us
  Pallas kernels  240 us (49%)
  starting transfers between devices  90.3 us (18%)
  waiting for transfers between devices  82.1 us (17%)
  other arithmetic  47.6 us (10%)
  local copies, waits for them, and re-layouts  20.2 us (4%)
    ppermute x29, waiting for transfers between devices, swap(): lax.ppermute(block, axis, [(place, place ^ bit) for place in range(size)])  81.2 us
    pallas_call x2, Pallas kernels, run_expert(): pl.pallas_call(functools.partial(expert_kernel, experts), grid=(hidden_si...  68.9 us
    all_to_all x7, starting transfers between devices, exchange(): lax.all_to_all(rows.reshape(experts, -1, D), 'expert', split_axis=0, conc...  57.7 us
    pallas_call x2, Pallas kernels, attend_back(): pl.pallas_call(attend_back_kernel, grid=(SIDE_PAIRS,), in_specs=[*(pl.Blo...  45.7 us
    ppermute x29, starting transfers between devices, swap(): lax.ppermute(block, axis, [(place, place ^ bit) for place in range(size)])  32.6 us
    pallas_call x1, Pallas kernels, expert_weights(): pl.pallas_call(functools.partial(expert_weights_kernel, parts, side is no...  31.1 us
    pallas_call x1, Pallas kernels, attend(): pl.pallas_call(attend_kernel, grid=(PAIRS,), in_specs=[*(pl.BlockSpec((TO...  22.1 us
    pallas_call x2, Pallas kernels, weights_back(): pl.pallas_call(weights_back_kernel, grid=(steps + 1,), in_specs=[whole(tu...  15.9 us
  transfers between devices with their start and end apart: 36, of which 13 were waited for; matrix products, arithmetic and copies ran while one was open for 13% of the time, Pallas kernels for 50%

profile of v8, /device:TPU:0, one launch (start us, length us, event | category | flops | bytes accessed | tf_op | source)
XLA Modules:
  0.0 482.6 jit_solution(1397341087775445909)
XLA Ops:
  10.3 22.3 %collective-permute-done.4 = bf16[16,12]{1,0:T(8,128)(2,1)S(1)} collective-permute-done((bf16[16,12]{1,0:T(8,128)(2,1)S(1)}, bf16[16,12]{1,0:T(8,128)(2,1)S(1)}, u32[]{:S(2)}, u32[]{:S(2)}) %collective-permute-start.4) | collective-permute-done | bytes 416 | tf_op jit(solution)/shard_map/ppermute | solution.py:924
  45.3 7.8 %slots.1 = (s32[1024,1]{1,0:T(8,128)}, s32[1,1024]{1,0:T(1,128)}, bf16[2048,768]{1,0:T(8,128)(2,1)}) custom-call(s32[1024,1]{1,0:T(8,128)} %copy.48.route_col, s32[1,1024]{1,0:T(1,128)} %bitcast.93, bf16[1024,768]{1,0:T(8,128)(2,1)} %refs_4_.1), custom_call_target="tpu_custom_call" | custom-call | flops 161061280 | bytes 471859 | tf_op jit(solution)/shard_map/slots/pallas_call | solution.py:116
  54.7 11.3 %collective-permute-done.10 = bf16[1,2,2,2,1,24,1536]{6,5,4,3,2,1,0:T(8,128)(2,1)S(1)} collective-permute-done((bf16[1,2,2,2,1,24,1536]{6,5,4,3,2,1,0:T(8,128)(2,1)S(1)}, bf16[1,2,2,2,1,24,1536]{6,5,4,3,2,1,0:T(8,128)(2,1)S(1)}, u32[]{:S(2)}, u32[]{:S(2)}) %collective-permute-start.10) | collective-permute-done | bytes 589856 | tf_op jit(solution)/shard_map/ppermute | solution.py:924
  89.3 8.3 %project.1 = (bf16[768,1024]{1,0:T(8,128)(2,1)}, bf16[1024,2304]{1,0:T(8,128)(2,1)}) custom-call(bf16[1024,768]{1,0:T(8,128)(2,1)} %tokens.3, f32[1,768]{1,0:T(1,128)} %reshape.378.gain, bf16[768,1536]{1,0:T(8,128)(2,1)} %bitcast.70, bf16[768,1664]{1,0:T(8,128)(2,1)} %bitcast.64), custom_call_target="tpu_custom_call" | custom-call | flops 181193936 | bytes 471859 | tf_op jit(solution)/shard_map/project/pallas_call | solution.py:141
  97.7 22.1 %attend.1 = (bf16[1024,768]{1,0:T(8,128)(2,1)}, f32[12,1,1024]{2,1,0:T(1,128)}) custom-call(bf16[1024,2304]{1,0:T(8,128)(2,1)} %get-tuple-element.94.q_ref.k_ref.v_ref, bf16[1024,2304]{1,0:T(8,128)(2,1)} %get-tuple-element.94.q_ref.k_ref.v_ref, bf16[1024,2304]{1,0:T(8,128)(2,1)} %get-tuple-element.94.q_ref.k_ref.v_ref, ...), custom_call_target="tpu_custom_call" | custom-call | flops 966367616 | bytes 393216 | tf_op jit(solution)/shard_map/attend/pallas_call | solution.py:274
  121.4 9.5 %middle.1 = (f32[1024,768]{1,0:T(8,128)}, bf16[1024,768]{1,0:T(8,128)(2,1)}, bf16[1024,768]{1,0:T(8,128)(2,1)}, f32[1024,1]{1,0:T(8,128)}) custom-call(bf16[1024,768]{1,0:T(8,128)(2,1)} %get-tuple-element.95.refs_0_.context, bf16[1024,768]{1,0:T(8,128)(2,1)} %tokens.3, bf16[768,1536]{1,0:T(8,128)(2,1)} %bitcast.71, bf16[768,1664]{1,0:T(8,128)(2,1)} %bitcast.66, ...), custom_call_target="tpu_custom_call" | custom-call | flops 221459248 | bytes 629145 | tf_op jit(solution)/shard_map/middle/pallas_call | solution.py:512
  134.1 13.9 %all-to-all-start.1 = ((bf16[16,64,768]{2,1,0:T(8,128)(2,1)}), bf16[16,64,768]{2,1,0:T(8,128)(2,1)S(1)}, u32[]{:S(2)}, u32[]{:S(2)}) async-start(bf16[16,64,768]{2,1,0:T(8,128)(2,1)} %bitcast.89), calls=%async_computation.1 | async-start | bytes 3145728 | tf_op jit(solution)/shard_map/all_to_all | solution.py:1087
  154.2 22.5 %collective-permute-done.13 = bf16[768,768]{1,0:T(8,128)(2,1)S(1)} collective-permute-done((bf16[768,768]{1,0:T(8,128)(2,1)}, bf16[768,768]{1,0:T(8,128)(2,1)S(1)}, u32[]{:S(2)}, u32[]{:S(2)}) %collective-permute-start.13) | collective-permute-done | bytes 1179680 | tf_op jit(solution)/shard_map/ppermute | solution.py:924
  180.0 9.7 %all-to-all-start.3 = ((bf16[16,64,768]{2,1,0:T(8,128)(2,1)}), bf16[16,64,768]{2,1,0:T(8,128)(2,1)S(1)}, u32[]{:S(2)}, u32[]{:S(2)}) async-start(bf16[16,64,768]{2,1,0:T(8,128)(2,1)} %bitcast.88), calls=%async_computation.3 | async-start | bytes 3145728 | tf_op jit(solution)/shard_map/all_to_all | solution.py:1087
  191.5 34.5 %expert.2 = (bf16[1024,3072]{1,0:T(8,128)(2,1)}, bf16[1024,3072]{1,0:T(8,128)(2,1)}, bf16[1024,768]{1,0:T(8,128)(2,1)}, bf16[1024,768]{1,0:T(8,128)(2,1)}, f32[1024,1]{1,0:T(8,128)}, /*index=5*/f32[768,128]{1,0:T(8,128)}) custom-call(bf16[1024,768]{1,0:T(8,128)(2,1)} %bitcast.78, bf16[16,128,768]{2,1,0:T(8,128)(2,1)} %all-to-all-done.c3.refs_9_, ...), custom_call_target="tpu_custom_call" | custom-call | flops 966367616 | bytes 1101004 | tf_op jit(solution)/shard_map/expert/pallas_call | solution.py:613
  226.0 6.3 %all-to-all-start.2 = ((bf16[16,64,768]{2,1,0:T(8,128)(2,1)}), bf16[16,64,768]{2,1,0:T(8,128)(2,1)S(1)}, u32[]{:S(2)}, u32[]{:S(2)}) async-start(bf16[16,64,768]{2,1,0:T(8,128)(2,1)} %bitcast.91), calls=%async_computation.2 | async-start | bytes 3145728 | tf_op jit(solution)/shard_map/all_to_all | solution.py:1087
  232.3 34.5 %expert.3 = (bf16[1024,3072]{1,0:T(8,128)(2,1)}, bf16[1024,3072]{1,0:T(8,128)(2,1)}, bf16[1024,768]{1,0:T(8,128)(2,1)}, bf16[1024,768]{1,0:T(8,128)(2,1)}, f32[1024,1]{1,0:T(8,128)}, /*index=5*/f32[768,128]{1,0:T(8,128)}) custom-call(bf16[1024,768]{1,0:T(8,128)(2,1)} %bitcast.80, bf16[16,128,768]{2,1,0:T(8,128)(2,1)} %all-to-all-done.c3.refs_9_, ...), custom_call_target="tpu_custom_call" | custom-call | flops 966367616 | bytes 1101004 | tf_op jit(solution)/shard_map/expert/pallas_call | solution.py:613
  266.8 6.6 %all-to-all-start.4 = ((bf16[16,64,768]{2,1,0:T(8,128)(2,1)}), bf16[16,64,768]{2,1,0:T(8,128)(2,1)S(1)}, u32[]{:S(2)}, u32[]{:S(2)}) async-start(bf16[16,64,768]{2,1,0:T(8,128)(2,1)} %bitcast.90), calls=%async_computation.4 | async-start | bytes 3145728 | tf_op jit(solution)/shard_map/all_to_all | solution.py:1087
  273.4 31.1 %expert_weights.1 = (bf16[384,3072]{1,0:T(8,128)(2,1)}, bf16[384,3072]{1,0:T(8,128)(2,1)}, bf16[1536,768]{1,0:T(8,128)(2,1)}, bf16[1536,768]{1,0:T(8,128)(2,1)}) custom-call(s32[1]{0:T(128)} %bitcast.26.refs_0_, bf16[1024,768]{1,0:T(8,128)(2,1)} %bitcast.79, bf16[1024,768]{1,0:T(8,128)(2,1)} %bitcast.81, f32[1024,1]{1,0:T(8,128)} %get-tuple-element.108.refs_3_, ...), custom_call_target="tpu_custom_call" | custom-call | flops 966367616 | bytes 1730150 | tf_op jit(solution)/shard_map/expert_weights/pallas_call | solution.py:738
  305.3 9.3 %all-to-all-start.5 = ((bf16[16,64,768]{2,1,0:T(8,128)(2,1)}), bf16[16,64,768]{2,1,0:T(8,128)(2,1)S(1)}, u32[]{:S(2)}, u32[]{:S(2)}) async-start(bf16[16,64,768]{2,1,0:T(8,128)(2,1)} %bitcast.87), calls=%async_computation.5 | async-start | bytes 3145728 | tf_op jit(solution)/shard_map/all_to_all | solution.py:1087
  319.2 12.9 %middle_back.1 = (f32[1024,768]{1,0:T(8,128)}, bf16[1024,768]{1,0:T(8,128)(2,1)}, bf16[1024,768]{1,0:T(8,128)(2,1)}, f32[1,768]{1,0:T(1,128)}) custom-call(bf16[1024,768]{1,0:T(8,128)(2,1)} %bitcast.82, bf16[1024,768]{1,0:T(8,128)(2,1)} %bitcast.83, s32[1024,1]{1,0:T(8,128)} %get-tuple-element.121.refs_2_, f32[1024,768]{1,0:T(8,128)} %get-tuple-element.122.refs_3_, ...), custom_call_target="tpu_custom_call" | custom-call | flops 221459248 | bytes 629145 | tf_op jit(solution)/shard_map/middle_back/pallas_call | solution.py:811
  332.8 22.9 %attend_back.2 = (bf16[1024,1152]{1,0:T(8,128)(2,1)}, f32[6,8,128]{2,1,0:T(8,128)}, f32[6,1,512]{2,1,0:T(1,128)}) custom-call(bf16[1024,2304]{1,0:T(8,128)(2,1)} %get-tuple-element.94.q_ref.k_ref.v_ref, bf16[1024,2304]{1,0:T(8,128)(2,1)} %get-tuple-element.94.q_ref.k_ref.v_ref, bf16[1024,2304]{1,0:T(8,128)(2,1)} %get-tuple-element.94.q_ref.k_ref.v_ref, ...), custom_call_target="tpu_custom_call" | custom-call | flops 4831838208 | bytes 1887436 | tf_op jit(solution)/shard_map/attend_back/pallas_call | solution.py:416
  355.7 7.9 %weights_back.2 = f32[768,1536]{1,0:T(8,128)} custom-call(bf16[768,1024]{1,0:T(8,128)(2,1)} %get-tuple-element.124.turned, bf16[1024,1152]{1,0:T(8,128)(2,1)} %get-tuple-element.128.grads.g_left, bf16[1024,768]{1,0:T(8,128)(2,1)} %get-tuple-element.95.refs_0_.context, bf16[1024,768]{1,0:T(8,128)(2,1)} %get-tuple-element.129.grad_attn), custom_call_target="tpu_custom_call" | custom-call | flops 120795952 | bytes 471859 | tf_op jit(solution)/shard_map/weights_back/pallas_call | solution.py:905
  364.1 6.6 %all-to-all-start.6 = ((bf16[16,64,768]{2,1,0:T(8,128)(2,1)}), bf16[16,64,768]{2,1,0:T(8,128)(2,1)}, u32[]{:S(2)}, u32[]{:S(2)}) async-start(bf16[16,64,768]{2,1,0:T(8,128)(2,1)} %bitcast.29), calls=%async_computation.6 | async-start | bytes 3145728 | tf_op jit(solution)/shard_map/all_to_all | solution.py:1087
  374.9 22.8 %attend_back.3 = (bf16[1024,1152]{1,0:T(8,128)(2,1)}, f32[6,8,128]{2,1,0:T(8,128)}, f32[6,1,512]{2,1,0:T(1,128)}) custom-call(bf16[1024,2304]{1,0:T(8,128)(2,1)} %get-tuple-element.94.q_ref.k_ref.v_ref, bf16[1024,2304]{1,0:T(8,128)(2,1)} %get-tuple-element.94.q_ref.k_ref.v_ref, bf16[1024,2304]{1,0:T(8,128)(2,1)} %get-tuple-element.94.q_ref.k_ref.v_ref, ...), custom_call_target="tpu_custom_call" | custom-call | flops 4831838208 | bytes 1887436 | tf_op jit(solution)/shard_map/attend_back/pallas_call | solution.py:416
  408.5 7.9 %weights_back.3 = f32[768,1536]{1,0:T(8,128)} custom-call(bf16[768,1024]{1,0:T(8,128)(2,1)} %get-tuple-element.124.turned, bf16[1024,1152]{1,0:T(8,128)(2,1)} %get-tuple-element.136.grads.g_right, bf16[1024,768]{1,0:T(8,128)(2,1)} %get-tuple-element.95.refs_0_.context, bf16[1024,768]{1,0:T(8,128)(2,1)} %get-tuple-element.129.grad_attn), custom_call_target="tpu_custom_call" | custom-call | flops 120795952 | bytes 471859 | tf_op jit(solution)/shard_map/weights_back/pallas_call | solution.py:905
  428.6 10.1 %tokens_back.1 = f32[1024,768]{1,0:T(8,128)} custom-call(bf16[1024,1152]{1,0:T(8,128)(2,1)} %get-tuple-element.128.grads.g_left, bf16[1024,1152]{1,0:T(8,128)(2,1)} %get-tuple-element.136.grads.g_right, bf16[768,1536]{1,0:T(8,128)(2,1)} %bitcast.73, bf16[768,1664]{1,0:T(8,128)(2,1)} %bitcast.69, bf16[1024,768]{1,0:T(8,128)(2,1)} %tokens.3, ...), custom_call_target="tpu_custom_call" | custom-call | flops 3623878656 | bytes 12582912 | tf_op jit(solution)/shard_map/tokens_back/pallas_call | solution.py:870
  444.0 8.1 %mix.1 = f32[1024,768]{1,0:T(8,128)} custom-call(bf16[1024,768]{1,0:T(8,128)(2,1)} %bitcast.86, bf16[1024,768]{1,0:T(8,128)(2,1)} %bitcast.30.refs_1_, s32[1024,1]{1,0:T(8,128)} %get-tuple-element.121.refs_2_, f32[1024,768]{1,0:T(8,128)} %get-tuple-element.122.refs_3_, f32[1024,1]{1,0:T(8,128)} %get-tuple-element.140.refs_4_), custom_call_target="tpu_custom_call" | custom-call | flops 3221225472 | bytes 9437184 | tf_op jit(solution)/shard_map/mix/pallas_call | solution.py:848
  473.4 7.0 %collective-permute-done.23 = bf16[1,1,1,1,1,24,3072]{6,5,4,3,2,1,0:T(8,128)(2,1)S(1)} collective-permute-done((bf16[1,1,1,1,1,24,3072]{6,5,4,3,2,1,0:T(8,128)(2,1)S(1)}, bf16[1,1,1,1,1,24,3072]{6,5,4,3,2,1,0:T(8,128)(2,1)S(1)}, u32[]{:S(2)}, u32[]{:S(2)}) %collective-permute-start.23) | collective-permute-done | bytes 147488 | tf_op jit(solution)/shard_map/ppermute | solution.py:924
  (264 shorter events, 124.9 us)
Async XLA Ops:
  3.6 37.7 %collective-permute-start.5 = (bf16[768,768]{1,0:T(8,128)(2,1)S(1)}, bf16[768,768]{1,0:T(8,128)(2,1)S(1)}, u32[]{:S(2)}, u32[]{:S(2)}) collective-permute-start(bf16[768,768]{1,0:T(8,128)(2,1)S(1)} %get-tuple-element.195), channel_id=1, source_target_pairs={{0,16},{16,0},{1,17},{17,1},{2,18},{18,2},{3,19},{19,3},{4,20},{20... | collective-permute-start | bytes 3538952 | tf_op jit(solution)/shard_map/ppermute | solution.py:924
  7.0 27.5 %collective-permute-start.2 = (bf16[1,1,1,1,1,24,1664]{6,5,4,3,2,1,0:T(8,128)(2,1)S(1)}, bf16[1,1,1,1,1,24,1664]{6,5,4,3,2,1,0:T(8,128)(2,1)S(1)}, u32[]{:S(2)}, u32[]{:S(2)}) collective-permute-start(bf16[1,1,1,1,1,24,1664]{6,5,4,3,2,1,0:T(8,128)(2,1)S(1)} %bitcast.92), channel_id=1, source_target_pairs={{0,8},{1,9},{2,10},{3,11},{4,12},{5,13},{6,14},{7,15},{8,0},{9,1},... | collective-permute-start | bytes 239624 | tf_op jit(solution)/shard_map/ppermute | solution.py:924
  9.7 22.9 %collective-permute-start = (bf16[1,1,1,1,1,24,1536]{6,5,4,3,2,1,0:T(8,128)(2,1)S(1)}, bf16[1,1,1,1,1,24,1536]{6,5,4,3,2,1,0:T(8,128)(2,1)S(1)}, u32[]{:S(2)}, u32[]{:S(2)}) collective-permute-start(bf16[1,1,1,1,1,24,1536]{6,5,4,3,2,1,0:T(8,128)(2,1)S(1)} %maximum_bitcast_fusion), channel_id=1, source_target_pairs={{0,8},{1,9},{2,10},{3,11},{4,12},{5,13},{6,14},{7,15},{8,0},{9,1},... | collective-permute-start | bytes 221192 | tf_op jit(solution)/shard_map/ppermute | solution.py:924
  10.0 22.6 %collective-permute-start.4 = (bf16[16,12]{1,0:T(8,128)(2,1)S(1)}, bf16[16,12]{1,0:T(8,128)(2,1)S(1)}, u32[]{:S(2)}, u32[]{:S(2)}) collective-permute-start(bf16[16,12]{1,0:T(8,128)(2,1)S(1)} %copy-done.27), channel_id=1, source_target_pairs={{0,16},{16,0},{1,17},{17,1},{2,18},{18,2},{3,19},{19,3},{4,20},{20... | collective-permute-start | bytes 1160 | tf_op jit(solution)/shard_map/ppermute | solution.py:924
  53.2 12.8 %collective-permute-start.10 = (bf16[1,2,2,2,1,24,1536]{6,5,4,3,2,1,0:T(8,128)(2,1)S(1)}, bf16[1,2,2,2,1,24,1536]{6,5,4,3,2,1,0:T(8,128)(2,1)S(1)}, u32[]{:S(2)}, u32[]{:S(2)}) collective-permute-start(bf16[1,2,2,2,1,24,1536]{6,5,4,3,2,1,0:T(8,128)(2,1)S(1)} %pad_maximum_fusion.8), channel_id=1, source_target_pairs={{0,16},{16,0},{1,17},{17,1},{2,18},{18,2},{3,19},{19,3},{4,20},{20... | collective-permute-start | bytes 1769480 | tf_op jit(solution)/shard_map/ppermute | solution.py:924
  54.0 13.5 %collective-permute-start.7 = (bf16[2,2,2,1,1,24,1664]{6,5,4,3,2,1,0:T(8,128)(2,1)S(1)}, bf16[2,2,2,1,1,24,1664]{6,5,4,3,2,1,0:T(8,128)(2,1)S(1)}, u32[]{:S(2)}, u32[]{:S(2)}) collective-permute-start(bf16[2,2,2,1,1,24,1664]{6,5,4,3,2,1,0:T(8,128)(2,1)S(1)} %pad_maximum_fusion.7), channel_id=1, source_target_pairs={{0,2},{1,3},{2,0},{3,1},{4,6},{5,7},{6,4},{7,5},{8,10},{9,11},{10,... | collective-permute-start | bytes 1916936 | tf_op jit(solution)/shard_map/ppermute | solution.py:924
  67.8 66.3 %all-to-all-start = ((bf16[16,128,768]{2,1,0:T(8,128)(2,1)}), bf16[16,128,768]{2,1,0:T(8,128)(2,1)}, u32[]{:S(2)}, u32[]{:S(2)}) async-start(bf16[16,128,768]{2,1,0:T(8,128)(2,1)} %bitcast.84), calls=%async_computation | async-start | bytes 6291456 | tf_op jit(solution)/shard_map/all_to_all | solution.py:1087
  80.1 54.0 %collective-permute-start.12 = (bf16[384,3072]{1,0:T(8,128)(2,1)}, bf16[384,3072]{1,0:T(8,128)(2,1)}, u32[]{:S(2)}, u32[]{:S(2)}) collective-permute-start(bf16[384,3072]{1,0:T(8,128)(2,1)} %bitcast.85), channel_id=1, source_target_pairs={{0,16},{16,0},{1,17},{17,1},{2,18},{18,2},{3,19},{19,3},{4,20},{20... | collective-permute-start | bytes 7077896 | tf_op jit(solution)/shard_map/ppermute | solution.py:924
  134.1 45.9 %all-to-all-start.1 = ((bf16[16,64,768]{2,1,0:T(8,128)(2,1)}), bf16[16,64,768]{2,1,0:T(8,128)(2,1)S(1)}, u32[]{:S(2)}, u32[]{:S(2)}) async-start(bf16[16,64,768]{2,1,0:T(8,128)(2,1)} %bitcast.89), calls=%async_computation.1 | async-start | bytes 3145728 | tf_op jit(solution)/shard_map/all_to_all | solution.py:1087
  148.1 28.6 %collective-permute-start.13 = (bf16[768,768]{1,0:T(8,128)(2,1)}, bf16[768,768]{1,0:T(8,128)(2,1)S(1)}, u32[]{:S(2)}, u32[]{:S(2)}) collective-permute-start(bf16[768,768]{1,0:T(8,128)(2,1)} %get-tuple-element.101), channel_id=1, source_target_pairs={{0,16},{16,0},{1,17},{17,1},{2,18},{18,2},{3,19},{19,3},{4,20},{20... | collective-permute-start | bytes 3538952 | tf_op jit(solution)/shard_map/ppermute | solution.py:924
  180.0 46.0 %all-to-all-start.3 = ((bf16[16,64,768]{2,1,0:T(8,128)(2,1)}), bf16[16,64,768]{2,1,0:T(8,128)(2,1)S(1)}, u32[]{:S(2)}, u32[]{:S(2)}) async-start(bf16[16,64,768]{2,1,0:T(8,128)(2,1)} %bitcast.88), calls=%async_computation.3 | async-start | bytes 3145728 | tf_op jit(solution)/shard_map/all_to_all | solution.py:1087
  226.0 40.8 %all-to-all-start.2 = ((bf16[16,64,768]{2,1,0:T(8,128)(2,1)}), bf16[16,64,768]{2,1,0:T(8,128)(2,1)S(1)}, u32[]{:S(2)}, u32[]{:S(2)}) async-start(bf16[16,64,768]{2,1,0:T(8,128)(2,1)} %bitcast.91), calls=%async_computation.2 | async-start | bytes 3145728 | tf_op jit(solution)/shard_map/all_to_all | solution.py:1087
  266.8 38.6 %all-to-all-start.4 = ((bf16[16,64,768]{2,1,0:T(8,128)(2,1)}), bf16[16,64,768]{2,1,0:T(8,128)(2,1)S(1)}, u32[]{:S(2)}, u32[]{:S(2)}) async-start(bf16[16,64,768]{2,1,0:T(8,128)(2,1)} %bitcast.90), calls=%async_computation.4 | async-start | bytes 3145728 | tf_op jit(solution)/shard_map/all_to_all | solution.py:1087
  305.3 58.8 %all-to-all-start.5 = ((bf16[16,64,768]{2,1,0:T(8,128)(2,1)}), bf16[16,64,768]{2,1,0:T(8,128)(2,1)S(1)}, u32[]{:S(2)}, u32[]{:S(2)}) async-start(bf16[16,64,768]{2,1,0:T(8,128)(2,1)} %bitcast.87), calls=%async_computation.5 | async-start | bytes 3145728 | tf_op jit(solution)/shard_map/all_to_all | solution.py:1087
  317.1 104.7 %collective-permute-start.15 = (bf16[1536,768]{1,0:T(8,128)(2,1)}, bf16[1536,768]{1,0:T(8,128)(2,1)}, u32[]{:S(2)}, u32[]{:S(2)}) collective-permute-start(bf16[1536,768]{1,0:T(8,128)(2,1)} %get-tuple-element.117), channel_id=1, source_target_pairs={{0,16},{16,0},{1,17},{17,1},{2,18},{18,2},{3,19},{19,3},{4,20},{20... | collective-permute-start | bytes 7077896 | tf_op jit(solution)/shard_map/ppermute | solution.py:924
  318.7 133.4 %collective-permute-start.19 = (bf16[384,3072]{1,0:T(8,128)(2,1)}, bf16[384,3072]{1,0:T(8,128)(2,1)}, u32[]{:S(2)}, u32[]{:S(2)}) collective-permute-start(bf16[384,3072]{1,0:T(8,128)(2,1)} %get-tuple-element.115), channel_id=1, source_target_pairs={{0,16},{16,0},{1,17},{17,1},{2,18},{18,2},{3,19},{19,3},{4,20},{20... | collective-permute-start | bytes 7077896 | tf_op jit(solution)/shard_map/ppermute | solution.py:924
  364.1 44.4 %all-to-all-start.6 = ((bf16[16,64,768]{2,1,0:T(8,128)(2,1)}), bf16[16,64,768]{2,1,0:T(8,128)(2,1)}, u32[]{:S(2)}, u32[]{:S(2)}) async-start(bf16[16,64,768]{2,1,0:T(8,128)(2,1)} %bitcast.29), calls=%async_computation.6 | async-start | bytes 3145728 | tf_op jit(solution)/shard_map/all_to_all | solution.py:1087
  374.3 44.8 %collective-permute-start.14 = (bf16[2,2,2,2,1,24,1536]{6,5,4,3,2,1,0:T(8,128)(2,1)}, bf16[2,2,2,2,1,24,1536]{6,5,4,3,2,1,0:T(8,128)(2,1)S(1)}, u32[]{:S(2)}, u32[]{:S(2)}) collective-permute-start(bf16[2,2,2,2,1,24,1536]{6,5,4,3,2,1,0:T(8,128)(2,1)} %select_convert_fusion.2), channel_id=1, source_target_pairs={{0,1},{1,0},{2,3},{3,2},{4,5},{5,4},{6,7},{7,6},{8,9},{9,8},{10,11... | collective-permute-start | bytes 3538952 | tf_op jit(solution)/shard_map/ppermute | solution.py:924
  407.0 16.6 %collective-permute-start.24 = (f32[105,128]{1,0:T(8,128)}, f32[105,128]{1,0:T(8,128)}, u32[]{:S(2)}, u32[]{:S(2)}) collective-permute-start(f32[105,128]{1,0:T(8,128)} %pad_maximum_fusion.17), channel_id=1, source_target_pairs={{0,16},{16,0},{1,17},{17,1},{2,18},{18,2},{3,19},{19,3},{4,20},{20... | collective-permute-start | bytes 161288 | tf_op jit(solution)/shard_map/ppermute | solution.py:924
  421.9 16.9 %collective-permute-start.17 = (bf16[2,2,2,1,1,24,1536]{6,5,4,3,2,1,0:T(8,128)(2,1)S(1)}, bf16[2,2,2,1,1,24,1536]{6,5,4,3,2,1,0:T(8,128)(2,1)S(1)}, u32[]{:S(2)}, u32[]{:S(2)}) collective-permute-start(bf16[2,2,2,1,1,24,1536]{6,5,4,3,2,1,0:T(8,128)(2,1)S(1)} %select_convert_fusion.4), channel_id=1, source_target_pairs={{0,2},{1,3},{2,0},{3,1},{4,6},{5,7},{6,4},{7,5},{8,10},{9,11},{10,... | collective-permute-start | bytes 1769480 | tf_op jit(solution)/shard_map/ppermute | solution.py:924
  424.5 15.6 %collective-permute-start.25 = (f32[105,128]{1,0:T(8,128)S(1)}, f32[105,128]{1,0:T(8,128)S(1)}, u32[]{:S(2)}, u32[]{:S(2)}) collective-permute-start(f32[105,128]{1,0:T(8,128)S(1)} %add.323), channel_id=1, source_target_pairs={{0,8},{1,9},{2,10},{3,11},{4,12},{5,13},{6,14},{7,15},{8,0},{9,1},... | collective-permute-start | bytes 161288 | tf_op jit(solution)/shard_map/ppermute | solution.py:924
  427.5 16.3 %collective-permute-start.18 = (bf16[1,2,2,2,1,24,1536]{6,5,4,3,2,1,0:T(8,128)(2,1)S(1)}, bf16[1,2,2,2,1,24,1536]{6,5,4,3,2,1,0:T(8,128)(2,1)S(1)}, u32[]{:S(2)}, u32[]{:S(2)}) collective-permute-start(bf16[1,2,2,2,1,24,1536]{6,5,4,3,2,1,0:T(8,128)(2,1)S(1)} %select_convert_fusion.3), channel_id=1, source_target_pairs={{0,16},{16,0},{1,17},{17,1},{2,18},{18,2},{3,19},{19,3},{4,20},{20... | collective-permute-start | bytes 1769480 | tf_op jit(solution)/shard_map/ppermute | solution.py:924
  439.0 13.2 %collective-permute-start.20 = (bf16[1,2,2,1,1,24,1536]{6,5,4,3,2,1,0:T(8,128)(2,1)S(1)}, bf16[1,2,2,1,1,24,1536]{6,5,4,3,2,1,0:T(8,128)(2,1)S(1)}, u32[]{:S(2)}, u32[]{:S(2)}) collective-permute-start(bf16[1,2,2,1,1,24,1536]{6,5,4,3,2,1,0:T(8,128)(2,1)S(1)} %select_convert_fusion.7), channel_id=1, source_target_pairs={{0,16},{16,0},{1,17},{17,1},{2,18},{18,2},{3,19},{19,3},{4,20},{20... | collective-permute-start | bytes 884744 | tf_op jit(solution)/shard_map/ppermute | solution.py:924
  452.4 17.5 %collective-permute-start.27 = (f32[105,128]{1,0:T(8,128)S(1)}, f32[105,128]{1,0:T(8,128)S(1)}, u32[]{:S(2)}, u32[]{:S(2)}) collective-permute-start(f32[105,128]{1,0:T(8,128)S(1)} %add.325), channel_id=1, source_target_pairs={{0,2},{1,3},{2,0},{3,1},{4,6},{5,7},{6,4},{7,5},{8,10},{9,11},{10,... | collective-permute-start | bytes 161288 | tf_op jit(solution)/shard_map/ppermute | solution.py:924
  (45 other events, 494.7 us)
